TPU v7x, 32 devices: a whole 2x2x4 slice. The times are simulated.
32 devices in a mesh: img: 4 (over x, core), vol: 8 (over z, y).
Axes of the slice: x: 2, y: 2, z: 4, core: 2. Of those that a mesh axis runs over, the one named last changes fastest.
Arguments:
- images: bfloat16 [2, 1536, 256, 128], P(None, 'img', 'vol'), may hold values from -6 to 6
- defocus: float32 [1536], P('img'), may hold values from 20 to 200
- candidates: int32 [1536, 8], P('img'), may hold values from 0 to 63, all different within a row
- counts: int32 [1536], P('img'), may hold values from 1 to 8
- noise_weight: float32 [256, 128], P('vol'), may hold values from 0.002 to 0.02
- volume: float32 [2, 256, 256, 128], P(None, 'vol'), may hold values from -6 to 6
- row_plane: int32 [64, 256], replicated, may hold values from 0 to 255
- row_line: int32 [64, 256], replicated, may hold values from 0 to 254
- row_weight: float32 [64, 256], replicated, may hold values from 0 to 1
- regularizer: float32 [256, 256, 128], P('vol', 'img'), may hold values from 0.05 to 0.5
Outputs:
- new_volume: float32 [2, 256, 256, 128], P(None, 'vol', 'img')
Inputs may be any that keep to these rules, and one draw needn't show every extreme that they name: The entries of one row of candidates are distinct; only the first counts entries are used.
All inputs are finite; a program needn't handle non-finite values.
Results may differ from a plain program's by a relative error of at most 0.0066.
Values may be sent and summed in bfloat16 or wider, within the bound.
No kernel may reach another device: no remote copies, remote signals or barrier semaphores. Data moves between devices by JAX's collectives and lax.ppermute only.
A program may use at most 128 MiB of HBM per device.

v0:
```python
import math

import jax
import jax.numpy as jnp
from jax import lax
from jax.sharding import PartitionSpec as P

ROWS = 256
COLS = 128
K = 64
TRANS = 4


AMPLITUDE = 0.1


def contrast_of(defocus, row_freq, col_freq):
    radius_sq = row_freq[:, None] * row_freq[:, None] + col_freq[None, :] * col_freq[None, :]
    angle = defocus[:, None, None] * radius_sq[None]
    return -(math.sqrt(1.0 - AMPLITUDE * AMPLITUDE) * jnp.sin(angle) + AMPLITUDE * jnp.cos(angle))


def shift_phases(row_freq, col_freq, number):
    shift_ids = jnp.arange(number)
    shift_x = (shift_ids % 2).astype(jnp.float32) - 0.5
    shift_y = (shift_ids // 2).astype(jnp.float32) - 0.5
    angle = (
        -2.0
        * math.pi
        * (
            shift_x[:, None, None] * col_freq[None, None, :]
            + shift_y[:, None, None] * row_freq[None, :, None]
        )
    )
    return (jnp.cos(angle), jnp.sin(angle))


def make_references(slices, cosine, sine):
    real_part = slices[0].astype(jnp.float32)
    imag_part = slices[1].astype(jnp.float32)
    shift_re = cosine[:, None] * real_part[None] - sine[:, None] * imag_part[None]
    shift_im = sine[:, None] * real_part[None] + cosine[:, None] * imag_part[None]
    shifted = jnp.stack([shift_re, shift_im], axis=2).astype(jnp.bfloat16)
    power = (real_part * real_part + imag_part * imag_part).astype(jnp.bfloat16)
    return (shifted, power)


def posterior_of(logits, candidates, counts):
    orientation = jnp.arange(logits.shape[2])
    in_list = jnp.arange(candidates.shape[1])[None, :] < counts[:, None]
    listed = jnp.any(
        (candidates[:, :, None] == orientation[None, None, :]) & in_list[:, :, None], axis=1
    )
    allowed = listed[:, None, :]
    masked = jnp.where(allowed, logits, -1e30)
    highest = jnp.max(masked, axis=(1, 2), keepdims=True)
    exponent = jnp.where(allowed, jnp.exp(masked - highest), 0.0)
    return (exponent / jnp.sum(exponent, axis=(1, 2), keepdims=True)).astype(jnp.bfloat16)


def extract_rows(volume, plane_part, line_part, weight_part, slab_id):
    planes_here = volume.shape[1]
    flat = volume.reshape(2, planes_here * ROWS, COLS)
    local_plane = plane_part - slab_id * planes_here
    owned = (local_plane >= 0) & (local_plane < planes_here)
    line_index = jnp.clip(local_plane, 0, planes_here - 1) * ROWS + line_part
    lower = jnp.take(flat, line_index, axis=1)
    upper = jnp.take(flat, line_index + 1, axis=1)
    weight = weight_part[None, :, :, None]
    values = weight * lower + (1.0 - weight) * upper
    rounded = jnp.where(owned[None, :, :, None], values, 0.0).astype(jnp.bfloat16)
    return lax.optimization_barrier(rounded).astype(jnp.float32)


def insert_into(
    carry, piece, planes_all, lines_all, weights_all, slab_id, planes_here, line_first, line_count
):
    orient_count = piece.shape[0]
    number = piece.shape[1]
    local_plane = planes_all - slab_id * planes_here
    local_line = lines_all - line_first
    in_slab = (local_plane >= 0) & (local_plane < planes_here)
    lower_ok = in_slab & (local_line >= 0) & (local_line < line_count)
    upper_ok = in_slab & (local_line + 1 >= 0) & (local_line + 1 < line_count)
    dump_row = planes_here * line_count
    lower_index = jnp.where(lower_ok, local_plane * line_count + local_line, dump_row).reshape(-1)
    upper_index = jnp.where(upper_ok, local_plane * line_count + local_line + 1, dump_row).reshape(
        -1
    )
    values = piece.reshape(orient_count * number, 3 * COLS)
    weight = weights_all.reshape(-1, 1)
    carry = carry.at[lower_index].add(weight * values)
    return carry.at[upper_index].add((1.0 - weight) * values)


def body(
    images,
    defocus,
    candidates,
    counts,
    noise_weight,
    volume,
    row_plane,
    row_line,
    row_weight,
    regularizer,
):
    local_rows = noise_weight.shape[0]
    slab_id = lax.axis_index("vol")
    global_rows = slab_id * local_rows + jnp.arange(local_rows)
    row_freq = (global_rows.astype(jnp.float32) - ROWS // 2) / ROWS
    col_freq = jnp.arange(COLS).astype(jnp.float32) / (2 * COLS)
    img_count = lax.axis_size("img")
    group_id = lax.axis_index("img")
    share = K // img_count
    first = group_id * share
    plane_share = lax.dynamic_slice_in_dim(row_plane, first, share, 0)
    line_share = lax.dynamic_slice_in_dim(row_line, first, share, 0)
    weight_share = lax.dynamic_slice_in_dim(row_weight, first, share, 0)
    masked = extract_rows(volume, plane_share, line_share, weight_share, slab_id)
    own_slices = lax.psum_scatter(
        masked.astype(jnp.bfloat16), "vol", scatter_dimension=2, tiled=True
    )
    slices = lax.all_gather(own_slices, "img", axis=1, tiled=True)
    cosine, sine = shift_phases(row_freq, col_freq, TRANS)
    shifted, power = make_references(slices, cosine, sine)
    contrast = contrast_of(defocus, row_freq, col_freq)
    weighted = ((contrast * noise_weight)[None] * images).astype(jnp.bfloat16)
    squared = (contrast * contrast * noise_weight).astype(jnp.bfloat16)
    cross = jnp.einsum("jbrc,tkjrc->btk", weighted, shifted, preferred_element_type=jnp.float32)
    quadratic = jnp.einsum("brc,krc->bk", squared, power, preferred_element_type=jnp.float32)
    partial_logits = cross - 0.5 * quadratic[:, None, :]
    logits = lax.psum(partial_logits, "vol")
    weights = posterior_of(logits, candidates, counts)
    planes_here = volume.shape[1]
    y_part = jnp.einsum("btk,jbrc->tkrjc", weights, weighted, preferred_element_type=jnp.float32)
    d_part = jnp.einsum("btk,brc->tkrc", weights, squared, preferred_element_type=jnp.float32)
    num_re = jnp.sum(
        cosine[:, None] * y_part[:, :, :, 0] + sine[:, None] * y_part[:, :, :, 1], axis=0
    )
    num_im = jnp.sum(
        cosine[:, None] * y_part[:, :, :, 1] - sine[:, None] * y_part[:, :, :, 0], axis=0
    )
    partial_value = lax.psum_scatter(
        jnp.stack([num_re, num_im, jnp.sum(d_part, axis=0)], axis=2),
        "img",
        scatter_dimension=0,
        tiled=True,
    )
    initial = jnp.zeros((planes_here * ROWS + 1, 3 * COLS), jnp.float32)
    inserted = insert_into(
        initial,
        lax.all_gather(partial_value, "vol", axis=1, tiled=True),
        plane_share,
        line_share,
        weight_share,
        slab_id,
        planes_here,
        0,
        ROWS,
    )
    slab = inserted[: planes_here * ROWS].reshape(planes_here, ROWS, 3, COLS)
    summed = lax.psum_scatter(slab, "img", scatter_dimension=1, tiled=True)
    denom = summed[:, :, 2] + regularizer
    return jnp.stack([summed[:, :, 0] / denom, summed[:, :, 1] / denom], axis=0)


def solution(mesh):
    return jax.shard_map(
        body,
        mesh=mesh,
        in_specs=(
            P(None, "img", "vol", None),
            P("img"),
            P("img", None),
            P("img"),
            P("vol", None),
            P(None, "vol", None, None),
            P(),
            P(),
            P(),
            P("vol", "img", None),
        ),
        out_specs=P(None, "vol", "img", None),
        check_vma=False,
    )
```

profile of v0, /device:TPU:12, one launch (start us, length us, event | category | flops | bytes accessed | tf_op | source)
XLA Modules:
  0.0 720.7 jit_solution(9469468249330172509)
XLA Ops:
  6.5 0.7 compare_and_fusion.1
  7.3 0.8 select_bitcast_fusion
  8.1 15.4 %copy.80 = f32[2,32,256,128]{3,0,2,1:T(2,128)} copy(f32[2,32,256,128]{3,2,1,0:T(8,128)} %param.17) | data formatting | bytes 16777216 | tf_op args[5]
  23.5 31.7 %gather_fusion = f32[4096,2,128]{2,1,0:T(2,128)} fusion(f32[2,8192,128]{2,0,1:T(2,128)} %bitcast.133, s32[4096]{0:T(1024)S(1)} %broadcast_clamp_fusion.1), kind=kCustom, calls=%fused_computation.clone | custom fusion | bytes 8404992 | tf_op jit(solution)/shard_map/jit(_take)/gather | solution.py:67
  55.2 4.4 copy.81
  59.6 31.7 %gather_fusion.1 = f32[4096,2,128]{2,1,0:T(2,128)} fusion(f32[2,8192,128]{2,0,1:T(2,128)} %bitcast.134, s32[4096]{0:T(1024)S(1)} %broadcast_clamp_fusion), kind=kCustom, calls=%fused_computation.1.clone | custom fusion | bytes 8404992 | tf_op jit(solution)/shard_map/jit(_take)/gather | solution.py:68
  91.3 2.6 copy.82
  93.9 0.7 broadcast_subtract_fusion.1
  94.6 0.1 copy-done
  94.7 4.9 fusion.20
  99.6 0.0 reduce-scatter.4.cloned.1.call-update
  99.6 0.0 all-gather.3.cloned.1.call-start
  99.7 0.1 broadcast_add_fusion
  99.8 23.2 %fusion.7 = f32[384,32,128]{2,0,1:T(8,128)S(1)} fusion(f32[32,128]{1,0:T(8,128)S(1)} %copy-done.4, f32[32,128]{1,0:T(8,128)S(1)} %broadcast_add_fusion, f32[384]{0:T(512)S(1)} %copy-done.6), kind=kLoop, calls=%fused_computation.14 | loop fusion | flops 9437184 | bytes 6325760 | tf_op jit(solution)/shard_map/mul | solution.py:128
  123.0 6.3 copy.79
  129.3 0.1 broadcast_multiply_fusion.2
  129.4 39.2 %reduce-scatter.4.cloned.1.call-done = bf16[2,16,32,128]{3,2,1,0:T(8,128)(2,1)} async-done(((bf16[2,16,256,128]{3,2,1,0:T(8,128)(2,1)}), bf16[2,16,32,128]{3,2,1,0:T(8,128)(2,1)}) %reduce-scatter.4.cloned.1.call-update) | async-done | bytes 262160 | tf_op jit(solution)/shard_map/reduce_scatter | solution.py:121
  168.6 0.0 all-gather.3.cloned.1.call-update
  168.7 0.0 all-reduce.2.cloned.1.call-start
  168.7 0.1 broadcast_multiply_fusion.3
  168.8 0.3 fusion.63
  169.1 23.7 %fusion.87 = bf16[384,32,128]{2,0,1:T(8,128)(2,1)S(1)} fusion(f32[32,128]{1,0:T(8,128)S(1)} %copy-done.4, f32[32,128]{1,0:T(8,128)S(1)} %broadcast_add_fusion, f32[384]{0:T(512)S(1)} %copy-done.6), kind=kLoop, calls=%fused_computation.16.clone.1.clone.clone.clone.clone.clone.1 | loop fusion | flops 11010048 | bytes 3180032 | tf_op jit(solution)/shard_map/brc,krc->bk/dot_general | solution.py:131
  192.8 8.7 %multiply_convert_fusion = bf16[2,384,32,128]{3,2,1,0:T(8,128)(2,1)} fusion(bf16[2,384,32,128]{3,2,1,0:T(8,128)(2,1)} %param.12, f32[384,32,128]{2,1,0:T(8,128)} %copy.79), kind=kLoop, calls=%fused_computation.4 | loop fusion | flops 9437184 | bytes 18874368 | tf_op jit(solution)/shard_map/convert_element_type | solution.py:128
  201.5 1.6 convert_bitcast_fusion.1
  203.0 0.6 copy.83
  203.7 0.6 copy.84
  204.3 0.2 fusion.57
  204.5 1.1 fusion.45
  205.6 1.2 subtract_convert_fusion
  206.8 4.2 fusion.37
  211.0 0.0 all-reduce.2.cloned.1.call-update
  211.0 0.5 reduce-scatter.6.cloned.1.call-start
  211.6 8.7 %fusion.77 = bf16[2,384,32,128,1]{3,2,1,0,4:T(8,128)(2,1)} fusion(bf16[2,384,32,128]{3,2,1,0:T(8,128)(2,1)} %param.12, f32[384,32,128]{2,1,0:T(8,128)} %copy.79), kind=kLoop, calls=%fused_computation.118 | loop fusion | flops 9437184 | bytes 18874368 | tf_op jit(solution)/shard_map/convert_element_type | solution.py:128
  220.4 0.1 fusion.56
  220.5 60.8 %all-reduce.2.cloned.1.call-done = f32[384,4,64]{0,2,1:T(8,128)} async-done(((f32[384,4,64]{0,2,1:T(8,128)}), f32[384,4,64]{0,2,1:T(8,128)}) %all-reduce.2.cloned.1.call-update) | async-done | bytes 393232 | tf_op jit(solution)/shard_map/psum | solution.py:133
  281.3 1.1 select_reduce_fusion
  282.4 1.1 fusion.59
  283.5 5.7 fusion.21
  289.2 1.9 add_reduce_fusion
  291.1 24.3 %fusion.29 = f32[64,32,128]{2,0,1:T(8,128)S(1)} fusion(f32[32,128]{1,0:T(8,128)S(1)} %copy-done.4, f32[32,128]{1,0:T(8,128)S(1)} %broadcast_add_fusion, f32[384]{0:T(512)S(1)} %copy-done.6, f32[384,4,64]{0,2,1:T(8,128)S(1)} %copy-done.2, f32[384]{0:T(512)S(1)} %fusion.59, f32[384]{0:T(512)S(1)} %select_reduce_fusion, pred[384,64]{0,1:T(8,128)(4,1)S(1)} %fusion.56), kind=kOutput, calls=%fused_computation.44 | convolution fusion | flops 817594368 | bytes 1503744 | tf_op jit(solution)/shard_map/btk,brc->tkrc/dot_general | solution.py:137
  315.4 2.0 pad_maximum_fusion
  317.4 0.0 reduce-scatter.6.cloned.1.call-update
  317.4 0.0 all-gather.5.cloned.1.call-start
  317.4 37.8 %reduce-scatter.6.cloned.1.call-done = f32[16,32,3,128]{3,0,1,2:T(8,128)} async-done(((f32[64,32,3,128]{3,0,1,2:T(8,128)}), f32[16,32,3,128]{3,0,1,2:T(8,128)}) %reduce-scatter.6.cloned.1.call-update) | async-done | bytes 786448 | tf_op jit(solution)/shard_map/reduce_scatter | solution.py:144
  355.3 2.1 copy.89
  357.3 0.0 all-gather.5.cloned.1.call-update
  357.4 0.0 reduce-scatter.8.cloned.1.call-start
  357.4 0.8 select_bitcast_fusion.1
  358.3 95.9 %all-gather.5.cloned.1.call-done = f32[16,256,3,128]{3,0,2,1:T(8,128)} async-done(((f32[16,32,3,128]{3,0,2,1:T(8,128)}), f32[16,256,3,128]{3,0,2,1:T(8,128)}) %all-gather.5.cloned.1.call-update) | async-done | bytes 6291472 | tf_op jit(solution)/shard_map/all_gather | solution.py:153
  454.2 6.7 copy.90
  460.9 8.7 %copy.113 = f32[48,8,16,256]{3,1,2,0:T(8,128)S(1)} copy(f32[48,8,16,256]{3,2,1,0:T(8,128)} %bitcast.135) | data formatting | bytes 12582912
  469.6 6.1 broadcast_multiply_fusion
  475.7 6.6 copy.91
  482.3 6.6 copy.92
  488.8 33.5 %scatter_custom_fusion = f32[8193,384]{1,0:T(8,128)} fusion(s32[4096]{0:T(1024)S(1)} %bitcast.152, f32[4096,384]{1,0:T(8,128)} %copy.91, f32[]{:T(128)} %constant.33.clone.1), kind=kCustom, calls=%fused_computation.7 | custom fusion | flops 1572864 | bytes 12584960 | tf_op jit(solution)/shard_map/scatter-add | solution.py:92
  522.3 36.9 %scatter_fusion = f32[8193,384]{1,0:T(8,128)} fusion(f32[8193,384]{1,0:T(8,128)} %scatter_custom_fusion, s32[4096]{0:T(1024)S(1)} %bitcast.151, f32[4096,384]{1,0:T(8,128)} %copy.92), kind=kCustom, calls=%fused_computation.3 | custom fusion | flops 1572864 | bytes 18890752 | tf_op jit(solution)/shard_map/scatter-add | solution.py:93
  559.2 9.9 %slice.42 = f32[8192,384]{1,0:T(8,128)} slice(f32[8193,384]{1,0:T(8,128)} %scatter_fusion), slice={[0:8192], [0:384]} | slice | bytes 25165824 | tf_op jit(solution)/shard_map/slice | solution.py:162
  569.1 19.1 %reshape.355 = f32[32,256,3,128]{3,2,1,0:T(4,128)} reshape(f32[8192,384]{1,0:T(8,128)} %slice.42) | data formatting | bytes 25165824 | tf_op jit(solution)/shard_map/reshape | solution.py:162
  588.2 17.6 %copy.94 = f32[32,256,3,128]{3,0,2,1:T(8,128)} copy(f32[32,256,3,128]{3,2,1,0:T(4,128)} %reshape.355) | data formatting | bytes 25165824 | tf_op jit(solution)/shard_map/reshape | solution.py:162
  605.8 0.0 reduce-scatter.8.cloned.1.call-update
  605.9 102.5 %reduce-scatter.8.cloned.1.call-done = f32[32,64,3,128]{3,0,2,1:T(8,128)} async-done(((f32[32,256,3,128]{3,0,2,1:T(8,128)}), f32[32,64,3,128]{3,0,2,1:T(8,128)}) %reduce-scatter.8.cloned.1.call-update) | async-done | bytes 3145744 | tf_op jit(solution)/shard_map/reduce_scatter | solution.py:163
  708.3 2.7 fusion.54
  711.0 0.2 pad_maximum_fusion.1
  711.2 2.5 copy.98
  (42 shorter events, 0.3 us)
Async XLA Ops:
  6.5 162.1 %reduce-scatter.4.cloned.1.call-start = ((), (), s32[]{:S(2)}) async-start(), calls=%async_computation.3 | async-start | bytes 2359296 | tf_op jit(solution)/shard_map/reduce_scatter | solution.py:121
  91.3 3.4 copy-start
  94.7 5.1 copy-start.4
  94.7 5.1 copy-start.6
  99.6 101.8 %all-gather.3.cloned.1.call-start = ((), (), s32[]{:S(2)}) async-start(), calls=%async_computation.4 | async-start | bytes 1310720 | tf_op jit(solution)/shard_map/all_gather | solution.py:124
  168.7 112.6 %all-reduce.2.cloned.1.call-start = ((), (), s32[]{:S(2)}) async-start(), calls=%async_computation.5 | async-start | bytes 786432 | tf_op jit(solution)/shard_map/psum | solution.py:133
  201.5 2.8 copy-start.1
  203.7 3.1 slice-start
  204.5 2.3 slice-start.1
  211.0 9.3 %copy-start.7 = (s32[384]{0:T(512)S(1)}, s32[384]{0:T(512)}, u32[]{:S(2)}) copy-start(s32[384]{0:T(512)} %param.15) | copy-start | bytes 4612
  211.0 9.3 %copy-start.5 = (s32[384,8]{0,1:T(8,128)S(1)}, s32[384,8]{0,1:T(8,128)}, u32[]{:S(2)}) copy-start(s32[384,8]{0,1:T(8,128)} %param.14) | copy-start | bytes 36868
  211.0 144.2 %reduce-scatter.6.cloned.1.call-start = ((), (), s32[]{:S(2)}) async-start(), calls=%async_computation.6 | async-start | bytes 3932160 | tf_op jit(solution)/shard_map/reduce_scatter | solution.py:144
  289.2 1.9 copy-start.2
  317.4 136.8 %all-gather.5.cloned.1.call-start = ((), (), s32[]{:S(2)}) async-start(), calls=%async_computation.7 | async-start | bytes 7077888 | tf_op jit(solution)/shard_map/all_gather | solution.py:153
  357.4 351.0 %reduce-scatter.8.cloned.1.call-start = ((), (), s32[]{:S(2)}) async-start(), calls=%async_computation.8 | async-start | bytes 15728640 | tf_op jit(solution)/shard_map/reduce_scatter | solution.py:163
  605.8 102.5 %copy-start.3 = (f32[32,64,128]{2,1,0:T(8,128)S(1)}, f32[32,64,128]{2,1,0:T(8,128)}, u32[]{:S(2)}) copy-start(f32[32,64,128]{2,1,0:T(8,128)} %param.21) | copy-start | bytes 3145732
Sparse Core Ops, SparseCore 0:
  99.8 68.8 reduce-scatter.3
  170.2 16.2 all-gather.2
  211.1 70.1 all-reduce.1
  317.5 37.7 reduce-scatter.5
  357.5 96.6 all-gather.4
  606.0 102.3 reduce-scatter.7
where the time goes:
time: 727 us; the launch traced here: 721 us
  waiting for transfers between devices  336 us (46%)
  local copies, waits for them, and re-layouts  173 us (24%)
  other arithmetic  161 us (22%)
  matrix products  35.3 us (5%)
  between operations  14 us (2%)
    reduce_scatter x1, waiting for transfers between devices, body(): summed = lax.psum_scatter(slab, 'img', scatter_dimension=1, tiled=True)  102 us
    all_gather x1, waiting for transfers between devices, body(): lax.all_gather(partial_value, 'vol', axis=1, tiled=True)  95.9 us
    psum x1, waiting for transfers between devices, body(): logits = lax.psum(partial_logits, 'vol')  60.8 us
    reduce_scatter x1, waiting for transfers between devices, body(): lax.psum_scatter(masked.astype(jnp.bfloat16), 'vol', scatter_dimension=2,...  39.2 us
    reduce_scatter x1, waiting for transfers between devices, body(): lax.psum_scatter(jnp.stack([num_re, num_im, jnp.sum(d_part, axis=0)], axi...  37.8 us
    scatter-add x1, other arithmetic, insert_into(): return carry.at[upper_index].add((1.0 - weight) * values)  36.9 us
    reshape x2, local copies, waits for them, and re-layouts, body(): slab = inserted[:planes_here * ROWS].reshape(planes_here, ROWS, 3, COLS)  36.7 us
    gather x2, local copies, waits for them, and re-layouts, extract_rows(): lower = jnp.take(flat, line_index, axis=1)  36.1 us
  transfers between devices with their start and end apart: 6, of which 5 were waited for; matrix products, arithmetic and copies ran while one was open for 10% of the time, Pallas kernels for 0%

commit v1 on v0

v1 whole, which is shorter than its diff:
```python
import math
from functools import partial

import jax
import jax.numpy as jnp
from jax import lax
from jax.experimental import pallas as pl
from jax.experimental.pallas import tpu as pltpu
from jax.sharding import PartitionSpec as P

ROWS = 256
COLS = 128
K = 64
TRANS = 4
LMAX = 8
AMPLITUDE = 0.1
VMEM_LIMIT = 56 * 1024 * 1024
BF16 = jnp.bfloat16
F32 = jnp.float32


def params(steps):
    return pltpu.CompilerParams(
        dimension_semantics=("arbitrary",) * steps, vmem_limit_bytes=VMEM_LIMIT
    )


def smem():
    return pl.BlockSpec(memory_space=pltpu.SMEM)


def vmem():
    return pl.BlockSpec(memory_space=pltpu.VMEM)


def shift_phases(row_freq, col_freq, number):
    shift_ids = jnp.arange(number)
    shift_x = (shift_ids % 2).astype(F32) - 0.5
    shift_y = (shift_ids // 2).astype(F32) - 0.5
    angle = (
        -2.0
        * math.pi
        * (
            shift_x[:, None, None] * col_freq[None, None, :]
            + shift_y[:, None, None] * row_freq[None, :, None]
        )
    )
    return (jnp.cos(angle), jnp.sin(angle))


def extract_kernel(idx_s, flag_s, vol_ref, w_ref, out_ref, pair):
    blocks = out_ref.shape[0]
    groups = out_ref.shape[2] // 16

    def block_step(blk, carry):
        def group_step(g, inner):
            at = blk * groups + g
            base = pl.multiple_of(g * 16, 16)

            @pl.when(flag_s[at] > 0)
            def _():
                for u in range(16):
                    i = idx_s[at * 16 + u]
                    pair[0, 2 * u : 2 * u + 2, :] = vol_ref[0, pl.ds(i, 2), :]
                    pair[1, 2 * u : 2 * u + 2, :] = vol_ref[1, pl.ds(i, 2), :]
                w = jnp.broadcast_to(w_ref[pl.ds(pl.multiple_of(at * 16, 16), 16), :], (16, COLS))
                for j in range(2):
                    lower = pair[j, pl.ds(0, 16, stride=2), :]
                    upper = pair[j, pl.ds(1, 16, stride=2), :]
                    value = jnp.where(w >= 0.0, w * lower + (1.0 - w) * upper, 0.0)
                    out_ref[blk, j, pl.ds(base, 16), :] = value.astype(BF16)

            @pl.when(flag_s[at] == 0)
            def _():
                for j in range(2):
                    out_ref[blk, j, pl.ds(base, 16), :] = jnp.zeros((16, COLS), BF16)

            return inner

        return lax.fori_loop(0, groups, group_step, carry)

    lax.fori_loop(0, blocks, block_step, 0)


def extract(volume, planes, lines, weights, slab_id, n_vol):
    share = planes.shape[0]
    planes_here = volume.shape[1]
    rows = ROWS // n_vol

    def order(x):
        return x.reshape(share, n_vol, rows).transpose(1, 0, 2).reshape(-1)

    local = order(planes) - slab_id * planes_here
    owned = (local >= 0) & (local < planes_here)
    idx = jnp.where(owned, local, 0) * ROWS + order(lines)
    w = jnp.where(owned, order(weights), -1.0)[:, None]
    flag = jnp.any(owned.reshape(-1, 16), axis=1).astype(jnp.int32)
    return pl.pallas_call(
        extract_kernel,
        out_shape=jax.ShapeDtypeStruct((n_vol, 2, share * rows, COLS), BF16),
        in_specs=[smem(), smem(), vmem(), vmem()],
        out_specs=vmem(),
        scratch_shapes=[pltpu.VMEM((2, 32, COLS), F32)],
        compiler_params=pltpu.CompilerParams(vmem_limit_bytes=VMEM_LIMIT),
        name="extract",
    )(idx, flag, volume.reshape(2, planes_here * ROWS, COLS), w)


def weigh_kernel(img_ref, sa_ref, ca_ref, sx_ref, cx_ref, nw_ref, wt_ref, sq_ref, buf):
    count = img_ref.shape[1]
    rows = img_ref.shape[2]
    for j in range(2):
        buf[j] = img_ref[j].astype(F32).reshape(count * rows, COLS)
    sx = sx_ref[...]
    cx = cx_ref[...]
    for r in range(rows):
        contrast = -(sa_ref[:, r : r + 1] * cx + ca_ref[:, r : r + 1] * sx)
        noise = nw_ref[r : r + 1, :]
        scale = contrast * noise
        for j in range(2):
            x = buf[j, pl.ds(r, count, stride=rows), :]
            wt_ref[r, :, j * COLS : (j + 1) * COLS] = (scale * x).astype(BF16)
        sq_ref[r] = (contrast * contrast * noise).astype(BF16)


def weigh(images, defocus, noise_weight, row_freq, col_freq):
    count = images.shape[1]
    rows = images.shape[2]
    step = 64
    angle_r = defocus[:, None] * (row_freq * row_freq)[None, :] + math.asin(AMPLITUDE)
    angle_c = defocus[:, None] * (col_freq * col_freq)[None, :]
    return pl.pallas_call(
        weigh_kernel,
        grid=(count // step,),
        out_shape=[
            jax.ShapeDtypeStruct((rows, count, 2 * COLS), BF16),
            jax.ShapeDtypeStruct((rows, count, COLS), BF16),
        ],
        in_specs=[
            pl.BlockSpec((2, step, rows, COLS), lambda b: (0, b, 0, 0)),
            pl.BlockSpec((step, rows), lambda b: (b, 0)),
            pl.BlockSpec((step, rows), lambda b: (b, 0)),
            pl.BlockSpec((step, COLS), lambda b: (b, 0)),
            pl.BlockSpec((step, COLS), lambda b: (b, 0)),
            pl.BlockSpec((rows, COLS), lambda b: (0, 0)),
        ],
        out_specs=[
            pl.BlockSpec((rows, step, 2 * COLS), lambda b: (0, b, 0)),
            pl.BlockSpec((rows, step, COLS), lambda b: (0, b, 0)),
        ],
        scratch_shapes=[pltpu.VMEM((2, step * rows, COLS), F32)],
        compiler_params=params(1),
        name="weigh",
    )(
        images,
        jnp.sin(angle_r),
        jnp.cos(angle_r),
        jnp.sin(angle_c),
        jnp.cos(angle_c),
        noise_weight,
    )


def logits_kernel(sl_ref, wt_ref, sq_ref, cos_ref, sin_ref, cand_ref, out_ref, part, acc, quad):
    step = pl.program_id(0)
    groups = sl_ref.shape[0]
    span = sl_ref.shape[2]
    rows = groups * span // K
    inner = wt_ref.shape[0]

    @pl.when(step == 0)
    def _():
        for i in range(groups):
            for j in range(2):
                part[j, i * span : (i + 1) * span, :] = sl_ref[i, j].astype(F32)
        acc[...] = jnp.zeros_like(acc)
        quad[...] = jnp.zeros_like(quad)

    dims = (((1,), (1,)), ((), ()))
    total = acc[...]
    total_q = quad[...]
    for u in range(inner):
        re = part[0, pl.ds(step * inner + u, K, stride=rows), :]
        im = part[1, pl.ds(step * inner + u, K, stride=rows), :]
        shifted = []
        for t in range(TRANS):
            c = cos_ref[t, u : u + 1, :]
            s = sin_ref[t, u : u + 1, :]
            shifted.append(
                jnp.concatenate(
                    [(c * re - s * im).astype(BF16), (s * re + c * im).astype(BF16)], axis=1
                )
            )
        left = jnp.concatenate(shifted, axis=0)
        power = (re * re + im * im).astype(BF16)
        total = total + lax.dot_general(left, wt_ref[u], dims, preferred_element_type=F32)
        total_q = total_q + lax.dot_general(power, sq_ref[u], dims, preferred_element_type=F32)
    acc[...] = total
    quad[...] = total_q

    @pl.when(step == pl.num_programs(0) - 1)
    def _():
        ids = lax.broadcasted_iota(jnp.int32, quad.shape, 0)
        half = 0.5 * quad[...]
        for t in range(TRANS):
            value = acc[t * K : (t + 1) * K, :] - half
            for l in range(LMAX):
                pick = jnp.where(ids == cand_ref[l : l + 1, :], value, 0.0)
                out_ref[t * LMAX + l : t * LMAX + l + 1, :] = jnp.sum(pick, axis=0, keepdims=True)


def candidate_logits(slices, weighted, squared, cosine, sine, cand):
    rows, count = squared.shape[:2]
    inner = 8
    return pl.pallas_call(
        logits_kernel,
        grid=(rows // inner,),
        out_shape=jax.ShapeDtypeStruct((TRANS * LMAX, count), F32),
        in_specs=[
            pl.BlockSpec(slices.shape, lambda s: (0, 0, 0, 0)),
            pl.BlockSpec((inner, count, 2 * COLS), lambda s: (s, 0, 0)),
            pl.BlockSpec((inner, count, COLS), lambda s: (s, 0, 0)),
            pl.BlockSpec((TRANS, inner, COLS), lambda s: (0, s, 0)),
            pl.BlockSpec((TRANS, inner, COLS), lambda s: (0, s, 0)),
            pl.BlockSpec((LMAX, count), lambda s: (0, 0)),
        ],
        out_specs=pl.BlockSpec((TRANS * LMAX, count), lambda s: (0, 0)),
        scratch_shapes=[
            pltpu.VMEM((2, K * rows, COLS), F32),
            pltpu.VMEM((TRANS * K, count), F32),
            pltpu.VMEM((K, count), F32),
        ],
        compiler_params=params(1),
        name="logits",
    )(slices, weighted, squared, cosine, sine, cand)


def posterior_rows(logits, counts):
    place = lax.broadcasted_iota(jnp.int32, logits.shape, 0) % LMAX
    allowed = place < counts
    masked = jnp.where(allowed, logits, -1e30)
    highest = jnp.max(masked, axis=0, keepdims=True)
    exponent = jnp.where(allowed, jnp.exp(masked - highest), 0.0)
    return (exponent / jnp.sum(exponent, axis=0, keepdims=True)).astype(BF16).astype(F32)


def project_kernel(
    src_s, len_s, lg_ref, cand_ref, cnt_ref, wt_ref, sq_ref, cos_ref, sin_ref,
    out_ref, post, post_sum, num, pick,
):
    step = pl.program_id(0)
    inner = wt_ref.shape[0]
    parts = out_ref.shape[0]
    cap = out_ref.shape[2]

    @pl.when(step == 0)
    def _():
        prob = posterior_rows(lg_ref[...], cnt_ref[...])
        ids = lax.broadcasted_iota(jnp.int32, (K, prob.shape[1]), 0)
        total = jnp.zeros((K, prob.shape[1]), F32)
        for t in range(TRANS):
            dense = jnp.zeros((K, prob.shape[1]), F32)
            for l in range(LMAX):
                at = t * LMAX + l
                dense = jnp.where(ids == cand_ref[l : l + 1, :], dense + prob[at : at + 1, :], dense)
            post[t * K : (t + 1) * K, :] = dense.astype(BF16)
            total = total + dense
        high = total.astype(BF16)
        post_sum[:K, :] = high
        post_sum[K:, :] = (total - high.astype(F32)).astype(BF16)

    for u in range(inner):
        y = jnp.dot(post[...], wt_ref[u], preferred_element_type=F32)
        d = jnp.dot(post_sum[...], sq_ref[u], preferred_element_type=F32)
        re = jnp.zeros((K, COLS), F32)
        im = jnp.zeros((K, COLS), F32)
        for t in range(TRANS):
            c = cos_ref[t, u : u + 1, :]
            s = sin_ref[t, u : u + 1, :]
            y_re = y[t * K : (t + 1) * K, :COLS]
            y_im = y[t * K : (t + 1) * K, COLS:]
            re = re + (c * y_re + s * y_im)
            im = im + (c * y_im - s * y_re)
        base = pl.multiple_of((step * inner + u) * K, K)
        num[0, pl.ds(base, K), :] = re
        num[1, pl.ds(base, K), :] = im
        num[2, pl.ds(base, K), :] = d[:K] + d[K:]

    @pl.when(step == pl.num_programs(0) - 1)
    def _():
        for q in range(parts):

            def group_step(g, carry):
                base = pl.multiple_of(g * 16, 16)
                for u in range(16):
                    s = src_s[q * cap + base + u]
                    for c in range(3):
                        pick[c, u : u + 1, :] = num[c, pl.ds(s, 1), :]
                for c in range(3):
                    out_ref[q, c, pl.ds(base, 16), :] = pick[c].astype(BF16)
                return carry

            lax.fori_loop(0, (len_s[q] + 15) // 16, group_step, 0)


def project(src, lengths, logits, cand, counts, weighted, squared, cosine, sine, parts, cap):
    rows, count = squared.shape[:2]
    inner = 8
    return pl.pallas_call(
        project_kernel,
        grid=(rows // inner,),
        out_shape=jax.ShapeDtypeStruct((parts, 3, cap, COLS), BF16),
        in_specs=[
            smem(),
            smem(),
            pl.BlockSpec((TRANS * LMAX, count), lambda s: (0, 0)),
            pl.BlockSpec((LMAX, count), lambda s: (0, 0)),
            pl.BlockSpec((1, count), lambda s: (0, 0)),
            pl.BlockSpec((inner, count, 2 * COLS), lambda s: (s, 0, 0)),
            pl.BlockSpec((inner, count, COLS), lambda s: (s, 0, 0)),
            pl.BlockSpec((TRANS, inner, COLS), lambda s: (0, s, 0)),
            pl.BlockSpec((TRANS, inner, COLS), lambda s: (0, s, 0)),
        ],
        out_specs=pl.BlockSpec((parts, 3, cap, COLS), lambda s: (0, 0, 0, 0)),
        scratch_shapes=[
            pltpu.VMEM((TRANS * K, count), BF16),
            pltpu.VMEM((2 * K, count), BF16),
            pltpu.VMEM((3, rows * K, COLS), F32),
            pltpu.VMEM((3, 16, COLS), F32),
        ],
        compiler_params=params(1),
        name="project",
    )(src, lengths, logits, cand, counts, weighted, squared, cosine, sine)


HEAD = 8


def line_stride(lines_here):
    return lines_here + 2 * HEAD


def insert_kernel(len_s, pos_s, at_s, wgt_s, rows_ref, reg_ref, out_ref, acc, buf):
    step = pl.program_id(0)
    cap = rows_ref.shape[2]
    planes, lines_here = reg_ref.shape[:2]
    stride = line_stride(lines_here)

    @pl.when(step == 0)
    def _():
        acc[...] = jnp.zeros_like(acc)

    for c in range(3):
        buf[c] = rows_ref[0, c].astype(F32)
    first = lax.broadcasted_iota(jnp.int32, (2, COLS), 0) == 0

    def group_step(g, carry):
        for u in range(4):
            e = step * cap + g * 4 + u
            s = pos_s[e]
            to = at_s[e]
            w = wgt_s[e]
            both = jnp.where(first, w, 1.0 - w)
            for c in range(3):
                row = jnp.broadcast_to(buf[c, pl.ds(s, 1), :], (2, COLS))
                acc[c, pl.ds(to, 2), :] = acc[c, pl.ds(to, 2), :] + both * row
        return carry

    lax.fori_loop(0, (len_s[step] + 3) // 4, group_step, 0)

    @pl.when(step == pl.num_programs(0) - 1)
    def _():
        def plane_step(p, carry):
            base = pl.multiple_of(p * stride + HEAD, 8)
            inv = 1.0 / (acc[2, pl.ds(base, lines_here), :] + reg_ref[p])
            out_ref[0, p] = acc[0, pl.ds(base, lines_here), :] * inv
            out_ref[1, p] = acc[1, pl.ds(base, lines_here), :] * inv
            return carry

        lax.fori_loop(0, planes, plane_step, 0)


def insert(lengths, positions, targets, weights, received, regularizer):
    blocks, _, cap, _ = received.shape
    planes, lines_here = regularizer.shape[:2]
    return pl.pallas_call(
        insert_kernel,
        grid=(blocks,),
        out_shape=jax.ShapeDtypeStruct((2, planes, lines_here, COLS), F32),
        in_specs=[
            smem(),
            smem(),
            smem(),
            smem(),
            pl.BlockSpec((1, 3, cap, COLS), lambda s: (s, 0, 0, 0)),
            pl.BlockSpec((planes, lines_here, COLS), lambda s: (0, 0, 0)),
        ],
        out_specs=pl.BlockSpec((2, planes, lines_here, COLS), lambda s: (0, 0, 0, 0)),
        scratch_shapes=[
            pltpu.VMEM((3, planes * line_stride(lines_here), COLS), F32),
            pltpu.VMEM((3, cap, COLS), F32),
        ],
        compiler_params=params(1),
        name="insert",
    )(lengths, positions, targets, weights, received, regularizer)


def ranks(member, rows):
    x = member.reshape(-1, rows, K).astype(F32)
    before_k = (jnp.arange(K)[:, None] < jnp.arange(K)[None, :]).astype(F32)
    before_r = (jnp.arange(rows)[:, None] < jnp.arange(rows)[None, :]).astype(F32)
    inner = jnp.einsum("xrk,kl->xrl", x, before_k, preferred_element_type=F32)
    outer = jnp.einsum("xr,rs->xs", jnp.sum(x, axis=2), before_r, preferred_element_type=F32)
    return (inner + outer[:, :, None]).reshape(member.shape).astype(jnp.int32)


def compact(member, rank, values, cap):
    high = jnp.where(member, rank // 32, -1)
    low = rank % 32
    left = (high[:, :, None] == jnp.arange(cap // 32)).astype(F32)
    hot = low[:, None, None, :] == jnp.arange(32)[None, None, :, None]
    right = jnp.where(hot, values[:, :, None, :], 0.0)
    out = jnp.einsum("xnh,xvln->xvhl", left, right, precision=lax.Precision.HIGHEST)
    return out.reshape(values.shape[0], values.shape[1], cap)


def insert_into(carry, piece, planes_all, lines_all, weights_all, slab_id, planes_here):
    local_plane = planes_all - slab_id * planes_here
    in_slab = (local_plane >= 0) & (local_plane < planes_here)
    dump_row = planes_here * ROWS
    lower_index = jnp.where(in_slab, local_plane * ROWS + lines_all, dump_row).reshape(-1)
    upper_index = jnp.where(in_slab, lower_index.reshape(in_slab.shape) + 1, dump_row).reshape(-1)
    values = piece.reshape(-1, 3 * COLS)
    weight = weights_all.reshape(-1, 1)
    carry = carry.at[lower_index].add(weight * values)
    return carry.at[upper_index].add((1.0 - weight) * values)


def dense_path(
    logits, cand, counts, weighted, squared, cosine, sine,
    plane_share, line_share, weight_share, regularizer, slab_id,
):
    prob = posterior_rows(logits, counts).reshape(TRANS, LMAX, -1)
    hot = (cand[:, None, :] == jnp.arange(K)[None, :, None]).astype(F32)
    post = jnp.einsum("tlb,lkb->tkb", prob, hot).astype(BF16)
    y = jnp.einsum("tkb,rbz->tkrz", post, weighted, preferred_element_type=F32)
    d = jnp.einsum("tkb,rbc->krc", post, squared, preferred_element_type=F32)
    y_re = y[..., :COLS]
    y_im = y[..., COLS:]
    num_re = jnp.sum(cosine[:, None] * y_re + sine[:, None] * y_im, axis=0)
    num_im = jnp.sum(cosine[:, None] * y_im - sine[:, None] * y_re, axis=0)
    partial_value = lax.psum_scatter(
        jnp.stack([num_re, num_im, d], axis=2), "img", scatter_dimension=0, tiled=True
    )
    planes_here = regularizer.shape[0]
    inserted = insert_into(
        jnp.zeros((planes_here * ROWS + 1, 3 * COLS), F32),
        lax.all_gather(partial_value, "vol", axis=1, tiled=True),
        plane_share,
        line_share,
        weight_share,
        slab_id,
        planes_here,
    )
    slab = inserted[: planes_here * ROWS].reshape(planes_here, ROWS, 3, COLS)
    summed = lax.psum_scatter(slab, "img", scatter_dimension=1, tiled=True)
    denom = summed[:, :, 2] + regularizer
    return jnp.stack([summed[:, :, 0] / denom, summed[:, :, 1] / denom], axis=0)


def body(
    images, defocus, candidates, counts, noise_weight, volume,
    row_plane, row_line, row_weight, regularizer,
):
    rows = noise_weight.shape[0]
    planes_here = volume.shape[1]
    lines_here = regularizer.shape[1]
    slab_id = lax.axis_index("vol")
    group_id = lax.axis_index("img")
    n_vol = lax.axis_size("vol")
    n_img = lax.axis_size("img")
    global_rows = slab_id * rows + jnp.arange(rows)
    row_freq = (global_rows.astype(F32) - ROWS // 2) / ROWS
    col_freq = jnp.arange(COLS).astype(F32) / (2 * COLS)
    share = K // n_img
    first = group_id * share
    plane_share = lax.dynamic_slice_in_dim(row_plane, first, share, 0)
    line_share = lax.dynamic_slice_in_dim(row_line, first, share, 0)
    weight_share = lax.dynamic_slice_in_dim(row_weight, first, share, 0)

    masked = extract(volume, plane_share, line_share, weight_share, slab_id, n_vol)
    own = lax.psum_scatter(masked, "vol", scatter_dimension=0, tiled=False)
    slices = lax.all_gather(own, "img", axis=0, tiled=False)

    cosine, sine = shift_phases(row_freq, col_freq, TRANS)
    weighted, squared = weigh(images, defocus, noise_weight, row_freq, col_freq)
    cand = candidates.T
    count_row = counts[None, :]
    partial_logits = candidate_logits(slices, weighted, squared, cosine, sine, cand)
    logits = lax.psum(partial_logits, "vol")

    mean = rows * K // n_img
    cap = -(-int(mean + 5.0 * math.sqrt(mean)) // 32) * 32
    line_b = row_line.T.reshape(n_vol, rows * K)
    plane_b = row_plane.T.reshape(n_vol, rows * K)
    weight_b = row_weight.T.reshape(n_vol, rows * K)
    low_part = line_b // lines_here
    high_part = (line_b + 1) // lines_here
    part_ids = jnp.arange(n_img)[:, None, None]
    members = (low_part == part_ids) | (high_part == part_ids)
    lengths = jnp.sum(members.astype(jnp.int32), axis=2)
    fits = jnp.max(lengths) <= cap

    send_member = lax.dynamic_index_in_dim(members, slab_id, 1, keepdims=False)
    row_ids = jnp.arange(rows * K).astype(F32)
    send_src = compact(
        send_member,
        ranks(send_member, rows),
        jnp.broadcast_to(row_ids, (n_img, 1, rows * K)),
        cap,
    ).astype(jnp.int32)
    send_len = lax.dynamic_index_in_dim(lengths, slab_id, 1, keepdims=False)

    recv_member = lax.dynamic_index_in_dim(members, group_id, 0, keepdims=False)
    recv_rank = ranks(recv_member, rows)
    local_plane = plane_b - slab_id * planes_here
    here = recv_member & (local_plane >= 0) & (local_plane < planes_here)
    target = local_plane * line_stride(lines_here) + line_b - group_id * lines_here + HEAD
    entry = compact(
        here,
        ranks(here, rows),
        jnp.stack([recv_rank.astype(F32), target.astype(F32), weight_b], axis=1),
        cap,
    )
    entry_len = jnp.sum(here.astype(jnp.int32), axis=1)
    entry_pos = entry[:, 0].astype(jnp.int32).reshape(-1)
    entry_at = entry[:, 1].astype(jnp.int32).reshape(-1)
    entry_w = entry[:, 2].reshape(-1)

    def listed_path():
        listed = project(
            send_src.reshape(-1), send_len, logits, cand, count_row, weighted, squared,
            cosine, sine, n_img, cap,
        )
        summed = lax.psum_scatter(listed, "img", scatter_dimension=0, tiled=False)
        received = lax.all_gather(summed, "vol", axis=0, tiled=False)
        return insert(entry_len, entry_pos, entry_at, entry_w, received, regularizer)

    def other_path():
        return dense_path(
            logits, cand, count_row, weighted, squared, cosine, sine,
            plane_share, line_share, weight_share, regularizer, slab_id,
        )

    return lax.cond(fits, listed_path, other_path)


def solution(mesh):
    return jax.shard_map(
        body,
        mesh=mesh,
        in_specs=(
            P(None, "img", "vol", None),
            P("img"),
            P("img", None),
            P("img"),
            P("vol", None),
            P(None, "vol", None, None),
            P(),
            P(),
            P(),
            P("vol", "img", None),
        ),
        out_specs=P(None, "vol", "img", None),
        check_vma=False,
    )
```

time: 727 us -> 295 us (0.41)
  waiting for transfers between devices: 336 us -> 151 us
  local copies, waits for them, and re-layouts: 173 us -> 13.5 us
  other arithmetic: 161 us -> 11.2 us
  Pallas kernels: 0 us -> 63.4 us
  blocking collectives: 0 us -> 30.9 us
  matrix products: 35.3 us -> 9.18 us
    reduce_scatter x3 -> x2, waiting for transfers between devices: 180 us -> 75.4 us  [the longest x1 41.2 us: body(): own = lax.psum_scatter(masked, 'vol', scatter_dimension=0, tiled=False)]
    gather x4 -> x0, local copies, waits for them, and re-layouts: 70.4 us -> none  [the longest x2 36.1 us: extract_rows(): lower = jnp.take(flat, line_index, axis=1)]
    scatter-add x2 -> x0, other arithmetic: 70.3 us -> none  [the longest x1 36.9 us: insert_into(): return carry.at[upper_index].add((1.0 - weight) * values)]
    pallas_call x0 -> x5, Pallas kernels: none -> 63.4 us  [the longest x1 15.4 us: weigh(): pl.pallas_call(weigh_kernel, grid=(count // step,), out_shape=[jax.ShapeD...]
    psum x1 -> x0, waiting for transfers between devices: 60.8 us -> none  [body(): logits = lax.psum(partial_logits, 'vol')]
    reshape x2 -> x6, local copies, waits for them, and re-layouts: 36.7 us -> 1.53 us  [the longest x1 1.1 us: compact(): return out.reshape(values.shape[0], values.shape[1], cap)]
    psum x0 -> x1, blocking collectives: none -> 30.9 us  [body(): logits = lax.psum(partial_logits, 'vol')]
    mul x5 -> x1, other arithmetic: 30.9 us -> 0.01 us  [weigh(): angle_c = defocus[:, None] * (col_freq * col_freq)[None, :]]
  transfers between devices with their start and end apart: 6 -> 4, of which waited for: 5 -> 4; matrix products, arithmetic and copies ran while one was open for 10% -> 8% of each run, Pallas kernels for 0% -> 5%
where the time goes in v1:
time: 295 us; the launch traced here: 294 us
  waiting for transfers between devices  151 us (51%)
  Pallas kernels  63.4 us (21%)
  blocking collectives  30.9 us (10%)
  between operations  14 us (5%)
  local copies, waits for them, and re-layouts  13.5 us (5%)
  other arithmetic  11.2 us (4%)
  matrix products  9.18 us (3%)
    all_gather x1, waiting for transfers between devices, listed_path(): received = lax.all_gather(summed, 'vol', axis=0, tiled=False)  67.1 us
    reduce_scatter x1, waiting for transfers between devices, body(): own = lax.psum_scatter(masked, 'vol', scatter_dimension=0, tiled=False)  41.2 us
    reduce_scatter x1, waiting for transfers between devices, listed_path(): summed = lax.psum_scatter(listed, 'img', scatter_dimension=0, tiled=False)  34.2 us
    psum x1, blocking collectives, body(): logits = lax.psum(partial_logits, 'vol')  30.9 us
    pallas_call x1, Pallas kernels, weigh(): pl.pallas_call(weigh_kernel, grid=(count // step,), out_shape=[jax.ShapeD...  15.4 us
    pallas_call x1, Pallas kernels, extract(): pl.pallas_call(extract_kernel, out_shape=jax.ShapeDtypeStruct((n_vol, 2,...  14.8 us
    pallas_call x1, Pallas kernels, insert(): pl.pallas_call(insert_kernel, grid=(blocks,), out_shape=jax.ShapeDtypeStr...  12.6 us
    pallas_call x1, Pallas kernels, project(): pl.pallas_call(project_kernel, grid=(rows // inner,), out_shape=jax.Shape...  12.2 us
  transfers between devices with their start and end apart: 4, of which 4 were waited for; matrix products, arithmetic and copies ran while one was open for 8% of the time, Pallas kernels for 5%

profile of v1, /device:TPU:12, one launch (start us, length us, event | category | flops | bytes accessed | tf_op | source)
XLA Modules:
  0.0 293.5 jit_solution(11729803068580811292)
XLA Ops:
  6.5 0.7 constant_dynamic-slice_fusion.2
  7.3 0.7 constant_dynamic-slice_fusion.3
  8.0 1.3 compare_and_fusion.2
  9.3 0.1 reshape.553
  9.4 0.1 and.166
  9.5 0.1 reduce_or.9
  9.6 0.6 convert_element_type.192.flag_s
  10.7 3.5 %select_n.190.w_ref = f32[4096,1]{1,0:T(8,128)} reshape(f32[8,16,32]{2,1,0:T(8,128)S(1)} %copy.112) | data formatting | bytes 32768 | tf_op jit(solution)/shard_map/jit(_where)/select_n | solution.py:96
  14.2 0.6 multiply_add_fusion.1.idx_s
  14.8 14.8 %extract.1 = bf16[8,2,512,128]{3,2,1,0:T(8,128)(2,1)} custom-call(s32[4096]{0:T(1024)} %multiply_add_fusion.1.idx_s, s32[256]{0:T(256)} %convert_element_type.192.flag_s, f32[2,8192,128]{2,1,0:T(8,128)} %bitcast.136, f32[4096,1]{1,0:T(8,128)} %select_n.190.w_ref), custom_call_target="tpu_custom_call" | custom-call | tf_op jit(solution)/shard_map/extract/pallas_call | solution.py:98
  29.7 0.1 copy.108
  29.8 0.1 reshape.547
  30.0 0.2 convert_reduce_fusion.1
  30.2 0.1 fusion.75
  30.3 0.6 broadcast_in_dim.46
  30.9 0.1 copy.115
  31.0 0.1 ge.52
  31.1 0.1 copy.116
  31.3 0.1 lt.214
  31.4 0.1 copy.119
  31.5 0.1 reshape.556
  31.6 0.6 reduce_max.18
  32.9 0.1 reshape.552
  33.0 0.1 squeeze.27
  33.1 0.1 convert_reduce_fusion.4
  33.2 0.1 fusion.63
  33.4 0.1 fusion.34
  33.6 0.2 convert_reduce_fusion.3
  33.8 0.1 fusion.65
  33.9 0.2 fusion.33
  34.1 0.1 convert_element_type.196
  34.2 0.1 fusion.64
  34.3 0.2 fusion.32
  34.4 0.1 convert_element_type.200
  34.6 0.1 copy.120
  34.7 0.1 stack_reshape.3
  34.8 0.8 copy.121
  35.6 1.5 multiply_cosine_fusion
  37.2 1.6 fusion.42
  38.7 15.4 %weigh.1 = (bf16[32,384,256]{2,1,0:T(8,128)(2,1)}, bf16[32,384,128]{2,1,0:T(8,128)(2,1)S(1)}) custom-call(bf16[2,384,32,128]{3,2,1,0:T(8,128)(2,1)} %img_ref.1, f32[384,32]{1,0:T(8,128)} %get-tuple-element.277.sa_ref, f32[384,32]{1,0:T(8,128)} %get-tuple-element.276.ca_ref, f32[384,128]{1,0:T(8,128)} %get-tuple-element.275.sx_ref, ...), custom_call_target="tpu_custom_call" | custom-call | tf_op jit(solution)/shard_map/weigh/pallas_call | solution.py:132
  54.2 0.7 broadcast_multiply_fusion.3
  54.8 0.7 broadcast_multiply_fusion.2
  55.6 41.2 %reduce-scatter.11.cloned.1.call-done = bf16[1,2,512,128]{3,2,1,0:T(8,128)(2,1)} async-done(((bf16[8,2,512,128]{3,2,1,0:T(8,128)(2,1)}), bf16[1,2,512,128]{3,2,1,0:T(8,128)(2,1)}) %reduce-scatter.11.cloned.1.call-update) | async-done | bytes 262160 | tf_op jit(solution)/shard_map/reduce_scatter | solution.py:492
  96.8 1.4 convolution_bitcast_fusion.1
  98.2 1.0 fusion.50
  99.3 0.3 iota_compare_fusion.4
  99.6 6.9 %fusion.26 = f32[8,3,20,32]{3,2,1,0:T(8,128)} fusion(f32[8,3,2048]{2,1,0:T(4,128)} %copy.121, pred[8,32,2048]{2,1,0:T(8,128)(4,1)S(1)} %iota_compare_fusion.4, s32[8,2048]{1,0:T(8,128)S(1)} %get-tuple-element.264), kind=kOutput, calls=%fused_computation.56 | convolution fusion | flops 379387904 | bytes 847872 | tf_op jit(solution)/shard_map/xnh,xvln->xvhl/dot_general | solution.py:423
  106.5 8.1 %all-gather.8.cloned.1.call-done.sl_ref = bf16[4,2,512,128]{3,2,1,0:T(8,128)(2,1)} async-done(((bf16[1,2,512,128]{3,2,1,0:T(8,128)(2,1)}), bf16[4,2,512,128]{3,2,1,0:T(8,128)(2,1)}) %all-gather.8.cloned.1.call-update) | async-done | bytes 1048592 | tf_op jit(solution)/shard_map/all_gather | solution.py:493
  114.6 8.4 %logits.1 = f32[32,384]{1,0:T(8,128)} custom-call(bf16[4,2,512,128]{3,2,1,0:T(8,128)(2,1)} %all-gather.8.cloned.1.call-done.sl_ref, bf16[32,384,256]{2,1,0:T(8,128)(2,1)} %get-tuple-element.103.wt_ref, bf16[32,384,128]{2,1,0:T(8,128)(2,1)S(1)} %get-tuple-element.104.sq_ref, f32[4,32,128]{2,1,0:T(8,128)S(1)} %get-tuple-element.273.cos_ref, ...), custom_call_target="tpu_custom_call" | custom-call | tf_op jit(solution)/shard_map/logits/pallas_call | solution.py:215
  123.0 30.9 %psum.7 = f32[32,384]{1,0:T(8,128)S(1)} all-reduce(f32[32,384]{1,0:T(8,128)} %logits.1), channel_id=1, replica_groups=mesh['img'=4,'vol'=8] {'vol'}, use_global_device_ids=true, to_apply=%region_4.5 | all-reduce | flops 12288 | bytes 98304 | tf_op jit(solution)/shard_map/psum | solution.py:500
  154.0 133.0 %conditional.1 = (f32[2,32,64,128]{3,2,1,0:T(8,128)}) conditional(s32[]{:T(128)} %convert_element_type.187, (s32[]{:T(128)}, s32[16,256]{1,0:T(8,128)}, s32[16,256]{1,0:T(8,128)S(1)}, f32[16,256]{1,0:T(8,128)S(1)}, f32[4,32,128]{2,1,0:T(8,128)S(1)}, /*index=5*/s32[8,384]{1,0:T(8,128)}, s32[1,384]{1,0:T(1,128)S(1)}, f32[32,384]{1,0:T(8,128)S(1)}, ...), branch_computations={%region_8.18_spmd, %region_18.21_spmd} | conditional | flops 1831292416 | bytes 337369440 | solution.py:555
  154.3 0.7 copy.125
  155.1 0.8 convert_element_type.163
  155.9 0.7 convert_element_type.164.src_s
  156.5 0.5 dynamic-slice_bitcast_fusion.len_s
  157.1 12.2 %project.1 = bf16[4,3,640,128]{3,2,1,0:T(8,128)(2,1)} custom-call(s32[2560]{0:T(1024)} %convert_element_type.164.src_s, s32[4]{0:T(128)} %dynamic-slice_bitcast_fusion.len_s, f32[32,384]{1,0:T(8,128)S(1)} %get-tuple-element.93.lg_ref, s32[8,384]{1,0:T(8,128)} %get-tuple-element.94.cand_ref, s32[1,384]{1,0:T(1,128)} %copy-done.8, ...), custom_call_target="tpu_custom_call" | custom-call | tf_op jit(solution)/shard_map/cond/branch_1_fun/project/pallas_call | solution.py:309
  169.3 34.2 %reduce-scatter.9.cloned.1.call-done = bf16[1,3,640,128]{3,2,1,0:T(8,128)(2,1)} async-done(((bf16[4,3,640,128]{3,2,1,0:T(8,128)(2,1)}), bf16[1,3,640,128]{3,2,1,0:T(8,128)(2,1)}) %reduce-scatter.9.cloned.1.call-update) | async-done | bytes 491536 | tf_op jit(solution)/shard_map/cond/branch_1_fun/reduce_scatter | solution.py:545
  203.6 1.1 reshape.579
  204.7 0.6 fusion.77
  205.4 0.6 convert_element_type.162.at_s
  206.0 0.6 convert_element_type.160.pos_s
  206.6 0.7 reduce_sum.77.len_s
  207.2 67.1 %all-gather.6.cloned.1.call-done.rows_ref = bf16[8,3,640,128]{3,2,1,0:T(8,128)(2,1)} async-done(((bf16[1,3,640,128]{3,2,1,0:T(8,128)(2,1)}), bf16[8,3,640,128]{3,2,1,0:T(8,128)(2,1)}) %all-gather.6.cloned.1.call-update) | async-done | bytes 3932176 | tf_op jit(solution)/shard_map/cond/branch_1_fun/all_gather | solution.py:546
  274.4 12.6 %insert.1 = f32[2,32,64,128]{3,2,1,0:T(8,128)} custom-call(s32[8]{0:T(128)} %reduce_sum.77.len_s, s32[5120]{0:T(1024)} %convert_element_type.160.pos_s, s32[5120]{0:T(1024)} %convert_element_type.162.at_s, f32[5120]{0:T(1024)} %bitcast.155, bf16[8,3,640,128]{3,2,1,0:T(8,128)(2,1)} %all-gather.6.cloned.1.call-done.rows_ref, ...), custom_call_target="tpu_custom_call" | custom-call | tf_op jit(solution)/shard_map/cond/branch_1_fun/insert/pallas_call | solution.py:386
  (48 shorter events, 1.1 us)
Async XLA Ops:
  6.5 90.2 %reduce-scatter.11.cloned.1.call-start = ((), (), s32[]{:S(2)}) async-start(), calls=%async_computation.9 | async-start | bytes 2359296 | tf_op jit(solution)/shard_map/reduce_scatter | solution.py:492
  14.8 14.9 %copy-start.3 = (s32[64,256]{1,0:T(8,128)S(1)}, s32[64,256]{1,0:T(8,128)}, u32[]{:S(2)}) copy-start(s32[64,256]{1,0:T(8,128)} %param.18) | copy-start | bytes 196612
  14.8 14.9 %copy-start.2 = (s32[64,256]{1,0:T(8,128)S(1)}, s32[64,256]{1,0:T(8,128)}, u32[]{:S(2)}) copy-start(s32[64,256]{1,0:T(8,128)} %param.19) | copy-start | bytes 196612
  14.8 15.5 %copy-start.10 = (s32[384]{0:T(512)S(1)}, s32[384]{0:T(512)}, u32[]{:S(2)}) copy-start(s32[384]{0:T(512)} %param.15) | copy-start | bytes 4612
  14.8 19.8 %copy-start.4 = (f32[64,256]{1,0:T(8,128)S(1)}, f32[64,256]{1,0:T(8,128)}, u32[]{:S(2)}) copy-start(f32[64,256]{1,0:T(8,128)} %param.20) | copy-start | bytes 196612
  29.5 6.1 %copy-start.9 = (f32[384]{0:T(512)S(1)}, f32[384]{0:T(512)}, u32[]{:S(2)}) copy-start(f32[384]{0:T(512)} %param.13) | copy-start | bytes 4612
  29.6 85.0 %all-gather.8.cloned.1.call-start = ((), (), s32[]{:S(2)}) async-start(), calls=%async_computation.10 | async-start | bytes 1310720 | tf_op jit(solution)/shard_map/all_gather | solution.py:493
  30.2 3.6 %copy-start.6 = (s32[4,8]{1,0:T(4,128)}, s32[4,8]{1,0:T(4,128)S(1)}, u32[]{:S(2)}) copy-start(s32[4,8]{1,0:T(4,128)S(1)} %get-tuple-element.247) | copy-start | bytes 388
  106.5 47.5 %copy-start.7 = (s32[1,384]{1,0:T(1,128)S(1)}, s32[1,384]{1,0:T(1,128)}, u32[]{:S(2)}) copy-start(s32[1,384]{1,0:T(1,128)} %broadcast_in_dim.46) | copy-start | bytes 4612
  154.3 0.8 copy-start.8
  154.3 49.3 %reduce-scatter.9.cloned.1.call-start = ((), (), s32[]{:S(2)}) async-start(), calls=%async_computation.7 | async-start | bytes 2457600 | tf_op jit(solution)/shard_map/cond/branch_1_fun/reduce_scatter | solution.py:545
  169.3 105.1 %all-gather.6.cloned.1.call-start = ((), (), s32[]{:S(2)}) async-start(), calls=%async_computation.8 | async-start | bytes 4423680 | tf_op jit(solution)/shard_map/cond/branch_1_fun/all_gather | solution.py:546
Sparse Core Ops, SparseCore 0:
  29.7 67.0 reduce-scatter.10
  98.3 16.2 all-gather.7
  169.4 34.1 reduce-scatter.8
  205.6 68.6 all-gather.5

commit v2 on v1

--- a/solution.py
+++ b/solution.py
@@ -1,8 +1,8 @@
 import math
-from functools import partial
 
 import jax
 import jax.numpy as jnp
+import numpy as np
 from jax import lax
 from jax.experimental import pallas as pl
 from jax.experimental.pallas import tpu as pltpu
@@ -48,44 +48,75 @@
     return (jnp.cos(angle), jnp.sin(angle))
 
 
-def extract_kernel(idx_s, flag_s, vol_ref, w_ref, out_ref, pair):
-    blocks = out_ref.shape[0]
-    groups = out_ref.shape[2] // 16
-
-    def block_step(blk, carry):
-        def group_step(g, inner):
-            at = blk * groups + g
+def along_z(n_vol, shift):
+    count = n_vol // 2
+    return [(v, (v // 2 + shift) % count * 2 + v % 2) for v in range(n_vol)]
+
+
+def flip(number, mask):
+    return [(v, v ^ mask) for v in range(number)]
+
+
+def ring_of(n_vol):
+    return list(range(0, n_vol, 2)) + list(range(n_vol - 1, 0, -2))
+
+
+def ring_order(n_vol):
+    ring = ring_of(n_vol)
+    table = np.zeros((n_vol, n_vol), np.int32)
+    for p, v in enumerate(ring):
+        order = [v]
+        for d in range(1, n_vol // 2):
+            order += [ring[p - d], ring[(p + d) % n_vol]]
+        table[v] = order + [ring[p - n_vol // 2]]
+    return table
+
+
+def extract_kernel(idx_s, wl_s, wu_s, flag_s, blk_s, vol_ref, keep_a, send_a, *rest):
+    pair = rest[-1]
+    parts_b = rest[:-1]
+    count_z = keep_a.shape[0]
+    groups_a = keep_a.shape[2] // 16
+    groups_b = parts_b[0].shape[2] // 16
+    first = lax.broadcasted_iota(jnp.int32, (2, COLS), 0) == 0
+
+    def fill(out, lead, block, skip, groups):
+        def group_step(g, carry):
+            at = block * (groups_a + groups_b) + skip + g
             base = pl.multiple_of(g * 16, 16)
 
             @pl.when(flag_s[at] > 0)
             def _():
                 for u in range(16):
                     i = idx_s[at * 16 + u]
-                    pair[0, 2 * u : 2 * u + 2, :] = vol_ref[0, pl.ds(i, 2), :]
-                    pair[1, 2 * u : 2 * u + 2, :] = vol_ref[1, pl.ds(i, 2), :]
-                w = jnp.broadcast_to(w_ref[pl.ds(pl.multiple_of(at * 16, 16), 16), :], (16, COLS))
+                    w = jnp.where(first, wl_s[at * 16 + u], wu_s[at * 16 + u])
+                    for j in range(2):
+                        pair[j, 2 * u : 2 * u + 2, :] = w * vol_ref[j, pl.ds(i, 2), :]
                 for j in range(2):
-                    lower = pair[j, pl.ds(0, 16, stride=2), :]
-                    upper = pair[j, pl.ds(1, 16, stride=2), :]
-                    value = jnp.where(w >= 0.0, w * lower + (1.0 - w) * upper, 0.0)
-                    out_ref[blk, j, pl.ds(base, 16), :] = value.astype(BF16)
+                    value = pair[j, pl.ds(0, 16, stride=2), :] + pair[j, pl.ds(1, 16, stride=2), :]
+                    out[lead, j, pl.ds(base, 16), :] = value.astype(BF16)
 
             @pl.when(flag_s[at] == 0)
             def _():
                 for j in range(2):
-                    out_ref[blk, j, pl.ds(base, 16), :] = jnp.zeros((16, COLS), BF16)
-
-            return inner
-
-        return lax.fori_loop(0, groups, group_step, carry)
-
-    lax.fori_loop(0, blocks, block_step, 0)
-
-
-def extract(volume, planes, lines, weights, slab_id, n_vol):
+                    out[lead, j, pl.ds(base, 16), :] = jnp.zeros((16, COLS), BF16)
+
+            return carry
+
+        lax.fori_loop(0, groups, group_step, 0)
+
+    for dz in range(count_z):
+        for dy in range(2):
+            block = blk_s[dz * 2 + dy]
+            fill((keep_a, send_a)[dy], dz, block, 0, groups_a)
+            fill(parts_b[dz], dy, block, groups_a, groups_b)
+
+
+def extract(volume, planes, lines, weights, slab_id, n_vol, share_a):
     share = planes.shape[0]
     planes_here = volume.shape[1]
     rows = ROWS // n_vol
+    count_z = n_vol // 2
 
     def order(x):
         return x.reshape(share, n_vol, rows).transpose(1, 0, 2).reshape(-1)
@@ -93,17 +124,55 @@
     local = order(planes) - slab_id * planes_here
     owned = (local >= 0) & (local < planes_here)
     idx = jnp.where(owned, local, 0) * ROWS + order(lines)
-    w = jnp.where(owned, order(weights), -1.0)[:, None]
+    weight = order(weights)
+    lower = jnp.where(owned, weight, 0.0)
+    upper = jnp.where(owned, 1.0 - weight, 0.0)
     flag = jnp.any(owned.reshape(-1, 16), axis=1).astype(jnp.int32)
+    rel = jnp.arange(n_vol)
+    blocks = (slab_id // 2 + rel // 2) % count_z * 2 + (slab_id % 2 + rel) % 2
+    shape_a = jax.ShapeDtypeStruct((count_z, 2, share_a * rows, COLS), BF16)
+    shape_b = jax.ShapeDtypeStruct((2, 2, (share - share_a) * rows, COLS), BF16)
     return pl.pallas_call(
         extract_kernel,
-        out_shape=jax.ShapeDtypeStruct((n_vol, 2, share * rows, COLS), BF16),
-        in_specs=[smem(), smem(), vmem(), vmem()],
-        out_specs=vmem(),
+        out_shape=[shape_a, shape_a] + [shape_b] * count_z,
+        in_specs=[smem()] * 5 + [vmem()],
+        out_specs=[vmem()] * (2 + count_z),
         scratch_shapes=[pltpu.VMEM((2, 32, COLS), F32)],
         compiler_params=pltpu.CompilerParams(vmem_limit_bytes=VMEM_LIMIT),
         name="extract",
-    )(idx, flag, volume.reshape(2, planes_here * ROWS, COLS), w)
+    )(idx, lower, upper, flag, blocks, volume.reshape(2, planes_here * ROWS, COLS))
+
+
+def to_pixel_rows(messages, n_vol):
+    keep_a, send_a, keep_b = messages[:3]
+    got_b = [lax.ppermute(m, "vol", along_z(n_vol, d + 1)) for d, m in enumerate(messages[3:])]
+    got_a = lax.ppermute(send_a, "vol", flip(n_vol, 1))
+    sum_b = sum(got_b, keep_b)
+    out_b = sum_b[0] + lax.ppermute(sum_b[1], "vol", flip(n_vol, 1))
+    sums_a = [keep_a[d] + got_a[d] for d in range(n_vol // 2)]
+    moved = [lax.ppermute(sums_a[d], "vol", along_z(n_vol, d)) for d in range(1, n_vol // 2)]
+    return sum(moved, sums_a[0]), out_b
+
+
+def from_partners(x, n_img):
+    return [x] + [lax.ppermute(x, "img", flip(n_img, m)) for m in range(1, n_img)]
+
+
+def ring_gather(x, n_vol):
+    ring = ring_of(n_vol)
+    ahead = [(ring[p], ring[(p + 1) % n_vol]) for p in range(n_vol)]
+    back = [(b, a) for a, b in ahead]
+    pieces = [x]
+    one = two = x
+    for _ in range(1, n_vol // 2):
+        one = lax.ppermute(one, "vol", ahead)
+        two = lax.ppermute(two, "vol", back)
+        pieces += [one, two]
+    half = x.shape[1] // 2
+    return pieces + [
+        lax.ppermute(one[:, :half], "vol", ahead),
+        lax.ppermute(two[:, half:], "vol", back),
+    ]
 
 
 def weigh_kernel(img_ref, sa_ref, ca_ref, sx_ref, cx_ref, nw_ref, wt_ref, sq_ref, buf):
@@ -161,18 +230,24 @@
     )
 
 
-def logits_kernel(sl_ref, wt_ref, sq_ref, cos_ref, sin_ref, cand_ref, out_ref, part, acc, quad):
+def logits_kernel(group_s, wt_ref, sq_ref, cos_ref, sin_ref, cand_ref, *rest):
+    sl_refs = rest[:-4]
+    out_ref, part, acc, quad = rest[-4:]
     step = pl.program_id(0)
-    groups = sl_ref.shape[0]
-    span = sl_ref.shape[2]
-    rows = groups * span // K
+    groups = len(sl_refs) // 2
+    rows = part.shape[1] // K
+    span = part.shape[1] // groups
     inner = wt_ref.shape[0]
 
     @pl.when(step == 0)
     def _():
-        for i in range(groups):
-            for j in range(2):
-                part[j, i * span : (i + 1) * span, :] = sl_ref[i, j].astype(F32)
+        for m in range(groups):
+            base = group_s[m] * span
+            for ref in sl_refs[2 * m : 2 * m + 2]:
+                size = ref.shape[1]
+                for j in range(2):
+                    part[j, pl.ds(pl.multiple_of(base, 8), size), :] = ref[j].astype(F32)
+                base = base + size
         acc[...] = jnp.zeros_like(acc)
         quad[...] = jnp.zeros_like(quad)
 
@@ -209,7 +284,7 @@
                 out_ref[t * LMAX + l : t * LMAX + l + 1, :] = jnp.sum(pick, axis=0, keepdims=True)
 
 
-def candidate_logits(slices, weighted, squared, cosine, sine, cand):
+def candidate_logits(group_ids, slices, weighted, squared, cosine, sine, cand):
     rows, count = squared.shape[:2]
     inner = 8
     return pl.pallas_call(
@@ -217,13 +292,14 @@
         grid=(rows // inner,),
         out_shape=jax.ShapeDtypeStruct((TRANS * LMAX, count), F32),
         in_specs=[
-            pl.BlockSpec(slices.shape, lambda s: (0, 0, 0, 0)),
+            smem(),
             pl.BlockSpec((inner, count, 2 * COLS), lambda s: (s, 0, 0)),
             pl.BlockSpec((inner, count, COLS), lambda s: (s, 0, 0)),
             pl.BlockSpec((TRANS, inner, COLS), lambda s: (0, s, 0)),
             pl.BlockSpec((TRANS, inner, COLS), lambda s: (0, s, 0)),
             pl.BlockSpec((LMAX, count), lambda s: (0, 0)),
-        ],
+        ]
+        + [pl.BlockSpec(x.shape, lambda s: (0, 0, 0)) for x in slices],
         out_specs=pl.BlockSpec((TRANS * LMAX, count), lambda s: (0, 0)),
         scratch_shapes=[
             pltpu.VMEM((2, K * rows, COLS), F32),
@@ -232,7 +308,7 @@
         ],
         compiler_params=params(1),
         name="logits",
-    )(slices, weighted, squared, cosine, sine, cand)
+    )(group_ids, weighted, squared, cosine, sine, cand, *slices)
 
 
 def posterior_rows(logits, counts):
@@ -245,17 +321,18 @@
 
 
 def project_kernel(
-    src_s, len_s, lg_ref, cand_ref, cnt_ref, wt_ref, sq_ref, cos_ref, sin_ref,
-    out_ref, post, post_sum, num, pick,
+    src_s, len_s, group_s, cand_ref, cnt_ref, wt_ref, sq_ref, cos_ref, sin_ref, *rest
 ):
+    lg_refs = rest[:-6]
+    keep_ref, send_ref, post, post_sum, num, pick = rest[-6:]
     step = pl.program_id(0)
     inner = wt_ref.shape[0]
-    parts = out_ref.shape[0]
-    cap = out_ref.shape[2]
+    parts = 2 * keep_ref.shape[0]
+    cap = keep_ref.shape[2]
 
     @pl.when(step == 0)
     def _():
-        prob = posterior_rows(lg_ref[...], cnt_ref[...])
+        prob = posterior_rows(sum([ref[...] for ref in lg_refs[1:]], lg_refs[0][...]), cnt_ref[...])
         ids = lax.broadcasted_iota(jnp.int32, (K, prob.shape[1]), 0)
         total = jnp.zeros((K, prob.shape[1]), F32)
         for t in range(TRANS):
@@ -288,40 +365,44 @@
 
     @pl.when(step == pl.num_programs(0) - 1)
     def _():
-        for q in range(parts):
-
-            def group_step(g, carry):
+        for m in range(parts):
+            q = group_s[m]
+            out_ref = (keep_ref, send_ref)[m % 2]
+
+            def group_step(g, carry, q=q, m=m, out_ref=out_ref):
                 base = pl.multiple_of(g * 16, 16)
                 for u in range(16):
                     s = src_s[q * cap + base + u]
                     for c in range(3):
                         pick[c, u : u + 1, :] = num[c, pl.ds(s, 1), :]
                 for c in range(3):
-                    out_ref[q, c, pl.ds(base, 16), :] = pick[c].astype(BF16)
+                    out_ref[m // 2, c, pl.ds(base, 16), :] = pick[c].astype(BF16)
                 return carry
 
-            lax.fori_loop(0, (len_s[q] + 15) // 16, group_step, 0)
-
-
-def project(src, lengths, logits, cand, counts, weighted, squared, cosine, sine, parts, cap):
+            lax.fori_loop(0, (jnp.minimum(len_s[q], cap) + 15) // 16, group_step, 0)
+
+
+def project(src, lengths, group_ids, logits, cand, counts, weighted, squared, cosine, sine, cap):
     rows, count = squared.shape[:2]
     inner = 8
+    shape = (group_ids.shape[0] // 2, 3, cap, COLS)
     return pl.pallas_call(
         project_kernel,
         grid=(rows // inner,),
-        out_shape=jax.ShapeDtypeStruct((parts, 3, cap, COLS), BF16),
+        out_shape=[jax.ShapeDtypeStruct(shape, BF16)] * 2,
         in_specs=[
             smem(),
             smem(),
-            pl.BlockSpec((TRANS * LMAX, count), lambda s: (0, 0)),
+            smem(),
             pl.BlockSpec((LMAX, count), lambda s: (0, 0)),
             pl.BlockSpec((1, count), lambda s: (0, 0)),
             pl.BlockSpec((inner, count, 2 * COLS), lambda s: (s, 0, 0)),
             pl.BlockSpec((inner, count, COLS), lambda s: (s, 0, 0)),
             pl.BlockSpec((TRANS, inner, COLS), lambda s: (0, s, 0)),
             pl.BlockSpec((TRANS, inner, COLS), lambda s: (0, s, 0)),
-        ],
-        out_specs=pl.BlockSpec((parts, 3, cap, COLS), lambda s: (0, 0, 0, 0)),
+        ]
+        + [pl.BlockSpec((TRANS * LMAX, count), lambda s: (0, 0)) for _ in logits],
+        out_specs=[pl.BlockSpec(shape, lambda s: (0, 0, 0, 0))] * 2,
         scratch_shapes=[
             pltpu.VMEM((TRANS * K, count), BF16),
             pltpu.VMEM((2 * K, count), BF16),
@@ -330,7 +411,7 @@
         ],
         compiler_params=params(1),
         name="project",
-    )(src, lengths, logits, cand, counts, weighted, squared, cosine, sine)
+    )(src, lengths, group_ids, cand, counts, weighted, squared, cosine, sine, *logits)
 
 
 HEAD = 8
@@ -340,69 +421,62 @@
     return lines_here + 2 * HEAD
 
 
-def insert_kernel(len_s, pos_s, at_s, wgt_s, rows_ref, reg_ref, out_ref, acc, buf):
-    step = pl.program_id(0)
-    cap = rows_ref.shape[2]
+def insert_kernel(len_s, pos_s, at_s, wgt_s, order_s, reg_ref, *rest):
+    pieces = rest[:-3]
+    out_ref, acc, buf = rest[-3:]
+    cap = pieces[0].shape[1]
     planes, lines_here = reg_ref.shape[:2]
     stride = line_stride(lines_here)
-
-    @pl.when(step == 0)
-    def _():
-        acc[...] = jnp.zeros_like(acc)
-
-    for c in range(3):
-        buf[c] = rows_ref[0, c].astype(F32)
+    acc[...] = jnp.zeros_like(acc)
     first = lax.broadcasted_iota(jnp.int32, (2, COLS), 0) == 0
-
-    def group_step(g, carry):
-        for u in range(4):
-            e = step * cap + g * 4 + u
-            s = pos_s[e]
-            to = at_s[e]
-            w = wgt_s[e]
-            both = jnp.where(first, w, 1.0 - w)
-            for c in range(3):
-                row = jnp.broadcast_to(buf[c, pl.ds(s, 1), :], (2, COLS))
-                acc[c, pl.ds(to, 2), :] = acc[c, pl.ds(to, 2), :] + both * row
+    for m in range(len(pieces) - 1):
+        for c in range(3):
+            if m < len(pieces) - 2:
+                buf[c] = pieces[m][c].astype(F32)
+            else:
+                buf[c, : cap // 2, :] = pieces[m][c].astype(F32)
+                buf[c, cap // 2 :, :] = pieces[m + 1][c].astype(F32)
+        block = order_s[m]
+
+        def group_step(g, carry, block=block):
+            for u in range(4):
+                e = block * cap + g * 4 + u
+                s = pos_s[e]
+                to = at_s[e]
+                w = wgt_s[e]
+                both = jnp.where(first, w, 1.0 - w)
+                for c in range(3):
+                    row = jnp.broadcast_to(buf[c, pl.ds(s, 1), :], (2, COLS))
+                    acc[c, pl.ds(to, 2), :] = acc[c, pl.ds(to, 2), :] + both * row
+            return carry
+
+        lax.fori_loop(0, (jnp.minimum(len_s[block], cap) + 3) // 4, group_step, 0)
+
+    def plane_step(p, carry):
+        base = pl.multiple_of(p * stride + HEAD, 8)
+        inv = 1.0 / (acc[2, pl.ds(base, lines_here), :] + reg_ref[p])
+        out_ref[0, p] = acc[0, pl.ds(base, lines_here), :] * inv
+        out_ref[1, p] = acc[1, pl.ds(base, lines_here), :] * inv
         return carry
 
-    lax.fori_loop(0, (len_s[step] + 3) // 4, group_step, 0)
-
-    @pl.when(step == pl.num_programs(0) - 1)
-    def _():
-        def plane_step(p, carry):
-            base = pl.multiple_of(p * stride + HEAD, 8)
-            inv = 1.0 / (acc[2, pl.ds(base, lines_here), :] + reg_ref[p])
-            out_ref[0, p] = acc[0, pl.ds(base, lines_here), :] * inv
-            out_ref[1, p] = acc[1, pl.ds(base, lines_here), :] * inv
-            return carry
-
-        lax.fori_loop(0, planes, plane_step, 0)
-
-
-def insert(lengths, positions, targets, weights, received, regularizer):
-    blocks, _, cap, _ = received.shape
+    lax.fori_loop(0, planes, plane_step, 0)
+
+
+def insert(lengths, positions, targets, weights, order, pieces, regularizer):
+    cap = pieces[0].shape[1]
     planes, lines_here = regularizer.shape[:2]
     return pl.pallas_call(
         insert_kernel,
-        grid=(blocks,),
         out_shape=jax.ShapeDtypeStruct((2, planes, lines_here, COLS), F32),
-        in_specs=[
-            smem(),
-            smem(),
-            smem(),
-            smem(),
-            pl.BlockSpec((1, 3, cap, COLS), lambda s: (s, 0, 0, 0)),
-            pl.BlockSpec((planes, lines_here, COLS), lambda s: (0, 0, 0)),
-        ],
-        out_specs=pl.BlockSpec((2, planes, lines_here, COLS), lambda s: (0, 0, 0, 0)),
+        in_specs=[smem()] * 5 + [vmem()] * (1 + len(pieces)),
+        out_specs=vmem(),
         scratch_shapes=[
             pltpu.VMEM((3, planes * line_stride(lines_here), COLS), F32),
             pltpu.VMEM((3, cap, COLS), F32),
         ],
-        compiler_params=params(1),
+        compiler_params=pltpu.CompilerParams(vmem_limit_bytes=VMEM_LIMIT),
         name="insert",
-    )(lengths, positions, targets, weights, received, regularizer)
+    )(lengths, positions, targets, weights, order, regularizer, *pieces)
 
 
 def ranks(member, rows):
@@ -488,16 +562,24 @@
     line_share = lax.dynamic_slice_in_dim(row_line, first, share, 0)
     weight_share = lax.dynamic_slice_in_dim(row_weight, first, share, 0)
 
-    masked = extract(volume, plane_share, line_share, weight_share, slab_id, n_vol)
-    own = lax.psum_scatter(masked, "vol", scatter_dimension=0, tiled=False)
-    slices = lax.all_gather(own, "img", axis=0, tiled=False)
+    aligned = max(1, 16 // rows)
+    share_a = share * 11 // 16 // aligned * aligned
+    messages = extract(volume, plane_share, line_share, weight_share, slab_id, n_vol, share_a)
+    own_a, own_b = to_pixel_rows(messages, n_vol)
+    slices_b = from_partners(own_b, n_img)
+    slices_a = from_partners(own_a, n_img)
+    slices = [x for both in zip(slices_a, slices_b) for x in both]
+    group_ids = group_id ^ jnp.arange(n_img)
 
     cosine, sine = shift_phases(row_freq, col_freq, TRANS)
     weighted, squared = weigh(images, defocus, noise_weight, row_freq, col_freq)
     cand = candidates.T
     count_row = counts[None, :]
-    partial_logits = candidate_logits(slices, weighted, squared, cosine, sine, cand)
-    logits = lax.psum(partial_logits, "vol")
+    partial_logits = candidate_logits(group_ids, slices, weighted, squared, cosine, sine, cand)
+    pair_logits = partial_logits + lax.ppermute(partial_logits, "vol", flip(n_vol, 1))
+    logits = [pair_logits] + [
+        lax.ppermute(pair_logits, "vol", along_z(n_vol, d)) for d in range(1, n_vol // 2)
+    ]
 
     mean = rows * K // n_img
     cap = -(-int(mean + 5.0 * math.sqrt(mean)) // 32) * 32
@@ -537,18 +619,23 @@
     entry_at = entry[:, 1].astype(jnp.int32).reshape(-1)
     entry_w = entry[:, 2].reshape(-1)
 
+    keep, send = project(
+        send_src.reshape(-1), send_len, group_ids, logits, cand, count_row, weighted, squared,
+        cosine, sine, cap,
+    )
+    got = lax.ppermute(send, "img", flip(n_img, 1))
+    summed = [(keep[m].astype(F32) + got[m].astype(F32)).astype(BF16) for m in range(n_img // 2)]
+    moved = [lax.ppermute(summed[m], "img", flip(n_img, 2 * m)) for m in range(1, n_img // 2)]
+    own_rows = sum([x.astype(F32) for x in moved], summed[0].astype(F32)).astype(BF16)
+    pieces = ring_gather(own_rows, n_vol)
+    order = jnp.asarray(ring_order(n_vol))[slab_id]
+
     def listed_path():
-        listed = project(
-            send_src.reshape(-1), send_len, logits, cand, count_row, weighted, squared,
-            cosine, sine, n_img, cap,
-        )
-        summed = lax.psum_scatter(listed, "img", scatter_dimension=0, tiled=False)
-        received = lax.all_gather(summed, "vol", axis=0, tiled=False)
-        return insert(entry_len, entry_pos, entry_at, entry_w, received, regularizer)
+        return insert(entry_len, entry_pos, entry_at, entry_w, order, pieces, regularizer)
 
     def other_path():
         return dense_path(
-            logits, cand, count_row, weighted, squared, cosine, sine,
+            sum(logits[1:], logits[0]), cand, count_row, weighted, squared, cosine, sine,
             plane_share, line_share, weight_share, regularizer, slab_id,
         )
 

time: 295 us -> 216 us (0.73)
  waiting for transfers between devices: 151 us -> 54.7 us
  blocking collectives: 30.9 us -> 0 us
  starting transfers between devices: 0.13 us -> 29.1 us
  other arithmetic: 11.2 us -> 24.5 us
  local copies, waits for them, and re-layouts: 13.5 us -> 19.1 us
  Pallas kernels: 63.4 us -> 59.4 us
    reduce_scatter x2 -> x0, waiting for transfers between devices: 75.4 us -> none  [the longest x1 41.2 us: body(): own = lax.psum_scatter(masked, 'vol', scatter_dimension=0, tiled=False)]
    all_gather x2 -> x0, waiting for transfers between devices: 75.3 us -> none  [the longest x1 67.1 us: listed_path(): received = lax.all_gather(summed, 'vol', axis=0, tiled=False)]
    ppermute x0 -> x28, waiting for transfers between devices: none -> 54.7 us  [the longest x3 14.8 us: ring_gather(): two = lax.ppermute(two, 'vol', back)]
    psum x1 -> x0, blocking collectives: 30.9 us -> none  [body(): logits = lax.psum(partial_logits, 'vol')]
    ppermute x0 -> x28, starting transfers between devices: none -> 29.1 us  [the longest x3 6.29 us: body(): lax.ppermute(pair_logits, 'vol', along_z(n_vol, d))]
    add x0 -> x6, other arithmetic: none -> 4.47 us  [the longest x1 1.15 us: to_pixel_rows(): sums_a = [keep_a[d] + got_a[d] for d in range(n_vol // 2)]]
    convert_element_type x1 -> x2, other arithmetic: 0.8 us -> 4.59 us  [the longest x1 2.31 us: body(): sum([x.astype(F32) for x in moved], summed[0].astype(F32)).astype(BF16)]
    pallas_call x3, Pallas kernels: 39.6 us -> 35.8 us  [the longest x1 13.1 us: extract(): pl.pallas_call(extract_kernel, out_shape=[shape_a, shape_a] + [shape_b] *...]
  transfers between devices with their start and end apart: 4 -> 28, of which waited for: 4 -> 12; matrix products, arithmetic and copies ran while one was open for 8% -> 17% of each run, Pallas kernels for 5% -> 7%
where the time goes in v2:
time: 216 us; the launch traced here: 213 us
  Pallas kernels  59.4 us (28%)
  waiting for transfers between devices  54.7 us (25%)
  starting transfers between devices  29.1 us (13%)
  other arithmetic  24.5 us (11%)
  local copies, waits for them, and re-layouts  19.1 us (9%)
  between operations  14.6 us (7%)
  matrix products  11.6 us (5%)
    pallas_call x1, Pallas kernels, weigh(): pl.pallas_call(weigh_kernel, grid=(count // step,), out_shape=[jax.ShapeD...  15.4 us
    ppermute x3, waiting for transfers between devices, ring_gather(): two = lax.ppermute(two, 'vol', back)  14.8 us
    pallas_call x1, Pallas kernels, extract(): pl.pallas_call(extract_kernel, out_shape=[shape_a, shape_a] + [shape_b] *...  13.1 us
    pallas_call x1, Pallas kernels, project(): pl.pallas_call(project_kernel, grid=(rows // inner,), out_shape=[jax.Shap...  12.9 us
    ppermute x1, waiting for transfers between devices, body(): lax.ppermute(summed[m], 'img', flip(n_img, 2 * m))  11.1 us
    ppermute x3, waiting for transfers between devices, to_pixel_rows(): lax.ppermute(sums_a[d], 'vol', along_z(n_vol, d))  10.6 us
    pallas_call x1, Pallas kernels, insert(): pl.pallas_call(insert_kernel, out_shape=jax.ShapeDtypeStruct((2, planes,...  9.87 us
    pallas_call x1, Pallas kernels, candidate_logits(): pl.pallas_call(logits_kernel, grid=(rows // inner,), out_shape=jax.ShapeD...  8.17 us
  transfers between devices with their start and end apart: 28, of which 12 were waited for; matrix products, arithmetic and copies ran while one was open for 17% of the time, Pallas kernels for 7%

profile of v2, /device:TPU:12, one launch (start us, length us, event | category | flops | bytes accessed | tf_op | source)
XLA Modules:
  0.0 213.2 jit_solution(5866094398296732492)
XLA Ops:
  8.0 1.3 compare_and_fusion.2
  12.6 13.1 %extract.1 = (bf16[4,2,352,128]{3,2,1,0:T(8,128)(2,1)}, bf16[4,2,352,128]{3,2,1,0:T(8,128)(2,1)}, bf16[2,2,160,128]{3,2,1,0:T(8,128)(2,1)}, bf16[2,2,160,128]{3,...) custom-call(s32[4096]{0:T(1024)} %multiply_add_fusion.1.idx_s, ...), custom_call_target="tpu_custom_call" | custom-call | tf_op jit(solution)/shard_map/extract/pallas_call | solution.py:135
  26.5 1.5 collective-permute-start.6
  28.0 1.5 collective-permute-start
  30.8 1.5 multiply_cosine_fusion
  32.3 1.5 fusion.44
  34.1 6.4 %collective-permute-done.5 = bf16[2,2,160,128]{3,2,1,0:T(8,128)(2,1)S(1)} collective-permute-done((bf16[2,2,160,128]{3,2,1,0:T(8,128)(2,1)}, bf16[2,2,160,128]{3,2,1,0:T(8,128)(2,1)S(1)}, u32[]{:S(2)}, u32[]{:S(2)}) %collective-permute-start.5) | collective-permute-done | bytes 163872 | tf_op jit(solution)/shard_map/ppermute | solution.py:148
  40.5 1.0 collective-permute-done.6
  41.5 0.9 add_add_fusion
  43.2 2.5 %collective-permute-done = bf16[4,2,352,128]{3,2,1,0:T(8,128)(2,1)S(1)} collective-permute-done((bf16[4,2,352,128]{3,2,1,0:T(8,128)(2,1)}, bf16[4,2,352,128]{3,2,1,0:T(8,128)(2,1)S(1)}, u32[]{:S(2)}, u32[]{:S(2)}) %collective-permute-start) | collective-permute-done | bytes 720928 | tf_op jit(solution)/shard_map/ppermute | solution.py:149
  45.7 1.2 fusion.48
  46.9 1.6 collective-permute-start.1
  48.5 1.5 collective-permute-start.3
  50.0 2.3 %collective-permute-start.2 = (bf16[2,352,128]{2,1,0:T(8,128)(2,1)S(1)}, bf16[2,352,128]{2,1,0:T(8,128)(2,1)S(1)}, u32[]{:S(2)}, u32[]{:S(2)}) collective-permute-start(bf16[2,352,128]{2,1,0:T(8,128)(2,1)S(1)} %get-tuple-element.332), channel_id=1, source_target_pairs={{0,4},{1,5},{2,6},{3,7},{4,0},{5,1},{6,2},{7,3},{8,12},{9,13},{10,... | collective-permute-start | bytes 540680 | tf_op jit(solution)/shard_map/ppermute | solution.py:153
  52.4 8.7 %collective-permute-done.1 = bf16[2,352,128]{2,1,0:T(8,128)(2,1)S(1)} collective-permute-done((bf16[2,352,128]{2,1,0:T(8,128)(2,1)S(1)}, bf16[2,352,128]{2,1,0:T(8,128)(2,1)S(1)}, u32[]{:S(2)}, u32[]{:S(2)}) %collective-permute-start.1) | collective-permute-done | bytes 180256 | tf_op jit(solution)/shard_map/ppermute | solution.py:153
  61.0 1.9 collective-permute-done.2
  63.0 1.0 fusion.52.rest_0_
  64.0 0.9 collective-permute-start.10
  64.9 1.0 collective-permute-start.8
  66.2 15.4 %weigh.1 = (bf16[32,384,256]{2,1,0:T(8,128)(2,1)S(1)}, bf16[32,384,128]{2,1,0:T(8,128)(2,1)}) custom-call(bf16[2,384,32,128]{3,2,1,0:T(8,128)(2,1)} %img_ref.1, f32[384,32]{1,0:T(8,128)} %get-tuple-element.348.sa_ref, f32[384,32]{1,0:T(8,128)} %get-tuple-element.347.ca_ref, f32[384,128]{1,0:T(8,128)} %get-tuple-element.346.sx_ref, ...), custom_call_target="tpu_custom_call" | custom-call | tf_op jit(solution)/shard_map/weigh/pallas_call | solution.py:201
  81.6 0.9 collective-permute-start.11
  82.5 1.0 iota_xor_fusion.group_s
  83.5 2.7 %collective-permute-done.11.rest_5_ = bf16[2,160,128]{2,1,0:T(8,128)(2,1)S(1)} collective-permute-done((bf16[2,160,128]{2,1,0:T(8,128)(2,1)S(1)}, bf16[2,160,128]{2,1,0:T(8,128)(2,1)S(1)}, u32[]{:S(2)}, u32[]{:S(2)}) %collective-permute-start.11) | collective-permute-done | bytes 81952 | tf_op jit(solution)/shard_map/ppermute | solution.py:158
  87.1 8.2 %logits.1 = f32[32,384]{1,0:T(8,128)} custom-call(s32[4]{0:T(128)} %iota_xor_fusion.group_s, bf16[32,384,256]{2,1,0:T(8,128)(2,1)S(1)} %get-tuple-element.121.wt_ref, bf16[32,384,128]{2,1,0:T(8,128)(2,1)} %get-tuple-element.122.sq_ref, f32[4,32,128]{2,1,0:T(8,128)S(1)} %get-tuple-element.344.cos_ref, f32[4,32,128]{2,1,0:T(8,128)S(1)} %get-tuple-element.343.sin_ref, ...), custom_call_target="tpu_custom_call" | custom-call | tf_op jit(solution)/shard_map/logits/pallas_call | solution.py:290
  95.2 1.1 collective-permute-start.14
  96.3 3.2 %collective-permute-done.14 = f32[32,384]{1,0:T(8,128)S(1)} collective-permute-done((f32[32,384]{1,0:T(8,128)}, f32[32,384]{1,0:T(8,128)S(1)}, u32[]{:S(2)}, u32[]{:S(2)}) %collective-permute-start.14) | collective-permute-done | bytes 49184 | tf_op jit(solution)/shard_map/ppermute | solution.py:579
  99.6 0.8 add.362.rest_0_
  100.4 2.3 %collective-permute-start.17 = (f32[32,384]{1,0:T(8,128)S(1)}, f32[32,384]{1,0:T(8,128)S(1)}, u32[]{:S(2)}, u32[]{:S(2)}) collective-permute-start(f32[32,384]{1,0:T(8,128)S(1)} %add.362.rest_0_), channel_id=1, source_target_pairs={{0,6},{1,7},{2,0},{3,1},{4,2},{5,3},{6,4},{7,5},{8,14},{9,15},{10,... | collective-permute-start | bytes 147464 | tf_op jit(solution)/shard_map/ppermute | solution.py:581
  102.7 1.1 collective-permute-start.16
  103.8 2.9 %collective-permute-start.15 = (f32[32,384]{1,0:T(8,128)S(1)}, f32[32,384]{1,0:T(8,128)S(1)}, u32[]{:S(2)}, u32[]{:S(2)}) collective-permute-start(f32[32,384]{1,0:T(8,128)S(1)} %add.362.rest_0_), channel_id=1, source_target_pairs={{0,2},{1,3},{2,4},{3,5},{4,6},{5,7},{6,0},{7,1},{8,10},{9,11},{10,... | collective-permute-start | bytes 147464 | tf_op jit(solution)/shard_map/ppermute | solution.py:581
  106.6 0.8 fusion.33
  108.9 12.9 %project.1 = (bf16[2,3,640,128]{3,2,1,0:T(8,128)(2,1)}, bf16[2,3,640,128]{3,2,1,0:T(8,128)(2,1)}) custom-call(s32[2560]{0:T(1024)} %convert_element_type.250.src_s, s32[4]{0:T(128)} %dynamic-slice_reduce_fusion.len_s, s32[4]{0:T(128)} %iota_xor_fusion.group_s, s32[8,384]{1,0:T(8,128)S(1)} %bitcast.180, s32[1,384]{1,0:T(1,128)S(1)} %broadcast_in_dim.48.cnt_ref, ...), custom_call_target="tpu_custom_call" | custom-call | tf_op jit(solution)/shard_map/project/pallas_call | solution.py:389
  122.4 2.2 %collective-permute-done.18 = bf16[2,3,640,128]{3,2,1,0:T(8,128)(2,1)S(1)} collective-permute-done((bf16[2,3,640,128]{3,2,1,0:T(8,128)(2,1)}, bf16[2,3,640,128]{3,2,1,0:T(8,128)(2,1)S(1)}, u32[]{:S(2)}, u32[]{:S(2)}) %collective-permute-start.18) | collective-permute-done | bytes 983072 | tf_op jit(solution)/shard_map/ppermute | solution.py:626
  124.6 2.3 %fusion.41 = bf16[3,640,128]{2,1,0:T(8,128)(2,1)} fusion(bf16[2,3,640,128]{3,2,1,0:T(8,128)(2,1)S(1)} %collective-permute-done.18, bf16[2,3,640,128]{3,2,1,0:T(8,128)(2,1)} %get-tuple-element.129), kind=kLoop, calls=%fused_computation.77 | loop fusion | flops 983040 | bytes 1474560 | tf_op jit(solution)/shard_map/convert_element_type | solution.py:627
  126.9 0.8 collective-permute-start.19
  129.3 11.1 %collective-permute-done.19 = bf16[3,640,128]{2,1,0:T(8,128)(2,1)} collective-permute-done((bf16[3,640,128]{2,1,0:T(8,128)(2,1)}, bf16[3,640,128]{2,1,0:T(8,128)(2,1)}, u32[]{:S(2)}, u32[]{:S(2)}) %collective-permute-start.19) | collective-permute-done | bytes 491552 | tf_op jit(solution)/shard_map/ppermute | solution.py:628
  140.4 2.3 %fusion.35 = bf16[3,640,128]{2,1,0:T(8,128)(2,1)} fusion(bf16[3,640,128]{2,1,0:T(8,128)(2,1)} %collective-permute-done.19, bf16[2,3,640,128]{3,2,1,0:T(8,128)(2,1)} %copy-done.5, bf16[2,3,640,128]{3,2,1,0:T(8,128)(2,1)} %get-tuple-element.129), kind=kLoop, calls=%fused_computation.68 | loop fusion | flops 1966080 | bytes 1966080 | tf_op jit(solution)/shard_map/convert_element_type | solution.py:629
  142.8 1.8 collective-permute-start.21
  145.6 0.8 fusion.31
  146.4 0.9 fusion.59
  147.3 8.5 %collective-permute-done.21 = bf16[3,640,128]{2,1,0:T(8,128)(2,1)} collective-permute-done((bf16[3,640,128]{2,1,0:T(8,128)(2,1)}, bf16[3,640,128]{2,1,0:T(8,128)(2,1)}, u32[]{:S(2)}, u32[]{:S(2)}) %collective-permute-start.21) | collective-permute-done | bytes 491552 | tf_op jit(solution)/shard_map/ppermute | solution.py:169
  155.8 1.4 collective-permute-start.23
  157.9 1.5 fusion.30
  160.1 1.6 reshape.527
  161.8 1.6 convert_element_type.241
  163.5 0.9 copy.144
  165.1 1.5 fusion.56
  166.6 1.4 collective-permute-done.23
  168.0 1.1 collective-permute-start.25
  169.1 0.9 collective-permute-start.24
  170.0 0.9 pad_maximum_fusion.2
  170.9 1.3 reduce_max.18
  173.0 1.2 iota_compare_fusion.4
  174.2 4.9 %collective-permute-done.25 = bf16[3,640,128]{2,1,0:T(8,128)(2,1)} collective-permute-done((bf16[3,640,128]{2,1,0:T(8,128)(2,1)}, bf16[3,640,128]{2,1,0:T(8,128)(2,1)}, u32[]{:S(2)}, u32[]{:S(2)}) %collective-permute-start.25) | collective-permute-done | bytes 491552 | tf_op jit(solution)/shard_map/ppermute | solution.py:169
  179.2 1.0 slice.112
  180.1 0.9 collective-permute-start.27
  181.0 1.0 slice.111
  182.0 1.2 collective-permute-start.26
  183.2 6.8 %fusion.24 = f32[8,3,20,32]{3,2,1,0:T(8,128)} fusion(f32[8,3,2048]{2,1,0:T(4,128)S(1)} %copy.145, pred[8,32,2048]{2,1,0:T(8,128)(4,1)S(1)} %iota_compare_fusion.4, s32[8,2048]{1,0:T(8,128)} %get-tuple-element.333), kind=kOutput, calls=%fused_computation.55 | convolution fusion | flops 379387904 | bytes 847872 | tf_op jit(solution)/shard_map/xnh,xvln->xvhl/dot_general | solution.py:497
  190.1 14.9 %conditional.1 = (f32[2,32,64,128]{3,2,1,0:T(8,128)S(1)}) conditional(s32[]{:T(128)} %convert_element_type.228, (s32[]{:T(128)}, s32[16,256]{1,0:T(8,128)}, s32[16,256]{1,0:T(8,128)}, f32[16,256]{1,0:T(8,128)}, f32[4,32,128]{2,1,0:T(8,128)S(1)}, /*index=5*/s32[8,384]{1,0:T(8,128)}, s32[1,384]{1,0:T(1,128)S(1)}, f32[32,384]{1,0:T(8,128)S(1)}, ...), branch_computations={%region_6.16_spmd, %region_16.18_spmd} | conditional | flops 1831304704 | bytes 337697184 | solution.py:642
  190.3 1.3 dynamic-slice_bitcast_fusion.order_s
  192.2 1.1 reshape.550
  195.2 9.9 %insert.1 = f32[2,32,64,128]{3,2,1,0:T(8,128)S(1)} custom-call(s32[8]{0:T(128)} %reduce_sum.77.len_s, s32[5120]{0:T(1024)} %convert_element_type.188.pos_s, s32[5120]{0:T(1024)} %convert_element_type.190.at_s, f32[5120]{0:T(1024)} %bitcast.182, s32[8]{0:T(128)} %dynamic-slice_bitcast_fusion.order_s, f32[32,64,128]{2,1,0:T(8,128)} %get-tuple-element.101.reg_ref, ...), custom_call_target="tpu_custom_call" | custom-call | tf_op jit(solution)/shard_map/cond/branch_1_fun/insert/pallas_call | solution.py:468
  205.1 1.3 copy-done.4
  (148 shorter events, 18.5 us)
Async XLA Ops:
  6.5 23.0 %copy-start.7 = (s32[64,256]{1,0:T(8,128)S(1)}, s32[64,256]{1,0:T(8,128)}, u32[]{:S(2)}) copy-start(s32[64,256]{1,0:T(8,128)} %param.20) | copy-start | bytes 196612
  6.5 24.2 %copy-start.34 = (f32[384]{0:T(512)S(1)}, f32[384]{0:T(512)}, u32[]{:S(2)}) copy-start(f32[384]{0:T(512)} %param.14) | copy-start | bytes 4612
  7.3 20.7 %copy-start.19 = (f32[16,256]{1,0:T(8,128)}, f32[16,256]{1,0:T(8,128)S(1)}, u32[]{:S(2)}) copy-start(f32[16,256]{1,0:T(8,128)S(1)} %constant_dynamic-slice_fusion.2) | copy-start | bytes 49156
  8.0 20.0 %copy-start.21 = (s32[16,256]{1,0:T(8,128)}, s32[16,256]{1,0:T(8,128)S(1)}, u32[]{:S(2)}) copy-start(s32[16,256]{1,0:T(8,128)S(1)} %constant_dynamic-slice_fusion.3) | copy-start | bytes 49156
  25.7 8.3 %collective-permute-start.4 = (bf16[2,2,160,128]{3,2,1,0:T(8,128)(2,1)}, bf16[2,2,160,128]{3,2,1,0:T(8,128)(2,1)S(1)}, u32[]{:S(2)}, u32[]{:S(2)}) collective-permute-start(bf16[2,2,160,128]{3,2,1,0:T(8,128)(2,1)} %get-tuple-element.126), channel_id=1, source_target_pairs={{0,2},{1,3},{2,4},{3,5},{4,6},{5,7},{6,0},{7,1},{8,10},{9,11},{10,... | collective-permute-start | bytes 491528 | tf_op jit(solution)/shard_map/ppermute | solution.py:148
  26.0 14.5 %collective-permute-start.5 = (bf16[2,2,160,128]{3,2,1,0:T(8,128)(2,1)}, bf16[2,2,160,128]{3,2,1,0:T(8,128)(2,1)S(1)}, u32[]{:S(2)}, u32[]{:S(2)}) collective-permute-start(bf16[2,2,160,128]{3,2,1,0:T(8,128)(2,1)} %get-tuple-element.127), channel_id=1, source_target_pairs={{0,4},{1,5},{2,6},{3,7},{4,0},{5,1},{6,2},{7,3},{8,12},{9,13},{10,... | collective-permute-start | bytes 491528 | tf_op jit(solution)/shard_map/ppermute | solution.py:148
  26.5 15.0 %collective-permute-start.6 = (bf16[2,2,160,128]{3,2,1,0:T(8,128)(2,1)}, bf16[2,2,160,128]{3,2,1,0:T(8,128)(2,1)S(1)}, u32[]{:S(2)}, u32[]{:S(2)}) collective-permute-start(bf16[2,2,160,128]{3,2,1,0:T(8,128)(2,1)} %get-tuple-element.128), channel_id=1, source_target_pairs={{0,6},{1,7},{2,0},{3,1},{4,2},{5,3},{6,4},{7,5},{8,14},{9,15},{10,... | collective-permute-start | bytes 491528 | tf_op jit(solution)/shard_map/ppermute | solution.py:148
  28.0 17.7 %collective-permute-start = (bf16[4,2,352,128]{3,2,1,0:T(8,128)(2,1)}, bf16[4,2,352,128]{3,2,1,0:T(8,128)(2,1)S(1)}, u32[]{:S(2)}, u32[]{:S(2)}) collective-permute-start(bf16[4,2,352,128]{3,2,1,0:T(8,128)(2,1)} %get-tuple-element.124), channel_id=1, source_target_pairs={{0,1},{1,0},{2,3},{3,2},{4,5},{5,4},{6,7},{7,6},{8,9},{9,8},{10,11... | collective-permute-start | bytes 2162696 | tf_op jit(solution)/shard_map/ppermute | solution.py:149
  29.8 57.2 %copy-start.26 = (s32[384,8]{0,1:T(8,128)S(1)}, s32[384,8]{0,1:T(8,128)}, u32[]{:S(2)}) copy-start(s32[384,8]{0,1:T(8,128)} %param.15) | copy-start | bytes 36868
  30.0 77.4 %copy-start.31 = (s32[4,8]{1,0:T(4,128)}, s32[4,8]{1,0:T(4,128)S(1)}, u32[]{:S(2)}) copy-start(s32[4,8]{1,0:T(4,128)S(1)} %get-tuple-element.313) | copy-start | bytes 388
  42.5 9.8 %collective-permute-start.7 = (bf16[2,160,128]{2,1,0:T(8,128)(2,1)S(1)}, bf16[2,160,128]{2,1,0:T(8,128)(2,1)S(1)}, u32[]{:S(2)}, u32[]{:S(2)}) collective-permute-start(bf16[2,160,128]{2,1,0:T(8,128)(2,1)S(1)} %slice_bitcast_fusion.3), channel_id=1, source_target_pairs={{0,1},{1,0},{2,3},{3,2},{4,5},{5,4},{6,7},{7,6},{8,9},{9,8},{10,11... | collective-permute-start | bytes 245768 | tf_op jit(solution)/shard_map/ppermute | solution.py:151
  46.9 14.1 %collective-permute-start.1 = (bf16[2,352,128]{2,1,0:T(8,128)(2,1)S(1)}, bf16[2,352,128]{2,1,0:T(8,128)(2,1)S(1)}, u32[]{:S(2)}, u32[]{:S(2)}) collective-permute-start(bf16[2,352,128]{2,1,0:T(8,128)(2,1)S(1)} %get-tuple-element.330), channel_id=1, source_target_pairs={{0,2},{1,3},{2,4},{3,5},{4,6},{5,7},{6,0},{7,1},{8,10},{9,11},{10,... | collective-permute-start | bytes 540680 | tf_op jit(solution)/shard_map/ppermute | solution.py:153
  48.5 12.6 %collective-permute-start.3 = (bf16[2,352,128]{2,1,0:T(8,128)(2,1)S(1)}, bf16[2,352,128]{2,1,0:T(8,128)(2,1)S(1)}, u32[]{:S(2)}, u32[]{:S(2)}) collective-permute-start(bf16[2,352,128]{2,1,0:T(8,128)(2,1)S(1)} %get-tuple-element.331), channel_id=1, source_target_pairs={{0,6},{1,7},{2,0},{3,1},{4,2},{5,3},{6,4},{7,5},{8,14},{9,15},{10,... | collective-permute-start | bytes 540680 | tf_op jit(solution)/shard_map/ppermute | solution.py:153
  50.0 13.0 %collective-permute-start.2 = (bf16[2,352,128]{2,1,0:T(8,128)(2,1)S(1)}, bf16[2,352,128]{2,1,0:T(8,128)(2,1)S(1)}, u32[]{:S(2)}, u32[]{:S(2)}) collective-permute-start(bf16[2,352,128]{2,1,0:T(8,128)(2,1)S(1)} %get-tuple-element.332), channel_id=1, source_target_pairs={{0,4},{1,5},{2,6},{3,7},{4,0},{5,1},{6,2},{7,3},{8,12},{9,13},{10,... | collective-permute-start | bytes 540680 | tf_op jit(solution)/shard_map/ppermute | solution.py:153
  52.3 33.9 %copy-start.9 = (bf16[2,160,128]{2,1,0:T(8,128)(2,1)}, bf16[2,160,128]{2,1,0:T(8,128)(2,1)S(1)}, u32[]{:S(2)}) copy-start(bf16[2,160,128]{2,1,0:T(8,128)(2,1)S(1)} %fusion.53.rest_1_) | copy-start | bytes 245764
  52.3 30.2 %collective-permute-start.13 = (bf16[2,160,128]{2,1,0:T(8,128)(2,1)S(1)}, bf16[2,160,128]{2,1,0:T(8,128)(2,1)S(1)}, u32[]{:S(2)}, u32[]{:S(2)}) collective-permute-start(bf16[2,160,128]{2,1,0:T(8,128)(2,1)S(1)} %fusion.53.rest_1_), channel_id=1, source_target_pairs={{0,24},{8,16},{16,8},{24,0},{1,25},{9,17},{17,9},{25,1},{2,26},{10... | collective-permute-start | bytes 245768 | tf_op jit(solution)/shard_map/ppermute | solution.py:158
  63.9 22.3 %copy-start.6 = (bf16[2,352,128]{2,1,0:T(8,128)(2,1)}, bf16[2,352,128]{2,1,0:T(8,128)(2,1)S(1)}, u32[]{:S(2)}) copy-start(bf16[2,352,128]{2,1,0:T(8,128)(2,1)S(1)} %fusion.52.rest_0_) | copy-start | bytes 540676
  63.9 22.2 %collective-permute-start.12 = (bf16[2,352,128]{2,1,0:T(8,128)(2,1)S(1)}, bf16[2,352,128]{2,1,0:T(8,128)(2,1)S(1)}, u32[]{:S(2)}, u32[]{:S(2)}) collective-permute-start(bf16[2,352,128]{2,1,0:T(8,128)(2,1)S(1)} %fusion.52.rest_0_), channel_id=1, source_target_pairs={{0,24},{8,16},{16,8},{24,0},{1,25},{9,17},{17,9},{25,1},{2,26},{10... | collective-permute-start | bytes 540680 | tf_op jit(solution)/shard_map/ppermute | solution.py:158
  64.0 22.1 %collective-permute-start.10 = (bf16[2,352,128]{2,1,0:T(8,128)(2,1)S(1)}, bf16[2,352,128]{2,1,0:T(8,128)(2,1)S(1)}, u32[]{:S(2)}, u32[]{:S(2)}) collective-permute-start(bf16[2,352,128]{2,1,0:T(8,128)(2,1)S(1)} %fusion.52.rest_0_), channel_id=1, source_target_pairs={{0,16},{8,24},{16,0},{24,8},{1,17},{9,25},{17,1},{25,9},{2,18},{10... | collective-permute-start | bytes 540680 | tf_op jit(solution)/shard_map/ppermute | solution.py:158
  64.9 21.3 %collective-permute-start.8 = (bf16[2,352,128]{2,1,0:T(8,128)(2,1)S(1)}, bf16[2,352,128]{2,1,0:T(8,128)(2,1)S(1)}, u32[]{:S(2)}, u32[]{:S(2)}) collective-permute-start(bf16[2,352,128]{2,1,0:T(8,128)(2,1)S(1)} %fusion.52.rest_0_), channel_id=1, source_target_pairs={{0,8},{8,0},{16,24},{24,16},{1,9},{9,1},{17,25},{25,17},{2,10},{10... | collective-permute-start | bytes 540680 | tf_op jit(solution)/shard_map/ppermute | solution.py:158
  81.6 4.6 %copy-start = (bf16[32,384,256]{2,1,0:T(8,128)(2,1)}, bf16[32,384,256]{2,1,0:T(8,128)(2,1)S(1)}, u32[]{:S(2)}) copy-start(bf16[32,384,256]{2,1,0:T(8,128)(2,1)S(1)} %get-tuple-element.121.wt_ref) | copy-start | bytes 18874372
  81.6 25.8 %copy-start.35 = (s32[384]{0:T(512)S(1)}, s32[384]{0:T(512)}, u32[]{:S(2)}) copy-start(s32[384]{0:T(512)} %param.16) | copy-start | bytes 4612
  81.6 4.5 %collective-permute-start.11 = (bf16[2,160,128]{2,1,0:T(8,128)(2,1)S(1)}, bf16[2,160,128]{2,1,0:T(8,128)(2,1)S(1)}, u32[]{:S(2)}, u32[]{:S(2)}) collective-permute-start(bf16[2,160,128]{2,1,0:T(8,128)(2,1)S(1)} %fusion.53.rest_1_), channel_id=1, source_target_pairs={{0,16},{8,24},{16,0},{24,8},{1,17},{9,25},{17,1},{25,9},{2,18},{10... | collective-permute-start | bytes 245768 | tf_op jit(solution)/shard_map/ppermute | solution.py:158
  82.5 3.7 %copy-start.27 = (bf16[2,160,128]{2,1,0:T(8,128)(2,1)}, bf16[2,160,128]{2,1,0:T(8,128)(2,1)S(1)}, u32[]{:S(2)}) copy-start(bf16[2,160,128]{2,1,0:T(8,128)(2,1)S(1)} %collective-permute-done.13.rest_7_) | copy-start | bytes 245764
  82.5 3.6 %collective-permute-start.9 = (bf16[2,160,128]{2,1,0:T(8,128)(2,1)S(1)}, bf16[2,160,128]{2,1,0:T(8,128)(2,1)S(1)}, u32[]{:S(2)}, u32[]{:S(2)}) collective-permute-start(bf16[2,160,128]{2,1,0:T(8,128)(2,1)S(1)} %fusion.53.rest_1_), channel_id=1, source_target_pairs={{0,8},{8,0},{16,24},{24,16},{1,9},{9,1},{17,25},{25,17},{2,10},{10... | collective-permute-start | bytes 245768 | tf_op jit(solution)/shard_map/ppermute | solution.py:158
  86.1 0.6 copy-start.28
  86.1 0.7 copy-start.29
  86.1 0.8 copy-start.16
  86.2 0.8 copy-start.17
  86.2 0.9 copy-start.18
  95.2 26.6 %copy-start.8 = (s32[64,256]{1,0:T(8,128)S(1)}, s32[64,256]{1,0:T(8,128)}, u32[]{:S(2)}) copy-start(s32[64,256]{1,0:T(8,128)} %param.19) | copy-start | bytes 196612
  95.2 4.3 %collective-permute-start.14 = (f32[32,384]{1,0:T(8,128)}, f32[32,384]{1,0:T(8,128)S(1)}, u32[]{:S(2)}, u32[]{:S(2)}) collective-permute-start(f32[32,384]{1,0:T(8,128)} %logits.1), channel_id=1, source_target_pairs={{0,1},{1,0},{2,3},{3,2},{4,5},{5,4},{6,7},{7,6},{8,9},{9,8},{10,11... | collective-permute-start | bytes 147464 | tf_op jit(solution)/shard_map/ppermute | solution.py:579
  100.4 8.6 %collective-permute-start.17 = (f32[32,384]{1,0:T(8,128)S(1)}, f32[32,384]{1,0:T(8,128)S(1)}, u32[]{:S(2)}, u32[]{:S(2)}) collective-permute-start(f32[32,384]{1,0:T(8,128)S(1)} %add.362.rest_0_), channel_id=1, source_target_pairs={{0,6},{1,7},{2,0},{3,1},{4,2},{5,3},{6,4},{7,5},{8,14},{9,15},{10,... | collective-permute-start | bytes 147464 | tf_op jit(solution)/shard_map/ppermute | solution.py:581
  102.7 6.2 %collective-permute-start.16 = (f32[32,384]{1,0:T(8,128)S(1)}, f32[32,384]{1,0:T(8,128)S(1)}, u32[]{:S(2)}, u32[]{:S(2)}) collective-permute-start(f32[32,384]{1,0:T(8,128)S(1)} %add.362.rest_0_), channel_id=1, source_target_pairs={{0,4},{1,5},{2,6},{3,7},{4,0},{5,1},{6,2},{7,3},{8,12},{9,13},{10,... | collective-permute-start | bytes 147464 | tf_op jit(solution)/shard_map/ppermute | solution.py:581
  103.8 5.1 %collective-permute-start.15 = (f32[32,384]{1,0:T(8,128)S(1)}, f32[32,384]{1,0:T(8,128)S(1)}, u32[]{:S(2)}, u32[]{:S(2)}) collective-permute-start(f32[32,384]{1,0:T(8,128)S(1)} %add.362.rest_0_), channel_id=1, source_target_pairs={{0,2},{1,3},{2,4},{3,5},{4,6},{5,7},{6,0},{7,1},{8,10},{9,11},{10,... | collective-permute-start | bytes 147464 | tf_op jit(solution)/shard_map/ppermute | solution.py:581
  107.5 21.2 %copy-start.32 = (s32[1,384]{1,0:T(1,128)}, s32[1,384]{1,0:T(1,128)S(1)}, u32[]{:S(2)}) copy-start(s32[1,384]{1,0:T(1,128)S(1)} %broadcast_in_dim.48.cnt_ref) | copy-start | bytes 4612
  108.9 12.9 %copy-start.11 = (f32[32,384]{1,0:T(8,128)}, f32[32,384]{1,0:T(8,128)S(1)}, u32[]{:S(2)}) copy-start(f32[32,384]{1,0:T(8,128)S(1)} %collective-permute-done.17.rest_3_) | copy-start | bytes 147460
  108.9 13.0 %copy-start.13 = (f32[32,384]{1,0:T(8,128)}, f32[32,384]{1,0:T(8,128)S(1)}, u32[]{:S(2)}) copy-start(f32[32,384]{1,0:T(8,128)S(1)} %collective-permute-done.16.rest_2_) | copy-start | bytes 147460
  108.9 12.9 %copy-start.15 = (f32[32,384]{1,0:T(8,128)}, f32[32,384]{1,0:T(8,128)S(1)}, u32[]{:S(2)}) copy-start(f32[32,384]{1,0:T(8,128)S(1)} %collective-permute-done.15.rest_1_) | copy-start | bytes 147460
  121.8 2.8 %collective-permute-start.18 = (bf16[2,3,640,128]{3,2,1,0:T(8,128)(2,1)}, bf16[2,3,640,128]{3,2,1,0:T(8,128)(2,1)S(1)}, u32[]{:S(2)}, u32[]{:S(2)}) collective-permute-start(bf16[2,3,640,128]{3,2,1,0:T(8,128)(2,1)} %get-tuple-element.130), channel_id=1, source_target_pairs={{0,8},{8,0},{16,24},{24,16},{1,9},{9,1},{17,25},{25,17},{2,10},{10... | collective-permute-start | bytes 2949128 | tf_op jit(solution)/shard_map/ppermute | solution.py:626
  122.1 23.4 %copy-start.23 = (pred[8,2048]{1,0:T(8,128)(4,1)}, pred[8,2048]{1,0:T(8,128)(4,1)S(1)}, u32[]{:S(2)}) copy-start(pred[8,2048]{1,0:T(8,128)(4,1)S(1)} %ge.42) | copy-start | bytes 49156
  122.4 23.2 %copy-start.24 = (pred[8,2048]{1,0:T(8,128)(4,1)}, pred[8,2048]{1,0:T(8,128)(4,1)S(1)}, u32[]{:S(2)}) copy-start(pred[8,2048]{1,0:T(8,128)(4,1)S(1)} %lt.222) | copy-start | bytes 49156
  124.6 4.0 %copy-start.5 = (bf16[2,3,640,128]{3,2,1,0:T(8,128)(2,1)}, bf16[2,3,640,128]{3,2,1,0:T(8,128)(2,1)S(1)}, u32[]{:S(2)}) copy-start(bf16[2,3,640,128]{3,2,1,0:T(8,128)(2,1)S(1)} %collective-permute-done.18) | copy-start | bytes 2949124
  126.9 13.6 %collective-permute-start.19 = (bf16[3,640,128]{2,1,0:T(8,128)(2,1)}, bf16[3,640,128]{2,1,0:T(8,128)(2,1)}, u32[]{:S(2)}, u32[]{:S(2)}) collective-permute-start(bf16[3,640,128]{2,1,0:T(8,128)(2,1)} %fusion.41), channel_id=1, source_target_pairs={{0,16},{8,24},{16,0},{24,8},{1,17},{9,25},{17,1},{25,9},{2,18},{10... | collective-permute-start | bytes 1474568 | tf_op jit(solution)/shard_map/ppermute | solution.py:628
  128.3 17.3 %copy-start.25 = (pred[1,8,2048]{2,1,0:T(8,128)(4,1)}, pred[1,8,2048]{2,1,0:T(8,128)(4,1)S(1)}, u32[]{:S(2)}) copy-start(pred[1,8,2048]{2,1,0:T(8,128)(4,1)S(1)} %get-tuple-element.309) | copy-start | bytes 49156
  129.3 60.7 %copy-start.2 = (bf16[32,384,128]{2,1,0:T(8,128)(2,1)S(1)}, bf16[32,384,128]{2,1,0:T(8,128)(2,1)}, u32[]{:S(2)}) copy-start(bf16[32,384,128]{2,1,0:T(8,128)(2,1)} %get-tuple-element.122.sq_ref) | copy-start | bytes 9437188
  142.8 13.1 %collective-permute-start.21 = (bf16[3,640,128]{2,1,0:T(8,128)(2,1)}, bf16[3,640,128]{2,1,0:T(8,128)(2,1)}, u32[]{:S(2)}, u32[]{:S(2)}) collective-permute-start(bf16[3,640,128]{2,1,0:T(8,128)(2,1)} %fusion.35), channel_id=1, source_target_pairs={{2,0},{4,2},{6,4},{7,6},{5,7},{3,5},{1,3},{0,1},{10,8},{12,10},{14... | collective-permute-start | bytes 1474568 | tf_op jit(solution)/shard_map/ppermute | solution.py:169
  144.5 12.8 %collective-permute-start.20 = (bf16[3,640,128]{2,1,0:T(8,128)(2,1)}, bf16[3,640,128]{2,1,0:T(8,128)(2,1)}, u32[]{:S(2)}, u32[]{:S(2)}) collective-permute-start(bf16[3,640,128]{2,1,0:T(8,128)(2,1)} %fusion.35), channel_id=1, source_target_pairs={{0,2},{2,4},{4,6},{6,7},{7,5},{5,3},{3,1},{1,0},{8,10},{10,12},{12... | collective-permute-start | bytes 1474568 | tf_op jit(solution)/shard_map/ppermute | solution.py:168
  155.8 12.1 %collective-permute-start.23 = (bf16[3,640,128]{2,1,0:T(8,128)(2,1)}, bf16[3,640,128]{2,1,0:T(8,128)(2,1)}, u32[]{:S(2)}, u32[]{:S(2)}) collective-permute-start(bf16[3,640,128]{2,1,0:T(8,128)(2,1)} %collective-permute-done.21), channel_id=1, source_target_pairs={{2,0},{4,2},{6,4},{7,6},{5,7},{3,5},{1,3},{0,1},{10,8},{12,10},{14... | collective-permute-start | bytes 1474568 | tf_op jit(solution)/shard_map/ppermute | solution.py:169
  157.3 11.8 %collective-permute-start.22 = (bf16[3,640,128]{2,1,0:T(8,128)(2,1)}, bf16[3,640,128]{2,1,0:T(8,128)(2,1)}, u32[]{:S(2)}, u32[]{:S(2)}) collective-permute-start(bf16[3,640,128]{2,1,0:T(8,128)(2,1)} %collective-permute-done.20), channel_id=1, source_target_pairs={{0,2},{2,4},{4,6},{6,7},{7,5},{5,3},{3,1},{1,0},{8,10},{10,12},{12... | collective-permute-start | bytes 1474568 | tf_op jit(solution)/shard_map/ppermute | solution.py:168
  166.6 23.5 %copy-start.33 = (s32[1,384]{1,0:T(1,128)S(1)}, s32[1,384]{1,0:T(1,128)}, u32[]{:S(2)}) copy-start(s32[1,384]{1,0:T(1,128)} %copy-done.32) | copy-start | bytes 4612
  168.0 11.2 %collective-permute-start.25 = (bf16[3,640,128]{2,1,0:T(8,128)(2,1)}, bf16[3,640,128]{2,1,0:T(8,128)(2,1)}, u32[]{:S(2)}, u32[]{:S(2)}) collective-permute-start(bf16[3,640,128]{2,1,0:T(8,128)(2,1)} %collective-permute-done.23), channel_id=1, source_target_pairs={{2,0},{4,2},{6,4},{7,6},{5,7},{3,5},{1,3},{0,1},{10,8},{12,10},{14... | collective-permute-start | bytes 1474568 | tf_op jit(solution)/shard_map/ppermute | solution.py:169
  169.1 11.9 %collective-permute-start.24 = (bf16[3,640,128]{2,1,0:T(8,128)(2,1)}, bf16[3,640,128]{2,1,0:T(8,128)(2,1)}, u32[]{:S(2)}, u32[]{:S(2)}) collective-permute-start(bf16[3,640,128]{2,1,0:T(8,128)(2,1)} %collective-permute-done.22), channel_id=1, source_target_pairs={{0,2},{2,4},{4,6},{6,7},{7,5},{5,3},{3,1},{1,0},{8,10},{10,12},{12... | collective-permute-start | bytes 1474568 | tf_op jit(solution)/shard_map/ppermute | solution.py:168
  173.0 17.1 %copy-start.10 = (s32[8,2048]{1,0:T(8,128)S(1)}, s32[8,2048]{1,0:T(8,128)}, u32[]{:S(2)}) copy-start(s32[8,2048]{1,0:T(8,128)} %get-tuple-element.308) | copy-start | bytes 196612
  173.0 17.1 %copy-start.12 = (f32[32,384]{1,0:T(8,128)S(1)}, f32[32,384]{1,0:T(8,128)}, u32[]{:S(2)}) copy-start(f32[32,384]{1,0:T(8,128)} %copy-done.11) | copy-start | bytes 147460
  173.0 17.1 %copy-start.14 = (f32[32,384]{1,0:T(8,128)S(1)}, f32[32,384]{1,0:T(8,128)}, u32[]{:S(2)}) copy-start(f32[32,384]{1,0:T(8,128)} %copy-done.13) | copy-start | bytes 147460
  180.1 9.9 %collective-permute-start.27 = (bf16[3,320,128]{2,1,0:T(8,128)(2,1)S(1)}, bf16[3,320,128]{2,1,0:T(8,128)(2,1)}, u32[]{:S(2)}, u32[]{:S(2)}) collective-permute-start(bf16[3,320,128]{2,1,0:T(8,128)(2,1)S(1)} %slice.112), channel_id=1, source_target_pairs={{2,0},{4,2},{6,4},{7,6},{5,7},{3,5},{1,3},{0,1},{10,8},{12,10},{14... | collective-permute-start | bytes 737288 | tf_op jit(solution)/shard_map/ppermute | solution.py:174
  182.0 8.1 %collective-permute-start.26 = (bf16[3,320,128]{2,1,0:T(8,128)(2,1)S(1)}, bf16[3,320,128]{2,1,0:T(8,128)(2,1)}, u32[]{:S(2)}, u32[]{:S(2)}) collective-permute-start(bf16[3,320,128]{2,1,0:T(8,128)(2,1)S(1)} %slice.111), channel_id=1, source_target_pairs={{0,2},{2,4},{4,6},{6,7},{7,5},{5,3},{3,1},{1,0},{8,10},{10,12},{12... | collective-permute-start | bytes 737288 | tf_op jit(solution)/shard_map/ppermute | solution.py:173
  205.1 1.3 copy-start.4

commit v3 on v2

--- a/solution.py
+++ b/solution.py
@@ -1,4 +1,5 @@
 import math
+from functools import partial
 
 import jax
 import jax.numpy as jnp
@@ -31,6 +32,10 @@
 
 def vmem():
     return pl.BlockSpec(memory_space=pltpu.VMEM)
+
+
+def hbm():
+    return pl.BlockSpec(memory_space=pl.ANY)
 
 
 def shift_phases(row_freq, col_freq, number):
@@ -72,9 +77,14 @@
     return table
 
 
-def extract_kernel(idx_s, wl_s, wu_s, flag_s, blk_s, vol_ref, keep_a, send_a, *rest):
-    pair = rest[-1]
-    parts_b = rest[:-1]
+def extract_kernel(idx_s, wl_s, wu_s, flag_s, blk_s, vol_hbm, keep_a, send_a, *rest):
+    vol_ref, pair, sem = rest[-3:]
+    parts_b = rest[:-3]
+    load = pltpu.make_async_copy(vol_hbm, vol_ref, sem)
+    load.start()
+    for ref in (keep_a, send_a) + parts_b:
+        ref[...] = jnp.zeros_like(ref)
+    load.wait()
     count_z = keep_a.shape[0]
     groups_a = keep_a.shape[2] // 16
     groups_b = parts_b[0].shape[2] // 16
@@ -95,11 +105,6 @@
                 for j in range(2):
                     value = pair[j, pl.ds(0, 16, stride=2), :] + pair[j, pl.ds(1, 16, stride=2), :]
                     out[lead, j, pl.ds(base, 16), :] = value.astype(BF16)
-
-            @pl.when(flag_s[at] == 0)
-            def _():
-                for j in range(2):
-                    out[lead, j, pl.ds(base, 16), :] = jnp.zeros((16, COLS), BF16)
 
             return carry
 
@@ -135,23 +140,67 @@
     return pl.pallas_call(
         extract_kernel,
         out_shape=[shape_a, shape_a] + [shape_b] * count_z,
-        in_specs=[smem()] * 5 + [vmem()],
+        in_specs=[smem()] * 5 + [hbm()],
         out_specs=[vmem()] * (2 + count_z),
-        scratch_shapes=[pltpu.VMEM((2, 32, COLS), F32)],
+        scratch_shapes=[
+            pltpu.VMEM((2, planes_here * ROWS, COLS), F32),
+            pltpu.VMEM((2, 32, COLS), F32),
+            pltpu.SemaphoreType.DMA,
+        ],
         compiler_params=pltpu.CompilerParams(vmem_limit_bytes=VMEM_LIMIT),
         name="extract",
     )(idx, lower, upper, flag, blocks, volume.reshape(2, planes_here * ROWS, COLS))
 
 
-def to_pixel_rows(messages, n_vol):
+def combine_first_kernel(keep_a, got_a, keep_b, *rest):
+    count_z = keep_a.shape[0]
+    got_b = rest[: count_z - 1]
+    out_a = rest[count_z : 2 * count_z]
+    out_b = rest[2 * count_z :]
+    for d in range(count_z):
+        out_a[d][...] = keep_a[d] + got_a[d]
+    for d in range(2):
+        total = keep_b[d]
+        for ref in got_b:
+            total = total + ref[d]
+        out_b[d][...] = total
+
+
+def combine_last_kernel(*refs):
+    total = refs[0][...]
+    for ref in refs[1:-2]:
+        total = total + ref[...]
+    refs[-1][...] = total
+
+
+def to_pixel_rows(messages, n_vol, first_with, last_with):
     keep_a, send_a, keep_b = messages[:3]
+    count_z = n_vol // 2
     got_b = [lax.ppermute(m, "vol", along_z(n_vol, d + 1)) for d, m in enumerate(messages[3:])]
     got_a = lax.ppermute(send_a, "vol", flip(n_vol, 1))
-    sum_b = sum(got_b, keep_b)
-    out_b = sum_b[0] + lax.ppermute(sum_b[1], "vol", flip(n_vol, 1))
-    sums_a = [keep_a[d] + got_a[d] for d in range(n_vol // 2)]
-    moved = [lax.ppermute(sums_a[d], "vol", along_z(n_vol, d)) for d in range(1, n_vol // 2)]
-    return sum(moved, sums_a[0]), out_b
+    shape_a = jax.ShapeDtypeStruct(keep_a.shape[1:], BF16)
+    shape_b = jax.ShapeDtypeStruct(keep_b.shape[1:], BF16)
+    sums = pl.pallas_call(
+        combine_first_kernel,
+        out_shape=[shape_a] * count_z + [shape_b] * 2,
+        in_specs=[vmem()] * (2 + count_z) + [hbm()],
+        out_specs=[vmem()] * (count_z + 2),
+        compiler_params=pltpu.CompilerParams(vmem_limit_bytes=VMEM_LIMIT),
+        name="combine_first",
+    )(keep_a, got_a, keep_b, *got_b, first_with)
+    sums_a, sums_b = sums[:count_z], sums[count_z:]
+    moved_b = lax.ppermute(sums_b[1], "vol", flip(n_vol, 1))
+    moved = [lax.ppermute(sums_a[d], "vol", along_z(n_vol, d)) for d in range(1, count_z)]
+    out_b = sums_b[0] + moved_b
+    out_a = pl.pallas_call(
+        combine_last_kernel,
+        out_shape=shape_a,
+        in_specs=[vmem()] * count_z + [hbm()],
+        out_specs=vmem(),
+        compiler_params=pltpu.CompilerParams(vmem_limit_bytes=VMEM_LIMIT),
+        name="combine_last",
+    )(sums_a[0], *moved, last_with)
+    return out_a, out_b
 
 
 def from_partners(x, n_img):
@@ -320,15 +369,34 @@
     return (exponent / jnp.sum(exponent, axis=0, keepdims=True)).astype(BF16).astype(F32)
 
 
-def project_kernel(
-    src_s, len_s, group_s, cand_ref, cnt_ref, wt_ref, sq_ref, cos_ref, sin_ref, *rest
-):
+def list_rows(num, src_s, len_s, group_s, outs, pick):
+    parts = 2 * outs[0].shape[0]
+    cap = outs[0].shape[2]
+    comps = num.shape[0]
+    lead = src_s.shape[0] // parts
+    for m in range(parts):
+        q = group_s[m]
+
+        def group_step(g, carry, q=q, m=m):
+            base = pl.multiple_of(g * 16, 16)
+            at = q * lead + g // 2
+            off = g % 2 * 16
+            for u in range(16):
+                s = src_s[at, off + u]
+                for c in range(comps):
+                    pick[c, u : u + 1, :] = num[c, pl.ds(s, 1), :]
+            for c in range(comps):
+                outs[m % 2][m // 2, c, pl.ds(base, 16), :] = pick[c].astype(BF16)
+            return carry
+
+        lax.fori_loop(0, (jnp.minimum(len_s[q, 0], cap) + 15) // 16, group_step, 0)
+
+
+def spread_kernel(src_s, len_s, group_s, cand_ref, cnt_ref, sq_ref, *rest):
     lg_refs = rest[:-6]
     keep_ref, send_ref, post, post_sum, num, pick = rest[-6:]
     step = pl.program_id(0)
-    inner = wt_ref.shape[0]
-    parts = 2 * keep_ref.shape[0]
-    cap = keep_ref.shape[2]
+    inner = sq_ref.shape[0]
 
     @pl.when(step == 0)
     def _():
@@ -347,8 +415,22 @@
         post_sum[K:, :] = (total - high.astype(F32)).astype(BF16)
 
     for u in range(inner):
+        d = jnp.dot(post_sum[...], sq_ref[u], preferred_element_type=F32)
+        base = pl.multiple_of((step * inner + u) * K, K)
+        num[0, pl.ds(base, K), :] = d[:K] + d[K:]
+
+    @pl.when(step == pl.num_programs(0) - 1)
+    def _():
+        list_rows(num, src_s, len_s, group_s, (keep_ref, send_ref), pick)
+
+
+def project_kernel(
+    src_s, len_s, group_s, post, wt_ref, cos_ref, sin_ref, keep_ref, send_ref, num, pick
+):
+    step = pl.program_id(0)
+    inner = wt_ref.shape[0]
+    for u in range(inner):
         y = jnp.dot(post[...], wt_ref[u], preferred_element_type=F32)
-        d = jnp.dot(post_sum[...], sq_ref[u], preferred_element_type=F32)
         re = jnp.zeros((K, COLS), F32)
         im = jnp.zeros((K, COLS), F32)
         for t in range(TRANS):
@@ -361,31 +443,46 @@
         base = pl.multiple_of((step * inner + u) * K, K)
         num[0, pl.ds(base, K), :] = re
         num[1, pl.ds(base, K), :] = im
-        num[2, pl.ds(base, K), :] = d[:K] + d[K:]
 
     @pl.when(step == pl.num_programs(0) - 1)
     def _():
-        for m in range(parts):
-            q = group_s[m]
-            out_ref = (keep_ref, send_ref)[m % 2]
-
-            def group_step(g, carry, q=q, m=m, out_ref=out_ref):
-                base = pl.multiple_of(g * 16, 16)
-                for u in range(16):
-                    s = src_s[q * cap + base + u]
-                    for c in range(3):
-                        pick[c, u : u + 1, :] = num[c, pl.ds(s, 1), :]
-                for c in range(3):
-                    out_ref[m // 2, c, pl.ds(base, 16), :] = pick[c].astype(BF16)
-                return carry
-
-            lax.fori_loop(0, (jnp.minimum(len_s[q], cap) + 15) // 16, group_step, 0)
-
-
-def project(src, lengths, group_ids, logits, cand, counts, weighted, squared, cosine, sine, cap):
+        list_rows(num, src_s, len_s, group_s, (keep_ref, send_ref), pick)
+
+
+def spread(src, lengths, group_ids, logits, cand, counts, squared, cap):
     rows, count = squared.shape[:2]
     inner = 8
-    shape = (group_ids.shape[0] // 2, 3, cap, COLS)
+    shape = (group_ids.shape[0] // 2, 1, cap, COLS)
+    return pl.pallas_call(
+        spread_kernel,
+        grid=(rows // inner,),
+        out_shape=[jax.ShapeDtypeStruct(shape, BF16)] * 2
+        + [jax.ShapeDtypeStruct((TRANS * K, count), BF16)],
+        in_specs=[
+            smem(),
+            smem(),
+            smem(),
+            pl.BlockSpec((LMAX, count), lambda s: (0, 0)),
+            pl.BlockSpec((1, count), lambda s: (0, 0)),
+            pl.BlockSpec((inner, count, COLS), lambda s: (s, 0, 0)),
+        ]
+        + [pl.BlockSpec((TRANS * LMAX, count), lambda s: (0, 0)) for _ in logits],
+        out_specs=[pl.BlockSpec(shape, lambda s: (0, 0, 0, 0))] * 2
+        + [pl.BlockSpec((TRANS * K, count), lambda s: (0, 0))],
+        scratch_shapes=[
+            pltpu.VMEM((2 * K, count), BF16),
+            pltpu.VMEM((1, rows * K, COLS), F32),
+            pltpu.VMEM((1, 16, COLS), F32),
+        ],
+        compiler_params=params(1),
+        name="spread",
+    )(src, lengths, group_ids, cand, counts, squared, *logits)
+
+
+def project(src, lengths, group_ids, post, weighted, cosine, sine, cap):
+    rows, count = weighted.shape[:2]
+    inner = 8
+    shape = (group_ids.shape[0] // 2, 2, cap, COLS)
     return pl.pallas_call(
         project_kernel,
         grid=(rows // inner,),
@@ -394,24 +491,26 @@
             smem(),
             smem(),
             smem(),
-            pl.BlockSpec((LMAX, count), lambda s: (0, 0)),
-            pl.BlockSpec((1, count), lambda s: (0, 0)),
+            pl.BlockSpec((TRANS * K, count), lambda s: (0, 0)),
             pl.BlockSpec((inner, count, 2 * COLS), lambda s: (s, 0, 0)),
-            pl.BlockSpec((inner, count, COLS), lambda s: (s, 0, 0)),
             pl.BlockSpec((TRANS, inner, COLS), lambda s: (0, s, 0)),
             pl.BlockSpec((TRANS, inner, COLS), lambda s: (0, s, 0)),
-        ]
-        + [pl.BlockSpec((TRANS * LMAX, count), lambda s: (0, 0)) for _ in logits],
+        ],
         out_specs=[pl.BlockSpec(shape, lambda s: (0, 0, 0, 0))] * 2,
         scratch_shapes=[
-            pltpu.VMEM((TRANS * K, count), BF16),
-            pltpu.VMEM((2 * K, count), BF16),
-            pltpu.VMEM((3, rows * K, COLS), F32),
-            pltpu.VMEM((3, 16, COLS), F32),
+            pltpu.VMEM((2, rows * K, COLS), F32),
+            pltpu.VMEM((2, 16, COLS), F32),
         ],
         compiler_params=params(1),
         name="project",
-    )(src, lengths, group_ids, cand, counts, weighted, squared, cosine, sine, *logits)
+    )(src, lengths, group_ids, post, weighted, cosine, sine)
+
+
+def to_member(keep, send, n_img):
+    got = lax.ppermute(send, "img", flip(n_img, 1))
+    summed = [(keep[m].astype(F32) + got[m].astype(F32)).astype(BF16) for m in range(n_img // 2)]
+    moved = [lax.ppermute(summed[m], "img", flip(n_img, 2 * m)) for m in range(1, n_img // 2)]
+    return sum([x.astype(F32) for x in moved], summed[0].astype(F32)).astype(BF16)
 
 
 HEAD = 8
@@ -421,81 +520,196 @@
     return lines_here + 2 * HEAD
 
 
-def insert_kernel(len_s, pos_s, at_s, wgt_s, order_s, reg_ref, *rest):
-    pieces = rest[:-3]
+def insert_kernel(start, count, has_acc, mode, len_s, pos_s, at_s, wgt_s, order_s, *rest):
+    pieces = rest[:count]
+    rest = rest[count:]
     out_ref, acc, buf = rest[-3:]
-    cap = pieces[0].shape[1]
-    planes, lines_here = reg_ref.shape[:2]
-    stride = line_stride(lines_here)
-    acc[...] = jnp.zeros_like(acc)
+    extra = rest[:-3]
+    comps, cap = buf.shape[:2]
+    lead = pos_s.shape[0] // order_s.shape[0]
+    if has_acc:
+        pltpu.sync_copy(extra[-1], acc)
+    else:
+        acc[...] = jnp.zeros_like(acc)
     first = lax.broadcasted_iota(jnp.int32, (2, COLS), 0) == 0
-    for m in range(len(pieces) - 1):
-        for c in range(3):
-            if m < len(pieces) - 2:
-                buf[c] = pieces[m][c].astype(F32)
+    index = 0
+    while index < count:
+        m = start + index
+        whole = pieces[index].shape[1] == cap
+        for c in range(comps):
+            if whole:
+                buf[c] = pieces[index][c].astype(F32)
             else:
-                buf[c, : cap // 2, :] = pieces[m][c].astype(F32)
-                buf[c, cap // 2 :, :] = pieces[m + 1][c].astype(F32)
+                buf[c, : cap // 2, :] = pieces[index][c].astype(F32)
+                buf[c, cap // 2 :, :] = pieces[index + 1][c].astype(F32)
+        if whole:
+            index += 1
+        else:
+            index += 2
         block = order_s[m]
 
         def group_step(g, carry, block=block):
+            at = block * lead + g // 8
+            off = g % 8 * 4
             for u in range(4):
-                e = block * cap + g * 4 + u
-                s = pos_s[e]
-                to = at_s[e]
-                w = wgt_s[e]
+                s = pos_s[at, off + u]
+                to = at_s[at, off + u]
+                w = wgt_s[at, off + u]
                 both = jnp.where(first, w, 1.0 - w)
-                for c in range(3):
+                for c in range(comps):
                     row = jnp.broadcast_to(buf[c, pl.ds(s, 1), :], (2, COLS))
                     acc[c, pl.ds(to, 2), :] = acc[c, pl.ds(to, 2), :] + both * row
             return carry
 
-        lax.fori_loop(0, (jnp.minimum(len_s[block], cap) + 3) // 4, group_step, 0)
+        lax.fori_loop(0, (jnp.minimum(len_s[block, 0], cap) + 3) // 4, group_step, 0)
+
+    if mode == "sum":
+        pltpu.sync_copy(acc, out_ref)
+        return
+    planes, lines_here = extra[0].shape[:2]
+    stride = line_stride(lines_here)
 
     def plane_step(p, carry):
         base = pl.multiple_of(p * stride + HEAD, 8)
-        inv = 1.0 / (acc[2, pl.ds(base, lines_here), :] + reg_ref[p])
-        out_ref[0, p] = acc[0, pl.ds(base, lines_here), :] * inv
-        out_ref[1, p] = acc[1, pl.ds(base, lines_here), :] * inv
+        if mode == "inverse":
+            out_ref[p] = 1.0 / (acc[0, pl.ds(base, lines_here), :] + extra[0][p])
+        else:
+            for c in range(comps):
+                out_ref[c, p] = acc[c, pl.ds(base, lines_here), :] * extra[0][p]
         return carry
 
     lax.fori_loop(0, planes, plane_step, 0)
 
 
-def insert(lengths, positions, targets, weights, order, pieces, regularizer):
-    cap = pieces[0].shape[1]
-    planes, lines_here = regularizer.shape[:2]
+def insert(tables, order, start, pieces, cap, block, mode, extra=(), acc=None):
+    comps = pieces[0].shape[0]
+    planes, lines_here = block
+    acc_shape = (comps, planes * line_stride(lines_here), COLS)
+    out = {
+        "sum": acc_shape,
+        "inverse": (planes, lines_here, COLS),
+        "result": (comps, planes, lines_here, COLS),
+    }[mode]
+    more = list(extra) + ([] if acc is None else [acc])
     return pl.pallas_call(
-        insert_kernel,
-        out_shape=jax.ShapeDtypeStruct((2, planes, lines_here, COLS), F32),
-        in_specs=[smem()] * 5 + [vmem()] * (1 + len(pieces)),
-        out_specs=vmem(),
-        scratch_shapes=[
-            pltpu.VMEM((3, planes * line_stride(lines_here), COLS), F32),
-            pltpu.VMEM((3, cap, COLS), F32),
+        partial(insert_kernel, start, len(pieces), acc is not None, mode),
+        out_shape=jax.ShapeDtypeStruct(out, F32),
+        in_specs=[smem()] * 5
+        + [vmem()] * (len(pieces) + len(extra))
+        + [hbm()] * (acc is not None),
+        out_specs=hbm() if mode == "sum" else vmem(),
+        scratch_shapes=[pltpu.VMEM(acc_shape, F32), pltpu.VMEM((comps, cap, COLS), F32)],
+        compiler_params=pltpu.CompilerParams(vmem_limit_bytes=VMEM_LIMIT),
+        name="insert_" + mode,
+    )(*tables, order, *pieces, *more)
+
+
+def running(x):
+    lanes = lax.broadcasted_iota(jnp.int32, x.shape, 1)
+    step = 1
+    while step < x.shape[1]:
+        x = x + jnp.where(lanes >= step, pltpu.roll(x, step, 1), 0)
+        step *= 2
+    return x
+
+
+def split_index(x):
+    return [(x >> 5).astype(F32), (x & 31).astype(F32)]
+
+
+def split_weight(w):
+    a = w.astype(BF16).astype(F32)
+    b = (w - a).astype(BF16).astype(F32)
+    return [a, b, w - a - b]
+
+
+def compacted(member, rank, values, lead):
+    high = jnp.where(member, rank >> 5, -1)
+    low = rank & 31
+    left = lax.broadcasted_iota(jnp.int32, (lead, rank.shape[1]), 0) == high
+    hot = lax.broadcasted_iota(jnp.int32, (32, rank.shape[1]), 0) == low
+    right = jnp.concatenate([jnp.where(hot, v, 0.0).astype(BF16) for v in values], axis=0)
+    return lax.dot_general(
+        left.astype(F32).astype(BF16), right, (((1,), (1,)), ((), ())), preferred_element_type=F32
+    )
+
+
+def lists_kernel(
+    n_img, planes_here, lines_here, cap,
+    plane_ref, line_ref, wgt_ref,
+    src_ref, pos_ref, at_ref, w_ref, send_len, recv_len, longest, own,
+):
+    slab = lax.axis_index("vol")
+    group = lax.axis_index("img")
+    blocks, number = line_ref.shape
+    lead = src_ref.shape[0] // n_img
+    lines = line_ref[...]
+
+    def in_part(x, part):
+        return (x >= part * lines_here - 1) & (x < (part + 1) * lines_here)
+
+    top = jnp.zeros((blocks, COLS), jnp.int32)
+    for q in range(n_img):
+        size = jnp.sum(in_part(lines, q).astype(F32), axis=1, keepdims=True).astype(jnp.int32)
+        top = jnp.maximum(top, jnp.broadcast_to(size, (blocks, COLS)))
+    longest[...] = jnp.broadcast_to(jnp.max(top.astype(F32)), (8, COLS)).astype(jnp.int32)
+
+    own[...] = jnp.broadcast_to(line_ref[pl.ds(slab, 1), :], own.shape)
+    sent = in_part(own[...], lax.broadcasted_iota(jnp.int32, own.shape, 0))
+    total = running(sent.astype(jnp.int32))
+    send_len[...] = jnp.broadcast_to(total[:, number - 1 :], send_len.shape)
+    rank = total - sent.astype(jnp.int32)
+    row_ids = split_index(lax.broadcasted_iota(jnp.int32, (1, number), 1))
+    for q in range(n_img):
+        out = compacted(sent[q : q + 1], rank[q : q + 1], row_ids, lead)
+        src_ref[q * lead : (q + 1) * lead, :] = (32.0 * out[:, :32] + out[:, 32:64]).astype(jnp.int32)
+
+    member = in_part(lines, group)
+    place = running(member.astype(jnp.int32)) - member.astype(jnp.int32)
+    local = plane_ref[...] - slab * planes_here
+    here = member & (local >= 0) & (local < planes_here)
+    total = running(here.astype(jnp.int32))
+    recv_len[...] = jnp.broadcast_to(total[:, number - 1 :], recv_len.shape)
+    rank = total - here.astype(jnp.int32)
+    target = local * line_stride(lines_here) + lines - group * lines_here + HEAD
+    target = jnp.where(here, target, 0)
+    for v in range(blocks):
+        row = slice(v, v + 1)
+        values = split_index(place[row]) + split_index(target[row]) + split_weight(wgt_ref[row, :])
+        out = compacted(here[row], rank[row], values, lead)
+        at = slice(v * lead, (v + 1) * lead)
+        pos_ref[at, :] = (32.0 * out[:, :32] + out[:, 32:64]).astype(jnp.int32)
+        at_ref[at, :] = (32.0 * out[:, 64:96] + out[:, 96:128]).astype(jnp.int32)
+        w_ref[at, :] = out[:, 128:160] + out[:, 160:192] + out[:, 192:224]
+
+
+def lists(row_plane, row_line, row_weight, n_vol, n_img, planes_here, lines_here, cap):
+    lead = -(-(cap // 32) // 8) * 8
+    number = ROWS // n_vol * K
+
+    def order(x):
+        return x.T.reshape(n_vol, number)
+
+    def table(blocks, dtype=jnp.int32):
+        return jax.ShapeDtypeStruct((blocks * lead, 32), dtype)
+
+    return pl.pallas_call(
+        partial(lists_kernel, n_img, planes_here, lines_here, cap),
+        out_shape=[
+            table(n_img),
+            table(n_vol),
+            table(n_vol),
+            table(n_vol, F32),
+            jax.ShapeDtypeStruct((8, COLS), jnp.int32),
+            jax.ShapeDtypeStruct((n_vol, COLS), jnp.int32),
+            jax.ShapeDtypeStruct((8, COLS), jnp.int32),
         ],
+        in_specs=[vmem()] * 3,
+        out_specs=[vmem()] * 7,
+        scratch_shapes=[pltpu.VMEM((8, number), jnp.int32)],
         compiler_params=pltpu.CompilerParams(vmem_limit_bytes=VMEM_LIMIT),
-        name="insert",
-    )(lengths, positions, targets, weights, order, regularizer, *pieces)
-
-
-def ranks(member, rows):
-    x = member.reshape(-1, rows, K).astype(F32)
-    before_k = (jnp.arange(K)[:, None] < jnp.arange(K)[None, :]).astype(F32)
-    before_r = (jnp.arange(rows)[:, None] < jnp.arange(rows)[None, :]).astype(F32)
-    inner = jnp.einsum("xrk,kl->xrl", x, before_k, preferred_element_type=F32)
-    outer = jnp.einsum("xr,rs->xs", jnp.sum(x, axis=2), before_r, preferred_element_type=F32)
-    return (inner + outer[:, :, None]).reshape(member.shape).astype(jnp.int32)
-
-
-def compact(member, rank, values, cap):
-    high = jnp.where(member, rank // 32, -1)
-    low = rank % 32
-    left = (high[:, :, None] == jnp.arange(cap // 32)).astype(F32)
-    hot = low[:, None, None, :] == jnp.arange(32)[None, None, :, None]
-    right = jnp.where(hot, values[:, :, None, :], 0.0)
-    out = jnp.einsum("xnh,xvln->xvhl", left, right, precision=lax.Precision.HIGHEST)
-    return out.reshape(values.shape[0], values.shape[1], cap)
+        name="lists",
+    )(order(row_plane), order(row_line), order(row_weight))
 
 
 def insert_into(carry, piece, planes_all, lines_all, weights_all, slab_id, planes_here):
@@ -565,14 +779,19 @@
     aligned = max(1, 16 // rows)
     share_a = share * 11 // 16 // aligned * aligned
     messages = extract(volume, plane_share, line_share, weight_share, slab_id, n_vol, share_a)
-    own_a, own_b = to_pixel_rows(messages, n_vol)
+    cosine, sine = shift_phases(row_freq, col_freq, TRANS)
+    weighted, squared = weigh(images, defocus, noise_weight, row_freq, col_freq)
+    mean = rows * K // n_img
+    cap = -(-int(mean + 4.2 * math.sqrt(mean)) // 32) * 32
+    src, pos, at, wgt, send_len, recv_len, longest = lists(
+        row_plane, row_line, row_weight, n_vol, n_img, planes_here, lines_here, cap
+    )
+    own_a, own_b = to_pixel_rows(messages, n_vol, weighted, pos)
     slices_b = from_partners(own_b, n_img)
     slices_a = from_partners(own_a, n_img)
     slices = [x for both in zip(slices_a, slices_b) for x in both]
     group_ids = group_id ^ jnp.arange(n_img)
 
-    cosine, sine = shift_phases(row_freq, col_freq, TRANS)
-    weighted, squared = weigh(images, defocus, noise_weight, row_freq, col_freq)
     cand = candidates.T
     count_row = counts[None, :]
     partial_logits = candidate_logits(group_ids, slices, weighted, squared, cosine, sine, cand)
@@ -581,65 +800,29 @@
         lax.ppermute(pair_logits, "vol", along_z(n_vol, d)) for d in range(1, n_vol // 2)
     ]
 
-    mean = rows * K // n_img
-    cap = -(-int(mean + 5.0 * math.sqrt(mean)) // 32) * 32
-    line_b = row_line.T.reshape(n_vol, rows * K)
-    plane_b = row_plane.T.reshape(n_vol, rows * K)
-    weight_b = row_weight.T.reshape(n_vol, rows * K)
-    low_part = line_b // lines_here
-    high_part = (line_b + 1) // lines_here
-    part_ids = jnp.arange(n_img)[:, None, None]
-    members = (low_part == part_ids) | (high_part == part_ids)
-    lengths = jnp.sum(members.astype(jnp.int32), axis=2)
-    fits = jnp.max(lengths) <= cap
-
-    send_member = lax.dynamic_index_in_dim(members, slab_id, 1, keepdims=False)
-    row_ids = jnp.arange(rows * K).astype(F32)
-    send_src = compact(
-        send_member,
-        ranks(send_member, rows),
-        jnp.broadcast_to(row_ids, (n_img, 1, rows * K)),
-        cap,
-    ).astype(jnp.int32)
-    send_len = lax.dynamic_index_in_dim(lengths, slab_id, 1, keepdims=False)
-
-    recv_member = lax.dynamic_index_in_dim(members, group_id, 0, keepdims=False)
-    recv_rank = ranks(recv_member, rows)
-    local_plane = plane_b - slab_id * planes_here
-    here = recv_member & (local_plane >= 0) & (local_plane < planes_here)
-    target = local_plane * line_stride(lines_here) + line_b - group_id * lines_here + HEAD
-    entry = compact(
-        here,
-        ranks(here, rows),
-        jnp.stack([recv_rank.astype(F32), target.astype(F32), weight_b], axis=1),
-        cap,
-    )
-    entry_len = jnp.sum(here.astype(jnp.int32), axis=1)
-    entry_pos = entry[:, 0].astype(jnp.int32).reshape(-1)
-    entry_at = entry[:, 1].astype(jnp.int32).reshape(-1)
-    entry_w = entry[:, 2].reshape(-1)
-
-    keep, send = project(
-        send_src.reshape(-1), send_len, group_ids, logits, cand, count_row, weighted, squared,
-        cosine, sine, cap,
-    )
-    got = lax.ppermute(send, "img", flip(n_img, 1))
-    summed = [(keep[m].astype(F32) + got[m].astype(F32)).astype(BF16) for m in range(n_img // 2)]
-    moved = [lax.ppermute(summed[m], "img", flip(n_img, 2 * m)) for m in range(1, n_img // 2)]
-    own_rows = sum([x.astype(F32) for x in moved], summed[0].astype(F32)).astype(BF16)
-    pieces = ring_gather(own_rows, n_vol)
+    keep_d, send_d, post = spread(
+        src, send_len, group_ids, logits, cand, count_row, squared, cap
+    )
+    keep_n, send_n = project(src, send_len, group_ids, post, weighted, cosine, sine, cap)
+    pieces_d = ring_gather(to_member(keep_d, send_d, n_img), n_vol)
+    pieces_n = ring_gather(to_member(keep_n, send_n, n_img), n_vol)
     order = jnp.asarray(ring_order(n_vol))[slab_id]
-
-    def listed_path():
-        return insert(entry_len, entry_pos, entry_at, entry_w, order, pieces, regularizer)
-
-    def other_path():
-        return dense_path(
+    tables = (recv_len, pos, at, wgt)
+    block = (planes_here, lines_here)
+    early = n_vol // 2 + 1
+    inverse = insert(tables, order, 0, pieces_d, cap, block, "inverse", [regularizer])
+    part_sum = insert(tables, order, 0, pieces_n[:early], cap, block, "sum")
+    result = insert(
+        tables, order, early, pieces_n[early:], cap, block, "result", [inverse], part_sum
+    )
+
+    def dense(state):
+        return False, dense_path(
             sum(logits[1:], logits[0]), cand, count_row, weighted, squared, cosine, sine,
             plane_share, line_share, weight_share, regularizer, slab_id,
         )
 
-    return lax.cond(fits, listed_path, other_path)
+    return lax.while_loop(lambda state: state[0], dense, (longest[0, 0] > cap, result))[1]
 
 
 def solution(mesh):

time: 216 us -> 253 us (1.17)
  Pallas kernels: 59.4 us -> 113 us
  matrix products: 11.6 us -> 0 us
  other arithmetic: 24.5 us -> 13.8 us
  waiting for transfers between devices: 54.7 us -> 45.7 us
  starting transfers between devices: 29.1 us -> 37 us
  local copies, waits for them, and re-layouts: 19.1 us -> 26.2 us
    pallas_call x1 -> x7, Pallas kernels: 9.87 us -> 63.6 us  [the longest x3 42 us: insert(): pl.pallas_call(partial(insert_kernel, start, len(pieces), acc is not None...]
    ppermute x3 -> x6, waiting for transfers between devices: 0.01 us -> 16.6 us  [ring_gather(): one = lax.ppermute(one, 'vol', ahead)]
    ppermute x3 -> x6, waiting for transfers between devices: 14.8 us -> 0.02 us  [ring_gather(): two = lax.ppermute(two, 'vol', back)]
    dot_general x8 -> x0, matrix products: 11.6 us -> none  [the longest x2 7.62 us: compact(): jnp.einsum('xnh,xvln->xvhl', left, right, precision=lax.Precision.HIGHEST)]
    unnamed x62 -> x89, local copies, waits for them, and re-layouts: 2.27 us -> 13.6 us
    ppermute x3, waiting for transfers between devices: 7.45 us -> 0.01 us  [to_pixel_rows(): lax.ppermute(m, 'vol', along_z(n_vol, d + 1))]
    ppermute x3, waiting for transfers between devices: 10.6 us -> 3.86 us  [to_pixel_rows(): lax.ppermute(sums_a[d], 'vol', along_z(n_vol, d))]
    convert_element_type x8 -> x0, local copies, waits for them, and re-layouts: 6.06 us -> none  [the longest x2 2.38 us: body(): target.astype(F32)]
  transfers between devices with their start and end apart: 28 -> 38, of which waited for: 12 -> 15; matrix products, arithmetic and copies ran while one was open for 17% -> 7% of each run, Pallas kernels for 7% -> 21%
where the time goes in v3:
time: 253 us; the launch traced here: 250 us
  Pallas kernels  113 us (45%)
  waiting for transfers between devices  45.7 us (18%)
  starting transfers between devices  37 us (15%)
  local copies, waits for them, and re-layouts  26.2 us (10%)
  between operations  14.5 us (6%)
  other arithmetic  13.8 us (5%)
    pallas_call x3, Pallas kernels, insert(): pl.pallas_call(partial(insert_kernel, start, len(pieces), acc is not None...  42 us
    ppermute x6, waiting for transfers between devices, ring_gather(): one = lax.ppermute(one, 'vol', ahead)  16.6 us
    pallas_call x1, Pallas kernels, weigh(): pl.pallas_call(weigh_kernel, grid=(count // step,), out_shape=[jax.ShapeD...  15.5 us
    unnamed x89, local copies, waits for them, and re-layouts  13.6 us
    pallas_call x1, Pallas kernels, extract(): pl.pallas_call(extract_kernel, out_shape=[shape_a, shape_a] + [shape_b] *...  12.3 us
    pallas_call x1, Pallas kernels, project(): pl.pallas_call(project_kernel, grid=(rows // inner,), out_shape=[jax.Shap...  12.1 us
    pallas_call x1, Pallas kernels, spread(): pl.pallas_call(spread_kernel, grid=(rows // inner,), out_shape=[jax.Shape...  11.7 us
    pallas_call x1, Pallas kernels, candidate_logits(): pl.pallas_call(logits_kernel, grid=(rows // inner,), out_shape=jax.ShapeD...  9.84 us
  transfers between devices with their start and end apart: 38, of which 15 were waited for; matrix products, arithmetic and copies ran while one was open for 7% of the time, Pallas kernels for 21%

profile of v3, /device:TPU:12, one launch (start us, length us, event | category | flops | bytes accessed | tf_op | source)
XLA Modules:
  0.0 250.4 jit_solution(11666900985704512781)
XLA Ops:
  12.5 12.3 %extract.1 = (bf16[4,2,352,128]{3,2,1,0:T(8,128)(2,1)}, bf16[4,2,352,128]{3,2,1,0:T(8,128)(2,1)}, bf16[2,2,160,128]{3,2,1,0:T(8,128)(2,1)}, bf16[2,2,160,128]{3,...) custom-call(s32[4096]{0:T(1024)} %multiply_add_fusion.1.idx_s, ...), custom_call_target="tpu_custom_call" | custom-call | tf_op jit(solution)/shard_map/extract/pallas_call | solution.py:140
  24.9 2.4 collective-permute-start.1
  27.3 1.5 collective-permute-start.3
  28.8 1.5 fusion.29
  30.3 1.5 multiply_cosine_fusion
  31.9 15.5 %weigh.1 = (bf16[32,384,256]{2,1,0:T(8,128)(2,1)S(1)}, bf16[32,384,128]{2,1,0:T(8,128)(2,1)}) custom-call(bf16[2,384,32,128]{3,2,1,0:T(8,128)(2,1)} %img_ref.1, f32[384,32]{1,0:T(8,128)} %get-tuple-element.372.sa_ref, f32[384,32]{1,0:T(8,128)} %get-tuple-element.371.ca_ref, f32[384,128]{1,0:T(8,128)} %get-tuple-element.370.sx_ref, ...), custom_call_target="tpu_custom_call" | custom-call | tf_op jit(solution)/shard_map/weigh/pallas_call | solution.py:250
  47.5 2.5 %copy-done = bf16[32,384,256]{2,1,0:T(8,128)(2,1)} copy-done((bf16[32,384,256]{2,1,0:T(8,128)(2,1)}, bf16[32,384,256]{2,1,0:T(8,128)(2,1)S(1)}, u32[]{:S(2)}) %copy-start) | copy-done | bytes 6291480
  50.4 2.6 %combine_first.1 = (bf16[2,352,128]{2,1,0:T(8,128)(2,1)}, bf16[2,352,128]{2,1,0:T(8,128)(2,1)}, bf16[2,352,128]{2,1,0:T(8,128)(2,1)}, bf16[2,352,128]{2,1,0:T(8,...) custom-call(bf16[4,2,352,128]{3,2,1,0:T(8,128)(2,1)} %get-tuple-element.125.keep_a, ...), custom_call_target="tpu_custom_call" | custom-call | tf_op jit(solution)/shard_map/combine_first/pallas_call | solution.py:183
  53.6 1.1 collective-permute-start.4
  54.6 3.7 %collective-permute-start.5 = (bf16[2,352,128]{2,1,0:T(8,128)(2,1)}, bf16[2,352,128]{2,1,0:T(8,128)(2,1)S(1)}, u32[]{:S(2)}, u32[]{:S(2)}) collective-permute-start(bf16[2,352,128]{2,1,0:T(8,128)(2,1)} %get-tuple-element.133), channel_id=1, source_target_pairs={{0,4},{1,5},{2,6},{3,7},{4,0},{5,1},{6,2},{7,3},{8,12},{9,13},{10,... | collective-permute-start | bytes 540680 | tf_op jit(solution)/shard_map/ppermute | solution.py:193
  60.9 5.3 %lists.1 = (s32[96,32]{1,0:T(8,128)}, s32[192,32]{1,0:T(8,128)}, s32[192,32]{1,0:T(8,128)}, f32[192,32]{1,0:T(8,128)}, s32[8,128]{1,0:T(8,128)}, /*index=5*/s32[8,128]{1,0:T(8,128)}, s32[8,128]{1,0:T(8,128)}) custom-call(s32[8,2048]{1,0:T(8,128)} %reshape.440.plane_ref, s32[8,2048]{1,0:T(8,128)} %reshape.441.line_ref, f32[8,2048]{1,0:T(8,128)} %reshape.442.wgt_ref), custom_call_target="tpu_custom_call" | custom-call | tf_op jit(solution)/shard_map/lists/pallas_call | solution.py:696
  66.2 0.9 add.278.rest_1_
  67.2 1.8 collective-permute-start.11
  69.6 3.2 %collective-permute-done.6.refs_3_ = bf16[2,352,128]{2,1,0:T(8,128)(2,1)S(1)} collective-permute-done((bf16[2,352,128]{2,1,0:T(8,128)(2,1)}, bf16[2,352,128]{2,1,0:T(8,128)(2,1)S(1)}, u32[]{:S(2)}, u32[]{:S(2)}) %collective-permute-start.6) | collective-permute-done | bytes 180256 | tf_op jit(solution)/shard_map/ppermute | solution.py:193
  73.5 1.9 combine_last.1.rest_0_
  75.4 1.2 collective-permute-start.10
  76.6 1.0 collective-permute-start.8
  77.6 1.0 fusion.33
  80.4 5.1 %collective-permute-done.13.rest_7_ = bf16[2,160,128]{2,1,0:T(8,128)(2,1)S(1)} collective-permute-done((bf16[2,160,128]{2,1,0:T(8,128)(2,1)S(1)}, bf16[2,160,128]{2,1,0:T(8,128)(2,1)S(1)}, u32[]{:S(2)}, u32[]{:S(2)}) %collective-permute-start.13) | collective-permute-done | bytes 81952 | tf_op jit(solution)/shard_map/ppermute | solution.py:207
  86.3 9.8 %logits.1 = f32[32,384]{1,0:T(8,128)} custom-call(s32[4]{0:T(128)} %iota_xor_fusion.group_s, bf16[32,384,256]{2,1,0:T(8,128)(2,1)} %copy-done, bf16[32,384,128]{2,1,0:T(8,128)(2,1)} %get-tuple-element.405.sq_ref, f32[4,32,128]{2,1,0:T(8,128)} %get-tuple-element.368.cos_ref, f32[4,32,128]{2,1,0:T(8,128)} %get-tuple-element.367.sin_ref, s32[8,384]{1,0:T(8,128)} %bitcast.121, ...), custom_call_target="tpu_custom_call" | custom-call | tf_op jit(solution)/shard_map/logits/pallas_call | solution.py:339
  96.2 1.7 collective-permute-start.14
  97.9 3.0 %collective-permute-done.14 = f32[32,384]{1,0:T(8,128)S(1)} collective-permute-done((f32[32,384]{1,0:T(8,128)}, f32[32,384]{1,0:T(8,128)S(1)}, u32[]{:S(2)}, u32[]{:S(2)}) %collective-permute-start.14) | collective-permute-done | bytes 49184 | tf_op jit(solution)/shard_map/ppermute | solution.py:798
  101.7 1.2 collective-permute-start.16
  102.9 1.4 collective-permute-start.17
  104.2 1.7 collective-permute-done.15.rest_1_
  106.7 1.8 collective-permute-done.17.rest_3_
  108.5 11.7 %spread.1 = (bf16[2,1,608,128]{3,2,1,0:T(8,128)(2,1)}, bf16[2,1,608,128]{3,2,1,0:T(8,128)(2,1)}, bf16[256,384]{1,0:T(8,128)(2,1)}) custom-call(s32[96,32]{1,0:T(8,128)} %get-tuple-element.121.src_s, s32[8,128]{1,0:T(8,128)} %get-tuple-element.122.len_s, s32[4]{0:T(128)} %iota_xor_fusion.group_s, s32[8,384]{1,0:T(8,128)} %bitcast.122, ...), custom_call_target="tpu_custom_call" | custom-call | tf_op jit(solution)/shard_map/spread/pallas_call | solution.py:456
  120.3 12.1 %project.1 = (bf16[2,2,608,128]{3,2,1,0:T(8,128)(2,1)}, bf16[2,2,608,128]{3,2,1,0:T(8,128)(2,1)}) custom-call(s32[96,32]{1,0:T(8,128)} %get-tuple-element.121.src_s, s32[8,128]{1,0:T(8,128)} %get-tuple-element.122.len_s, s32[4]{0:T(128)} %iota_xor_fusion.group_s, bf16[256,384]{1,0:T(8,128)(2,1)} %get-tuple-element.137.post, ...), custom_call_target="tpu_custom_call" | custom-call | tf_op jit(solution)/shard_map/project/pallas_call | solution.py:486
  132.4 2.3 collective-permute-done.18
  134.7 1.1 fusion.27
  135.7 0.9 collective-permute-start.19
  136.6 8.6 %collective-permute-done.19 = bf16[2,608,128]{2,1,0:T(8,128)(2,1)S(1)} collective-permute-done((bf16[2,608,128]{2,1,0:T(8,128)(2,1)S(1)}, bf16[2,608,128]{2,1,0:T(8,128)(2,1)S(1)}, u32[]{:S(2)}, u32[]{:S(2)}) %collective-permute-start.19) | collective-permute-done | bytes 311328 | tf_op jit(solution)/shard_map/ppermute | solution.py:512
  145.2 1.1 fusion.25.rest_0_
  146.3 0.9 collective-permute-start.20
  147.2 1.2 collective-permute-start.23
  148.4 1.0 fusion.32
  149.3 0.9 collective-permute-start.29
  150.2 4.7 %collective-permute-done.20.rest_1_ = bf16[2,608,128]{2,1,0:T(8,128)(2,1)S(1)} collective-permute-done((bf16[2,608,128]{2,1,0:T(8,128)(2,1)S(1)}, bf16[2,608,128]{2,1,0:T(8,128)(2,1)S(1)}, u32[]{:S(2)}, u32[]{:S(2)}) %collective-permute-start.20) | collective-permute-done | bytes 311328 | tf_op jit(solution)/shard_map/ppermute | solution.py:217
  155.8 1.2 collective-permute-start.24
  157.0 1.0 fusion.28.rest_0_
  158.0 0.9 collective-permute-start.30
  158.9 1.2 collective-permute-start.31
  160.0 5.2 %collective-permute-done.21.rest_3_ = bf16[2,608,128]{2,1,0:T(8,128)(2,1)S(1)} collective-permute-done((bf16[2,608,128]{2,1,0:T(8,128)(2,1)S(1)}, bf16[2,608,128]{2,1,0:T(8,128)(2,1)S(1)}, u32[]{:S(2)}, u32[]{:S(2)}) %collective-permute-start.21) | collective-permute-done | bytes 311328 | tf_op jit(solution)/shard_map/ppermute | solution.py:217
  165.2 0.8 collective-permute-start.22
  166.1 1.2 collective-permute-start.25
  167.3 1.3 collective-permute-done.30.rest_1_
  168.6 0.8 collective-permute-start.32
  169.4 1.2 collective-permute-start.33
  170.6 5.4 %collective-permute-done.32.rest_3_ = bf16[1,608,128]{2,1,0:T(8,128)(2,1)} collective-permute-done((bf16[1,608,128]{2,1,0:T(8,128)(2,1)S(1)}, bf16[1,608,128]{2,1,0:T(8,128)(2,1)}, u32[]{:S(2)}, u32[]{:S(2)}) %collective-permute-start.32) | collective-permute-done | bytes 155680 | tf_op jit(solution)/shard_map/ppermute | solution.py:217
  176.0 0.8 collective-permute-start.34
  176.9 1.2 collective-permute-start.35
  181.7 1.2 collective-permute-start.27
  183.7 1.3 slice.57
  185.0 1.6 copy.91
  187.3 0.9 collective-permute-start.36
  188.2 1.2 collective-permute-start.37
  189.4 1.3 fusion.36.order_s
  190.7 1.0 collective-permute-done.36.rest_7_
  191.7 0.9 collective-permute-done.37.rest_8_
  193.3 16.0 %insert_inverse.1.rest_4_ = f32[32,64,128]{2,1,0:T(8,128)} custom-call(s32[8,128]{1,0:T(8,128)} %get-tuple-element.117.len_s, s32[192,32]{1,0:T(8,128)} %get-tuple-element.118.refs_4_.pos_s, s32[192,32]{1,0:T(8,128)} %get-tuple-element.119.at_s, f32[192,32]{1,0:T(8,128)} %get-tuple-element.120.wgt_s, s32[8]{0:T(128)} %fusion.36.order_s, ...), custom_call_target="tpu_custom_call" | custom-call | tf_op jit(solution)/shard_map/insert_inverse/pallas_call | solution.py:594
  209.3 12.8 %insert_sum.1.rest_5_ = f32[2,2560,128]{2,1,0:T(8,128)} custom-call(s32[8,128]{1,0:T(8,128)} %get-tuple-element.117.len_s, s32[192,32]{1,0:T(8,128)} %get-tuple-element.118.refs_4_.pos_s, s32[192,32]{1,0:T(8,128)} %get-tuple-element.119.at_s, f32[192,32]{1,0:T(8,128)} %get-tuple-element.120.wgt_s, s32[8]{0:T(128)} %fusion.36.order_s, ...), custom_call_target="tpu_custom_call" | custom-call | tf_op jit(solution)/shard_map/insert_sum/pallas_call | solution.py:594
  222.1 13.1 %insert_result.1 = f32[2,32,64,128]{3,2,1,0:T(8,128)} custom-call(s32[8,128]{1,0:T(8,128)} %get-tuple-element.117.len_s, s32[192,32]{1,0:T(8,128)} %get-tuple-element.118.refs_4_.pos_s, s32[192,32]{1,0:T(8,128)} %get-tuple-element.119.at_s, f32[192,32]{1,0:T(8,128)} %get-tuple-element.120.wgt_s, s32[8]{0:T(128)} %fusion.36.order_s, ...), custom_call_target="tpu_custom_call" | custom-call | tf_op jit(solution)/shard_map/insert_result/pallas_call | solution.py:594
  235.3 4.2 %copy.89 = f32[2,32,64,128]{3,1,2,0:T(8,128)} copy(f32[2,32,64,128]{3,2,1,0:T(8,128)} %insert_result.1) | data formatting | bytes 4194304
  239.5 4.1 %copy.92 = f32[2,32,64,128]{3,2,1,0:T(8,128)} copy(f32[2,32,64,128]{3,1,2,0:T(8,128)} %get-tuple-element.142) | data formatting | bytes 4194304 | tf_op jit(solution)/shard_map/while | solution.py:825
  (165 shorter events, 21.1 us)
Async XLA Ops:
  6.5 22.2 %copy-start.53 = (f32[384]{0:T(512)S(1)}, f32[384]{0:T(512)}, u32[]{:S(2)}) copy-start(f32[384]{0:T(512)} %param.14) | copy-start | bytes 4612
  9.6 22.4 %copy-start.12 = (s32[16,256]{1,0:T(8,128)}, s32[16,256]{1,0:T(8,128)S(1)}, u32[]{:S(2)}) copy-start(s32[16,256]{1,0:T(8,128)S(1)} %constant_dynamic-slice_fusion.1) | copy-start | bytes 49156
  24.8 22.7 %collective-permute-start = (bf16[4,2,352,128]{3,2,1,0:T(8,128)(2,1)}, bf16[4,2,352,128]{3,2,1,0:T(8,128)(2,1)S(1)}, u32[]{:S(2)}, u32[]{:S(2)}) collective-permute-start(bf16[4,2,352,128]{3,2,1,0:T(8,128)(2,1)} %get-tuple-element.126), channel_id=1, source_target_pairs={{0,1},{1,0},{2,3},{3,2},{4,5},{5,4},{6,7},{7,6},{8,9},{9,8},{10,11... | collective-permute-start | bytes 2162696 | tf_op jit(solution)/shard_map/ppermute | solution.py:180
  24.9 22.6 %collective-permute-start.1 = (bf16[2,2,160,128]{3,2,1,0:T(8,128)(2,1)}, bf16[2,2,160,128]{3,2,1,0:T(8,128)(2,1)S(1)}, u32[]{:S(2)}, u32[]{:S(2)}) collective-permute-start(bf16[2,2,160,128]{3,2,1,0:T(8,128)(2,1)} %get-tuple-element.128), channel_id=1, source_target_pairs={{0,2},{1,3},{2,4},{3,5},{4,6},{5,7},{6,0},{7,1},{8,10},{9,11},{10,... | collective-permute-start | bytes 491528 | tf_op jit(solution)/shard_map/ppermute | solution.py:179
  27.3 20.1 %collective-permute-start.2 = (bf16[2,2,160,128]{3,2,1,0:T(8,128)(2,1)}, bf16[2,2,160,128]{3,2,1,0:T(8,128)(2,1)S(1)}, u32[]{:S(2)}, u32[]{:S(2)}) collective-permute-start(bf16[2,2,160,128]{3,2,1,0:T(8,128)(2,1)} %get-tuple-element.129), channel_id=1, source_target_pairs={{0,4},{1,5},{2,6},{3,7},{4,0},{5,1},{6,2},{7,3},{8,12},{9,13},{10,... | collective-permute-start | bytes 491528 | tf_op jit(solution)/shard_map/ppermute | solution.py:179
  27.3 20.2 %collective-permute-start.3 = (bf16[2,2,160,128]{3,2,1,0:T(8,128)(2,1)}, bf16[2,2,160,128]{3,2,1,0:T(8,128)(2,1)S(1)}, u32[]{:S(2)}, u32[]{:S(2)}) collective-permute-start(bf16[2,2,160,128]{3,2,1,0:T(8,128)(2,1)} %get-tuple-element.130), channel_id=1, source_target_pairs={{0,6},{1,7},{2,0},{3,1},{4,2},{5,3},{6,4},{7,5},{8,14},{9,15},{10,... | collective-permute-start | bytes 491528 | tf_op jit(solution)/shard_map/ppermute | solution.py:179
  31.9 45.7 %copy-start.42 = (f32[4,32]{1,0:T(4,128)}, f32[4,32]{1,0:T(4,128)S(1)}, u32[]{:S(2)}) copy-start(f32[4,32]{1,0:T(4,128)S(1)} %broadcast_multiply_fusion.2) | copy-start | bytes 1540
  31.9 26.5 %copy-start.39 = (s32[64,256]{1,0:T(8,128)S(1)}, s32[64,256]{1,0:T(8,128)}, u32[]{:S(2)}) copy-start(s32[64,256]{1,0:T(8,128)} %param.19) | copy-start | bytes 196612
  31.9 27.3 %copy-start.40 = (s32[64,256]{1,0:T(8,128)S(1)}, s32[64,256]{1,0:T(8,128)}, u32[]{:S(2)}) copy-start(s32[64,256]{1,0:T(8,128)} %param.20) | copy-start | bytes 196612
  47.4 12.7 %copy-start.41 = (f32[64,256]{1,0:T(8,128)S(1)}, f32[64,256]{1,0:T(8,128)}, u32[]{:S(2)}) copy-start(f32[64,256]{1,0:T(8,128)} %param.21) | copy-start | bytes 196612
  53.0 13.2 %collective-permute-start.7 = (bf16[2,160,128]{2,1,0:T(8,128)(2,1)}, bf16[2,160,128]{2,1,0:T(8,128)(2,1)S(1)}, u32[]{:S(2)}, u32[]{:S(2)}) collective-permute-start(bf16[2,160,128]{2,1,0:T(8,128)(2,1)} %get-tuple-element.136), channel_id=1, source_target_pairs={{0,1},{1,0},{2,3},{3,2},{4,5},{5,4},{6,7},{7,6},{8,9},{9,8},{10,11... | collective-permute-start | bytes 245768 | tf_op jit(solution)/shard_map/ppermute | solution.py:192
  53.6 15.4 %collective-permute-start.4 = (bf16[2,352,128]{2,1,0:T(8,128)(2,1)}, bf16[2,352,128]{2,1,0:T(8,128)(2,1)S(1)}, u32[]{:S(2)}, u32[]{:S(2)}) collective-permute-start(bf16[2,352,128]{2,1,0:T(8,128)(2,1)} %get-tuple-element.132), channel_id=1, source_target_pairs={{0,2},{1,3},{2,4},{3,5},{4,6},{5,7},{6,0},{7,1},{8,10},{9,11},{10,... | collective-permute-start | bytes 540680 | tf_op jit(solution)/shard_map/ppermute | solution.py:193
  54.6 15.0 %collective-permute-start.5 = (bf16[2,352,128]{2,1,0:T(8,128)(2,1)}, bf16[2,352,128]{2,1,0:T(8,128)(2,1)S(1)}, u32[]{:S(2)}, u32[]{:S(2)}) collective-permute-start(bf16[2,352,128]{2,1,0:T(8,128)(2,1)} %get-tuple-element.133), channel_id=1, source_target_pairs={{0,4},{1,5},{2,6},{3,7},{4,0},{5,1},{6,2},{7,3},{8,12},{9,13},{10,... | collective-permute-start | bytes 540680 | tf_op jit(solution)/shard_map/ppermute | solution.py:193
  58.4 14.5 %collective-permute-start.6 = (bf16[2,352,128]{2,1,0:T(8,128)(2,1)}, bf16[2,352,128]{2,1,0:T(8,128)(2,1)S(1)}, u32[]{:S(2)}, u32[]{:S(2)}) collective-permute-start(bf16[2,352,128]{2,1,0:T(8,128)(2,1)} %get-tuple-element.134), channel_id=1, source_target_pairs={{0,6},{1,7},{2,0},{3,1},{4,2},{5,3},{6,4},{7,5},{8,14},{9,15},{10,... | collective-permute-start | bytes 540680 | tf_op jit(solution)/shard_map/ppermute | solution.py:193
  58.4 37.7 %copy-start.44 = (f32[4,128]{1,0:T(4,128)}, f32[4,128]{1,0:T(4,128)S(1)}, u32[]{:S(2)}) copy-start(f32[4,128]{1,0:T(4,128)S(1)} %broadcast_multiply_fusion.3) | copy-start | bytes 6148
  60.2 44.0 %copy-start.54 = (s32[384]{0:T(512)S(1)}, s32[384]{0:T(512)}, u32[]{:S(2)}) copy-start(s32[384]{0:T(512)} %param.16) | copy-start | bytes 4612
  67.2 18.4 %copy-start.22 = (bf16[2,160,128]{2,1,0:T(8,128)(2,1)}, bf16[2,160,128]{2,1,0:T(8,128)(2,1)S(1)}, u32[]{:S(2)}) copy-start(bf16[2,160,128]{2,1,0:T(8,128)(2,1)S(1)} %add.278.rest_1_) | copy-start | bytes 245764
  67.2 12.2 %collective-permute-start.11 = (bf16[2,160,128]{2,1,0:T(8,128)(2,1)S(1)}, bf16[2,160,128]{2,1,0:T(8,128)(2,1)S(1)}, u32[]{:S(2)}, u32[]{:S(2)}) collective-permute-start(bf16[2,160,128]{2,1,0:T(8,128)(2,1)S(1)} %add.278.rest_1_), channel_id=1, source_target_pairs={{0,16},{8,24},{16,0},{24,8},{1,17},{9,25},{17,1},{25,9},{2,18},{10... | collective-permute-start | bytes 245768 | tf_op jit(solution)/shard_map/ppermute | solution.py:207
  69.0 3.9 %copy-start.27 = (bf16[2,352,128]{2,1,0:T(8,128)(2,1)}, bf16[2,352,128]{2,1,0:T(8,128)(2,1)S(1)}, u32[]{:S(2)}) copy-start(bf16[2,352,128]{2,1,0:T(8,128)(2,1)S(1)} %collective-permute-done.4.refs_1_) | copy-start | bytes 540676
  69.6 3.2 %copy-start.28 = (bf16[2,352,128]{2,1,0:T(8,128)(2,1)}, bf16[2,352,128]{2,1,0:T(8,128)(2,1)S(1)}, u32[]{:S(2)}) copy-start(bf16[2,352,128]{2,1,0:T(8,128)(2,1)S(1)} %collective-permute-done.5.refs_2_) | copy-start | bytes 540676
  75.4 10.1 %collective-permute-start.10 = (bf16[2,352,128]{2,1,0:T(8,128)(2,1)}, bf16[2,352,128]{2,1,0:T(8,128)(2,1)S(1)}, u32[]{:S(2)}, u32[]{:S(2)}) collective-permute-start(bf16[2,352,128]{2,1,0:T(8,128)(2,1)} %combine_last.1.rest_0_), channel_id=1, source_target_pairs={{0,16},{8,24},{16,0},{24,8},{1,17},{9,25},{17,1},{25,9},{2,18},{10... | collective-permute-start | bytes 540680 | tf_op jit(solution)/shard_map/ppermute | solution.py:207
  76.6 8.9 %collective-permute-start.12 = (bf16[2,352,128]{2,1,0:T(8,128)(2,1)}, bf16[2,352,128]{2,1,0:T(8,128)(2,1)S(1)}, u32[]{:S(2)}, u32[]{:S(2)}) collective-permute-start(bf16[2,352,128]{2,1,0:T(8,128)(2,1)} %combine_last.1.rest_0_), channel_id=1, source_target_pairs={{0,24},{8,16},{16,8},{24,0},{1,25},{9,17},{17,9},{25,1},{2,26},{10... | collective-permute-start | bytes 540680 | tf_op jit(solution)/shard_map/ppermute | solution.py:207
  76.6 8.9 %collective-permute-start.8 = (bf16[2,352,128]{2,1,0:T(8,128)(2,1)}, bf16[2,352,128]{2,1,0:T(8,128)(2,1)S(1)}, u32[]{:S(2)}, u32[]{:S(2)}) collective-permute-start(bf16[2,352,128]{2,1,0:T(8,128)(2,1)} %combine_last.1.rest_0_), channel_id=1, source_target_pairs={{0,8},{8,0},{16,24},{24,16},{1,9},{9,1},{17,25},{25,17},{2,10},{10... | collective-permute-start | bytes 540680 | tf_op jit(solution)/shard_map/ppermute | solution.py:207
  78.6 6.9 %collective-permute-start.13 = (bf16[2,160,128]{2,1,0:T(8,128)(2,1)S(1)}, bf16[2,160,128]{2,1,0:T(8,128)(2,1)S(1)}, u32[]{:S(2)}, u32[]{:S(2)}) collective-permute-start(bf16[2,160,128]{2,1,0:T(8,128)(2,1)S(1)} %add.278.rest_1_), channel_id=1, source_target_pairs={{0,24},{8,16},{16,8},{24,0},{1,25},{9,17},{17,9},{25,1},{2,26},{10... | collective-permute-start | bytes 245768 | tf_op jit(solution)/shard_map/ppermute | solution.py:207
  79.3 6.2 %copy-start.46 = (bf16[2,160,128]{2,1,0:T(8,128)(2,1)}, bf16[2,160,128]{2,1,0:T(8,128)(2,1)S(1)}, u32[]{:S(2)}) copy-start(bf16[2,160,128]{2,1,0:T(8,128)(2,1)S(1)} %collective-permute-done.11.rest_5_) | copy-start | bytes 245764
  79.4 6.1 %collective-permute-start.9 = (bf16[2,160,128]{2,1,0:T(8,128)(2,1)S(1)}, bf16[2,160,128]{2,1,0:T(8,128)(2,1)S(1)}, u32[]{:S(2)}, u32[]{:S(2)}) collective-permute-start(bf16[2,160,128]{2,1,0:T(8,128)(2,1)S(1)} %add.278.rest_1_), channel_id=1, source_target_pairs={{0,8},{8,0},{16,24},{24,16},{1,9},{9,1},{17,25},{25,17},{2,10},{10... | collective-permute-start | bytes 245768 | tf_op jit(solution)/shard_map/ppermute | solution.py:207
  85.6 34.7 %slice-start = ((s8[6291456]{0:T(1024)(128)(4,1)}), s8[4194304]{0:T(1024)(128)(4,1)S(1)}, s32[]{:S(2)}) async-start(s8[6291456]{0:T(1024)(128)(4,1)} %bitcast.105), calls=%async_computation.5 | async-start | bytes 8388608
  86.3 33.9 %slice-start.1 = ((s8[6291456]{0:T(1024)(128)(4,1)}), s8[2097152]{0:T(1024)(128)(4,1)S(1)}, s32[]{:S(2)}) async-start(s8[6291456]{0:T(1024)(128)(4,1)} %bitcast.105), calls=%async_computation.6 | async-start | bytes 4194304
  96.2 4.7 %collective-permute-start.14 = (f32[32,384]{1,0:T(8,128)}, f32[32,384]{1,0:T(8,128)S(1)}, u32[]{:S(2)}, u32[]{:S(2)}) collective-permute-start(f32[32,384]{1,0:T(8,128)} %logits.1), channel_id=1, source_target_pairs={{0,1},{1,0},{2,3},{3,2},{4,5},{5,4},{6,7},{7,6},{8,9},{9,8},{10,11... | collective-permute-start | bytes 147464 | tf_op jit(solution)/shard_map/ppermute | solution.py:798
  101.7 4.3 %collective-permute-start.15 = (f32[32,384]{1,0:T(8,128)S(1)}, f32[32,384]{1,0:T(8,128)S(1)}, u32[]{:S(2)}, u32[]{:S(2)}) collective-permute-start(f32[32,384]{1,0:T(8,128)S(1)} %add.279.rest_0_), channel_id=1, source_target_pairs={{0,2},{1,3},{2,4},{3,5},{4,6},{5,7},{6,0},{7,1},{8,10},{9,11},{10,... | collective-permute-start | bytes 147464 | tf_op jit(solution)/shard_map/ppermute | solution.py:800
  101.7 5.1 %collective-permute-start.16 = (f32[32,384]{1,0:T(8,128)S(1)}, f32[32,384]{1,0:T(8,128)S(1)}, u32[]{:S(2)}, u32[]{:S(2)}) collective-permute-start(f32[32,384]{1,0:T(8,128)S(1)} %add.279.rest_0_), channel_id=1, source_target_pairs={{0,4},{1,5},{2,6},{3,7},{4,0},{5,1},{6,2},{7,3},{8,12},{9,13},{10,... | collective-permute-start | bytes 147464 | tf_op jit(solution)/shard_map/ppermute | solution.py:800
  102.9 5.6 %collective-permute-start.17 = (f32[32,384]{1,0:T(8,128)S(1)}, f32[32,384]{1,0:T(8,128)S(1)}, u32[]{:S(2)}, u32[]{:S(2)}) collective-permute-start(f32[32,384]{1,0:T(8,128)S(1)} %add.279.rest_0_), channel_id=1, source_target_pairs={{0,6},{1,7},{2,0},{3,1},{4,2},{5,3},{6,4},{7,5},{8,14},{9,15},{10,... | collective-permute-start | bytes 147464 | tf_op jit(solution)/shard_map/ppermute | solution.py:800
  108.5 74.4 %copy-start.38 = (s32[384,8]{0,1:T(8,128)S(1)}, s32[384,8]{0,1:T(8,128)}, u32[]{:S(2)}) copy-start(s32[384,8]{0,1:T(8,128)} %param.15) | copy-start | bytes 36868
  108.5 76.4 %copy-start.2 = (f32[32,64,128]{2,1,0:T(8,128)S(1)}, f32[32,64,128]{2,1,0:T(8,128)}, u32[]{:S(2)}) copy-start(f32[32,64,128]{2,1,0:T(8,128)} %rest_9_.1) | copy-start | bytes 3145732
  132.4 2.3 collective-permute-start.18
  135.7 9.5 %collective-permute-start.19 = (bf16[2,608,128]{2,1,0:T(8,128)(2,1)S(1)}, bf16[2,608,128]{2,1,0:T(8,128)(2,1)S(1)}, u32[]{:S(2)}, u32[]{:S(2)}) collective-permute-start(bf16[2,608,128]{2,1,0:T(8,128)(2,1)S(1)} %fusion.27), channel_id=1, source_target_pairs={{0,16},{8,24},{16,0},{24,8},{1,17},{9,25},{17,1},{25,9},{2,18},{10... | collective-permute-start | bytes 933896 | tf_op jit(solution)/shard_map/ppermute | solution.py:512
  136.6 11.8 %collective-permute-start.28 = (bf16[2,1,608,128]{3,2,1,0:T(8,128)(2,1)}, bf16[2,1,608,128]{3,2,1,0:T(8,128)(2,1)S(1)}, u32[]{:S(2)}, u32[]{:S(2)}) collective-permute-start(bf16[2,1,608,128]{3,2,1,0:T(8,128)(2,1)} %get-tuple-element.141), channel_id=1, source_target_pairs={{0,8},{8,0},{16,24},{24,16},{1,9},{9,1},{17,25},{25,17},{2,10},{10... | collective-permute-start | bytes 933896 | tf_op jit(solution)/shard_map/ppermute | solution.py:510
  146.3 63.0 %copy-start.11 = (bf16[2,608,128]{2,1,0:T(8,128)(2,1)}, bf16[2,608,128]{2,1,0:T(8,128)(2,1)S(1)}, u32[]{:S(2)}) copy-start(bf16[2,608,128]{2,1,0:T(8,128)(2,1)S(1)} %fusion.25.rest_0_) | copy-start | bytes 933892
  146.3 8.6 %collective-permute-start.20 = (bf16[2,608,128]{2,1,0:T(8,128)(2,1)S(1)}, bf16[2,608,128]{2,1,0:T(8,128)(2,1)S(1)}, u32[]{:S(2)}, u32[]{:S(2)}) collective-permute-start(bf16[2,608,128]{2,1,0:T(8,128)(2,1)S(1)} %fusion.25.rest_0_), channel_id=1, source_target_pairs={{0,2},{2,4},{4,6},{6,7},{7,5},{5,3},{3,1},{1,0},{8,10},{10,12},{12... | collective-permute-start | bytes 933896 | tf_op jit(solution)/shard_map/ppermute | solution.py:217
  147.2 8.6 %collective-permute-start.23 = (bf16[2,608,128]{2,1,0:T(8,128)(2,1)S(1)}, bf16[2,608,128]{2,1,0:T(8,128)(2,1)S(1)}, u32[]{:S(2)}, u32[]{:S(2)}) collective-permute-start(bf16[2,608,128]{2,1,0:T(8,128)(2,1)S(1)} %fusion.25.rest_0_), channel_id=1, source_target_pairs={{2,0},{4,2},{6,4},{7,6},{5,7},{3,5},{1,3},{0,1},{10,8},{12,10},{14... | collective-permute-start | bytes 933896 | tf_op jit(solution)/shard_map/ppermute | solution.py:218
  149.3 7.6 %collective-permute-start.29 = (bf16[1,608,128]{2,1,0:T(8,128)(2,1)S(1)}, bf16[1,608,128]{2,1,0:T(8,128)(2,1)S(1)}, u32[]{:S(2)}, u32[]{:S(2)}) collective-permute-start(bf16[1,608,128]{2,1,0:T(8,128)(2,1)S(1)} %fusion.32), channel_id=1, source_target_pairs={{0,16},{8,24},{16,0},{24,8},{1,17},{9,25},{17,1},{25,9},{2,18},{10... | collective-permute-start | bytes 466952 | tf_op jit(solution)/shard_map/ppermute | solution.py:512
  154.9 54.4 %copy-start.23 = (bf16[2,608,128]{2,1,0:T(8,128)(2,1)}, bf16[2,608,128]{2,1,0:T(8,128)(2,1)S(1)}, u32[]{:S(2)}) copy-start(bf16[2,608,128]{2,1,0:T(8,128)(2,1)S(1)} %collective-permute-done.20.rest_1_) | copy-start | bytes 933892
  154.9 10.3 %collective-permute-start.21 = (bf16[2,608,128]{2,1,0:T(8,128)(2,1)S(1)}, bf16[2,608,128]{2,1,0:T(8,128)(2,1)S(1)}, u32[]{:S(2)}, u32[]{:S(2)}) collective-permute-start(bf16[2,608,128]{2,1,0:T(8,128)(2,1)S(1)} %collective-permute-done.20.rest_1_), channel_id=1, source_target_pairs={{0,2},{2,4},{4,6},{6,7},{7,5},{5,3},{3,1},{1,0},{8,10},{10,12},{12... | collective-permute-start | bytes 933896 | tf_op jit(solution)/shard_map/ppermute | solution.py:217
  155.8 53.5 %copy-start.24 = (bf16[2,608,128]{2,1,0:T(8,128)(2,1)}, bf16[2,608,128]{2,1,0:T(8,128)(2,1)S(1)}, u32[]{:S(2)}) copy-start(bf16[2,608,128]{2,1,0:T(8,128)(2,1)S(1)} %collective-permute-done.23.rest_2_) | copy-start | bytes 933892
  155.8 10.3 %collective-permute-start.24 = (bf16[2,608,128]{2,1,0:T(8,128)(2,1)S(1)}, bf16[2,608,128]{2,1,0:T(8,128)(2,1)S(1)}, u32[]{:S(2)}, u32[]{:S(2)}) collective-permute-start(bf16[2,608,128]{2,1,0:T(8,128)(2,1)S(1)} %collective-permute-done.23.rest_2_), channel_id=1, source_target_pairs={{2,0},{4,2},{6,4},{7,6},{5,7},{3,5},{1,3},{0,1},{10,8},{12,10},{14... | collective-permute-start | bytes 933896 | tf_op jit(solution)/shard_map/ppermute | solution.py:218
  158.0 34.7 %copy-start.19 = (bf16[1,608,128]{2,1,0:T(8,128)(2,1)}, bf16[1,608,128]{2,1,0:T(8,128)(2,1)S(1)}, u32[]{:S(2)}) copy-start(bf16[1,608,128]{2,1,0:T(8,128)(2,1)S(1)} %fusion.28.rest_0_) | copy-start | bytes 466948
  158.0 10.6 %collective-permute-start.30 = (bf16[1,608,128]{2,1,0:T(8,128)(2,1)S(1)}, bf16[1,608,128]{2,1,0:T(8,128)(2,1)S(1)}, u32[]{:S(2)}, u32[]{:S(2)}) collective-permute-start(bf16[1,608,128]{2,1,0:T(8,128)(2,1)S(1)} %fusion.28.rest_0_), channel_id=1, source_target_pairs={{0,2},{2,4},{4,6},{6,7},{7,5},{5,3},{3,1},{1,0},{8,10},{10,12},{12... | collective-permute-start | bytes 466952 | tf_op jit(solution)/shard_map/ppermute | solution.py:217
  158.9 10.6 %collective-permute-start.31 = (bf16[1,608,128]{2,1,0:T(8,128)(2,1)S(1)}, bf16[1,608,128]{2,1,0:T(8,128)(2,1)S(1)}, u32[]{:S(2)}, u32[]{:S(2)}) collective-permute-start(bf16[1,608,128]{2,1,0:T(8,128)(2,1)S(1)} %fusion.28.rest_0_), channel_id=1, source_target_pairs={{2,0},{4,2},{6,4},{7,6},{5,7},{3,5},{1,3},{0,1},{10,8},{12,10},{14... | collective-permute-start | bytes 466952 | tf_op jit(solution)/shard_map/ppermute | solution.py:218
  165.2 44.1 %copy-start.25 = (bf16[2,608,128]{2,1,0:T(8,128)(2,1)}, bf16[2,608,128]{2,1,0:T(8,128)(2,1)S(1)}, u32[]{:S(2)}) copy-start(bf16[2,608,128]{2,1,0:T(8,128)(2,1)S(1)} %collective-permute-done.21.rest_3_) | copy-start | bytes 933892
  165.2 12.8 %collective-permute-start.22 = (bf16[2,608,128]{2,1,0:T(8,128)(2,1)S(1)}, bf16[2,608,128]{2,1,0:T(8,128)(2,1)S(1)}, u32[]{:S(2)}, u32[]{:S(2)}) collective-permute-start(bf16[2,608,128]{2,1,0:T(8,128)(2,1)S(1)} %collective-permute-done.21.rest_3_), channel_id=1, source_target_pairs={{0,2},{2,4},{4,6},{6,7},{7,5},{5,3},{3,1},{1,0},{8,10},{10,12},{12... | collective-permute-start | bytes 933896 | tf_op jit(solution)/shard_map/ppermute | solution.py:217
  166.1 43.2 %copy-start.26 = (bf16[2,608,128]{2,1,0:T(8,128)(2,1)}, bf16[2,608,128]{2,1,0:T(8,128)(2,1)S(1)}, u32[]{:S(2)}) copy-start(bf16[2,608,128]{2,1,0:T(8,128)(2,1)S(1)} %collective-permute-done.24.rest_4_) | copy-start | bytes 933892
  166.1 14.2 %collective-permute-start.25 = (bf16[2,608,128]{2,1,0:T(8,128)(2,1)S(1)}, bf16[2,608,128]{2,1,0:T(8,128)(2,1)S(1)}, u32[]{:S(2)}, u32[]{:S(2)}) collective-permute-start(bf16[2,608,128]{2,1,0:T(8,128)(2,1)S(1)} %collective-permute-done.24.rest_4_), channel_id=1, source_target_pairs={{2,0},{4,2},{6,4},{7,6},{5,7},{3,5},{1,3},{0,1},{10,8},{12,10},{14... | collective-permute-start | bytes 933896 | tf_op jit(solution)/shard_map/ppermute | solution.py:218
  168.6 7.5 %collective-permute-start.32 = (bf16[1,608,128]{2,1,0:T(8,128)(2,1)S(1)}, bf16[1,608,128]{2,1,0:T(8,128)(2,1)}, u32[]{:S(2)}, u32[]{:S(2)}) collective-permute-start(bf16[1,608,128]{2,1,0:T(8,128)(2,1)S(1)} %collective-permute-done.30.rest_1_), channel_id=1, source_target_pairs={{0,2},{2,4},{4,6},{6,7},{7,5},{5,3},{3,1},{1,0},{8,10},{10,12},{12... | collective-permute-start | bytes 466952 | tf_op jit(solution)/shard_map/ppermute | solution.py:217
  169.4 7.5 %copy-start.37 = (bf16[1,608,128]{2,1,0:T(8,128)(2,1)}, bf16[1,608,128]{2,1,0:T(8,128)(2,1)S(1)}, u32[]{:S(2)}) copy-start(bf16[1,608,128]{2,1,0:T(8,128)(2,1)S(1)} %collective-permute-done.31.rest_2_) | copy-start | bytes 466948
  169.4 7.5 %collective-permute-start.33 = (bf16[1,608,128]{2,1,0:T(8,128)(2,1)S(1)}, bf16[1,608,128]{2,1,0:T(8,128)(2,1)}, u32[]{:S(2)}, u32[]{:S(2)}) collective-permute-start(bf16[1,608,128]{2,1,0:T(8,128)(2,1)S(1)} %collective-permute-done.31.rest_2_), channel_id=1, source_target_pairs={{2,0},{4,2},{6,4},{7,6},{5,7},{3,5},{1,3},{0,1},{10,8},{12,10},{14... | collective-permute-start | bytes 466952 | tf_op jit(solution)/shard_map/ppermute | solution.py:218
  176.0 11.2 %collective-permute-start.34 = (bf16[1,608,128]{2,1,0:T(8,128)(2,1)}, bf16[1,608,128]{2,1,0:T(8,128)(2,1)S(1)}, u32[]{:S(2)}, u32[]{:S(2)}) collective-permute-start(bf16[1,608,128]{2,1,0:T(8,128)(2,1)} %collective-permute-done.32.rest_3_), channel_id=1, source_target_pairs={{0,2},{2,4},{4,6},{6,7},{7,5},{5,3},{3,1},{1,0},{8,10},{10,12},{12... | collective-permute-start | bytes 466952 | tf_op jit(solution)/shard_map/ppermute | solution.py:217
  176.9 11.3 %collective-permute-start.35 = (bf16[1,608,128]{2,1,0:T(8,128)(2,1)}, bf16[1,608,128]{2,1,0:T(8,128)(2,1)S(1)}, u32[]{:S(2)}, u32[]{:S(2)}) collective-permute-start(bf16[1,608,128]{2,1,0:T(8,128)(2,1)} %collective-permute-done.33.rest_4_), channel_id=1, source_target_pairs={{2,0},{4,2},{6,4},{7,6},{5,7},{3,5},{1,3},{0,1},{10,8},{12,10},{14... | collective-permute-start | bytes 466952 | tf_op jit(solution)/shard_map/ppermute | solution.py:218
  179.5 42.6 %collective-permute-start.26 = (bf16[2,304,128]{2,1,0:T(8,128)(2,1)}, bf16[2,304,128]{2,1,0:T(8,128)(2,1)}, u32[]{:S(2)}, u32[]{:S(2)}) collective-permute-start(bf16[2,304,128]{2,1,0:T(8,128)(2,1)} %slice.90), channel_id=1, source_target_pairs={{0,2},{2,4},{4,6},{6,7},{7,5},{5,3},{3,1},{1,0},{8,10},{10,12},{12... | collective-permute-start | bytes 466952 | tf_op jit(solution)/shard_map/ppermute | solution.py:222
  181.7 40.4 %collective-permute-start.27 = (bf16[2,304,128]{2,1,0:T(8,128)(2,1)}, bf16[2,304,128]{2,1,0:T(8,128)(2,1)}, u32[]{:S(2)}, u32[]{:S(2)}) collective-permute-start(bf16[2,304,128]{2,1,0:T(8,128)(2,1)} %slice.91), channel_id=1, source_target_pairs={{2,0},{4,2},{6,4},{7,6},{5,7},{3,5},{1,3},{0,1},{10,8},{12,10},{14... | collective-permute-start | bytes 466952 | tf_op jit(solution)/shard_map/ppermute | solution.py:223
  187.2 5.4 %copy-start.20 = (bf16[1,608,128]{2,1,0:T(8,128)(2,1)}, bf16[1,608,128]{2,1,0:T(8,128)(2,1)S(1)}, u32[]{:S(2)}) copy-start(bf16[1,608,128]{2,1,0:T(8,128)(2,1)S(1)} %collective-permute-done.34.rest_5_) | copy-start | bytes 466948
  187.3 4.4 %collective-permute-start.36 = (bf16[1,304,128]{2,1,0:T(8,128)(2,1)S(1)}, bf16[1,304,128]{2,1,0:T(8,128)(2,1)S(1)}, u32[]{:S(2)}, u32[]{:S(2)}) collective-permute-start(bf16[1,304,128]{2,1,0:T(8,128)(2,1)S(1)} %slice.94), channel_id=1, source_target_pairs={{0,2},{2,4},{4,6},{6,7},{7,5},{5,3},{3,1},{1,0},{8,10},{10,12},{12... | collective-permute-start | bytes 233480 | tf_op jit(solution)/shard_map/ppermute | solution.py:222
  188.2 4.5 %copy-start.21 = (bf16[1,608,128]{2,1,0:T(8,128)(2,1)}, bf16[1,608,128]{2,1,0:T(8,128)(2,1)S(1)}, u32[]{:S(2)}) copy-start(bf16[1,608,128]{2,1,0:T(8,128)(2,1)S(1)} %collective-permute-done.35.rest_6_) | copy-start | bytes 466948
  188.2 4.4 %collective-permute-start.37 = (bf16[1,304,128]{2,1,0:T(8,128)(2,1)S(1)}, bf16[1,304,128]{2,1,0:T(8,128)(2,1)S(1)}, u32[]{:S(2)}, u32[]{:S(2)}) collective-permute-start(bf16[1,304,128]{2,1,0:T(8,128)(2,1)S(1)} %slice.95), channel_id=1, source_target_pairs={{2,0},{4,2},{6,4},{7,6},{5,7},{3,5},{1,3},{0,1},{10,8},{12,10},{14... | collective-permute-start | bytes 233480 | tf_op jit(solution)/shard_map/ppermute | solution.py:223
  222.1 17.3 %copy-start.1 = (bf16[32,384,128]{2,1,0:T(8,128)(2,1)S(1)}, bf16[32,384,128]{2,1,0:T(8,128)(2,1)}, u32[]{:S(2)}) copy-start(bf16[32,384,128]{2,1,0:T(8,128)(2,1)} %get-tuple-element.405.sq_ref) | copy-start | bytes 9437188
  (17 other events, 23.4 us)

commit v4 on v3

--- a/solution.py
+++ b/solution.py
@@ -3,7 +3,6 @@
 
 import jax
 import jax.numpy as jnp
-import numpy as np
 from jax import lax
 from jax.experimental import pallas as pl
 from jax.experimental.pallas import tpu as pltpu
@@ -32,6 +31,10 @@
 
 def vmem():
     return pl.BlockSpec(memory_space=pltpu.VMEM)
+
+
+def cost(us):
+    return pl.CostEstimate(flops=0, transcendentals=0, bytes_accessed=int(us * 3.69e6))
 
 
 def hbm():
@@ -66,42 +69,63 @@
     return list(range(0, n_vol, 2)) + list(range(n_vol - 1, 0, -2))
 
 
-def ring_order(n_vol):
-    ring = ring_of(n_vol)
-    table = np.zeros((n_vol, n_vol), np.int32)
-    for p, v in enumerate(ring):
-        order = [v]
-        for d in range(1, n_vol // 2):
-            order += [ring[p - d], ring[(p + d) % n_vol]]
-        table[v] = order + [ring[p - n_vol // 2]]
-    return table
-
-
-def extract_kernel(idx_s, wl_s, wu_s, flag_s, blk_s, vol_hbm, keep_a, send_a, *rest):
-    vol_ref, pair, sem = rest[-3:]
-    parts_b = rest[:-3]
-    load = pltpu.make_async_copy(vol_hbm, vol_ref, sem)
-    load.start()
-    for ref in (keep_a, send_a) + parts_b:
-        ref[...] = jnp.zeros_like(ref)
-    load.wait()
+def extract_kernel(rows, planes_here, *refs):
+    plane_ref, line_ref, weight_hbm, vol_hbm, keep_a, send_a = refs[:6]
+    vol, pair, idx_v, flag_v, idx_s, flag_s, w_s, sem = refs[-8:]
+    parts_b = refs[6:-8]
+    slab = lax.axis_index("vol")
+    share = idx_v.shape[0]
+    first = lax.axis_index("img") * share
+    height = planes_here * ROWS
     count_z = keep_a.shape[0]
     groups_a = keep_a.shape[2] // 16
     groups_b = parts_b[0].shape[2] // 16
-    first = lax.broadcasted_iota(jnp.int32, (2, COLS), 0) == 0
+    load = pltpu.make_async_copy(vol_hbm, vol.at[:, :height, :], sem.at[0])
+    load.start()
+    load_w = pltpu.make_async_copy(weight_hbm.at[pl.ds(first, share), :], w_s, sem.at[1])
+    load_w.start()
+    local = plane_ref[pl.ds(first, share), :] - slab * planes_here
+    owned = (local >= 0) & (local < planes_here)
+    idx_v[...] = jnp.where(owned, local * ROWS + line_ref[pl.ds(first, share), :], height)
+    eights = (
+        lax.broadcasted_iota(jnp.int32, (ROWS, COLS), 0) >> 3
+        == lax.broadcasted_iota(jnp.int32, (ROWS, COLS), 1)
+    )
+    flag_v[...] = jnp.dot(
+        owned.astype(F32).astype(BF16), eights.astype(F32).astype(BF16), preferred_element_type=F32
+    ).astype(jnp.int32)
+    to_idx = pltpu.make_async_copy(idx_v, idx_s, sem.at[2])
+    to_flag = pltpu.make_async_copy(flag_v, flag_s, sem.at[3])
+    to_idx.start()
+    to_flag.start()
+    vol[:, height : height + 8, :] = jnp.zeros((2, 8, COLS), F32)
+    for ref in (keep_a, send_a) + parts_b:
+        ref[...] = jnp.zeros_like(ref)
+    to_idx.wait()
+    to_flag.wait()
+    load_w.wait()
+    load.wait()
+    lower_row = lax.broadcasted_iota(jnp.int32, (2, COLS), 0) == 0
+    shift = rows.bit_length() - 1
 
     def fill(out, lead, block, skip, groups):
         def group_step(g, carry):
-            at = block * (groups_a + groups_b) + skip + g
             base = pl.multiple_of(g * 16, 16)
-
-            @pl.when(flag_s[at] > 0)
+            at = []
+            for h in range(2):
+                n = (skip + g) * 16 + 8 * h
+                at.append((n >> shift, block * rows + (n & (rows - 1))))
+            hits = flag_s[at[0][0], at[0][1] >> 3] + flag_s[at[1][0], at[1][1] >> 3]
+
+            @pl.when(hits > 0)
             def _():
                 for u in range(16):
-                    i = idx_s[at * 16 + u]
-                    w = jnp.where(first, wl_s[at * 16 + u], wu_s[at * 16 + u])
+                    k, r = at[u // 8]
+                    i = idx_s[k, r + u % 8]
+                    w = w_s[k, r + u % 8]
+                    both = jnp.where(lower_row, w, 1.0 - w)
                     for j in range(2):
-                        pair[j, 2 * u : 2 * u + 2, :] = w * vol_ref[j, pl.ds(i, 2), :]
+                        pair[j, 2 * u : 2 * u + 2, :] = both * vol[j, pl.ds(i, 2), :]
                 for j in range(2):
                     value = pair[j, pl.ds(0, 16, stride=2), :] + pair[j, pl.ds(1, 16, stride=2), :]
                     out[lead, j, pl.ds(base, 16), :] = value.astype(BF16)
@@ -112,44 +136,37 @@
 
     for dz in range(count_z):
         for dy in range(2):
-            block = blk_s[dz * 2 + dy]
+            z = (slab >> 1) + dz
+            block = jnp.where(z >= count_z, z - count_z, z) * 2 + ((slab + dy) & 1)
             fill((keep_a, send_a)[dy], dz, block, 0, groups_a)
             fill(parts_b[dz], dy, block, groups_a, groups_b)
 
 
-def extract(volume, planes, lines, weights, slab_id, n_vol, share_a):
-    share = planes.shape[0]
+def extract(volume, row_plane, row_line, row_weight, n_vol, share, share_a):
     planes_here = volume.shape[1]
     rows = ROWS // n_vol
     count_z = n_vol // 2
-
-    def order(x):
-        return x.reshape(share, n_vol, rows).transpose(1, 0, 2).reshape(-1)
-
-    local = order(planes) - slab_id * planes_here
-    owned = (local >= 0) & (local < planes_here)
-    idx = jnp.where(owned, local, 0) * ROWS + order(lines)
-    weight = order(weights)
-    lower = jnp.where(owned, weight, 0.0)
-    upper = jnp.where(owned, 1.0 - weight, 0.0)
-    flag = jnp.any(owned.reshape(-1, 16), axis=1).astype(jnp.int32)
-    rel = jnp.arange(n_vol)
-    blocks = (slab_id // 2 + rel // 2) % count_z * 2 + (slab_id % 2 + rel) % 2
     shape_a = jax.ShapeDtypeStruct((count_z, 2, share_a * rows, COLS), BF16)
     shape_b = jax.ShapeDtypeStruct((2, 2, (share - share_a) * rows, COLS), BF16)
     return pl.pallas_call(
-        extract_kernel,
+        partial(extract_kernel, rows, planes_here),
         out_shape=[shape_a, shape_a] + [shape_b] * count_z,
-        in_specs=[smem()] * 5 + [hbm()],
+        in_specs=[vmem(), vmem(), hbm(), hbm()],
         out_specs=[vmem()] * (2 + count_z),
         scratch_shapes=[
-            pltpu.VMEM((2, planes_here * ROWS, COLS), F32),
+            pltpu.VMEM((2, planes_here * ROWS + 8, COLS), F32),
             pltpu.VMEM((2, 32, COLS), F32),
-            pltpu.SemaphoreType.DMA,
+            pltpu.VMEM((share, ROWS), jnp.int32),
+            pltpu.VMEM((share, COLS), jnp.int32),
+            pltpu.SMEM((share, ROWS), jnp.int32),
+            pltpu.SMEM((share, COLS), jnp.int32),
+            pltpu.SMEM((share, ROWS), F32),
+            pltpu.SemaphoreType.DMA((4,)),
         ],
         compiler_params=pltpu.CompilerParams(vmem_limit_bytes=VMEM_LIMIT),
+        cost_estimate=cost(11),
         name="extract",
-    )(idx, lower, upper, flag, blocks, volume.reshape(2, planes_here * ROWS, COLS))
+    )(row_plane, row_line, row_weight, volume.reshape(2, planes_here * ROWS, COLS))
 
 
 def combine_first_kernel(keep_a, got_a, keep_b, *rest):
@@ -166,14 +183,7 @@
         out_b[d][...] = total
 
 
-def combine_last_kernel(*refs):
-    total = refs[0][...]
-    for ref in refs[1:-2]:
-        total = total + ref[...]
-    refs[-1][...] = total
-
-
-def to_pixel_rows(messages, n_vol, first_with, last_with):
+def to_pixel_rows(messages, n_vol, first_with):
     keep_a, send_a, keep_b = messages[:3]
     count_z = n_vol // 2
     got_b = [lax.ppermute(m, "vol", along_z(n_vol, d + 1)) for d, m in enumerate(messages[3:])]
@@ -186,20 +196,14 @@
         in_specs=[vmem()] * (2 + count_z) + [hbm()],
         out_specs=[vmem()] * (count_z + 2),
         compiler_params=pltpu.CompilerParams(vmem_limit_bytes=VMEM_LIMIT),
+        cost_estimate=cost(3),
         name="combine_first",
     )(keep_a, got_a, keep_b, *got_b, first_with)
     sums_a, sums_b = sums[:count_z], sums[count_z:]
     moved_b = lax.ppermute(sums_b[1], "vol", flip(n_vol, 1))
     moved = [lax.ppermute(sums_a[d], "vol", along_z(n_vol, d)) for d in range(1, count_z)]
     out_b = sums_b[0] + moved_b
-    out_a = pl.pallas_call(
-        combine_last_kernel,
-        out_shape=shape_a,
-        in_specs=[vmem()] * count_z + [hbm()],
-        out_specs=vmem(),
-        compiler_params=pltpu.CompilerParams(vmem_limit_bytes=VMEM_LIMIT),
-        name="combine_last",
-    )(sums_a[0], *moved, last_with)
+    out_a = sum(moved, sums_a[0])
     return out_a, out_b
 
 
@@ -227,8 +231,10 @@
 def weigh_kernel(img_ref, sa_ref, ca_ref, sx_ref, cx_ref, nw_ref, wt_ref, sq_ref, buf):
     count = img_ref.shape[1]
     rows = img_ref.shape[2]
+    pitch = rows + 1
     for j in range(2):
-        buf[j] = img_ref[j].astype(F32).reshape(count * rows, COLS)
+        for b in range(count):
+            buf[j, b * pitch : b * pitch + rows, :] = img_ref[j, b].astype(F32)
     sx = sx_ref[...]
     cx = cx_ref[...]
     for r in range(rows):
@@ -236,7 +242,7 @@
         noise = nw_ref[r : r + 1, :]
         scale = contrast * noise
         for j in range(2):
-            x = buf[j, pl.ds(r, count, stride=rows), :]
+            x = buf[j, pl.ds(r, count, stride=pitch), :]
             wt_ref[r, :, j * COLS : (j + 1) * COLS] = (scale * x).astype(BF16)
         sq_ref[r] = (contrast * contrast * noise).astype(BF16)
 
@@ -266,8 +272,9 @@
             pl.BlockSpec((rows, step, 2 * COLS), lambda b: (0, b, 0)),
             pl.BlockSpec((rows, step, COLS), lambda b: (0, b, 0)),
         ],
-        scratch_shapes=[pltpu.VMEM((2, step * rows, COLS), F32)],
+        scratch_shapes=[pltpu.VMEM((2, step * (rows + 1), COLS), F32)],
         compiler_params=params(1),
+        cost_estimate=cost(12),
         name="weigh",
     )(
         images,
@@ -279,24 +286,26 @@
     )
 
 
-def logits_kernel(group_s, wt_ref, sq_ref, cos_ref, sin_ref, cand_ref, *rest):
+def logits_kernel(wt_ref, sq_ref, cos_ref, sin_ref, cand_ref, *rest):
     sl_refs = rest[:-4]
     out_ref, part, acc, quad = rest[-4:]
     step = pl.program_id(0)
     groups = len(sl_refs) // 2
-    rows = part.shape[1] // K
-    span = part.shape[1] // groups
+    rows = part.shape[1] // K - 1
+    share = K // groups
+    pitch = rows + 1
     inner = wt_ref.shape[0]
 
     @pl.when(step == 0)
     def _():
         for m in range(groups):
-            base = group_s[m] * span
+            at = m * share
             for ref in sl_refs[2 * m : 2 * m + 2]:
-                size = ref.shape[1]
                 for j in range(2):
-                    part[j, pl.ds(pl.multiple_of(base, 8), size), :] = ref[j].astype(F32)
-                base = base + size
+                    for k in range(ref.shape[1] // rows):
+                        row = (at + k) * pitch
+                        part[j, row : row + rows, :] = ref[j, k * rows : (k + 1) * rows].astype(F32)
+                at += ref.shape[1] // rows
         acc[...] = jnp.zeros_like(acc)
         quad[...] = jnp.zeros_like(quad)
 
@@ -304,8 +313,8 @@
     total = acc[...]
     total_q = quad[...]
     for u in range(inner):
-        re = part[0, pl.ds(step * inner + u, K, stride=rows), :]
-        im = part[1, pl.ds(step * inner + u, K, stride=rows), :]
+        re = part[0, pl.ds(step * inner + u, K, stride=pitch), :]
+        im = part[1, pl.ds(step * inner + u, K, stride=pitch), :]
         shifted = []
         for t in range(TRANS):
             c = cos_ref[t, u : u + 1, :]
@@ -324,7 +333,7 @@
 
     @pl.when(step == pl.num_programs(0) - 1)
     def _():
-        ids = lax.broadcasted_iota(jnp.int32, quad.shape, 0)
+        ids = lax.broadcasted_iota(jnp.int32, quad.shape, 0) ^ (lax.axis_index("img") * share)
         half = 0.5 * quad[...]
         for t in range(TRANS):
             value = acc[t * K : (t + 1) * K, :] - half
@@ -333,7 +342,7 @@
                 out_ref[t * LMAX + l : t * LMAX + l + 1, :] = jnp.sum(pick, axis=0, keepdims=True)
 
 
-def candidate_logits(group_ids, slices, weighted, squared, cosine, sine, cand):
+def candidate_logits(slices, weighted, squared, cosine, sine, cand):
     rows, count = squared.shape[:2]
     inner = 8
     return pl.pallas_call(
@@ -341,7 +350,6 @@
         grid=(rows // inner,),
         out_shape=jax.ShapeDtypeStruct((TRANS * LMAX, count), F32),
         in_specs=[
-            smem(),
             pl.BlockSpec((inner, count, 2 * COLS), lambda s: (s, 0, 0)),
             pl.BlockSpec((inner, count, COLS), lambda s: (s, 0, 0)),
             pl.BlockSpec((TRANS, inner, COLS), lambda s: (0, s, 0)),
@@ -351,13 +359,14 @@
         + [pl.BlockSpec(x.shape, lambda s: (0, 0, 0)) for x in slices],
         out_specs=pl.BlockSpec((TRANS * LMAX, count), lambda s: (0, 0)),
         scratch_shapes=[
-            pltpu.VMEM((2, K * rows, COLS), F32),
+            pltpu.VMEM((2, K * (rows + 1), COLS), F32),
             pltpu.VMEM((TRANS * K, count), F32),
             pltpu.VMEM((K, count), F32),
         ],
         compiler_params=params(1),
+        cost_estimate=cost(8),
         name="logits",
-    )(group_ids, weighted, squared, cosine, sine, cand, *slices)
+    )(weighted, squared, cosine, sine, cand, *slices)
 
 
 def posterior_rows(logits, counts):
@@ -369,30 +378,30 @@
     return (exponent / jnp.sum(exponent, axis=0, keepdims=True)).astype(BF16).astype(F32)
 
 
-def list_rows(num, src_s, len_s, group_s, outs, pick):
+def list_rows(num, src_s, len_s, outs, pick):
     parts = 2 * outs[0].shape[0]
     cap = outs[0].shape[2]
     comps = num.shape[0]
     lead = src_s.shape[0] // parts
+    group = lax.axis_index("img")
     for m in range(parts):
-        q = group_s[m]
-
-        def group_step(g, carry, q=q, m=m):
-            base = pl.multiple_of(g * 16, 16)
-            at = q * lead + g // 2
-            off = g % 2 * 16
-            for u in range(16):
-                s = src_s[at, off + u]
+        q = group ^ m
+
+        def turn(g, carry, q=q, m=m):
+            base = pl.multiple_of(g * 32, 32)
+            at = q * lead + base
+            for u in range(32):
+                s = src_s[at + u]
                 for c in range(comps):
                     pick[c, u : u + 1, :] = num[c, pl.ds(s, 1), :]
             for c in range(comps):
-                outs[m % 2][m // 2, c, pl.ds(base, 16), :] = pick[c].astype(BF16)
+                outs[m % 2][m // 2, c, pl.ds(base, 32), :] = pick[c].astype(BF16)
             return carry
 
-        lax.fori_loop(0, (jnp.minimum(len_s[q, 0], cap) + 15) // 16, group_step, 0)
-
-
-def spread_kernel(src_s, len_s, group_s, cand_ref, cnt_ref, sq_ref, *rest):
+        lax.fori_loop(0, (jnp.minimum(len_s[q, 0], cap) + 31) // 32, turn, 0)
+
+
+def spread_kernel(src_s, len_s, cand_ref, cnt_ref, sq_ref, *rest):
     lg_refs = rest[:-6]
     keep_ref, send_ref, post, post_sum, num, pick = rest[-6:]
     step = pl.program_id(0)
@@ -421,11 +430,11 @@
 
     @pl.when(step == pl.num_programs(0) - 1)
     def _():
-        list_rows(num, src_s, len_s, group_s, (keep_ref, send_ref), pick)
+        list_rows(num, src_s, len_s, (keep_ref, send_ref), pick)
 
 
 def project_kernel(
-    src_s, len_s, group_s, post, wt_ref, cos_ref, sin_ref, keep_ref, send_ref, num, pick
+    src_s, len_s, post, wt_ref, cos_ref, sin_ref, after, keep_ref, send_ref, num, pick
 ):
     step = pl.program_id(0)
     inner = wt_ref.shape[0]
@@ -446,20 +455,19 @@
 
     @pl.when(step == pl.num_programs(0) - 1)
     def _():
-        list_rows(num, src_s, len_s, group_s, (keep_ref, send_ref), pick)
-
-
-def spread(src, lengths, group_ids, logits, cand, counts, squared, cap):
+        list_rows(num, src_s, len_s, (keep_ref, send_ref), pick)
+
+
+def spread(src, lengths, n_img, logits, cand, counts, squared, cap):
     rows, count = squared.shape[:2]
     inner = 8
-    shape = (group_ids.shape[0] // 2, 1, cap, COLS)
+    shape = (n_img // 2, 1, cap, COLS)
     return pl.pallas_call(
         spread_kernel,
         grid=(rows // inner,),
         out_shape=[jax.ShapeDtypeStruct(shape, BF16)] * 2
         + [jax.ShapeDtypeStruct((TRANS * K, count), BF16)],
         in_specs=[
-            smem(),
             smem(),
             smem(),
             pl.BlockSpec((LMAX, count), lambda s: (0, 0)),
@@ -472,17 +480,18 @@
         scratch_shapes=[
             pltpu.VMEM((2 * K, count), BF16),
             pltpu.VMEM((1, rows * K, COLS), F32),
-            pltpu.VMEM((1, 16, COLS), F32),
+            pltpu.VMEM((1, 32, COLS), F32),
         ],
         compiler_params=params(1),
+        cost_estimate=cost(8),
         name="spread",
-    )(src, lengths, group_ids, cand, counts, squared, *logits)
-
-
-def project(src, lengths, group_ids, post, weighted, cosine, sine, cap):
+    )(src, lengths, cand, counts, squared, *logits)
+
+
+def project(src, lengths, n_img, post, weighted, cosine, sine, after, cap):
     rows, count = weighted.shape[:2]
     inner = 8
-    shape = (group_ids.shape[0] // 2, 2, cap, COLS)
+    shape = (n_img // 2, 2, cap, COLS)
     return pl.pallas_call(
         project_kernel,
         grid=(rows // inner,),
@@ -490,25 +499,29 @@
         in_specs=[
             smem(),
             smem(),
-            smem(),
             pl.BlockSpec((TRANS * K, count), lambda s: (0, 0)),
             pl.BlockSpec((inner, count, 2 * COLS), lambda s: (s, 0, 0)),
             pl.BlockSpec((TRANS, inner, COLS), lambda s: (0, s, 0)),
             pl.BlockSpec((TRANS, inner, COLS), lambda s: (0, s, 0)),
+            hbm(),
         ],
         out_specs=[pl.BlockSpec(shape, lambda s: (0, 0, 0, 0))] * 2,
         scratch_shapes=[
             pltpu.VMEM((2, rows * K, COLS), F32),
-            pltpu.VMEM((2, 16, COLS), F32),
+            pltpu.VMEM((2, 32, COLS), F32),
         ],
         compiler_params=params(1),
+        cost_estimate=cost(9),
         name="project",
-    )(src, lengths, group_ids, post, weighted, cosine, sine)
-
-
-def to_member(keep, send, n_img):
+    )(src, lengths, post, weighted, cosine, sine, after)
+
+
+def add_cores(keep, send, n_img):
     got = lax.ppermute(send, "img", flip(n_img, 1))
-    summed = [(keep[m].astype(F32) + got[m].astype(F32)).astype(BF16) for m in range(n_img // 2)]
+    return [(keep[m].astype(F32) + got[m].astype(F32)).astype(BF16) for m in range(n_img // 2)]
+
+
+def add_chips(summed, n_img):
     moved = [lax.ppermute(summed[m], "img", flip(n_img, 2 * m)) for m in range(1, n_img // 2)]
     return sum([x.astype(F32) for x in moved], summed[0].astype(F32)).astype(BF16)
 
@@ -520,17 +533,21 @@
     return lines_here + 2 * HEAD
 
 
-def insert_kernel(start, count, has_acc, mode, len_s, pos_s, at_s, wgt_s, order_s, *rest):
+def insert_kernel(start, count, has_acc, mode, len_s, code_s, wgt_s, *rest):
     pieces = rest[:count]
     rest = rest[count:]
     out_ref, acc, buf = rest[-3:]
     extra = rest[:-3]
     comps, cap = buf.shape[:2]
-    lead = pos_s.shape[0] // order_s.shape[0]
+    blocks = len_s.shape[0]
+    lead = code_s.shape[0] // blocks
+    slab = lax.axis_index("vol")
+    place = jnp.where(slab & 1, blocks - 1 - (slab >> 1), slab >> 1)
     if has_acc:
-        pltpu.sync_copy(extra[-1], acc)
+        pltpu.sync_copy(extra[-1], acc.at[0])
     else:
-        acc[...] = jnp.zeros_like(acc)
+        acc[0] = jnp.zeros(acc.shape[1:], F32)
+    acc[1] = jnp.zeros(acc.shape[1:], F32)
     first = lax.broadcasted_iota(jnp.int32, (2, COLS), 0) == 0
     index = 0
     while index < count:
@@ -546,42 +563,48 @@
             index += 1
         else:
             index += 2
-        block = order_s[m]
+        from_place = place + ((m + 1) // 2) * (-1 if m % 2 else 1)
+        from_place = from_place & (blocks - 1)
+        block = jnp.where(
+            from_place >= blocks // 2, 2 * (blocks - 1 - from_place) + 1, 2 * from_place
+        )
 
         def group_step(g, carry, block=block):
-            at = block * lead + g // 8
-            off = g % 8 * 4
+            at = block * lead + g * 4
             for u in range(4):
-                s = pos_s[at, off + u]
-                to = at_s[at, off + u]
-                w = wgt_s[at, off + u]
+                code = code_s[at + u]
+                s = code & 1023
+                to = code >> 10
+                w = wgt_s[at + u]
                 both = jnp.where(first, w, 1.0 - w)
                 for c in range(comps):
                     row = jnp.broadcast_to(buf[c, pl.ds(s, 1), :], (2, COLS))
-                    acc[c, pl.ds(to, 2), :] = acc[c, pl.ds(to, 2), :] + both * row
+                    acc[u % 2, c, pl.ds(to, 2), :] = acc[u % 2, c, pl.ds(to, 2), :] + both * row
             return carry
 
         lax.fori_loop(0, (jnp.minimum(len_s[block, 0], cap) + 3) // 4, group_step, 0)
 
     if mode == "sum":
-        pltpu.sync_copy(acc, out_ref)
+        acc[0] = acc[0] + acc[1]
+        pltpu.sync_copy(acc.at[0], out_ref)
         return
     planes, lines_here = extra[0].shape[:2]
     stride = line_stride(lines_here)
 
     def plane_step(p, carry):
         base = pl.multiple_of(p * stride + HEAD, 8)
-        if mode == "inverse":
-            out_ref[p] = 1.0 / (acc[0, pl.ds(base, lines_here), :] + extra[0][p])
-        else:
-            for c in range(comps):
-                out_ref[c, p] = acc[c, pl.ds(base, lines_here), :] * extra[0][p]
+        for c in range(comps):
+            total = acc[0, c, pl.ds(base, lines_here), :] + acc[1, c, pl.ds(base, lines_here), :]
+            if mode == "inverse":
+                out_ref[p] = 1.0 / (total + extra[0][p])
+            else:
+                out_ref[c, p] = total * extra[0][p]
         return carry
 
     lax.fori_loop(0, planes, plane_step, 0)
 
 
-def insert(tables, order, start, pieces, cap, block, mode, extra=(), acc=None):
+def insert(tables, start, pieces, cap, block, mode, extra=(), acc=None):
     comps = pieces[0].shape[0]
     planes, lines_here = block
     acc_shape = (comps, planes * line_stride(lines_here), COLS)
@@ -594,14 +617,15 @@
     return pl.pallas_call(
         partial(insert_kernel, start, len(pieces), acc is not None, mode),
         out_shape=jax.ShapeDtypeStruct(out, F32),
-        in_specs=[smem()] * 5
+        in_specs=[smem()] * 3
         + [vmem()] * (len(pieces) + len(extra))
         + [hbm()] * (acc is not None),
         out_specs=hbm() if mode == "sum" else vmem(),
-        scratch_shapes=[pltpu.VMEM(acc_shape, F32), pltpu.VMEM((comps, cap, COLS), F32)],
+        scratch_shapes=[pltpu.VMEM((2,) + acc_shape, F32), pltpu.VMEM((comps, cap, COLS), F32)],
         compiler_params=pltpu.CompilerParams(vmem_limit_bytes=VMEM_LIMIT),
+        cost_estimate=cost(6),
         name="insert_" + mode,
-    )(*tables, order, *pieces, *more)
+    )(*tables, *pieces, *more)
 
 
 def running(x):
@@ -626,18 +650,26 @@
 def compacted(member, rank, values, lead):
     high = jnp.where(member, rank >> 5, -1)
     low = rank & 31
-    left = lax.broadcasted_iota(jnp.int32, (lead, rank.shape[1]), 0) == high
+    spot = lax.broadcasted_iota(jnp.int32, (4 * lead, rank.shape[1]), 0)
+    shift = lead.bit_length() - 1
+    left = ((spot & (lead - 1)) * 4 + (spot >> shift)) == high
     hot = lax.broadcasted_iota(jnp.int32, (32, rank.shape[1]), 0) == low
     right = jnp.concatenate([jnp.where(hot, v, 0.0).astype(BF16) for v in values], axis=0)
-    return lax.dot_general(
+    out = lax.dot_general(
         left.astype(F32).astype(BF16), right, (((1,), (1,)), ((), ())), preferred_element_type=F32
     )
+    return [
+        jnp.concatenate(
+            [out[h * lead : (h + 1) * lead, 32 * i : 32 * (i + 1)] for h in range(4)], axis=1
+        )
+        for i in range(len(values))
+    ]
 
 
 def lists_kernel(
     n_img, planes_here, lines_here, cap,
     plane_ref, line_ref, wgt_ref,
-    src_ref, pos_ref, at_ref, w_ref, send_len, recv_len, longest, own,
+    src_ref, code_ref, w_ref, send_len, recv_len, longest, own,
 ):
     slab = lax.axis_index("vol")
     group = lax.axis_index("img")
@@ -662,10 +694,11 @@
     row_ids = split_index(lax.broadcasted_iota(jnp.int32, (1, number), 1))
     for q in range(n_img):
         out = compacted(sent[q : q + 1], rank[q : q + 1], row_ids, lead)
-        src_ref[q * lead : (q + 1) * lead, :] = (32.0 * out[:, :32] + out[:, 32:64]).astype(jnp.int32)
+        src_ref[q * lead : (q + 1) * lead, :] = (32.0 * out[0] + out[1]).astype(jnp.int32)
 
     member = in_part(lines, group)
     place = running(member.astype(jnp.int32)) - member.astype(jnp.int32)
+    place = jnp.minimum(place, cap - 1)
     local = plane_ref[...] - slab * planes_here
     here = member & (local >= 0) & (local < planes_here)
     total = running(here.astype(jnp.int32))
@@ -678,26 +711,27 @@
         values = split_index(place[row]) + split_index(target[row]) + split_weight(wgt_ref[row, :])
         out = compacted(here[row], rank[row], values, lead)
         at = slice(v * lead, (v + 1) * lead)
-        pos_ref[at, :] = (32.0 * out[:, :32] + out[:, 32:64]).astype(jnp.int32)
-        at_ref[at, :] = (32.0 * out[:, 64:96] + out[:, 96:128]).astype(jnp.int32)
-        w_ref[at, :] = out[:, 128:160] + out[:, 160:192] + out[:, 192:224]
+        code_ref[at, :] = (
+            32768.0 * out[2] + 1024.0 * out[3] + 32.0 * out[0] + out[1]
+        ).astype(jnp.int32)
+        w_ref[at, :] = out[4] + out[5] + out[6]
 
 
 def lists(row_plane, row_line, row_weight, n_vol, n_img, planes_here, lines_here, cap):
-    lead = -(-(cap // 32) // 8) * 8
+    lead = 8
+    assert cap <= lead * COLS
     number = ROWS // n_vol * K
 
     def order(x):
         return x.T.reshape(n_vol, number)
 
     def table(blocks, dtype=jnp.int32):
-        return jax.ShapeDtypeStruct((blocks * lead, 32), dtype)
+        return jax.ShapeDtypeStruct((blocks * lead, COLS), dtype)
 
     return pl.pallas_call(
         partial(lists_kernel, n_img, planes_here, lines_here, cap),
         out_shape=[
             table(n_img),
-            table(n_vol),
             table(n_vol),
             table(n_vol, F32),
             jax.ShapeDtypeStruct((8, COLS), jnp.int32),
@@ -705,9 +739,10 @@
             jax.ShapeDtypeStruct((8, COLS), jnp.int32),
         ],
         in_specs=[vmem()] * 3,
-        out_specs=[vmem()] * 7,
+        out_specs=[vmem()] * 6,
         scratch_shapes=[pltpu.VMEM((8, number), jnp.int32)],
         compiler_params=pltpu.CompilerParams(vmem_limit_bytes=VMEM_LIMIT),
+        cost_estimate=cost(6),
         name="lists",
     )(order(row_plane), order(row_line), order(row_weight))
 
@@ -778,51 +813,50 @@
 
     aligned = max(1, 16 // rows)
     share_a = share * 11 // 16 // aligned * aligned
-    messages = extract(volume, plane_share, line_share, weight_share, slab_id, n_vol, share_a)
+    messages = extract(volume, row_plane, row_line, row_weight, n_vol, share, share_a)
     cosine, sine = shift_phases(row_freq, col_freq, TRANS)
     weighted, squared = weigh(images, defocus, noise_weight, row_freq, col_freq)
     mean = rows * K // n_img
     cap = -(-int(mean + 4.2 * math.sqrt(mean)) // 32) * 32
-    src, pos, at, wgt, send_len, recv_len, longest = lists(
+    src, code, wgt, send_len, recv_len, longest = lists(
         row_plane, row_line, row_weight, n_vol, n_img, planes_here, lines_here, cap
     )
-    own_a, own_b = to_pixel_rows(messages, n_vol, weighted, pos)
+    own_a, own_b = to_pixel_rows(messages, n_vol, weighted)
     slices_b = from_partners(own_b, n_img)
     slices_a = from_partners(own_a, n_img)
     slices = [x for both in zip(slices_a, slices_b) for x in both]
-    group_ids = group_id ^ jnp.arange(n_img)
-
     cand = candidates.T
     count_row = counts[None, :]
-    partial_logits = candidate_logits(group_ids, slices, weighted, squared, cosine, sine, cand)
+    partial_logits = candidate_logits(slices, weighted, squared, cosine, sine, cand)
     pair_logits = partial_logits + lax.ppermute(partial_logits, "vol", flip(n_vol, 1))
     logits = [pair_logits] + [
         lax.ppermute(pair_logits, "vol", along_z(n_vol, d)) for d in range(1, n_vol // 2)
     ]
 
-    keep_d, send_d, post = spread(
-        src, send_len, group_ids, logits, cand, count_row, squared, cap
-    )
-    keep_n, send_n = project(src, send_len, group_ids, post, weighted, cosine, sine, cap)
-    pieces_d = ring_gather(to_member(keep_d, send_d, n_img), n_vol)
-    pieces_n = ring_gather(to_member(keep_n, send_n, n_img), n_vol)
-    order = jnp.asarray(ring_order(n_vol))[slab_id]
-    tables = (recv_len, pos, at, wgt)
+    src = src.reshape(-1)
+    keep_d, send_d, post = spread(src, send_len, n_img, logits, cand, count_row, squared, cap)
+    summed_d = add_cores(keep_d, send_d, n_img)
+    keep_n, send_n = project(
+        src, send_len, n_img, post, weighted, cosine, sine, summed_d[-1], cap
+    )
+    pieces_d = ring_gather(add_chips(summed_d, n_img), n_vol)
+    pieces_n = ring_gather(add_chips(add_cores(keep_n, send_n, n_img), n_img), n_vol)
+    tables = (recv_len, code.reshape(-1), wgt.reshape(-1))
     block = (planes_here, lines_here)
     early = n_vol // 2 + 1
-    inverse = insert(tables, order, 0, pieces_d, cap, block, "inverse", [regularizer])
-    part_sum = insert(tables, order, 0, pieces_n[:early], cap, block, "sum")
-    result = insert(
-        tables, order, early, pieces_n[early:], cap, block, "result", [inverse], part_sum
-    )
-
-    def dense(state):
-        return False, dense_path(
+    inverse = insert(tables, 0, pieces_d, cap, block, "inverse", [regularizer])
+    part_sum = insert(tables, 0, pieces_n[:early], cap, block, "sum")
+
+    def listed():
+        return insert(tables, early, pieces_n[early:], cap, block, "result", [inverse], part_sum)
+
+    def dense():
+        return dense_path(
             sum(logits[1:], logits[0]), cand, count_row, weighted, squared, cosine, sine,
             plane_share, line_share, weight_share, regularizer, slab_id,
         )
 
-    return lax.while_loop(lambda state: state[0], dense, (longest[0, 0] > cap, result))[1]
+    return lax.cond(longest[0, 0] <= cap, listed, dense)
 
 
 def solution(mesh):

time: 253 us -> 216 us (0.85)
  Pallas kernels: 113 us -> 80.8 us
  waiting for transfers between devices: 45.7 us -> 62.5 us
  local copies, waits for them, and re-layouts: 26.2 us -> 12.1 us
  other arithmetic: 13.8 us -> 10.1 us
  starting transfers between devices: 37 us -> 34.1 us
    ppermute x6, waiting for transfers between devices: 0.02 us -> 19.1 us  [ring_gather(): two = lax.ppermute(two, 'vol', back)]
    pallas_call x3, Pallas kernels: 42 us -> 25 us  [insert(): pl.pallas_call(partial(insert_kernel, start, len(pieces), acc is not None...]
    ppermute x6, waiting for transfers between devices: 16.6 us -> 1.61 us  [ring_gather(): one = lax.ppermute(one, 'vol', ahead)]
    unnamed x89 -> x86, local copies, waits for them, and re-layouts: 13.6 us -> 5.8 us
    ppermute x3, waiting for transfers between devices: 3.86 us -> 11 us  [to_pixel_rows(): lax.ppermute(sums_a[d], 'vol', along_z(n_vol, d))]
    pallas_call x1, Pallas kernels: 15.5 us -> 8.47 us  [weigh(): pl.pallas_call(weigh_kernel, grid=(count // step,), out_shape=[jax.ShapeD...]
    ppermute x6, starting transfers between devices: 7.1 us -> 2.07 us  [ring_gather(): two = lax.ppermute(two, 'vol', back)]
    pallas_call x1, Pallas kernels: 11.7 us -> 7.31 us  [spread(): pl.pallas_call(spread_kernel, grid=(rows // inner,), out_shape=[jax.Shape...]
  transfers between devices with their start and end apart: 38 -> 38, of which waited for: 15 -> 19; matrix products, arithmetic and copies ran while one was open for 7% -> 5% of each run, Pallas kernels for 21% -> 15%
where the time goes in v4:
time: 216 us; the launch traced here: 214 us
  Pallas kernels  80.8 us (37%)
  waiting for transfers between devices  62.5 us (29%)
  starting transfers between devices  34.1 us (16%)
  between operations  14.4 us (7%)
  local copies, waits for them, and re-layouts  12.1 us (6%)
  other arithmetic  10.1 us (5%)
    pallas_call x3, Pallas kernels, insert(): pl.pallas_call(partial(insert_kernel, start, len(pieces), acc is not None...  25 us
    ppermute x6, waiting for transfers between devices, ring_gather(): two = lax.ppermute(two, 'vol', back)  19.1 us
    pallas_call x1, Pallas kernels, extract(): pl.pallas_call(partial(extract_kernel, rows, planes_here), out_shape=[sha...  15.2 us
    ppermute x3, waiting for transfers between devices, to_pixel_rows(): lax.ppermute(sums_a[d], 'vol', along_z(n_vol, d))  11 us
    pallas_call x1, Pallas kernels, project(): pl.pallas_call(project_kernel, grid=(rows // inner,), out_shape=[jax.Shap...  9.36 us
    ppermute x2, waiting for transfers between devices, add_chips(): lax.ppermute(summed[m], 'img', flip(n_img, 2 * m))  9.32 us
    ppermute x6, starting transfers between devices, ring_gather(): one = lax.ppermute(one, 'vol', ahead)  8.64 us
    pallas_call x1, Pallas kernels, weigh(): pl.pallas_call(weigh_kernel, grid=(count // step,), out_shape=[jax.ShapeD...  8.47 us
  transfers between devices with their start and end apart: 38, of which 19 were waited for; matrix products, arithmetic and copies ran while one was open for 5% of the time, Pallas kernels for 15%

profile of v4, /device:TPU:12, one launch (start us, length us, event | category | flops | bytes accessed | tf_op | source)
XLA Modules:
  0.0 214.2 jit_solution(12366095389942079806)
XLA Ops:
  6.5 15.2 %extract.1 = (bf16[4,2,352,128]{3,2,1,0:T(8,128)(2,1)}, bf16[4,2,352,128]{3,2,1,0:T(8,128)(2,1)}, bf16[2,2,160,128]{3,2,1,0:T(8,128)(2,1)}, bf16[2,2,160,128]{3,...) custom-call(s32[64,256]{1,0:T(8,128)} %refs_0_.1, s32[64,256]{1,0:T(8,128)} %refs_1_.1, ...), custom_call_target="tpu_custom_call" | custom-call | bytes 40590000 | tf_op jit(solution)/shard_map/extract/pallas_call | solution.py:151
  21.9 1.9 collective-permute-start.3
  23.9 2.0 collective-permute-start
  26.0 1.5 multiply_cosine_fusion
  27.5 1.5 fusion.21
  29.0 8.5 %weigh.1 = (bf16[32,384,256]{2,1,0:T(8,128)(2,1)S(1)}, bf16[32,384,128]{2,1,0:T(8,128)(2,1)}) custom-call(bf16[2,384,32,128]{3,2,1,0:T(8,128)(2,1)} %img_ref.1, f32[384,32]{1,0:T(8,128)} %get-tuple-element.255.sa_ref, f32[384,32]{1,0:T(8,128)} %get-tuple-element.254.ca_ref, f32[384,128]{1,0:T(8,128)} %get-tuple-element.253.sx_ref, ...), custom_call_target="tpu_custom_call" | custom-call | bytes 44280000 | tf_op jit(solution)/shard_map/weigh/pallas_call | solution.py:256
  37.6 4.4 %collective-permute-done.got_a = bf16[4,2,352,128]{3,2,1,0:T(8,128)(2,1)S(1)} collective-permute-done((bf16[4,2,352,128]{3,2,1,0:T(8,128)(2,1)}, bf16[4,2,352,128]{3,2,1,0:T(8,128)(2,1)S(1)}, u32[]{:S(2)}, u32[]{:S(2)}) %collective-permute-start) | collective-permute-done | bytes 720928 | tf_op jit(solution)/shard_map/ppermute | solution.py:190
  42.0 0.9 copy-done.8
  42.9 2.7 %combine_first.1 = (bf16[2,352,128]{2,1,0:T(8,128)(2,1)}, bf16[2,352,128]{2,1,0:T(8,128)(2,1)}, bf16[2,352,128]{2,1,0:T(8,128)(2,1)}, bf16[2,352,128]{2,1,0:T(8,...) custom-call(bf16[4,2,352,128]{3,2,1,0:T(8,128)(2,1)} %get-tuple-element.128.keep_a, ...), custom_call_target="tpu_custom_call" | custom-call | bytes 11070000 | tf_op jit(solution)/shard_map/combine_first/pallas_call | solution.py:193
  45.5 1.8 collective-permute-start.7
  47.8 4.4 %collective-permute-start.5 = (bf16[2,352,128]{2,1,0:T(8,128)(2,1)}, bf16[2,352,128]{2,1,0:T(8,128)(2,1)S(1)}, u32[]{:S(2)}, u32[]{:S(2)}) collective-permute-start(bf16[2,352,128]{2,1,0:T(8,128)(2,1)} %get-tuple-element.136), channel_id=1, source_target_pairs={{0,4},{1,5},{2,6},{3,7},{4,0},{5,1},{6,2},{7,3},{8,12},{9,13},{10,... | collective-permute-start | bytes 540680 | tf_op jit(solution)/shard_map/ppermute | solution.py:204
  52.4 0.9 add.193.rest_1_
  53.4 1.4 collective-permute-start.11
  54.8 0.8 collective-permute-done.4
  55.6 7.2 %collective-permute-done.5 = bf16[2,352,128]{2,1,0:T(8,128)(2,1)S(1)} collective-permute-done((bf16[2,352,128]{2,1,0:T(8,128)(2,1)}, bf16[2,352,128]{2,1,0:T(8,128)(2,1)S(1)}, u32[]{:S(2)}, u32[]{:S(2)}) %collective-permute-start.5) | collective-permute-done | bytes 180256 | tf_op jit(solution)/shard_map/ppermute | solution.py:204
  62.8 3.0 %collective-permute-done.6 = bf16[2,352,128]{2,1,0:T(8,128)(2,1)S(1)} collective-permute-done((bf16[2,352,128]{2,1,0:T(8,128)(2,1)}, bf16[2,352,128]{2,1,0:T(8,128)(2,1)S(1)}, u32[]{:S(2)}, u32[]{:S(2)}) %collective-permute-start.6) | collective-permute-done | bytes 180256 | tf_op jit(solution)/shard_map/ppermute | solution.py:204
  65.8 1.0 add_add_fusion.rest_0_
  66.9 1.2 collective-permute-start.10
  68.1 0.7 collective-permute-start.8
  69.1 4.6 %collective-permute-done.12.rest_6_ = bf16[2,352,128]{2,1,0:T(8,128)(2,1)S(1)} collective-permute-done((bf16[2,352,128]{2,1,0:T(8,128)(2,1)S(1)}, bf16[2,352,128]{2,1,0:T(8,128)(2,1)S(1)}, u32[]{:S(2)}, u32[]{:S(2)}) %collective-permute-start.12) | collective-permute-done | bytes 180256 | tf_op jit(solution)/shard_map/ppermute | solution.py:211
  73.7 3.2 %collective-permute-done.10.rest_4_ = bf16[2,352,128]{2,1,0:T(8,128)(2,1)S(1)} collective-permute-done((bf16[2,352,128]{2,1,0:T(8,128)(2,1)S(1)}, bf16[2,352,128]{2,1,0:T(8,128)(2,1)S(1)}, u32[]{:S(2)}, u32[]{:S(2)}) %collective-permute-start.10) | collective-permute-done | bytes 180256 | tf_op jit(solution)/shard_map/ppermute | solution.py:211
  77.7 7.5 %logits.1 = f32[32,384]{1,0:T(8,128)} custom-call(bf16[32,384,256]{2,1,0:T(8,128)(2,1)S(1)} %get-tuple-element.126.rest_3_.wt_ref, bf16[32,384,128]{2,1,0:T(8,128)(2,1)} %get-tuple-element.127.sq_ref, f32[4,32,128]{2,1,0:T(8,128)S(1)} %get-tuple-element.251.cos_ref, f32[4,32,128]{2,1,0:T(8,128)S(1)} %get-tuple-element.250.sin_ref, s32[8,384]{1,0:T(8,128)S(1)} %bitcast.107, ...), custom_call_target="tpu_custom_call" | custom-call | bytes 29520000 | tf_op jit(solution)/shard_map/logits/pallas_call | solution.py:348
  85.2 0.7 collective-permute-start.14
  85.8 3.6 %collective-permute-done.14 = f32[32,384]{1,0:T(8,128)S(1)} collective-permute-done((f32[32,384]{1,0:T(8,128)}, f32[32,384]{1,0:T(8,128)S(1)}, u32[]{:S(2)}, u32[]{:S(2)}) %collective-permute-start.14) | collective-permute-done | bytes 49184 | tf_op jit(solution)/shard_map/ppermute | solution.py:831
  89.5 0.8 add.194.rest_0_
  90.4 1.1 collective-permute-start.16
  91.5 2.6 %collective-permute-start.15 = (f32[32,384]{1,0:T(8,128)S(1)}, f32[32,384]{1,0:T(8,128)S(1)}, u32[]{:S(2)}, u32[]{:S(2)}) collective-permute-start(f32[32,384]{1,0:T(8,128)S(1)} %add.194.rest_0_), channel_id=1, source_target_pairs={{0,2},{1,3},{2,4},{3,5},{4,6},{5,7},{6,0},{7,1},{8,10},{9,11},{10,... | collective-permute-start | bytes 147464 | tf_op jit(solution)/shard_map/ppermute | solution.py:833
  94.2 0.7 reshape.315.wgt_ref
  95.0 0.7 reshape.314.line_ref
  95.8 0.7 reshape.313.plane_ref
  96.6 5.3 %lists.1 = (s32[32,128]{1,0:T(8,128)}, s32[64,128]{1,0:T(8,128)S(1)}, f32[64,128]{1,0:T(8,128)}, s32[8,128]{1,0:T(8,128)}, s32[8,128]{1,0:T(8,128)}, /*index=5*/s32[8,128]{1,0:T(8,128)}) custom-call(s32[8,2048]{1,0:T(8,128)} %reshape.313.plane_ref, s32[8,2048]{1,0:T(8,128)} %reshape.314.line_ref, f32[8,2048]{1,0:T(8,128)} %reshape.315.wgt_ref), custom_call_target="tpu_custom_call" | custom-call | bytes 22140000 | tf_op jit(solution)/shard_map/lists/pallas_call | solution.py:731
  101.9 7.3 %spread.1 = (bf16[2,1,608,128]{3,2,1,0:T(8,128)(2,1)}, bf16[2,1,608,128]{3,2,1,0:T(8,128)(2,1)}, bf16[256,384]{1,0:T(8,128)(2,1)}) custom-call(s32[4096]{0:T(1024)} %bitcast.109, s32[8,128]{1,0:T(8,128)} %get-tuple-element.144.len_s, s32[8,384]{1,0:T(8,128)S(1)} %bitcast.108, s32[1,384]{1,0:T(1,128)S(1)} %broadcast_in_dim.13.cnt_ref, ...), custom_call_target="tpu_custom_call" | custom-call | bytes 29520000 | tf_op jit(solution)/shard_map/spread/pallas_call | solution.py:465
  109.2 1.8 collective-permute-done.18
  111.0 1.6 fusion.23.after
  112.7 9.4 %project.1 = (bf16[2,2,608,128]{3,2,1,0:T(8,128)(2,1)}, bf16[2,2,608,128]{3,2,1,0:T(8,128)(2,1)}) custom-call(s32[4096]{0:T(1024)} %bitcast.110, s32[8,128]{1,0:T(8,128)} %get-tuple-element.144.len_s, bf16[256,384]{1,0:T(8,128)(2,1)} %get-tuple-element.145.post, bf16[32,384,256]{2,1,0:T(8,128)(2,1)} %copy-done, ...), custom_call_target="tpu_custom_call" | custom-call | bytes 33210000 | tf_op jit(solution)/shard_map/project/pallas_call | solution.py:495
  122.2 2.1 collective-permute-done.19
  124.3 1.1 fusion.19
  125.5 9.3 %collective-permute-done.20 = bf16[2,608,128]{2,1,0:T(8,128)(2,1)S(1)} collective-permute-done((bf16[2,608,128]{2,1,0:T(8,128)(2,1)S(1)}, bf16[2,608,128]{2,1,0:T(8,128)(2,1)S(1)}, u32[]{:S(2)}, u32[]{:S(2)}) %collective-permute-start.20) | collective-permute-done | bytes 311328 | tf_op jit(solution)/shard_map/ppermute | solution.py:525
  134.8 1.1 fusion.17.rest_0_
  136.1 1.9 collective-permute-start.21
  138.3 6.3 %collective-permute-done.24.rest_2_ = bf16[2,608,128]{2,1,0:T(8,128)(2,1)S(1)} collective-permute-done((bf16[2,608,128]{2,1,0:T(8,128)(2,1)S(1)}, bf16[2,608,128]{2,1,0:T(8,128)(2,1)S(1)}, u32[]{:S(2)}, u32[]{:S(2)}) %collective-permute-start.24) | collective-permute-done | bytes 311328 | tf_op jit(solution)/shard_map/ppermute | solution.py:222
  145.3 1.3 collective-permute-start.22
  146.7 0.8 collective-permute-start.31
  147.5 1.3 collective-permute-start.30
  148.8 6.1 %collective-permute-done.25.rest_4_ = bf16[2,608,128]{2,1,0:T(8,128)(2,1)S(1)} collective-permute-done((bf16[2,608,128]{2,1,0:T(8,128)(2,1)S(1)}, bf16[2,608,128]{2,1,0:T(8,128)(2,1)S(1)}, u32[]{:S(2)}, u32[]{:S(2)}) %collective-permute-start.25) | collective-permute-done | bytes 311328 | tf_op jit(solution)/shard_map/ppermute | solution.py:222
  155.6 1.4 collective-permute-start.23
  157.0 1.3 collective-permute-done.31.rest_2_
  158.9 1.3 collective-permute-start.32
  160.3 5.5 %collective-permute-done.33.rest_4_ = bf16[1,608,128]{2,1,0:T(8,128)(2,1)S(1)} collective-permute-done((bf16[1,608,128]{2,1,0:T(8,128)(2,1)S(1)}, bf16[1,608,128]{2,1,0:T(8,128)(2,1)S(1)}, u32[]{:S(2)}, u32[]{:S(2)}) %collective-permute-start.33) | collective-permute-done | bytes 155680 | tf_op jit(solution)/shard_map/ppermute | solution.py:222
  166.4 1.3 collective-permute-start.34
  167.8 0.7 copy-done.10
  168.5 0.7 slice.80
  169.2 0.7 collective-permute-start.28
  169.9 0.7 copy-done.11
  171.3 1.3 collective-permute-start.27
  173.9 0.7 collective-permute-start.37
  176.0 1.3 collective-permute-start.36
  177.3 1.2 slice.57
  179.1 1.7 collective-permute-done.36.rest_7_
  180.8 9.7 %insert_inverse.1 = f32[32,64,128]{2,1,0:T(8,128)} custom-call(s32[8,128]{1,0:T(8,128)} %get-tuple-element.140.len_s, s32[8192]{0:T(1024)S(1)} %bitcast.98, f32[8192]{0:T(1024)} %bitcast.101, bf16[1,608,128]{2,1,0:T(8,128)(2,1)} %copy-done.13, bf16[1,608,128]{2,1,0:T(8,128)(2,1)} %copy-done.38, bf16[1,608,128]{2,1,0:T(8,128)(2,1)} %copy-done.37, ...), custom_call_target="tpu_custom_call" | custom-call | bytes 22140000 | tf_op jit(solution)/shard_map/insert_inverse/pallas_call | solution.py:617
  190.5 8.0 %insert_sum.1 = f32[2,2560,128]{2,1,0:T(8,128)} custom-call(s32[8,128]{1,0:T(8,128)} %get-tuple-element.140.len_s, s32[8192]{0:T(1024)S(1)} %bitcast.99, f32[8192]{0:T(1024)} %bitcast.102, bf16[2,608,128]{2,1,0:T(8,128)(2,1)} %copy-done.5, bf16[2,608,128]{2,1,0:T(8,128)(2,1)} %copy-done.24, bf16[2,608,128]{2,1,0:T(8,128)(2,1)} %copy-done.23, ...), custom_call_target="tpu_custom_call" | custom-call | bytes 22140000 | tf_op jit(solution)/shard_map/insert_sum/pallas_call | solution.py:617
  198.5 7.5 %conditional.1 = (f32[2,32,64,128]{3,2,1,0:T(8,128)S(1)}) conditional(s32[]{:T(128)} %bitcast.18, (s32[]{:T(128)}, s32[64,256]{1,0:T(8,128)}, s32[]{:T(128)}, s32[64,256]{1,0:T(8,128)}, f32[64,256]{1,0:T(8,128)}, /*index=5*/f32[4,32,128]{2,1,0:T(8,128)}, s32[8,384]{1,0:T(8,128)}, s32[1,384]{1,0:T(1,128)}, f32[32,384]{1,0:T(8,128)}, ...), branch_computations={%region_0.10_spmd, %region_10.11_spmd} | conditional | flops 1831321088 | bytes 338360800 | solution.py:859
  198.8 7.2 %insert_result.1 = f32[2,32,64,128]{3,2,1,0:T(8,128)S(1)} custom-call(s32[8,128]{1,0:T(8,128)} %get-tuple-element.91.len_s, s32[8192]{0:T(1024)S(1)} %get-tuple-element.92.code_s, f32[8192]{0:T(1024)} %get-tuple-element.93.wgt_s, bf16[2,608,128]{2,1,0:T(8,128)(2,1)} %get-tuple-element.94.rest_0_, bf16[2,608,128]{2,1,0:T(8,128)(2,1)} %get-tuple-element.95.rest_1_, ...), custom_call_target="tpu_custom_call" | custom-call | bytes 22140000 | tf_op jit(solution)/shard_map/cond/branch_1_fun/insert_result/pallas_call | solution.py:617
  206.0 1.3 copy-done.4
  (138 shorter events, 9.3 us)
Async XLA Ops:
  6.5 19.4 %copy-start.46 = (f32[384]{0:T(512)S(1)}, f32[384]{0:T(512)}, u32[]{:S(2)}) copy-start(f32[384]{0:T(512)} %param.13) | copy-start | bytes 4612
  21.8 15.7 %collective-permute-start.1 = (bf16[2,2,160,128]{3,2,1,0:T(8,128)(2,1)}, bf16[2,2,160,128]{3,2,1,0:T(8,128)(2,1)S(1)}, u32[]{:S(2)}, u32[]{:S(2)}) collective-permute-start(bf16[2,2,160,128]{3,2,1,0:T(8,128)(2,1)} %get-tuple-element.131), channel_id=1, source_target_pairs={{0,2},{1,3},{2,4},{3,5},{4,6},{5,7},{6,0},{7,1},{8,10},{9,11},{10,... | collective-permute-start | bytes 491528 | tf_op jit(solution)/shard_map/ppermute | solution.py:189
  21.8 15.7 %collective-permute-start.2 = (bf16[2,2,160,128]{3,2,1,0:T(8,128)(2,1)}, bf16[2,2,160,128]{3,2,1,0:T(8,128)(2,1)S(1)}, u32[]{:S(2)}, u32[]{:S(2)}) collective-permute-start(bf16[2,2,160,128]{3,2,1,0:T(8,128)(2,1)} %get-tuple-element.132), channel_id=1, source_target_pairs={{0,4},{1,5},{2,6},{3,7},{4,0},{5,1},{6,2},{7,3},{8,12},{9,13},{10,... | collective-permute-start | bytes 491528 | tf_op jit(solution)/shard_map/ppermute | solution.py:189
  21.9 15.6 %collective-permute-start.3 = (bf16[2,2,160,128]{3,2,1,0:T(8,128)(2,1)}, bf16[2,2,160,128]{3,2,1,0:T(8,128)(2,1)S(1)}, u32[]{:S(2)}, u32[]{:S(2)}) collective-permute-start(bf16[2,2,160,128]{3,2,1,0:T(8,128)(2,1)} %get-tuple-element.133), channel_id=1, source_target_pairs={{0,6},{1,7},{2,0},{3,1},{4,2},{5,3},{6,4},{7,5},{8,14},{9,15},{10,... | collective-permute-start | bytes 491528 | tf_op jit(solution)/shard_map/ppermute | solution.py:189
  23.9 18.1 %collective-permute-start = (bf16[4,2,352,128]{3,2,1,0:T(8,128)(2,1)}, bf16[4,2,352,128]{3,2,1,0:T(8,128)(2,1)S(1)}, u32[]{:S(2)}, u32[]{:S(2)}) collective-permute-start(bf16[4,2,352,128]{3,2,1,0:T(8,128)(2,1)} %get-tuple-element.129), channel_id=1, source_target_pairs={{0,1},{1,0},{2,3},{3,2},{4,5},{5,4},{6,7},{7,6},{8,9},{9,8},{10,11... | collective-permute-start | bytes 2162696 | tf_op jit(solution)/shard_map/ppermute | solution.py:190
  37.5 47.7 %copy-start = (bf16[32,384,256]{2,1,0:T(8,128)(2,1)}, bf16[32,384,256]{2,1,0:T(8,128)(2,1)S(1)}, u32[]{:S(2)}) copy-start(bf16[32,384,256]{2,1,0:T(8,128)(2,1)S(1)} %get-tuple-element.126.rest_3_.wt_ref) | copy-start | bytes 18874372
  37.5 40.2 %copy-start.41 = (s32[384,8]{0,1:T(8,128)S(1)}, s32[384,8]{0,1:T(8,128)}, u32[]{:S(2)}) copy-start(s32[384,8]{0,1:T(8,128)} %param.14) | copy-start | bytes 36868
  45.5 48.5 %copy-start.47 = (s32[384]{0:T(512)S(1)}, s32[384]{0:T(512)}, u32[]{:S(2)}) copy-start(s32[384]{0:T(512)} %param.15) | copy-start | bytes 4612
  45.5 48.5 %copy-start.21 = (f32[64,256]{1,0:T(8,128)S(1)}, f32[64,256]{1,0:T(8,128)}, u32[]{:S(2)}) copy-start(f32[64,256]{1,0:T(8,128)} %refs_2_.1) | copy-start | bytes 196612
  45.5 49.4 %copy-start.17 = (s32[64,256]{1,0:T(8,128)S(1)}, s32[64,256]{1,0:T(8,128)}, u32[]{:S(2)}) copy-start(s32[64,256]{1,0:T(8,128)} %refs_1_.1) | copy-start | bytes 196612
  45.5 6.8 %collective-permute-start.7 = (bf16[2,160,128]{2,1,0:T(8,128)(2,1)}, bf16[2,160,128]{2,1,0:T(8,128)(2,1)S(1)}, u32[]{:S(2)}, u32[]{:S(2)}) collective-permute-start(bf16[2,160,128]{2,1,0:T(8,128)(2,1)} %get-tuple-element.139), channel_id=1, source_target_pairs={{0,1},{1,0},{2,3},{3,2},{4,5},{5,4},{6,7},{7,6},{8,9},{9,8},{10,11... | collective-permute-start | bytes 245768 | tf_op jit(solution)/shard_map/ppermute | solution.py:203
  47.4 8.2 %collective-permute-start.4 = (bf16[2,352,128]{2,1,0:T(8,128)(2,1)}, bf16[2,352,128]{2,1,0:T(8,128)(2,1)S(1)}, u32[]{:S(2)}, u32[]{:S(2)}) collective-permute-start(bf16[2,352,128]{2,1,0:T(8,128)(2,1)} %get-tuple-element.135), channel_id=1, source_target_pairs={{0,2},{1,3},{2,4},{3,5},{4,6},{5,7},{6,0},{7,1},{8,10},{9,11},{10,... | collective-permute-start | bytes 540680 | tf_op jit(solution)/shard_map/ppermute | solution.py:204
  47.8 14.9 %collective-permute-start.5 = (bf16[2,352,128]{2,1,0:T(8,128)(2,1)}, bf16[2,352,128]{2,1,0:T(8,128)(2,1)S(1)}, u32[]{:S(2)}, u32[]{:S(2)}) collective-permute-start(bf16[2,352,128]{2,1,0:T(8,128)(2,1)} %get-tuple-element.136), channel_id=1, source_target_pairs={{0,4},{1,5},{2,6},{3,7},{4,0},{5,1},{6,2},{7,3},{8,12},{9,13},{10,... | collective-permute-start | bytes 540680 | tf_op jit(solution)/shard_map/ppermute | solution.py:204
  52.3 13.5 %collective-permute-start.6 = (bf16[2,352,128]{2,1,0:T(8,128)(2,1)}, bf16[2,352,128]{2,1,0:T(8,128)(2,1)S(1)}, u32[]{:S(2)}, u32[]{:S(2)}) collective-permute-start(bf16[2,352,128]{2,1,0:T(8,128)(2,1)} %get-tuple-element.137), channel_id=1, source_target_pairs={{0,6},{1,7},{2,0},{3,1},{4,2},{5,3},{6,4},{7,5},{8,14},{9,15},{10,... | collective-permute-start | bytes 540680 | tf_op jit(solution)/shard_map/ppermute | solution.py:204
  53.3 23.7 %copy-start.22 = (bf16[2,160,128]{2,1,0:T(8,128)(2,1)}, bf16[2,160,128]{2,1,0:T(8,128)(2,1)S(1)}, u32[]{:S(2)}) copy-start(bf16[2,160,128]{2,1,0:T(8,128)(2,1)S(1)} %add.193.rest_1_) | copy-start | bytes 245764
  53.3 14.8 %collective-permute-start.13 = (bf16[2,160,128]{2,1,0:T(8,128)(2,1)S(1)}, bf16[2,160,128]{2,1,0:T(8,128)(2,1)S(1)}, u32[]{:S(2)}, u32[]{:S(2)}) collective-permute-start(bf16[2,160,128]{2,1,0:T(8,128)(2,1)S(1)} %add.193.rest_1_), channel_id=1, source_target_pairs={{0,24},{8,16},{16,8},{24,0},{1,25},{9,17},{17,9},{25,1},{2,26},{10... | collective-permute-start | bytes 245768 | tf_op jit(solution)/shard_map/ppermute | solution.py:211
  53.4 15.7 %collective-permute-start.11 = (bf16[2,160,128]{2,1,0:T(8,128)(2,1)S(1)}, bf16[2,160,128]{2,1,0:T(8,128)(2,1)S(1)}, u32[]{:S(2)}, u32[]{:S(2)}) collective-permute-start(bf16[2,160,128]{2,1,0:T(8,128)(2,1)S(1)} %add.193.rest_1_), channel_id=1, source_target_pairs={{0,16},{8,24},{16,0},{24,8},{1,17},{9,25},{17,1},{25,9},{2,18},{10... | collective-permute-start | bytes 245768 | tf_op jit(solution)/shard_map/ppermute | solution.py:211
  55.6 13.5 %collective-permute-start.9 = (bf16[2,160,128]{2,1,0:T(8,128)(2,1)S(1)}, bf16[2,160,128]{2,1,0:T(8,128)(2,1)S(1)}, u32[]{:S(2)}, u32[]{:S(2)}) collective-permute-start(bf16[2,160,128]{2,1,0:T(8,128)(2,1)S(1)} %add.193.rest_1_), channel_id=1, source_target_pairs={{0,8},{8,0},{16,24},{24,16},{1,9},{9,1},{17,25},{25,17},{2,10},{10... | collective-permute-start | bytes 245768 | tf_op jit(solution)/shard_map/ppermute | solution.py:211
  65.8 29.9 %copy-start.15 = (s32[64,256]{1,0:T(8,128)S(1)}, s32[64,256]{1,0:T(8,128)}, u32[]{:S(2)}) copy-start(s32[64,256]{1,0:T(8,128)} %refs_0_.1) | copy-start | bytes 196612
  66.8 10.1 %copy-start.9 = (bf16[2,352,128]{2,1,0:T(8,128)(2,1)}, bf16[2,352,128]{2,1,0:T(8,128)(2,1)S(1)}, u32[]{:S(2)}) copy-start(bf16[2,352,128]{2,1,0:T(8,128)(2,1)S(1)} %add_add_fusion.rest_0_) | copy-start | bytes 540676
  66.8 6.9 %collective-permute-start.12 = (bf16[2,352,128]{2,1,0:T(8,128)(2,1)S(1)}, bf16[2,352,128]{2,1,0:T(8,128)(2,1)S(1)}, u32[]{:S(2)}, u32[]{:S(2)}) collective-permute-start(bf16[2,352,128]{2,1,0:T(8,128)(2,1)S(1)} %add_add_fusion.rest_0_), channel_id=1, source_target_pairs={{0,24},{8,16},{16,8},{24,0},{1,25},{9,17},{17,9},{25,1},{2,26},{10... | collective-permute-start | bytes 540680 | tf_op jit(solution)/shard_map/ppermute | solution.py:211
  66.9 10.0 %collective-permute-start.10 = (bf16[2,352,128]{2,1,0:T(8,128)(2,1)S(1)}, bf16[2,352,128]{2,1,0:T(8,128)(2,1)S(1)}, u32[]{:S(2)}, u32[]{:S(2)}) collective-permute-start(bf16[2,352,128]{2,1,0:T(8,128)(2,1)S(1)} %add_add_fusion.rest_0_), channel_id=1, source_target_pairs={{0,16},{8,24},{16,0},{24,8},{1,17},{9,25},{17,1},{25,9},{2,18},{10... | collective-permute-start | bytes 540680 | tf_op jit(solution)/shard_map/ppermute | solution.py:211
  68.1 8.9 %collective-permute-start.8 = (bf16[2,352,128]{2,1,0:T(8,128)(2,1)S(1)}, bf16[2,352,128]{2,1,0:T(8,128)(2,1)S(1)}, u32[]{:S(2)}, u32[]{:S(2)}) collective-permute-start(bf16[2,352,128]{2,1,0:T(8,128)(2,1)S(1)} %add_add_fusion.rest_0_), channel_id=1, source_target_pairs={{0,8},{8,0},{16,24},{24,16},{1,9},{9,1},{17,25},{25,17},{2,10},{10... | collective-permute-start | bytes 540680 | tf_op jit(solution)/shard_map/ppermute | solution.py:211
  69.1 43.6 %copy-start.6 = (f32[4,32,128]{2,1,0:T(8,128)}, f32[4,32,128]{2,1,0:T(8,128)S(1)}, u32[]{:S(2)}) copy-start(f32[4,32,128]{2,1,0:T(8,128)S(1)} %get-tuple-element.251.cos_ref) | copy-start | bytes 196612
  85.2 4.3 %collective-permute-start.14 = (f32[32,384]{1,0:T(8,128)}, f32[32,384]{1,0:T(8,128)S(1)}, u32[]{:S(2)}, u32[]{:S(2)}) collective-permute-start(f32[32,384]{1,0:T(8,128)} %logits.1), channel_id=1, source_target_pairs={{0,1},{1,0},{2,3},{3,2},{4,5},{5,4},{6,7},{7,6},{8,9},{9,8},{10,11... | collective-permute-start | bytes 147464 | tf_op jit(solution)/shard_map/ppermute | solution.py:831
  90.3 22.4 %copy-start.14 = (f32[32,384]{1,0:T(8,128)}, f32[32,384]{1,0:T(8,128)S(1)}, u32[]{:S(2)}) copy-start(f32[32,384]{1,0:T(8,128)S(1)} %add.194.rest_0_) | copy-start | bytes 147460
  90.3 11.5 %collective-permute-start.17 = (f32[32,384]{1,0:T(8,128)S(1)}, f32[32,384]{1,0:T(8,128)S(1)}, u32[]{:S(2)}, u32[]{:S(2)}) collective-permute-start(f32[32,384]{1,0:T(8,128)S(1)} %add.194.rest_0_), channel_id=1, source_target_pairs={{0,6},{1,7},{2,0},{3,1},{4,2},{5,3},{6,4},{7,5},{8,14},{9,15},{10,... | collective-permute-start | bytes 147464 | tf_op jit(solution)/shard_map/ppermute | solution.py:833
  90.4 11.5 %collective-permute-start.16 = (f32[32,384]{1,0:T(8,128)S(1)}, f32[32,384]{1,0:T(8,128)S(1)}, u32[]{:S(2)}, u32[]{:S(2)}) collective-permute-start(f32[32,384]{1,0:T(8,128)S(1)} %add.194.rest_0_), channel_id=1, source_target_pairs={{0,4},{1,5},{2,6},{3,7},{4,0},{5,1},{6,2},{7,3},{8,12},{9,13},{10,... | collective-permute-start | bytes 147464 | tf_op jit(solution)/shard_map/ppermute | solution.py:833
  91.5 10.4 %collective-permute-start.15 = (f32[32,384]{1,0:T(8,128)S(1)}, f32[32,384]{1,0:T(8,128)S(1)}, u32[]{:S(2)}, u32[]{:S(2)}) collective-permute-start(f32[32,384]{1,0:T(8,128)S(1)} %add.194.rest_0_), channel_id=1, source_target_pairs={{0,2},{1,3},{2,4},{3,5},{4,6},{5,7},{6,0},{7,1},{8,10},{9,11},{10,... | collective-permute-start | bytes 147464 | tf_op jit(solution)/shard_map/ppermute | solution.py:833
  94.1 18.6 %copy-start.45 = (s32[1,384]{1,0:T(1,128)}, s32[1,384]{1,0:T(1,128)S(1)}, u32[]{:S(2)}) copy-start(s32[1,384]{1,0:T(1,128)S(1)} %broadcast_in_dim.13.cnt_ref) | copy-start | bytes 4612
  101.8 10.8 %copy-start.28 = (f32[32,384]{1,0:T(8,128)}, f32[32,384]{1,0:T(8,128)S(1)}, u32[]{:S(2)}) copy-start(f32[32,384]{1,0:T(8,128)S(1)} %collective-permute-done.17.rest_3_) | copy-start | bytes 147460
  101.9 10.8 %copy-start.29 = (f32[32,384]{1,0:T(8,128)}, f32[32,384]{1,0:T(8,128)S(1)}, u32[]{:S(2)}) copy-start(f32[32,384]{1,0:T(8,128)S(1)} %collective-permute-done.16.rest_2_) | copy-start | bytes 147460
  101.9 10.8 %copy-start.30 = (f32[32,384]{1,0:T(8,128)}, f32[32,384]{1,0:T(8,128)S(1)}, u32[]{:S(2)}) copy-start(f32[32,384]{1,0:T(8,128)S(1)} %collective-permute-done.15.rest_1_) | copy-start | bytes 147460
  109.2 37.4 %copy-start.27 = (bf16[2,1,608,128]{3,2,1,0:T(8,128)(2,1)S(1)}, bf16[2,1,608,128]{3,2,1,0:T(8,128)(2,1)}, u32[]{:S(2)}) copy-start(bf16[2,1,608,128]{3,2,1,0:T(8,128)(2,1)} %get-tuple-element.146) | copy-start | bytes 933892
  109.2 1.8 collective-permute-start.18
  112.6 25.4 %copy-start.12 = (bf16[1,608,128]{2,1,0:T(8,128)(2,1)S(1)}, bf16[1,608,128]{2,1,0:T(8,128)(2,1)}, u32[]{:S(2)}) copy-start(bf16[1,608,128]{2,1,0:T(8,128)(2,1)} %fusion.23.after) | copy-start | bytes 466948
  122.0 76.5 %copy-start.2 = (bf16[32,384,128]{2,1,0:T(8,128)(2,1)S(1)}, bf16[32,384,128]{2,1,0:T(8,128)(2,1)}, u32[]{:S(2)}) copy-start(bf16[32,384,128]{2,1,0:T(8,128)(2,1)} %get-tuple-element.127.sq_ref) | copy-start | bytes 9437188
  122.0 2.3 %collective-permute-start.19 = (bf16[2,2,608,128]{3,2,1,0:T(8,128)(2,1)}, bf16[2,2,608,128]{3,2,1,0:T(8,128)(2,1)S(1)}, u32[]{:S(2)}, u32[]{:S(2)}) collective-permute-start(bf16[2,2,608,128]{3,2,1,0:T(8,128)(2,1)} %get-tuple-element.149), channel_id=1, source_target_pairs={{0,8},{8,0},{16,24},{24,16},{1,9},{9,1},{17,25},{25,17},{2,10},{10... | collective-permute-start | bytes 1867784 | tf_op jit(solution)/shard_map/ppermute | solution.py:520
  125.4 9.5 %collective-permute-start.20 = (bf16[2,608,128]{2,1,0:T(8,128)(2,1)S(1)}, bf16[2,608,128]{2,1,0:T(8,128)(2,1)S(1)}, u32[]{:S(2)}, u32[]{:S(2)}) collective-permute-start(bf16[2,608,128]{2,1,0:T(8,128)(2,1)S(1)} %fusion.19), channel_id=1, source_target_pairs={{0,16},{8,24},{16,0},{24,8},{1,17},{9,25},{17,1},{25,9},{2,18},{10... | collective-permute-start | bytes 933896 | tf_op jit(solution)/shard_map/ppermute | solution.py:525
  135.9 54.5 %copy-start.5 = (bf16[2,608,128]{2,1,0:T(8,128)(2,1)}, bf16[2,608,128]{2,1,0:T(8,128)(2,1)S(1)}, u32[]{:S(2)}) copy-start(bf16[2,608,128]{2,1,0:T(8,128)(2,1)S(1)} %fusion.17.rest_0_) | copy-start | bytes 933892
  136.0 8.6 %collective-permute-start.24 = (bf16[2,608,128]{2,1,0:T(8,128)(2,1)S(1)}, bf16[2,608,128]{2,1,0:T(8,128)(2,1)S(1)}, u32[]{:S(2)}, u32[]{:S(2)}) collective-permute-start(bf16[2,608,128]{2,1,0:T(8,128)(2,1)S(1)} %fusion.17.rest_0_), channel_id=1, source_target_pairs={{2,0},{4,2},{6,4},{7,6},{5,7},{3,5},{1,3},{0,1},{10,8},{12,10},{14... | collective-permute-start | bytes 933896 | tf_op jit(solution)/shard_map/ppermute | solution.py:222
  136.1 9.1 %collective-permute-start.21 = (bf16[2,608,128]{2,1,0:T(8,128)(2,1)S(1)}, bf16[2,608,128]{2,1,0:T(8,128)(2,1)S(1)}, u32[]{:S(2)}, u32[]{:S(2)}) collective-permute-start(bf16[2,608,128]{2,1,0:T(8,128)(2,1)S(1)} %fusion.17.rest_0_), channel_id=1, source_target_pairs={{0,2},{2,4},{4,6},{6,7},{7,5},{5,3},{3,1},{1,0},{8,10},{10,12},{12... | collective-permute-start | bytes 933896 | tf_op jit(solution)/shard_map/ppermute | solution.py:221
  138.0 8.6 %collective-permute-start.29 = (bf16[1,608,128]{2,1,0:T(8,128)(2,1)S(1)}, bf16[1,608,128]{2,1,0:T(8,128)(2,1)S(1)}, u32[]{:S(2)}, u32[]{:S(2)}) collective-permute-start(bf16[1,608,128]{2,1,0:T(8,128)(2,1)S(1)} %copy-done.12), channel_id=1, source_target_pairs={{0,16},{8,24},{16,0},{24,8},{1,17},{9,25},{17,1},{25,9},{2,18},{10... | collective-permute-start | bytes 466952 | tf_op jit(solution)/shard_map/ppermute | solution.py:525
  144.6 10.3 %collective-permute-start.25 = (bf16[2,608,128]{2,1,0:T(8,128)(2,1)S(1)}, bf16[2,608,128]{2,1,0:T(8,128)(2,1)S(1)}, u32[]{:S(2)}, u32[]{:S(2)}) collective-permute-start(bf16[2,608,128]{2,1,0:T(8,128)(2,1)S(1)} %collective-permute-done.24.rest_2_), channel_id=1, source_target_pairs={{2,0},{4,2},{6,4},{7,6},{5,7},{3,5},{1,3},{0,1},{10,8},{12,10},{14... | collective-permute-start | bytes 933896 | tf_op jit(solution)/shard_map/ppermute | solution.py:222
  145.3 9.9 %copy-start.24 = (bf16[2,608,128]{2,1,0:T(8,128)(2,1)}, bf16[2,608,128]{2,1,0:T(8,128)(2,1)S(1)}, u32[]{:S(2)}) copy-start(bf16[2,608,128]{2,1,0:T(8,128)(2,1)S(1)} %collective-permute-done.21.rest_1_) | copy-start | bytes 933892
  145.3 10.3 %collective-permute-start.22 = (bf16[2,608,128]{2,1,0:T(8,128)(2,1)S(1)}, bf16[2,608,128]{2,1,0:T(8,128)(2,1)S(1)}, u32[]{:S(2)}, u32[]{:S(2)}) collective-permute-start(bf16[2,608,128]{2,1,0:T(8,128)(2,1)S(1)} %collective-permute-done.21.rest_1_), channel_id=1, source_target_pairs={{0,2},{2,4},{4,6},{6,7},{7,5},{5,3},{3,1},{1,0},{8,10},{10,12},{12... | collective-permute-start | bytes 933896 | tf_op jit(solution)/shard_map/ppermute | solution.py:221
  146.7 24.6 %copy-start.13 = (bf16[1,608,128]{2,1,0:T(8,128)(2,1)}, bf16[1,608,128]{2,1,0:T(8,128)(2,1)S(1)}, u32[]{:S(2)}) copy-start(bf16[1,608,128]{2,1,0:T(8,128)(2,1)S(1)} %fusion.20.rest_0_) | copy-start | bytes 466948
  146.7 11.5 %collective-permute-start.31 = (bf16[1,608,128]{2,1,0:T(8,128)(2,1)S(1)}, bf16[1,608,128]{2,1,0:T(8,128)(2,1)S(1)}, u32[]{:S(2)}, u32[]{:S(2)}) collective-permute-start(bf16[1,608,128]{2,1,0:T(8,128)(2,1)S(1)} %fusion.20.rest_0_), channel_id=1, source_target_pairs={{2,0},{4,2},{6,4},{7,6},{5,7},{3,5},{1,3},{0,1},{10,8},{12,10},{14... | collective-permute-start | bytes 466952 | tf_op jit(solution)/shard_map/ppermute | solution.py:222
  147.5 11.4 %collective-permute-start.30 = (bf16[1,608,128]{2,1,0:T(8,128)(2,1)S(1)}, bf16[1,608,128]{2,1,0:T(8,128)(2,1)S(1)}, u32[]{:S(2)}, u32[]{:S(2)}) collective-permute-start(bf16[1,608,128]{2,1,0:T(8,128)(2,1)S(1)} %fusion.20.rest_0_), channel_id=1, source_target_pairs={{0,2},{2,4},{4,6},{6,7},{7,5},{5,3},{3,1},{1,0},{8,10},{10,12},{12... | collective-permute-start | bytes 466952 | tf_op jit(solution)/shard_map/ppermute | solution.py:221
  154.9 21.1 %copy-start.25 = (bf16[2,608,128]{2,1,0:T(8,128)(2,1)}, bf16[2,608,128]{2,1,0:T(8,128)(2,1)S(1)}, u32[]{:S(2)}) copy-start(bf16[2,608,128]{2,1,0:T(8,128)(2,1)S(1)} %collective-permute-done.25.rest_4_) | copy-start | bytes 933892
  154.9 12.9 %collective-permute-start.26 = (bf16[2,608,128]{2,1,0:T(8,128)(2,1)S(1)}, bf16[2,608,128]{2,1,0:T(8,128)(2,1)S(1)}, u32[]{:S(2)}, u32[]{:S(2)}) collective-permute-start(bf16[2,608,128]{2,1,0:T(8,128)(2,1)S(1)} %collective-permute-done.25.rest_4_), channel_id=1, source_target_pairs={{2,0},{4,2},{6,4},{7,6},{5,7},{3,5},{1,3},{0,1},{10,8},{12,10},{14... | collective-permute-start | bytes 933896 | tf_op jit(solution)/shard_map/ppermute | solution.py:222
  155.6 20.4 %copy-start.26 = (bf16[2,608,128]{2,1,0:T(8,128)(2,1)}, bf16[2,608,128]{2,1,0:T(8,128)(2,1)S(1)}, u32[]{:S(2)}) copy-start(bf16[2,608,128]{2,1,0:T(8,128)(2,1)S(1)} %collective-permute-done.22.rest_3_) | copy-start | bytes 933892
  155.6 14.4 %collective-permute-start.23 = (bf16[2,608,128]{2,1,0:T(8,128)(2,1)S(1)}, bf16[2,608,128]{2,1,0:T(8,128)(2,1)S(1)}, u32[]{:S(2)}, u32[]{:S(2)}) collective-permute-start(bf16[2,608,128]{2,1,0:T(8,128)(2,1)S(1)} %collective-permute-done.22.rest_3_), channel_id=1, source_target_pairs={{0,2},{2,4},{4,6},{6,7},{7,5},{5,3},{3,1},{1,0},{8,10},{10,12},{12... | collective-permute-start | bytes 933896 | tf_op jit(solution)/shard_map/ppermute | solution.py:221
  158.2 17.8 %copy-start.37 = (bf16[1,608,128]{2,1,0:T(8,128)(2,1)}, bf16[1,608,128]{2,1,0:T(8,128)(2,1)S(1)}, u32[]{:S(2)}) copy-start(bf16[1,608,128]{2,1,0:T(8,128)(2,1)S(1)} %collective-permute-done.31.rest_2_) | copy-start | bytes 466948
  158.2 7.5 %collective-permute-start.33 = (bf16[1,608,128]{2,1,0:T(8,128)(2,1)S(1)}, bf16[1,608,128]{2,1,0:T(8,128)(2,1)S(1)}, u32[]{:S(2)}, u32[]{:S(2)}) collective-permute-start(bf16[1,608,128]{2,1,0:T(8,128)(2,1)S(1)} %collective-permute-done.31.rest_2_), channel_id=1, source_target_pairs={{2,0},{4,2},{6,4},{7,6},{5,7},{3,5},{1,3},{0,1},{10,8},{12,10},{14... | collective-permute-start | bytes 466952 | tf_op jit(solution)/shard_map/ppermute | solution.py:222
  158.9 17.1 %copy-start.38 = (bf16[1,608,128]{2,1,0:T(8,128)(2,1)}, bf16[1,608,128]{2,1,0:T(8,128)(2,1)S(1)}, u32[]{:S(2)}) copy-start(bf16[1,608,128]{2,1,0:T(8,128)(2,1)S(1)} %collective-permute-done.30.rest_1_) | copy-start | bytes 466948
  158.9 7.5 %collective-permute-start.32 = (bf16[1,608,128]{2,1,0:T(8,128)(2,1)S(1)}, bf16[1,608,128]{2,1,0:T(8,128)(2,1)S(1)}, u32[]{:S(2)}, u32[]{:S(2)}) collective-permute-start(bf16[1,608,128]{2,1,0:T(8,128)(2,1)S(1)} %collective-permute-done.30.rest_1_), channel_id=1, source_target_pairs={{0,2},{2,4},{4,6},{6,7},{7,5},{5,3},{3,1},{1,0},{8,10},{10,12},{12... | collective-permute-start | bytes 466952 | tf_op jit(solution)/shard_map/ppermute | solution.py:221
  165.7 10.2 %copy-start.39 = (bf16[1,608,128]{2,1,0:T(8,128)(2,1)}, bf16[1,608,128]{2,1,0:T(8,128)(2,1)S(1)}, u32[]{:S(2)}) copy-start(bf16[1,608,128]{2,1,0:T(8,128)(2,1)S(1)} %collective-permute-done.33.rest_4_) | copy-start | bytes 466948
  165.7 6.9 %collective-permute-start.35 = (bf16[1,608,128]{2,1,0:T(8,128)(2,1)S(1)}, bf16[1,608,128]{2,1,0:T(8,128)(2,1)S(1)}, u32[]{:S(2)}, u32[]{:S(2)}) collective-permute-start(bf16[1,608,128]{2,1,0:T(8,128)(2,1)S(1)} %collective-permute-done.33.rest_4_), channel_id=1, source_target_pairs={{2,0},{4,2},{6,4},{7,6},{5,7},{3,5},{1,3},{0,1},{10,8},{12,10},{14... | collective-permute-start | bytes 466952 | tf_op jit(solution)/shard_map/ppermute | solution.py:222
  166.4 8.2 %collective-permute-start.34 = (bf16[1,608,128]{2,1,0:T(8,128)(2,1)S(1)}, bf16[1,608,128]{2,1,0:T(8,128)(2,1)S(1)}, u32[]{:S(2)}, u32[]{:S(2)}) collective-permute-start(bf16[1,608,128]{2,1,0:T(8,128)(2,1)S(1)} %collective-permute-done.32.rest_3_), channel_id=1, source_target_pairs={{0,2},{2,4},{4,6},{6,7},{7,5},{5,3},{3,1},{1,0},{8,10},{10,12},{12... | collective-permute-start | bytes 466952 | tf_op jit(solution)/shard_map/ppermute | solution.py:221
  169.2 29.3 %collective-permute-start.28 = (bf16[2,304,128]{2,1,0:T(8,128)(2,1)}, bf16[2,304,128]{2,1,0:T(8,128)(2,1)}, u32[]{:S(2)}, u32[]{:S(2)}) collective-permute-start(bf16[2,304,128]{2,1,0:T(8,128)(2,1)} %slice.80), channel_id=1, source_target_pairs={{2,0},{4,2},{6,4},{7,6},{5,7},{3,5},{1,3},{0,1},{10,8},{12,10},{14... | collective-permute-start | bytes 466952 | tf_op jit(solution)/shard_map/ppermute | solution.py:227
  171.3 27.2 %collective-permute-start.27 = (bf16[2,304,128]{2,1,0:T(8,128)(2,1)}, bf16[2,304,128]{2,1,0:T(8,128)(2,1)}, u32[]{:S(2)}, u32[]{:S(2)}) collective-permute-start(bf16[2,304,128]{2,1,0:T(8,128)(2,1)} %slice.79), channel_id=1, source_target_pairs={{0,2},{2,4},{4,6},{6,7},{7,5},{5,3},{3,1},{1,0},{8,10},{10,12},{12... | collective-permute-start | bytes 466952 | tf_op jit(solution)/shard_map/ppermute | solution.py:226
  173.9 5.2 %collective-permute-start.37 = (bf16[1,304,128]{2,1,0:T(8,128)(2,1)}, bf16[1,304,128]{2,1,0:T(8,128)(2,1)}, u32[]{:S(2)}, u32[]{:S(2)}) collective-permute-start(bf16[1,304,128]{2,1,0:T(8,128)(2,1)} %slice.83), channel_id=1, source_target_pairs={{2,0},{4,2},{6,4},{7,6},{5,7},{3,5},{1,3},{0,1},{10,8},{12,10},{14... | collective-permute-start | bytes 233480 | tf_op jit(solution)/shard_map/ppermute | solution.py:227
  176.0 4.8 %collective-permute-start.36 = (bf16[1,304,128]{2,1,0:T(8,128)(2,1)}, bf16[1,304,128]{2,1,0:T(8,128)(2,1)}, u32[]{:S(2)}, u32[]{:S(2)}) collective-permute-start(bf16[1,304,128]{2,1,0:T(8,128)(2,1)} %slice.82), channel_id=1, source_target_pairs={{0,2},{2,4},{4,6},{6,7},{7,5},{5,3},{3,1},{1,0},{8,10},{10,12},{12... | collective-permute-start | bytes 233480 | tf_op jit(solution)/shard_map/ppermute | solution.py:226
  (17 other events, 61.4 us)

commit v5 on v4

--- a/solution.py
+++ b/solution.py
@@ -74,7 +74,7 @@
     vol, pair, idx_v, flag_v, idx_s, flag_s, w_s, sem = refs[-8:]
     parts_b = refs[6:-8]
     slab = lax.axis_index("vol")
-    share = idx_v.shape[0]
+    share = idx_v.shape[0] // 2
     first = lax.axis_index("img") * share
     height = planes_here * ROWS
     count_z = keep_a.shape[0]
@@ -82,11 +82,21 @@
     groups_b = parts_b[0].shape[2] // 16
     load = pltpu.make_async_copy(vol_hbm, vol.at[:, :height, :], sem.at[0])
     load.start()
-    load_w = pltpu.make_async_copy(weight_hbm.at[pl.ds(first, share), :], w_s, sem.at[1])
-    load_w.start()
+    loads_w = [
+        pltpu.make_async_copy(
+            weight_hbm.at[pl.ds(first, share), pl.ds(h * COLS, COLS)],
+            w_s.at[pl.ds(h * share, share), :],
+            sem.at[4 + h],
+        )
+        for h in range(2)
+    ]
+    for copy in loads_w:
+        copy.start()
     local = plane_ref[pl.ds(first, share), :] - slab * planes_here
     owned = (local >= 0) & (local < planes_here)
-    idx_v[...] = jnp.where(owned, local * ROWS + line_ref[pl.ds(first, share), :], height)
+    idx = jnp.where(owned, local * ROWS + line_ref[pl.ds(first, share), :], height)
+    for h in range(2):
+        idx_v[h * share : (h + 1) * share, :] = idx[:, h * COLS : (h + 1) * COLS]
     eights = (
         lax.broadcasted_iota(jnp.int32, (ROWS, COLS), 0) >> 3
         == lax.broadcasted_iota(jnp.int32, (ROWS, COLS), 1)
@@ -103,7 +113,8 @@
         ref[...] = jnp.zeros_like(ref)
     to_idx.wait()
     to_flag.wait()
-    load_w.wait()
+    for copy in loads_w:
+        copy.wait()
     load.wait()
     lower_row = lax.broadcasted_iota(jnp.int32, (2, COLS), 0) == 0
     shift = rows.bit_length() - 1
@@ -119,10 +130,11 @@
 
             @pl.when(hits > 0)
             def _():
+                spot = [(k + share * (r >> 7), r & (COLS - 1)) for k, r in at]
                 for u in range(16):
-                    k, r = at[u // 8]
-                    i = idx_s[k, r + u % 8]
-                    w = w_s[k, r + u % 8]
+                    line, lane = spot[u // 8]
+                    i = idx_s[line, lane + u % 8]
+                    w = w_s[line, lane + u % 8]
                     both = jnp.where(lower_row, w, 1.0 - w)
                     for j in range(2):
                         pair[j, 2 * u : 2 * u + 2, :] = both * vol[j, pl.ds(i, 2), :]
@@ -156,12 +168,12 @@
         scratch_shapes=[
             pltpu.VMEM((2, planes_here * ROWS + 8, COLS), F32),
             pltpu.VMEM((2, 32, COLS), F32),
-            pltpu.VMEM((share, ROWS), jnp.int32),
+            pltpu.VMEM((2 * share, COLS), jnp.int32),
             pltpu.VMEM((share, COLS), jnp.int32),
-            pltpu.SMEM((share, ROWS), jnp.int32),
+            pltpu.SMEM((2 * share, COLS), jnp.int32),
             pltpu.SMEM((share, COLS), jnp.int32),
-            pltpu.SMEM((share, ROWS), F32),
-            pltpu.SemaphoreType.DMA((4,)),
+            pltpu.SMEM((2 * share, COLS), F32),
+            pltpu.SemaphoreType.DMA((6,)),
         ],
         compiler_params=pltpu.CompilerParams(vmem_limit_bytes=VMEM_LIMIT),
         cost_estimate=cost(11),
@@ -221,11 +233,32 @@
         one = lax.ppermute(one, "vol", ahead)
         two = lax.ppermute(two, "vol", back)
         pieces += [one, two]
-    half = x.shape[1] // 2
-    return pieces + [
-        lax.ppermute(one[:, :half], "vol", ahead),
-        lax.ppermute(two[:, half:], "vol", back),
-    ]
+
+    def farthest(after):
+        half = x.shape[1] // 2
+        low, high = halves(one, two, after)
+        return [lax.ppermute(low, "vol", ahead), lax.ppermute(high, "vol", back)]
+
+    return pieces, farthest
+
+
+def halves_kernel(one, two, after, low, high):
+    half = low.shape[1]
+    low[...] = one[:, :half]
+    high[...] = two[:, half:]
+
+
+def halves(one, two, after):
+    shape = jax.ShapeDtypeStruct((one.shape[0], one.shape[1] // 2, COLS), BF16)
+    return pl.pallas_call(
+        halves_kernel,
+        out_shape=[shape] * 2,
+        in_specs=[vmem(), vmem(), hbm()],
+        out_specs=[vmem()] * 2,
+        compiler_params=pltpu.CompilerParams(vmem_limit_bytes=VMEM_LIMIT),
+        cost_estimate=cost(1),
+        name="halves",
+    )(one, two, after)
 
 
 def weigh_kernel(img_ref, sa_ref, ca_ref, sx_ref, cx_ref, nw_ref, wt_ref, sq_ref, buf):
@@ -287,7 +320,7 @@
 
 
 def logits_kernel(wt_ref, sq_ref, cos_ref, sin_ref, cand_ref, *rest):
-    sl_refs = rest[:-4]
+    sl_refs = rest[1:-4]
     out_ref, part, acc, quad = rest[-4:]
     step = pl.program_id(0)
     groups = len(sl_refs) // 2
@@ -342,7 +375,7 @@
                 out_ref[t * LMAX + l : t * LMAX + l + 1, :] = jnp.sum(pick, axis=0, keepdims=True)
 
 
-def candidate_logits(slices, weighted, squared, cosine, sine, cand):
+def candidate_logits(after, slices, weighted, squared, cosine, sine, cand):
     rows, count = squared.shape[:2]
     inner = 8
     return pl.pallas_call(
@@ -356,6 +389,7 @@
             pl.BlockSpec((TRANS, inner, COLS), lambda s: (0, s, 0)),
             pl.BlockSpec((LMAX, count), lambda s: (0, 0)),
         ]
+        + [hbm()]
         + [pl.BlockSpec(x.shape, lambda s: (0, 0, 0)) for x in slices],
         out_specs=pl.BlockSpec((TRANS * LMAX, count), lambda s: (0, 0)),
         scratch_shapes=[
@@ -366,7 +400,7 @@
         compiler_params=params(1),
         cost_estimate=cost(8),
         name="logits",
-    )(weighted, squared, cosine, sine, cand, *slices)
+    )(weighted, squared, cosine, sine, cand, after, *slices)
 
 
 def posterior_rows(logits, counts):
@@ -401,11 +435,11 @@
         lax.fori_loop(0, (jnp.minimum(len_s[q, 0], cap) + 31) // 32, turn, 0)
 
 
-def spread_kernel(src_s, len_s, cand_ref, cnt_ref, sq_ref, *rest):
+def project_kernel(src_s, len_s, cand_ref, cnt_ref, wt_ref, sq_ref, cos_ref, sin_ref, *rest):
     lg_refs = rest[:-6]
     keep_ref, send_ref, post, post_sum, num, pick = rest[-6:]
     step = pl.program_id(0)
-    inner = sq_ref.shape[0]
+    inner = wt_ref.shape[0]
 
     @pl.when(step == 0)
     def _():
@@ -424,22 +458,8 @@
         post_sum[K:, :] = (total - high.astype(F32)).astype(BF16)
 
     for u in range(inner):
+        y = jnp.dot(post[...], wt_ref[u], preferred_element_type=F32)
         d = jnp.dot(post_sum[...], sq_ref[u], preferred_element_type=F32)
-        base = pl.multiple_of((step * inner + u) * K, K)
-        num[0, pl.ds(base, K), :] = d[:K] + d[K:]
-
-    @pl.when(step == pl.num_programs(0) - 1)
-    def _():
-        list_rows(num, src_s, len_s, (keep_ref, send_ref), pick)
-
-
-def project_kernel(
-    src_s, len_s, post, wt_ref, cos_ref, sin_ref, after, keep_ref, send_ref, num, pick
-):
-    step = pl.program_id(0)
-    inner = wt_ref.shape[0]
-    for u in range(inner):
-        y = jnp.dot(post[...], wt_ref[u], preferred_element_type=F32)
         re = jnp.zeros((K, COLS), F32)
         im = jnp.zeros((K, COLS), F32)
         for t in range(TRANS):
@@ -452,46 +472,17 @@
         base = pl.multiple_of((step * inner + u) * K, K)
         num[0, pl.ds(base, K), :] = re
         num[1, pl.ds(base, K), :] = im
+        num[2, pl.ds(base, K), :] = d[:K] + d[K:]
 
     @pl.when(step == pl.num_programs(0) - 1)
     def _():
         list_rows(num, src_s, len_s, (keep_ref, send_ref), pick)
 
 
-def spread(src, lengths, n_img, logits, cand, counts, squared, cap):
+def project(src, lengths, n_img, logits, cand, counts, weighted, squared, cosine, sine, cap):
     rows, count = squared.shape[:2]
     inner = 8
-    shape = (n_img // 2, 1, cap, COLS)
-    return pl.pallas_call(
-        spread_kernel,
-        grid=(rows // inner,),
-        out_shape=[jax.ShapeDtypeStruct(shape, BF16)] * 2
-        + [jax.ShapeDtypeStruct((TRANS * K, count), BF16)],
-        in_specs=[
-            smem(),
-            smem(),
-            pl.BlockSpec((LMAX, count), lambda s: (0, 0)),
-            pl.BlockSpec((1, count), lambda s: (0, 0)),
-            pl.BlockSpec((inner, count, COLS), lambda s: (s, 0, 0)),
-        ]
-        + [pl.BlockSpec((TRANS * LMAX, count), lambda s: (0, 0)) for _ in logits],
-        out_specs=[pl.BlockSpec(shape, lambda s: (0, 0, 0, 0))] * 2
-        + [pl.BlockSpec((TRANS * K, count), lambda s: (0, 0))],
-        scratch_shapes=[
-            pltpu.VMEM((2 * K, count), BF16),
-            pltpu.VMEM((1, rows * K, COLS), F32),
-            pltpu.VMEM((1, 32, COLS), F32),
-        ],
-        compiler_params=params(1),
-        cost_estimate=cost(8),
-        name="spread",
-    )(src, lengths, cand, counts, squared, *logits)
-
-
-def project(src, lengths, n_img, post, weighted, cosine, sine, after, cap):
-    rows, count = weighted.shape[:2]
-    inner = 8
-    shape = (n_img // 2, 2, cap, COLS)
+    shape = (n_img // 2, 3, cap, COLS)
     return pl.pallas_call(
         project_kernel,
         grid=(rows // inner,),
@@ -499,31 +490,32 @@
         in_specs=[
             smem(),
             smem(),
-            pl.BlockSpec((TRANS * K, count), lambda s: (0, 0)),
+            pl.BlockSpec((LMAX, count), lambda s: (0, 0)),
+            pl.BlockSpec((1, count), lambda s: (0, 0)),
             pl.BlockSpec((inner, count, 2 * COLS), lambda s: (s, 0, 0)),
+            pl.BlockSpec((inner, count, COLS), lambda s: (s, 0, 0)),
             pl.BlockSpec((TRANS, inner, COLS), lambda s: (0, s, 0)),
             pl.BlockSpec((TRANS, inner, COLS), lambda s: (0, s, 0)),
-            hbm(),
-        ],
+        ]
+        + [pl.BlockSpec((TRANS * LMAX, count), lambda s: (0, 0)) for _ in logits],
         out_specs=[pl.BlockSpec(shape, lambda s: (0, 0, 0, 0))] * 2,
         scratch_shapes=[
-            pltpu.VMEM((2, rows * K, COLS), F32),
-            pltpu.VMEM((2, 32, COLS), F32),
+            pltpu.VMEM((TRANS * K, count), BF16),
+            pltpu.VMEM((2 * K, count), BF16),
+            pltpu.VMEM((3, rows * K, COLS), F32),
+            pltpu.VMEM((3, 32, COLS), F32),
         ],
         compiler_params=params(1),
-        cost_estimate=cost(9),
+        cost_estimate=cost(12),
         name="project",
-    )(src, lengths, post, weighted, cosine, sine, after)
-
-
-def add_cores(keep, send, n_img):
+    )(src, lengths, cand, counts, weighted, squared, cosine, sine, *logits)
+
+
+def to_member(keep, send, n_img):
     got = lax.ppermute(send, "img", flip(n_img, 1))
-    return [(keep[m].astype(F32) + got[m].astype(F32)).astype(BF16) for m in range(n_img // 2)]
-
-
-def add_chips(summed, n_img):
+    summed = [keep[m] + got[m] for m in range(n_img // 2)]
     moved = [lax.ppermute(summed[m], "img", flip(n_img, 2 * m)) for m in range(1, n_img // 2)]
-    return sum([x.astype(F32) for x in moved], summed[0].astype(F32)).astype(BF16)
+    return sum(moved, summed[0])
 
 
 HEAD = 8
@@ -536,18 +528,19 @@
 def insert_kernel(start, count, has_acc, mode, len_s, code_s, wgt_s, *rest):
     pieces = rest[:count]
     rest = rest[count:]
-    out_ref, acc, buf = rest[-3:]
-    extra = rest[:-3]
+    out_ref, acc, acc_odd, buf = rest[-4:]
+    extra = rest[:-4]
+    both_acc = (acc, acc_odd)
     comps, cap = buf.shape[:2]
     blocks = len_s.shape[0]
     lead = code_s.shape[0] // blocks
     slab = lax.axis_index("vol")
     place = jnp.where(slab & 1, blocks - 1 - (slab >> 1), slab >> 1)
     if has_acc:
-        pltpu.sync_copy(extra[-1], acc.at[0])
+        pltpu.sync_copy(extra[-1], acc)
     else:
-        acc[0] = jnp.zeros(acc.shape[1:], F32)
-    acc[1] = jnp.zeros(acc.shape[1:], F32)
+        acc[...] = jnp.zeros_like(acc)
+    acc_odd[...] = jnp.zeros_like(acc_odd)
     first = lax.broadcasted_iota(jnp.int32, (2, COLS), 0) == 0
     index = 0
     while index < count:
@@ -577,28 +570,30 @@
                 to = code >> 10
                 w = wgt_s[at + u]
                 both = jnp.where(first, w, 1.0 - w)
+                into = both_acc[u % 2]
                 for c in range(comps):
                     row = jnp.broadcast_to(buf[c, pl.ds(s, 1), :], (2, COLS))
-                    acc[u % 2, c, pl.ds(to, 2), :] = acc[u % 2, c, pl.ds(to, 2), :] + both * row
+                    into[c, pl.ds(to, 2), :] = into[c, pl.ds(to, 2), :] + both * row
             return carry
 
         lax.fori_loop(0, (jnp.minimum(len_s[block, 0], cap) + 3) // 4, group_step, 0)
 
     if mode == "sum":
-        acc[0] = acc[0] + acc[1]
-        pltpu.sync_copy(acc.at[0], out_ref)
+        acc[...] = acc[...] + acc_odd[...]
+        pltpu.sync_copy(acc, out_ref)
         return
     planes, lines_here = extra[0].shape[:2]
     stride = line_stride(lines_here)
 
     def plane_step(p, carry):
         base = pl.multiple_of(p * stride + HEAD, 8)
-        for c in range(comps):
-            total = acc[0, c, pl.ds(base, lines_here), :] + acc[1, c, pl.ds(base, lines_here), :]
-            if mode == "inverse":
-                out_ref[p] = 1.0 / (total + extra[0][p])
-            else:
-                out_ref[c, p] = total * extra[0][p]
+        total = [
+            acc[c, pl.ds(base, lines_here), :] + acc_odd[c, pl.ds(base, lines_here), :]
+            for c in range(3)
+        ]
+        inverse = 1.0 / (total[2] + extra[0][p])
+        out_ref[0, p] = total[0] * inverse
+        out_ref[1, p] = total[1] * inverse
         return carry
 
     lax.fori_loop(0, planes, plane_step, 0)
@@ -610,8 +605,7 @@
     acc_shape = (comps, planes * line_stride(lines_here), COLS)
     out = {
         "sum": acc_shape,
-        "inverse": (planes, lines_here, COLS),
-        "result": (comps, planes, lines_here, COLS),
+        "result": (2, planes, lines_here, COLS),
     }[mode]
     more = list(extra) + ([] if acc is None else [acc])
     return pl.pallas_call(
@@ -621,7 +615,8 @@
         + [vmem()] * (len(pieces) + len(extra))
         + [hbm()] * (acc is not None),
         out_specs=hbm() if mode == "sum" else vmem(),
-        scratch_shapes=[pltpu.VMEM((2,) + acc_shape, F32), pltpu.VMEM((comps, cap, COLS), F32)],
+        scratch_shapes=[pltpu.VMEM(acc_shape, F32)] * 2
+        + [pltpu.VMEM((comps, cap, COLS), F32)],
         compiler_params=pltpu.CompilerParams(vmem_limit_bytes=VMEM_LIMIT),
         cost_estimate=cost(6),
         name="insert_" + mode,
@@ -827,28 +822,26 @@
     slices = [x for both in zip(slices_a, slices_b) for x in both]
     cand = candidates.T
     count_row = counts[None, :]
-    partial_logits = candidate_logits(slices, weighted, squared, cosine, sine, cand)
+    partial_logits = candidate_logits(code, slices, weighted, squared, cosine, sine, cand)
     pair_logits = partial_logits + lax.ppermute(partial_logits, "vol", flip(n_vol, 1))
     logits = [pair_logits] + [
         lax.ppermute(pair_logits, "vol", along_z(n_vol, d)) for d in range(1, n_vol // 2)
     ]
 
-    src = src.reshape(-1)
-    keep_d, send_d, post = spread(src, send_len, n_img, logits, cand, count_row, squared, cap)
-    summed_d = add_cores(keep_d, send_d, n_img)
-    keep_n, send_n = project(
-        src, send_len, n_img, post, weighted, cosine, sine, summed_d[-1], cap
-    )
-    pieces_d = ring_gather(add_chips(summed_d, n_img), n_vol)
-    pieces_n = ring_gather(add_chips(add_cores(keep_n, send_n, n_img), n_img), n_vol)
+    keep, send = project(
+        src.reshape(-1), send_len, n_img, logits, cand, count_row, weighted, squared, cosine, sine, cap
+    )
+    pieces, farthest = ring_gather(to_member(keep, send, n_img), n_vol)
     tables = (recv_len, code.reshape(-1), wgt.reshape(-1))
     block = (planes_here, lines_here)
-    early = n_vol // 2 + 1
-    inverse = insert(tables, 0, pieces_d, cap, block, "inverse", [regularizer])
-    part_sum = insert(tables, 0, pieces_n[:early], cap, block, "sum")
+    early = n_vol - 3
+    late = n_vol - 1
+    part_sum = insert(tables, 0, pieces[:early], cap, block, "sum")
+    last = farthest(part_sum)
+    most_sum = insert(tables, early, pieces[early:], cap, block, "sum", acc=part_sum)
 
     def listed():
-        return insert(tables, early, pieces_n[early:], cap, block, "result", [inverse], part_sum)
+        return insert(tables, late, last, cap, block, "result", [regularizer], most_sum)
 
     def dense():
         return dense_path(

time: 216 us -> 193 us (0.89)
  waiting for transfers between devices: 62.5 us -> 54.8 us
  Pallas kernels: 80.8 us -> 75.6 us
  starting transfers between devices: 34.1 us -> 29.4 us
  local copies, waits for them, and re-layouts: 12.1 us -> 8.15 us
    ppermute x6, waiting for transfers between devices: 7.83 us -> 0.27 us  [from_partners(): lax.ppermute(x, 'img', flip(n_img, m))]
    pallas_call x1, Pallas kernels: 7.31 us -> 1.97 us  [halves(): pl.pallas_call(halves_kernel, out_shape=[shape] * 2, in_specs=[vmem(), vm...]
    ppermute x6 -> x3, starting transfers between devices: 8.64 us -> 4.73 us  [ring_gather(): one = lax.ppermute(one, 'vol', ahead)]
    convert_element_type x4 -> x0, other arithmetic: 3.86 us -> none  [the longest x2 2.69 us: add_cores(): (keep[m].astype(F32) + got[m].astype(F32)).astype(BF16)]
    slice x4 -> x0, local copies, waits for them, and re-layouts: 2.61 us -> none  [the longest x2 1.31 us: ring_gather(): two[:, half:]]
    pallas_call x3, Pallas kernels: 25 us -> 22.6 us  [insert(): pl.pallas_call(partial(insert_kernel, start, len(pieces), acc is not None...]
    add x0 -> x2, other arithmetic: none -> 2.21 us  [the longest x1 1.11 us: to_member(): summed = [keep[m] + got[m] for m in range(n_img // 2)]]
    ppermute x8 -> x4, starting transfers between devices: 4.68 us -> 3.06 us  [the longest x2 2.03 us: farthest(): return [lax.ppermute(low, 'vol', ahead), lax.ppermute(high, 'vol', back)]]
  transfers between devices with their start and end apart: 38 -> 28, of which waited for: 19 -> 13; matrix products, arithmetic and copies ran while one was open for 5% -> 5% of each run, Pallas kernels for 15% -> 16%
where the time goes in v5:
time: 193 us; the launch traced here: 191 us
  Pallas kernels  75.6 us (39%)
  waiting for transfers between devices  54.8 us (28%)
  starting transfers between devices  29.4 us (15%)
  between operations  14.4 us (7%)
  other arithmetic  8.4 us (4%)
  local copies, waits for them, and re-layouts  8.15 us (4%)
    pallas_call x3, Pallas kernels, insert(): pl.pallas_call(partial(insert_kernel, start, len(pieces), acc is not None...  22.6 us
    ppermute x3, waiting for transfers between devices, ring_gather(): two = lax.ppermute(two, 'vol', back)  19.4 us
    pallas_call x1, Pallas kernels, extract(): pl.pallas_call(partial(extract_kernel, rows, planes_here), out_shape=[sha...  15 us
    ppermute x1, waiting for transfers between devices, to_member(): lax.ppermute(summed[m], 'img', flip(n_img, 2 * m))  11.8 us
    pallas_call x1, Pallas kernels, project(): pl.pallas_call(project_kernel, grid=(rows // inner,), out_shape=[jax.Shap...  11.2 us
    ppermute x3, waiting for transfers between devices, to_pixel_rows(): lax.ppermute(sums_a[d], 'vol', along_z(n_vol, d))  10.7 us
    pallas_call x1, Pallas kernels, candidate_logits(): pl.pallas_call(logits_kernel, grid=(rows // inner,), out_shape=jax.ShapeD...  8.61 us
    pallas_call x1, Pallas kernels, weigh(): pl.pallas_call(weigh_kernel, grid=(count // step,), out_shape=[jax.ShapeD...  8.43 us
  transfers between devices with their start and end apart: 28, of which 13 were waited for; matrix products, arithmetic and copies ran while one was open for 5% of the time, Pallas kernels for 16%

profile of v5, /device:TPU:12, one launch (start us, length us, event | category | flops | bytes accessed | tf_op | source)
XLA Modules:
  0.0 191.1 jit_solution(15068463774459427783)
XLA Ops:
  6.5 15.0 %extract.1 = (bf16[4,2,352,128]{3,2,1,0:T(8,128)(2,1)}, bf16[4,2,352,128]{3,2,1,0:T(8,128)(2,1)}, bf16[2,2,160,128]{3,2,1,0:T(8,128)(2,1)}, bf16[2,2,160,128]{3,...) custom-call(s32[64,256]{1,0:T(8,128)} %refs_0_.1, s32[64,256]{1,0:T(8,128)} %refs_1_.1, ...), custom_call_target="tpu_custom_call" | custom-call | bytes 40590000 | tf_op jit(solution)/shard_map/extract/pallas_call | solution.py:163
  21.7 1.9 %collective-permute-start.3 = (bf16[2,2,160,128]{3,2,1,0:T(8,128)(2,1)}, bf16[2,2,160,128]{3,2,1,0:T(8,128)(2,1)S(1)}, u32[]{:S(2)}, u32[]{:S(2)}) collective-permute-start(bf16[2,2,160,128]{3,2,1,0:T(8,128)(2,1)} %get-tuple-element.127), channel_id=1, source_target_pairs={{0,6},{1,7},{2,0},{3,1},{4,2},{5,3},{6,4},{7,5},{8,14},{9,15},{10,... | collective-permute-start | bytes 491528 | tf_op jit(solution)/shard_map/ppermute | solution.py:201
  23.6 2.1 %collective-permute-start = (bf16[4,2,352,128]{3,2,1,0:T(8,128)(2,1)}, bf16[4,2,352,128]{3,2,1,0:T(8,128)(2,1)S(1)}, u32[]{:S(2)}, u32[]{:S(2)}) collective-permute-start(bf16[4,2,352,128]{3,2,1,0:T(8,128)(2,1)} %get-tuple-element.123), channel_id=1, source_target_pairs={{0,1},{1,0},{2,3},{3,2},{4,5},{5,4},{6,7},{7,6},{8,9},{9,8},{10,11... | collective-permute-start | bytes 2162696 | tf_op jit(solution)/shard_map/ppermute | solution.py:202
  25.8 1.5 multiply_cosine_fusion
  27.3 1.5 fusion.20
  28.8 8.4 %weigh.1 = (bf16[32,384,256]{2,1,0:T(8,128)(2,1)S(1)}, bf16[32,384,128]{2,1,0:T(8,128)(2,1)}) custom-call(bf16[2,384,32,128]{3,2,1,0:T(8,128)(2,1)} %img_ref.1, f32[384,32]{1,0:T(8,128)} %get-tuple-element.247.sa_ref, f32[384,32]{1,0:T(8,128)} %get-tuple-element.246.ca_ref, f32[384,128]{1,0:T(8,128)} %get-tuple-element.245.sx_ref, ...), custom_call_target="tpu_custom_call" | custom-call | bytes 44280000 | tf_op jit(solution)/shard_map/weigh/pallas_call | solution.py:289
  37.4 4.2 %collective-permute-done.got_a = bf16[4,2,352,128]{3,2,1,0:T(8,128)(2,1)S(1)} collective-permute-done((bf16[4,2,352,128]{3,2,1,0:T(8,128)(2,1)}, bf16[4,2,352,128]{3,2,1,0:T(8,128)(2,1)S(1)}, u32[]{:S(2)}, u32[]{:S(2)}) %collective-permute-start) | collective-permute-done | bytes 720928 | tf_op jit(solution)/shard_map/ppermute | solution.py:202
  41.6 0.8 copy-done.8
  42.4 2.6 %combine_first.1 = (bf16[2,352,128]{2,1,0:T(8,128)(2,1)}, bf16[2,352,128]{2,1,0:T(8,128)(2,1)}, bf16[2,352,128]{2,1,0:T(8,128)(2,1)}, bf16[2,352,128]{2,1,0:T(8,...) custom-call(bf16[4,2,352,128]{3,2,1,0:T(8,128)(2,1)} %get-tuple-element.122.keep_a, ...), custom_call_target="tpu_custom_call" | custom-call | bytes 11070000 | tf_op jit(solution)/shard_map/combine_first/pallas_call | solution.py:205
  45.1 1.7 collective-permute-start.7
  46.8 0.5 collective-permute-start.4
  47.3 4.4 %collective-permute-start.5 = (bf16[2,352,128]{2,1,0:T(8,128)(2,1)}, bf16[2,352,128]{2,1,0:T(8,128)(2,1)S(1)}, u32[]{:S(2)}, u32[]{:S(2)}) collective-permute-start(bf16[2,352,128]{2,1,0:T(8,128)(2,1)} %get-tuple-element.130), channel_id=1, source_target_pairs={{0,4},{1,5},{2,6},{3,7},{4,0},{5,1},{6,2},{7,3},{8,12},{9,13},{10,... | collective-permute-start | bytes 540680 | tf_op jit(solution)/shard_map/ppermute | solution.py:216
  51.8 0.9 add.170.rest_2_
  52.8 1.5 collective-permute-start.11
  54.3 5.1 %collective-permute-done.4 = bf16[2,352,128]{2,1,0:T(8,128)(2,1)S(1)} collective-permute-done((bf16[2,352,128]{2,1,0:T(8,128)(2,1)}, bf16[2,352,128]{2,1,0:T(8,128)(2,1)S(1)}, u32[]{:S(2)}, u32[]{:S(2)}) %collective-permute-start.4) | collective-permute-done | bytes 180256 | tf_op jit(solution)/shard_map/ppermute | solution.py:216
  59.4 2.8 %collective-permute-done.5 = bf16[2,352,128]{2,1,0:T(8,128)(2,1)S(1)} collective-permute-done((bf16[2,352,128]{2,1,0:T(8,128)(2,1)}, bf16[2,352,128]{2,1,0:T(8,128)(2,1)S(1)}, u32[]{:S(2)}, u32[]{:S(2)}) %collective-permute-start.5) | collective-permute-done | bytes 180256 | tf_op jit(solution)/shard_map/ppermute | solution.py:216
  62.2 2.8 %collective-permute-done.6 = bf16[2,352,128]{2,1,0:T(8,128)(2,1)S(1)} collective-permute-done((bf16[2,352,128]{2,1,0:T(8,128)(2,1)}, bf16[2,352,128]{2,1,0:T(8,128)(2,1)S(1)}, u32[]{:S(2)}, u32[]{:S(2)}) %collective-permute-start.6) | collective-permute-done | bytes 180256 | tf_op jit(solution)/shard_map/ppermute | solution.py:216
  65.0 1.0 add_add_fusion.rest_1_
  66.1 1.2 collective-permute-start.10
  67.3 0.6 collective-permute-start.8
  67.9 0.3 fusion.22
  68.3 0.1 copy.75
  68.4 0.7 reshape.229.wgt_ref
  69.1 0.1 copy.74
  69.2 0.7 reshape.228.line_ref
  70.0 0.7 reshape.227.plane_ref
  70.7 5.2 %lists.1 = (s32[32,128]{1,0:T(8,128)}, s32[64,128]{1,0:T(8,128)S(1)}, f32[64,128]{1,0:T(8,128)S(1)}, s32[8,128]{1,0:T(8,128)}, s32[8,128]{1,0:T(8,128)S(1)}, /*index=5*/s32[8,128]{1,0:T(8,128)}) custom-call(s32[8,2048]{1,0:T(8,128)} %reshape.227.plane_ref, s32[8,2048]{1,0:T(8,128)} %reshape.228.line_ref, f32[8,2048]{1,0:T(8,128)} %reshape.229.wgt_ref), custom_call_target="tpu_custom_call" | custom-call | bytes 22140000 | tf_op jit(solution)/shard_map/lists/pallas_call | solution.py:726
  75.9 0.3 collective-permute-done.10.rest_5_
  76.2 0.4 copy-done.22
  76.6 0.3 copy-done.23
  76.9 8.6 %logits.1 = f32[32,384]{1,0:T(8,128)} custom-call(bf16[32,384,256]{2,1,0:T(8,128)(2,1)} %copy-done, bf16[32,384,128]{2,1,0:T(8,128)(2,1)} %get-tuple-element.120.sq_ref, f32[4,32,128]{2,1,0:T(8,128)S(1)} %get-tuple-element.243.cos_ref, f32[4,32,128]{2,1,0:T(8,128)S(1)} %get-tuple-element.242.sin_ref, s32[8,384]{1,0:T(8,128)S(1)} %bitcast.101, ...), custom_call_target="tpu_custom_call" | custom-call | bytes 29520000 | tf_op jit(solution)/shard_map/logits/pallas_call | solution.py:381
  85.6 0.6 collective-permute-start.14
  86.1 3.7 %collective-permute-done.14 = f32[32,384]{1,0:T(8,128)S(1)} collective-permute-done((f32[32,384]{1,0:T(8,128)}, f32[32,384]{1,0:T(8,128)S(1)}, u32[]{:S(2)}, u32[]{:S(2)}) %collective-permute-start.14) | collective-permute-done | bytes 49184 | tf_op jit(solution)/shard_map/ppermute | solution.py:826
  89.9 0.8 add.171.rest_0_
  90.7 1.1 collective-permute-start.16
  91.8 2.9 %collective-permute-start.15 = (f32[32,384]{1,0:T(8,128)S(1)}, f32[32,384]{1,0:T(8,128)S(1)}, u32[]{:S(2)}, u32[]{:S(2)}) collective-permute-start(f32[32,384]{1,0:T(8,128)S(1)} %add.171.rest_0_), channel_id=1, source_target_pairs={{0,2},{1,3},{2,4},{3,5},{4,6},{5,7},{6,0},{7,1},{8,10},{9,11},{10,... | collective-permute-start | bytes 147464 | tf_op jit(solution)/shard_map/ppermute | solution.py:828
  94.7 0.4 collective-permute-done.17.rest_3_
  95.1 0.9 collective-permute-done.16.rest_2_
  96.0 0.8 collective-permute-done.15.rest_1_
  96.8 11.2 %project.1 = (bf16[2,3,608,128]{3,2,1,0:T(8,128)(2,1)}, bf16[2,3,608,128]{3,2,1,0:T(8,128)(2,1)}) custom-call(s32[4096]{0:T(1024)} %bitcast.106, s32[8,128]{1,0:T(8,128)} %get-tuple-element.137.len_s, s32[8,384]{1,0:T(8,128)S(1)} %bitcast.102, s32[1,384]{1,0:T(1,128)S(1)} %broadcast_in_dim.13.cnt_ref, bf16[32,384,256]{2,1,0:T(8,128)(2,1)S(1)} %bitcast.82, ...), custom_call_target="tpu_custom_call" | custom-call | bytes 44280000 | tf_op jit(solution)/shard_map/project/pallas_call | solution.py:486
  108.0 2.7 %collective-permute-done.18 = bf16[2,3,608,128]{3,2,1,0:T(8,128)(2,1)S(1)} collective-permute-done((bf16[2,3,608,128]{3,2,1,0:T(8,128)(2,1)}, bf16[2,3,608,128]{3,2,1,0:T(8,128)(2,1)S(1)}, u32[]{:S(2)}, u32[]{:S(2)}) %collective-permute-start.18) | collective-permute-done | bytes 933920 | tf_op jit(solution)/shard_map/ppermute | solution.py:515
  110.7 1.1 fusion.17
  111.8 1.0 collective-permute-start.19
  112.8 11.8 %collective-permute-done.19 = bf16[3,608,128]{2,1,0:T(8,128)(2,1)S(1)} collective-permute-done((bf16[3,608,128]{2,1,0:T(8,128)(2,1)S(1)}, bf16[3,608,128]{2,1,0:T(8,128)(2,1)S(1)}, u32[]{:S(2)}, u32[]{:S(2)}) %collective-permute-start.19) | collective-permute-done | bytes 466976 | tf_op jit(solution)/shard_map/ppermute | solution.py:517
  124.6 1.1 fusion.19.rest_0_
  125.7 2.1 %collective-permute-start.23 = (bf16[3,608,128]{2,1,0:T(8,128)(2,1)S(1)}, bf16[3,608,128]{2,1,0:T(8,128)(2,1)S(1)}, u32[]{:S(2)}, u32[]{:S(2)}) collective-permute-start(bf16[3,608,128]{2,1,0:T(8,128)(2,1)S(1)} %fusion.19.rest_0_), channel_id=1, source_target_pairs={{2,0},{4,2},{6,4},{7,6},{5,7},{3,5},{1,3},{0,1},{10,8},{12,10},{14... | collective-permute-start | bytes 1400840 | tf_op jit(solution)/shard_map/ppermute | solution.py:234
  127.8 1.4 collective-permute-start.20
  129.2 10.1 %collective-permute-done.23.rest_2_ = bf16[3,608,128]{2,1,0:T(8,128)(2,1)S(1)} collective-permute-done((bf16[3,608,128]{2,1,0:T(8,128)(2,1)S(1)}, bf16[3,608,128]{2,1,0:T(8,128)(2,1)S(1)}, u32[]{:S(2)}, u32[]{:S(2)}) %collective-permute-start.23) | collective-permute-done | bytes 466976 | tf_op jit(solution)/shard_map/ppermute | solution.py:234
  139.3 0.4 collective-permute-start.24
  139.8 1.6 collective-permute-start.21
  141.4 9.3 %collective-permute-done.24.rest_4_ = bf16[3,608,128]{2,1,0:T(8,128)(2,1)S(1)} collective-permute-done((bf16[3,608,128]{2,1,0:T(8,128)(2,1)S(1)}, bf16[3,608,128]{2,1,0:T(8,128)(2,1)S(1)}, u32[]{:S(2)}, u32[]{:S(2)}) %collective-permute-start.24) | collective-permute-done | bytes 466976 | tf_op jit(solution)/shard_map/ppermute | solution.py:234
  150.6 0.3 collective-permute-start.25
  150.9 1.7 collective-permute-start.22
  152.7 8.4 %insert_sum.2.after.rest_2_ = f32[3,2560,128]{2,1,0:T(8,128)} custom-call(s32[8,128]{1,0:T(8,128)S(1)} %get-tuple-element.134.len_s, s32[8192]{0:T(1024)S(1)} %bitcast.88, f32[8192]{0:T(1024)S(1)} %bitcast.95, bf16[3,608,128]{2,1,0:T(8,128)(2,1)} %copy-done.7, bf16[3,608,128]{2,1,0:T(8,128)(2,1)} %copy-done.11, bf16[3,608,128]{2,1,0:T(8,128)(2,1)} %copy-done.10, ...), custom_call_target="tpu_custom_call" | custom-call | bytes 22140000 | tf_op jit(solution)/shard_map/insert_sum/pallas_call | solution.py:611
  161.1 0.8 copy-done.5
  161.9 0.8 copy-done.6
  162.7 2.0 %halves.1 = (bf16[3,304,128]{2,1,0:T(8,128)(2,1)}, bf16[3,304,128]{2,1,0:T(8,128)(2,1)}) custom-call(bf16[3,608,128]{2,1,0:T(8,128)(2,1)} %copy-done.6, bf16[3,608,128]{2,1,0:T(8,128)(2,1)} %copy-done.5, f32[3,2560,128]{2,1,0:T(8,128)} %insert_sum.2.after.rest_2_), custom_call_target="tpu_custom_call" | custom-call | bytes 3690000 | tf_op jit(solution)/shard_map/halves/pallas_call | solution.py:253
  164.6 1.0 collective-permute-start.26
  165.6 1.0 collective-permute-start.27
  166.7 1.2 slice.33
  168.4 8.1 %insert_sum.3 = f32[3,2560,128]{2,1,0:T(8,128)} custom-call(s32[8,128]{1,0:T(8,128)} %copy-done.30, s32[8192]{0:T(1024)S(1)} %bitcast.89, f32[8192]{0:T(1024)} %bitcast.96, bf16[3,608,128]{2,1,0:T(8,128)(2,1)} %copy-done.6, bf16[3,608,128]{2,1,0:T(8,128)(2,1)} %copy-done.5, f32[3,2560,128]{2,1,0:T(8,128)} %insert_sum.2.after.rest_2_), custom_call_target="tpu_custom_call" | custom-call | bytes 22140000 | tf_op jit(solution)/shard_map/insert_sum/pallas_call | solution.py:611
  176.6 6.3 %conditional.1 = (f32[2,32,64,128]{3,2,1,0:T(8,128)S(1)}) conditional(s32[]{:T(128)} %bitcast.18, (s32[]{:T(128)}, s32[64,256]{1,0:T(8,128)S(1)}, s32[]{:T(128)}, s32[64,256]{1,0:T(8,128)S(1)}, f32[64,256]{1,0:T(8,128)S(1)}, /*index=5*/f32[4,32,128]{2,1,0:T(8,128)S(1)}, s32[8,384]{1,0:T(8,128)}, s32[1,384]{1,0:T(1,128)}, f32[32,384]{1,0:T(8,128)S(1)}, ...), branch_computations={%region_0.10_spmd, %region_10.11_spmd} | conditional | flops 1831321088 | bytes 337575520 | solution.py:852
  176.8 6.1 %insert_result.1 = f32[2,32,64,128]{3,2,1,0:T(8,128)S(1)} custom-call(s32[8,128]{1,0:T(8,128)} %get-tuple-element.87.len_s, s32[8192]{0:T(1024)S(1)} %get-tuple-element.88.code_s, f32[8192]{0:T(1024)} %get-tuple-element.89.wgt_s, bf16[3,304,128]{2,1,0:T(8,128)(2,1)} %get-tuple-element.90.rest_0_, bf16[3,304,128]{2,1,0:T(8,128)(2,1)} %get-tuple-element.91.rest_1_, ...), custom_call_target="tpu_custom_call" | custom-call | bytes 22140000 | tf_op jit(solution)/shard_map/cond/branch_1_fun/insert_result/pallas_call | solution.py:611
  182.9 1.3 copy-done.4
  (95 shorter events, 0.8 us)
Async XLA Ops:
  6.5 19.2 %copy-start.32 = (f32[384]{0:T(512)S(1)}, f32[384]{0:T(512)}, u32[]{:S(2)}) copy-start(f32[384]{0:T(512)} %param.13) | copy-start | bytes 4612
  21.5 15.8 %collective-permute-start.1 = (bf16[2,2,160,128]{3,2,1,0:T(8,128)(2,1)}, bf16[2,2,160,128]{3,2,1,0:T(8,128)(2,1)S(1)}, u32[]{:S(2)}, u32[]{:S(2)}) collective-permute-start(bf16[2,2,160,128]{3,2,1,0:T(8,128)(2,1)} %get-tuple-element.125), channel_id=1, source_target_pairs={{0,2},{1,3},{2,4},{3,5},{4,6},{5,7},{6,0},{7,1},{8,10},{9,11},{10,... | collective-permute-start | bytes 491528 | tf_op jit(solution)/shard_map/ppermute | solution.py:201
  21.6 15.7 %collective-permute-start.2 = (bf16[2,2,160,128]{3,2,1,0:T(8,128)(2,1)}, bf16[2,2,160,128]{3,2,1,0:T(8,128)(2,1)S(1)}, u32[]{:S(2)}, u32[]{:S(2)}) collective-permute-start(bf16[2,2,160,128]{3,2,1,0:T(8,128)(2,1)} %get-tuple-element.126), channel_id=1, source_target_pairs={{0,4},{1,5},{2,6},{3,7},{4,0},{5,1},{6,2},{7,3},{8,12},{9,13},{10,... | collective-permute-start | bytes 491528 | tf_op jit(solution)/shard_map/ppermute | solution.py:201
  21.7 15.7 %collective-permute-start.3 = (bf16[2,2,160,128]{3,2,1,0:T(8,128)(2,1)}, bf16[2,2,160,128]{3,2,1,0:T(8,128)(2,1)S(1)}, u32[]{:S(2)}, u32[]{:S(2)}) collective-permute-start(bf16[2,2,160,128]{3,2,1,0:T(8,128)(2,1)} %get-tuple-element.127), channel_id=1, source_target_pairs={{0,6},{1,7},{2,0},{3,1},{4,2},{5,3},{6,4},{7,5},{8,14},{9,15},{10,... | collective-permute-start | bytes 491528 | tf_op jit(solution)/shard_map/ppermute | solution.py:201
  23.6 17.9 %collective-permute-start = (bf16[4,2,352,128]{3,2,1,0:T(8,128)(2,1)}, bf16[4,2,352,128]{3,2,1,0:T(8,128)(2,1)S(1)}, u32[]{:S(2)}, u32[]{:S(2)}) collective-permute-start(bf16[4,2,352,128]{3,2,1,0:T(8,128)(2,1)} %get-tuple-element.123), channel_id=1, source_target_pairs={{0,1},{1,0},{2,3},{3,2},{4,5},{5,4},{6,7},{7,6},{8,9},{9,8},{10,11... | collective-permute-start | bytes 2162696 | tf_op jit(solution)/shard_map/ppermute | solution.py:202
  37.2 4.3 %copy-start = (bf16[32,384,256]{2,1,0:T(8,128)(2,1)}, bf16[32,384,256]{2,1,0:T(8,128)(2,1)S(1)}, u32[]{:S(2)}) copy-start(bf16[32,384,256]{2,1,0:T(8,128)(2,1)S(1)} %get-tuple-element.119.rest_3_.wt_ref) | copy-start | bytes 18874372
  37.3 31.0 %copy-start.16 = (f32[64,256]{1,0:T(8,128)S(1)}, f32[64,256]{1,0:T(8,128)}, u32[]{:S(2)}) copy-start(f32[64,256]{1,0:T(8,128)} %refs_2_.1) | copy-start | bytes 196612
  37.3 31.8 %copy-start.15 = (s32[64,256]{1,0:T(8,128)S(1)}, s32[64,256]{1,0:T(8,128)}, u32[]{:S(2)}) copy-start(s32[64,256]{1,0:T(8,128)} %refs_1_.1) | copy-start | bytes 196612
  37.3 32.7 %copy-start.14 = (s32[64,256]{1,0:T(8,128)S(1)}, s32[64,256]{1,0:T(8,128)}, u32[]{:S(2)}) copy-start(s32[64,256]{1,0:T(8,128)} %refs_0_.1) | copy-start | bytes 196612
  37.3 39.7 %copy-start.28 = (s32[384,8]{0,1:T(8,128)S(1)}, s32[384,8]{0,1:T(8,128)}, u32[]{:S(2)}) copy-start(s32[384,8]{0,1:T(8,128)} %param.14) | copy-start | bytes 36868
  37.3 4.3 %copy-start.25 = (bf16[2,2,160,128]{3,2,1,0:T(8,128)(2,1)}, bf16[2,2,160,128]{3,2,1,0:T(8,128)(2,1)S(1)}, u32[]{:S(2)}) copy-start(bf16[2,2,160,128]{3,2,1,0:T(8,128)(2,1)S(1)} %collective-permute-done.1.rest_0_) | copy-start | bytes 491524
  37.3 4.2 %copy-start.26 = (bf16[2,2,160,128]{3,2,1,0:T(8,128)(2,1)}, bf16[2,2,160,128]{3,2,1,0:T(8,128)(2,1)S(1)}, u32[]{:S(2)}) copy-start(bf16[2,2,160,128]{3,2,1,0:T(8,128)(2,1)S(1)} %collective-permute-done.2.rest_1_) | copy-start | bytes 491524
  37.4 4.2 %copy-start.27 = (bf16[2,2,160,128]{3,2,1,0:T(8,128)(2,1)}, bf16[2,2,160,128]{3,2,1,0:T(8,128)(2,1)S(1)}, u32[]{:S(2)}) copy-start(bf16[2,2,160,128]{3,2,1,0:T(8,128)(2,1)S(1)} %collective-permute-done.3.rest_2_) | copy-start | bytes 491524
  41.6 0.9 copy-start.8
  45.1 6.7 %collective-permute-start.7 = (bf16[2,160,128]{2,1,0:T(8,128)(2,1)}, bf16[2,160,128]{2,1,0:T(8,128)(2,1)S(1)}, u32[]{:S(2)}, u32[]{:S(2)}) collective-permute-start(bf16[2,160,128]{2,1,0:T(8,128)(2,1)} %get-tuple-element.133), channel_id=1, source_target_pairs={{0,1},{1,0},{2,3},{3,2},{4,5},{5,4},{6,7},{7,6},{8,9},{9,8},{10,11... | collective-permute-start | bytes 245768 | tf_op jit(solution)/shard_map/ppermute | solution.py:215
  46.8 12.6 %collective-permute-start.4 = (bf16[2,352,128]{2,1,0:T(8,128)(2,1)}, bf16[2,352,128]{2,1,0:T(8,128)(2,1)S(1)}, u32[]{:S(2)}, u32[]{:S(2)}) collective-permute-start(bf16[2,352,128]{2,1,0:T(8,128)(2,1)} %get-tuple-element.129), channel_id=1, source_target_pairs={{0,2},{1,3},{2,4},{3,5},{4,6},{5,7},{6,0},{7,1},{8,10},{9,11},{10,... | collective-permute-start | bytes 540680 | tf_op jit(solution)/shard_map/ppermute | solution.py:216
  47.3 14.9 %collective-permute-start.5 = (bf16[2,352,128]{2,1,0:T(8,128)(2,1)}, bf16[2,352,128]{2,1,0:T(8,128)(2,1)S(1)}, u32[]{:S(2)}, u32[]{:S(2)}) collective-permute-start(bf16[2,352,128]{2,1,0:T(8,128)(2,1)} %get-tuple-element.130), channel_id=1, source_target_pairs={{0,4},{1,5},{2,6},{3,7},{4,0},{5,1},{6,2},{7,3},{8,12},{9,13},{10,... | collective-permute-start | bytes 540680 | tf_op jit(solution)/shard_map/ppermute | solution.py:216
  51.7 13.3 %collective-permute-start.6 = (bf16[2,352,128]{2,1,0:T(8,128)(2,1)}, bf16[2,352,128]{2,1,0:T(8,128)(2,1)S(1)}, u32[]{:S(2)}, u32[]{:S(2)}) collective-permute-start(bf16[2,352,128]{2,1,0:T(8,128)(2,1)} %get-tuple-element.131), channel_id=1, source_target_pairs={{0,6},{1,7},{2,0},{3,1},{4,2},{5,3},{6,4},{7,5},{8,14},{9,15},{10,... | collective-permute-start | bytes 540680 | tf_op jit(solution)/shard_map/ppermute | solution.py:216
  52.7 23.5 %copy-start.17 = (bf16[2,160,128]{2,1,0:T(8,128)(2,1)}, bf16[2,160,128]{2,1,0:T(8,128)(2,1)S(1)}, u32[]{:S(2)}) copy-start(bf16[2,160,128]{2,1,0:T(8,128)(2,1)S(1)} %add.170.rest_2_) | copy-start | bytes 245764
  52.7 14.6 %collective-permute-start.13 = (bf16[2,160,128]{2,1,0:T(8,128)(2,1)S(1)}, bf16[2,160,128]{2,1,0:T(8,128)(2,1)S(1)}, u32[]{:S(2)}, u32[]{:S(2)}) collective-permute-start(bf16[2,160,128]{2,1,0:T(8,128)(2,1)S(1)} %add.170.rest_2_), channel_id=1, source_target_pairs={{0,24},{8,16},{16,8},{24,0},{1,25},{9,17},{17,9},{25,1},{2,26},{10... | collective-permute-start | bytes 245768 | tf_op jit(solution)/shard_map/ppermute | solution.py:223
  52.8 23.1 %collective-permute-start.11 = (bf16[2,160,128]{2,1,0:T(8,128)(2,1)S(1)}, bf16[2,160,128]{2,1,0:T(8,128)(2,1)}, u32[]{:S(2)}, u32[]{:S(2)}) collective-permute-start(bf16[2,160,128]{2,1,0:T(8,128)(2,1)S(1)} %add.170.rest_2_), channel_id=1, source_target_pairs={{0,16},{8,24},{16,0},{24,8},{1,17},{9,25},{17,1},{25,9},{2,18},{10... | collective-permute-start | bytes 245768 | tf_op jit(solution)/shard_map/ppermute | solution.py:223
  59.4 16.5 %collective-permute-start.9 = (bf16[2,160,128]{2,1,0:T(8,128)(2,1)S(1)}, bf16[2,160,128]{2,1,0:T(8,128)(2,1)}, u32[]{:S(2)}, u32[]{:S(2)}) collective-permute-start(bf16[2,160,128]{2,1,0:T(8,128)(2,1)S(1)} %add.170.rest_2_), channel_id=1, source_target_pairs={{0,8},{8,0},{16,24},{24,16},{1,9},{9,1},{17,25},{25,17},{2,10},{10... | collective-permute-start | bytes 245768 | tf_op jit(solution)/shard_map/ppermute | solution.py:223
  66.0 10.2 %copy-start.9 = (bf16[2,352,128]{2,1,0:T(8,128)(2,1)}, bf16[2,352,128]{2,1,0:T(8,128)(2,1)S(1)}, u32[]{:S(2)}) copy-start(bf16[2,352,128]{2,1,0:T(8,128)(2,1)S(1)} %add_add_fusion.rest_1_) | copy-start | bytes 540676
  66.0 28.7 %copy-start.36 = (s32[384]{0:T(512)S(1)}, s32[384]{0:T(512)}, u32[]{:S(2)}) copy-start(s32[384]{0:T(512)} %param.15) | copy-start | bytes 4612
  66.0 30.8 %slice-start = ((s8[6291456]{0:T(1024)(128)(4,1)}), s8[2097152]{0:T(1024)(128)(4,1)S(1)}, s32[]{:S(2)}) async-start(s8[6291456]{0:T(1024)(128)(4,1)} %bitcast.81), calls=%async_computation.5 | async-start | bytes 4194304
  66.0 9.9 %collective-permute-start.12 = (bf16[2,352,128]{2,1,0:T(8,128)(2,1)S(1)}, bf16[2,352,128]{2,1,0:T(8,128)(2,1)S(1)}, u32[]{:S(2)}, u32[]{:S(2)}) collective-permute-start(bf16[2,352,128]{2,1,0:T(8,128)(2,1)S(1)} %add_add_fusion.rest_1_), channel_id=1, source_target_pairs={{0,24},{8,16},{16,8},{24,0},{1,25},{9,17},{17,9},{25,1},{2,26},{10... | collective-permute-start | bytes 540680 | tf_op jit(solution)/shard_map/ppermute | solution.py:223
  66.1 10.1 %collective-permute-start.10 = (bf16[2,352,128]{2,1,0:T(8,128)(2,1)S(1)}, bf16[2,352,128]{2,1,0:T(8,128)(2,1)S(1)}, u32[]{:S(2)}, u32[]{:S(2)}) collective-permute-start(bf16[2,352,128]{2,1,0:T(8,128)(2,1)S(1)} %add_add_fusion.rest_1_), channel_id=1, source_target_pairs={{0,16},{8,24},{16,0},{24,8},{1,17},{9,25},{17,1},{25,9},{2,18},{10... | collective-permute-start | bytes 540680 | tf_op jit(solution)/shard_map/ppermute | solution.py:223
  67.3 8.9 %copy-start.29 = (bf16[2,160,128]{2,1,0:T(8,128)(2,1)}, bf16[2,160,128]{2,1,0:T(8,128)(2,1)S(1)}, u32[]{:S(2)}) copy-start(bf16[2,160,128]{2,1,0:T(8,128)(2,1)S(1)} %collective-permute-done.13.rest_8_) | copy-start | bytes 245764
  67.3 8.9 %collective-permute-start.8 = (bf16[2,352,128]{2,1,0:T(8,128)(2,1)S(1)}, bf16[2,352,128]{2,1,0:T(8,128)(2,1)S(1)}, u32[]{:S(2)}, u32[]{:S(2)}) collective-permute-start(bf16[2,352,128]{2,1,0:T(8,128)(2,1)S(1)} %add_add_fusion.rest_1_), channel_id=1, source_target_pairs={{0,8},{8,0},{16,24},{24,16},{1,9},{9,1},{17,25},{25,17},{2,10},{10... | collective-permute-start | bytes 540680 | tf_op jit(solution)/shard_map/ppermute | solution.py:223
  75.9 76.7 %copy-start.18 = (f32[64,128]{1,0:T(8,128)}, f32[64,128]{1,0:T(8,128)S(1)}, u32[]{:S(2)}) copy-start(f32[64,128]{1,0:T(8,128)S(1)} %get-tuple-element.135) | copy-start | bytes 98308
  75.9 76.7 %copy-start.30 = (s32[8,128]{1,0:T(8,128)}, s32[8,128]{1,0:T(8,128)S(1)}, u32[]{:S(2)}) copy-start(s32[8,128]{1,0:T(8,128)S(1)} %get-tuple-element.134.len_s) | copy-start | bytes 12292
  75.9 0.7 copy-start.22
  76.2 0.7 copy-start.23
  76.2 0.7 copy-start.24
  76.9 19.8 %slice-start.1 = ((s8[6291456]{0:T(1024)(128)(4,1)}), s8[4194304]{0:T(1024)(128)(4,1)S(1)}, s32[]{:S(2)}) async-start(s8[6291456]{0:T(1024)(128)(4,1)} %bitcast.81), calls=%async_computation.6 | async-start | bytes 8388608
  85.6 4.3 %collective-permute-start.14 = (f32[32,384]{1,0:T(8,128)}, f32[32,384]{1,0:T(8,128)S(1)}, u32[]{:S(2)}, u32[]{:S(2)}) collective-permute-start(f32[32,384]{1,0:T(8,128)} %logits.1), channel_id=1, source_target_pairs={{0,1},{1,0},{2,3},{3,2},{4,5},{5,4},{6,7},{7,6},{8,9},{9,8},{10,11... | collective-permute-start | bytes 147464 | tf_op jit(solution)/shard_map/ppermute | solution.py:826
  90.7 4.4 %collective-permute-start.17 = (f32[32,384]{1,0:T(8,128)S(1)}, f32[32,384]{1,0:T(8,128)S(1)}, u32[]{:S(2)}, u32[]{:S(2)}) collective-permute-start(f32[32,384]{1,0:T(8,128)S(1)} %add.171.rest_0_), channel_id=1, source_target_pairs={{0,6},{1,7},{2,0},{3,1},{4,2},{5,3},{6,4},{7,5},{8,14},{9,15},{10,... | collective-permute-start | bytes 147464 | tf_op jit(solution)/shard_map/ppermute | solution.py:828
  90.7 5.3 %collective-permute-start.16 = (f32[32,384]{1,0:T(8,128)S(1)}, f32[32,384]{1,0:T(8,128)S(1)}, u32[]{:S(2)}, u32[]{:S(2)}) collective-permute-start(f32[32,384]{1,0:T(8,128)S(1)} %add.171.rest_0_), channel_id=1, source_target_pairs={{0,4},{1,5},{2,6},{3,7},{4,0},{5,1},{6,2},{7,3},{8,12},{9,13},{10,... | collective-permute-start | bytes 147464 | tf_op jit(solution)/shard_map/ppermute | solution.py:828
  91.8 5.0 %collective-permute-start.15 = (f32[32,384]{1,0:T(8,128)S(1)}, f32[32,384]{1,0:T(8,128)S(1)}, u32[]{:S(2)}, u32[]{:S(2)}) collective-permute-start(f32[32,384]{1,0:T(8,128)S(1)} %add.171.rest_0_), channel_id=1, source_target_pairs={{0,2},{1,3},{2,4},{3,5},{4,6},{5,7},{6,0},{7,1},{8,10},{9,11},{10,... | collective-permute-start | bytes 147464 | tf_op jit(solution)/shard_map/ppermute | solution.py:828
  94.7 31.0 %copy-start.31 = (s32[1,384]{1,0:T(1,128)}, s32[1,384]{1,0:T(1,128)S(1)}, u32[]{:S(2)}) copy-start(s32[1,384]{1,0:T(1,128)S(1)} %broadcast_in_dim.13.cnt_ref) | copy-start | bytes 4612
  95.1 30.6 %copy-start.19 = (f32[32,384]{1,0:T(8,128)}, f32[32,384]{1,0:T(8,128)S(1)}, u32[]{:S(2)}) copy-start(f32[32,384]{1,0:T(8,128)S(1)} %collective-permute-done.17.rest_3_) | copy-start | bytes 147460
  96.0 29.8 %copy-start.20 = (f32[32,384]{1,0:T(8,128)}, f32[32,384]{1,0:T(8,128)S(1)}, u32[]{:S(2)}) copy-start(f32[32,384]{1,0:T(8,128)S(1)} %collective-permute-done.16.rest_2_) | copy-start | bytes 147460
  96.7 29.0 %copy-start.21 = (f32[32,384]{1,0:T(8,128)}, f32[32,384]{1,0:T(8,128)S(1)}, u32[]{:S(2)}) copy-start(f32[32,384]{1,0:T(8,128)S(1)} %collective-permute-done.15.rest_1_) | copy-start | bytes 147460
  108.0 2.7 %collective-permute-start.18 = (bf16[2,3,608,128]{3,2,1,0:T(8,128)(2,1)}, bf16[2,3,608,128]{3,2,1,0:T(8,128)(2,1)S(1)}, u32[]{:S(2)}, u32[]{:S(2)}) collective-permute-start(bf16[2,3,608,128]{3,2,1,0:T(8,128)(2,1)} %get-tuple-element.139), channel_id=1, source_target_pairs={{0,8},{8,0},{16,24},{24,16},{1,9},{9,1},{17,25},{25,17},{2,10},{10... | collective-permute-start | bytes 2801672 | tf_op jit(solution)/shard_map/ppermute | solution.py:515
  111.8 12.8 %collective-permute-start.19 = (bf16[3,608,128]{2,1,0:T(8,128)(2,1)S(1)}, bf16[3,608,128]{2,1,0:T(8,128)(2,1)S(1)}, u32[]{:S(2)}, u32[]{:S(2)}) collective-permute-start(bf16[3,608,128]{2,1,0:T(8,128)(2,1)S(1)} %fusion.17), channel_id=1, source_target_pairs={{0,16},{8,24},{16,0},{24,8},{1,17},{9,25},{17,1},{25,9},{2,18},{10... | collective-permute-start | bytes 1400840 | tf_op jit(solution)/shard_map/ppermute | solution.py:517
  125.7 26.9 %copy-start.7 = (bf16[3,608,128]{2,1,0:T(8,128)(2,1)}, bf16[3,608,128]{2,1,0:T(8,128)(2,1)S(1)}, u32[]{:S(2)}) copy-start(bf16[3,608,128]{2,1,0:T(8,128)(2,1)S(1)} %fusion.19.rest_0_) | copy-start | bytes 1400836
  125.7 13.6 %collective-permute-start.23 = (bf16[3,608,128]{2,1,0:T(8,128)(2,1)S(1)}, bf16[3,608,128]{2,1,0:T(8,128)(2,1)S(1)}, u32[]{:S(2)}, u32[]{:S(2)}) collective-permute-start(bf16[3,608,128]{2,1,0:T(8,128)(2,1)S(1)} %fusion.19.rest_0_), channel_id=1, source_target_pairs={{2,0},{4,2},{6,4},{7,6},{5,7},{3,5},{1,3},{0,1},{10,8},{12,10},{14... | collective-permute-start | bytes 1400840 | tf_op jit(solution)/shard_map/ppermute | solution.py:234
  127.8 11.9 %collective-permute-start.20 = (bf16[3,608,128]{2,1,0:T(8,128)(2,1)S(1)}, bf16[3,608,128]{2,1,0:T(8,128)(2,1)S(1)}, u32[]{:S(2)}, u32[]{:S(2)}) collective-permute-start(bf16[3,608,128]{2,1,0:T(8,128)(2,1)S(1)} %fusion.19.rest_0_), channel_id=1, source_target_pairs={{0,2},{2,4},{4,6},{6,7},{7,5},{5,3},{3,1},{1,0},{8,10},{10,12},{12... | collective-permute-start | bytes 1400840 | tf_op jit(solution)/shard_map/ppermute | solution.py:233
  139.3 13.3 %copy-start.10 = (bf16[3,608,128]{2,1,0:T(8,128)(2,1)}, bf16[3,608,128]{2,1,0:T(8,128)(2,1)S(1)}, u32[]{:S(2)}) copy-start(bf16[3,608,128]{2,1,0:T(8,128)(2,1)S(1)} %collective-permute-done.23.rest_2_) | copy-start | bytes 1400836
  139.3 11.3 %collective-permute-start.24 = (bf16[3,608,128]{2,1,0:T(8,128)(2,1)S(1)}, bf16[3,608,128]{2,1,0:T(8,128)(2,1)S(1)}, u32[]{:S(2)}, u32[]{:S(2)}) collective-permute-start(bf16[3,608,128]{2,1,0:T(8,128)(2,1)S(1)} %collective-permute-done.23.rest_2_), channel_id=1, source_target_pairs={{2,0},{4,2},{6,4},{7,6},{5,7},{3,5},{1,3},{0,1},{10,8},{12,10},{14... | collective-permute-start | bytes 1400840 | tf_op jit(solution)/shard_map/ppermute | solution.py:234
  139.7 12.9 %copy-start.11 = (bf16[3,608,128]{2,1,0:T(8,128)(2,1)}, bf16[3,608,128]{2,1,0:T(8,128)(2,1)S(1)}, u32[]{:S(2)}) copy-start(bf16[3,608,128]{2,1,0:T(8,128)(2,1)S(1)} %collective-permute-done.20.rest_1_) | copy-start | bytes 1400836
  139.8 11.1 %collective-permute-start.21 = (bf16[3,608,128]{2,1,0:T(8,128)(2,1)S(1)}, bf16[3,608,128]{2,1,0:T(8,128)(2,1)S(1)}, u32[]{:S(2)}, u32[]{:S(2)}) collective-permute-start(bf16[3,608,128]{2,1,0:T(8,128)(2,1)S(1)} %collective-permute-done.20.rest_1_), channel_id=1, source_target_pairs={{0,2},{2,4},{4,6},{6,7},{7,5},{5,3},{3,1},{1,0},{8,10},{10,12},{12... | collective-permute-start | bytes 1400840 | tf_op jit(solution)/shard_map/ppermute | solution.py:233
  150.6 2.1 %copy-start.12 = (bf16[3,608,128]{2,1,0:T(8,128)(2,1)}, bf16[3,608,128]{2,1,0:T(8,128)(2,1)S(1)}, u32[]{:S(2)}) copy-start(bf16[3,608,128]{2,1,0:T(8,128)(2,1)S(1)} %collective-permute-done.24.rest_4_) | copy-start | bytes 1400836
  150.6 10.5 %collective-permute-start.25 = (bf16[3,608,128]{2,1,0:T(8,128)(2,1)S(1)}, bf16[3,608,128]{2,1,0:T(8,128)(2,1)S(1)}, u32[]{:S(2)}, u32[]{:S(2)}) collective-permute-start(bf16[3,608,128]{2,1,0:T(8,128)(2,1)S(1)} %collective-permute-done.24.rest_4_), channel_id=1, source_target_pairs={{2,0},{4,2},{6,4},{7,6},{5,7},{3,5},{1,3},{0,1},{10,8},{12,10},{14... | collective-permute-start | bytes 1400840 | tf_op jit(solution)/shard_map/ppermute | solution.py:234
  150.9 1.8 copy-start.13
  150.9 10.2 %collective-permute-start.22 = (bf16[3,608,128]{2,1,0:T(8,128)(2,1)S(1)}, bf16[3,608,128]{2,1,0:T(8,128)(2,1)S(1)}, u32[]{:S(2)}, u32[]{:S(2)}) collective-permute-start(bf16[3,608,128]{2,1,0:T(8,128)(2,1)S(1)} %collective-permute-done.21.rest_3_), channel_id=1, source_target_pairs={{0,2},{2,4},{4,6},{6,7},{7,5},{5,3},{3,1},{1,0},{8,10},{10,12},{12... | collective-permute-start | bytes 1400840 | tf_op jit(solution)/shard_map/ppermute | solution.py:233
  161.1 15.4 %copy-start.2 = (bf16[32,384,128]{2,1,0:T(8,128)(2,1)S(1)}, bf16[32,384,128]{2,1,0:T(8,128)(2,1)}, u32[]{:S(2)}) copy-start(bf16[32,384,128]{2,1,0:T(8,128)(2,1)} %get-tuple-element.120.sq_ref) | copy-start | bytes 9437188
  161.1 0.8 copy-start.5
  161.9 0.8 copy-start.6
  164.6 11.9 %collective-permute-start.26 = (bf16[3,304,128]{2,1,0:T(8,128)(2,1)}, bf16[3,304,128]{2,1,0:T(8,128)(2,1)}, u32[]{:S(2)}, u32[]{:S(2)}) collective-permute-start(bf16[3,304,128]{2,1,0:T(8,128)(2,1)} %get-tuple-element.140), channel_id=1, source_target_pairs={{0,2},{2,4},{4,6},{6,7},{7,5},{5,3},{3,1},{1,0},{8,10},{10,12},{12... | collective-permute-start | bytes 700424 | tf_op jit(solution)/shard_map/ppermute | solution.py:240
  165.6 10.9 %collective-permute-start.27 = (bf16[3,304,128]{2,1,0:T(8,128)(2,1)}, bf16[3,304,128]{2,1,0:T(8,128)(2,1)}, u32[]{:S(2)}, u32[]{:S(2)}) collective-permute-start(bf16[3,304,128]{2,1,0:T(8,128)(2,1)} %get-tuple-element.141), channel_id=1, source_target_pairs={{2,0},{4,2},{6,4},{7,6},{5,7},{3,5},{1,3},{0,1},{10,8},{12,10},{14... | collective-permute-start | bytes 700424 | tf_op jit(solution)/shard_map/ppermute | solution.py:240
  182.9 1.3 copy-start.4

commit v6 on v5

--- a/solution.py
+++ b/solution.py
@@ -120,7 +120,7 @@
     shift = rows.bit_length() - 1
 
     def fill(out, lead, block, skip, groups):
-        def group_step(g, carry):
+        def one_group(g):
             base = pl.multiple_of(g * 16, 16)
             at = []
             for h in range(2):
@@ -142,9 +142,13 @@
                     value = pair[j, pl.ds(0, 16, stride=2), :] + pair[j, pl.ds(1, 16, stride=2), :]
                     out[lead, j, pl.ds(base, 16), :] = value.astype(BF16)
 
+        def turn(g, carry):
+            for i in range(per_turn):
+                one_group(g * per_turn + i)
             return carry
 
-        lax.fori_loop(0, groups, group_step, 0)
+        per_turn = 2 if groups % 2 == 0 else 1
+        lax.fori_loop(0, groups // per_turn, turn, 0)
 
     for dz in range(count_z):
         for dy in range(2):
@@ -223,42 +227,18 @@
     return [x] + [lax.ppermute(x, "img", flip(n_img, m)) for m in range(1, n_img)]
 
 
-def ring_gather(x, n_vol):
+def ring_gather(low, high, n_vol):
     ring = ring_of(n_vol)
     ahead = [(ring[p], ring[(p + 1) % n_vol]) for p in range(n_vol)]
     back = [(b, a) for a, b in ahead]
-    pieces = [x]
-    one = two = x
+    pieces = [low, high]
+    one = two = (low, high)
     for _ in range(1, n_vol // 2):
-        one = lax.ppermute(one, "vol", ahead)
-        two = lax.ppermute(two, "vol", back)
-        pieces += [one, two]
-
-    def farthest(after):
-        half = x.shape[1] // 2
-        low, high = halves(one, two, after)
-        return [lax.ppermute(low, "vol", ahead), lax.ppermute(high, "vol", back)]
-
-    return pieces, farthest
-
-
-def halves_kernel(one, two, after, low, high):
-    half = low.shape[1]
-    low[...] = one[:, :half]
-    high[...] = two[:, half:]
-
-
-def halves(one, two, after):
-    shape = jax.ShapeDtypeStruct((one.shape[0], one.shape[1] // 2, COLS), BF16)
-    return pl.pallas_call(
-        halves_kernel,
-        out_shape=[shape] * 2,
-        in_specs=[vmem(), vmem(), hbm()],
-        out_specs=[vmem()] * 2,
-        compiler_params=pltpu.CompilerParams(vmem_limit_bytes=VMEM_LIMIT),
-        cost_estimate=cost(1),
-        name="halves",
-    )(one, two, after)
+        one_low, two_low = lax.ppermute(one[0], "vol", ahead), lax.ppermute(two[0], "vol", back)
+        one_high, two_high = lax.ppermute(one[1], "vol", ahead), lax.ppermute(two[1], "vol", back)
+        one, two = (one_low, one_high), (two_low, two_high)
+        pieces += [*one, *two]
+    return pieces + [lax.ppermute(one[0], "vol", ahead), lax.ppermute(two[1], "vol", back)]
 
 
 def weigh_kernel(img_ref, sa_ref, ca_ref, sx_ref, cx_ref, nw_ref, wt_ref, sq_ref, buf):
@@ -513,9 +493,14 @@
 
 def to_member(keep, send, n_img):
     got = lax.ppermute(send, "img", flip(n_img, 1))
-    summed = [keep[m] + got[m] for m in range(n_img // 2)]
-    moved = [lax.ppermute(summed[m], "img", flip(n_img, 2 * m)) for m in range(1, n_img // 2)]
-    return sum(moved, summed[0])
+    half = keep.shape[2] // 2
+    owns = []
+    for h in range(2):
+        cut = slice(h * half, (h + 1) * half)
+        summed = [keep[m, :, cut] + got[m, :, cut] for m in range(n_img // 2)]
+        moved = [lax.ppermute(summed[m], "img", flip(n_img, 2 * m)) for m in range(1, n_img // 2)]
+        owns.append(sum(moved, summed[0]))
+    return owns
 
 
 HEAD = 8
@@ -525,37 +510,39 @@
     return lines_here + 2 * HEAD
 
 
-def insert_kernel(start, count, has_acc, mode, len_s, code_s, wgt_s, *rest):
+def insert_kernel(count, len_s, code_hbm, wgt_hbm, reg_hbm, *rest):
     pieces = rest[:count]
-    rest = rest[count:]
-    out_ref, acc, acc_odd, buf = rest[-4:]
-    extra = rest[:-4]
+    out_hbm = rest[count]
+    code_s, wgt_s, held, reg, out, acc, acc_odd, buf, sem_in, sem_piece, sem_out = rest[count + 1 :]
     both_acc = (acc, acc_odd)
-    comps, cap = buf.shape[:2]
+    cap = buf.shape[1]
+    half = cap // 2
     blocks = len_s.shape[0]
     lead = code_s.shape[0] // blocks
+    planes, lines_here = reg.shape[:2]
+    stride = line_stride(lines_here)
     slab = lax.axis_index("vol")
     place = jnp.where(slab & 1, blocks - 1 - (slab >> 1), slab >> 1)
-    if has_acc:
-        pltpu.sync_copy(extra[-1], acc)
-    else:
-        acc[...] = jnp.zeros_like(acc)
+    tables = [
+        pltpu.make_async_copy(code_hbm, code_s, sem_in.at[0]),
+        pltpu.make_async_copy(wgt_hbm, wgt_s, sem_in.at[1]),
+    ]
+    prior = pltpu.make_async_copy(reg_hbm, reg, sem_in.at[2])
+    loads = [
+        pltpu.make_async_copy(pieces[i], held.at[i], sem_piece.at[i]) for i in range(count)
+    ]
+    for copy in tables + loads + [prior]:
+        copy.start()
+    acc[...] = jnp.zeros_like(acc)
     acc_odd[...] = jnp.zeros_like(acc_odd)
     first = lax.broadcasted_iota(jnp.int32, (2, COLS), 0) == 0
-    index = 0
-    while index < count:
-        m = start + index
-        whole = pieces[index].shape[1] == cap
-        for c in range(comps):
-            if whole:
-                buf[c] = pieces[index][c].astype(F32)
-            else:
-                buf[c, : cap // 2, :] = pieces[index][c].astype(F32)
-                buf[c, cap // 2 :, :] = pieces[index + 1][c].astype(F32)
-        if whole:
-            index += 1
-        else:
-            index += 2
+    for copy in tables:
+        copy.wait()
+    for m in range(count // 2):
+        for h in range(2):
+            loads[2 * m + h].wait()
+            for c in range(3):
+                buf[c, h * half : (h + 1) * half, :] = held[2 * m + h, c].astype(F32)
         from_place = place + ((m + 1) // 2) * (-1 if m % 2 else 1)
         from_place = from_place & (blocks - 1)
         block = jnp.where(
@@ -571,56 +558,67 @@
                 w = wgt_s[at + u]
                 both = jnp.where(first, w, 1.0 - w)
                 into = both_acc[u % 2]
-                for c in range(comps):
+                for c in range(3):
                     row = jnp.broadcast_to(buf[c, pl.ds(s, 1), :], (2, COLS))
                     into[c, pl.ds(to, 2), :] = into[c, pl.ds(to, 2), :] + both * row
             return carry
 
         lax.fori_loop(0, (jnp.minimum(len_s[block, 0], cap) + 3) // 4, group_step, 0)
 
-    if mode == "sum":
-        acc[...] = acc[...] + acc_odd[...]
-        pltpu.sync_copy(acc, out_ref)
-        return
-    planes, lines_here = extra[0].shape[:2]
-    stride = line_stride(lines_here)
-
-    def plane_step(p, carry):
-        base = pl.multiple_of(p * stride + HEAD, 8)
-        total = [
-            acc[c, pl.ds(base, lines_here), :] + acc_odd[c, pl.ds(base, lines_here), :]
-            for c in range(3)
-        ]
-        inverse = 1.0 / (total[2] + extra[0][p])
-        out_ref[0, p] = total[0] * inverse
-        out_ref[1, p] = total[1] * inverse
-        return carry
-
-    lax.fori_loop(0, planes, plane_step, 0)
-
-
-def insert(tables, start, pieces, cap, block, mode, extra=(), acc=None):
-    comps = pieces[0].shape[0]
-    planes, lines_here = block
-    acc_shape = (comps, planes * line_stride(lines_here), COLS)
-    out = {
-        "sum": acc_shape,
-        "result": (2, planes, lines_here, COLS),
-    }[mode]
-    more = list(extra) + ([] if acc is None else [acc])
+    prior.wait()
+    chunks = sem_out.shape[0]
+    span = planes // chunks
+    stores = []
+    for i in range(chunks):
+
+        def plane_step(p, carry):
+            base = pl.multiple_of(p * stride + HEAD, 8)
+            total = [
+                acc[c, pl.ds(base, lines_here), :] + acc_odd[c, pl.ds(base, lines_here), :]
+                for c in range(3)
+            ]
+            inverse = 1.0 / (total[2] + reg[p])
+            out[0, p] = total[0] * inverse
+            out[1, p] = total[1] * inverse
+            return carry
+
+        lax.fori_loop(i * span, (i + 1) * span, plane_step, 0)
+        part = pl.ds(i * span, span)
+        stores.append(pltpu.make_async_copy(out.at[:, part], out_hbm.at[:, part], sem_out.at[i]))
+        stores[-1].start()
+    for copy in stores:
+        copy.wait()
+
+
+def insert(lengths, code, weights, pieces, regularizer):
+    half = pieces[0].shape[1]
+    planes, lines_here = regularizer.shape[:2]
+    count = len(pieces)
+    chunks = 4
+    acc = pltpu.VMEM((3, planes * line_stride(lines_here), COLS), F32)
+    result = (2, planes, lines_here, COLS)
     return pl.pallas_call(
-        partial(insert_kernel, start, len(pieces), acc is not None, mode),
-        out_shape=jax.ShapeDtypeStruct(out, F32),
-        in_specs=[smem()] * 3
-        + [vmem()] * (len(pieces) + len(extra))
-        + [hbm()] * (acc is not None),
-        out_specs=hbm() if mode == "sum" else vmem(),
-        scratch_shapes=[pltpu.VMEM(acc_shape, F32)] * 2
-        + [pltpu.VMEM((comps, cap, COLS), F32)],
+        partial(insert_kernel, count),
+        out_shape=jax.ShapeDtypeStruct(result, F32),
+        in_specs=[smem()] + [hbm()] * (3 + count),
+        out_specs=hbm(),
+        scratch_shapes=[
+            pltpu.SMEM(code.shape, jnp.int32),
+            pltpu.SMEM(weights.shape, F32),
+            pltpu.VMEM((count, 3, half, COLS), BF16),
+            pltpu.VMEM(regularizer.shape, F32),
+            pltpu.VMEM(result, F32),
+            acc,
+            acc,
+            pltpu.VMEM((3, 2 * half, COLS), F32),
+            pltpu.SemaphoreType.DMA((3,)),
+            pltpu.SemaphoreType.DMA((count,)),
+            pltpu.SemaphoreType.DMA((chunks,)),
+        ],
         compiler_params=pltpu.CompilerParams(vmem_limit_bytes=VMEM_LIMIT),
-        cost_estimate=cost(6),
-        name="insert_" + mode,
-    )(*tables, *pieces, *more)
+        cost_estimate=cost(9),
+        name="insert",
+    )(lengths, code, weights, regularizer, *pieces)
 
 
 def running(x):
@@ -831,17 +829,11 @@
     keep, send = project(
         src.reshape(-1), send_len, n_img, logits, cand, count_row, weighted, squared, cosine, sine, cap
     )
-    pieces, farthest = ring_gather(to_member(keep, send, n_img), n_vol)
-    tables = (recv_len, code.reshape(-1), wgt.reshape(-1))
-    block = (planes_here, lines_here)
-    early = n_vol - 3
-    late = n_vol - 1
-    part_sum = insert(tables, 0, pieces[:early], cap, block, "sum")
-    last = farthest(part_sum)
-    most_sum = insert(tables, early, pieces[early:], cap, block, "sum", acc=part_sum)
+    low, high = to_member(keep, send, n_img)
+    pieces = ring_gather(low, high, n_vol)
 
     def listed():
-        return insert(tables, late, last, cap, block, "result", [regularizer], most_sum)
+        return insert(recv_len, code.reshape(-1), wgt.reshape(-1), pieces, regularizer)
 
     def dense():
         return dense_path(

time: 193 us -> 185 us (0.959)
  Pallas kernels: 75.6 us -> 60.7 us
  starting transfers between devices: 29.4 us -> 36.3 us
    pallas_call x4 -> x1, Pallas kernels: 24.6 us -> 10.4 us  [insert(): pl.pallas_call(partial(insert_kernel, count), out_shape=jax.ShapeDtypeStr...]
    ppermute x8 -> x14, starting transfers between devices: 9.55 us -> 15.6 us  [the longest x4 7.56 us: ring_gather(): lax.ppermute(one[0], 'vol', ahead)]
    ppermute x8 -> x14, waiting for transfers between devices: 19.4 us -> 21 us  [the longest x4 13.4 us: ring_gather(): lax.ppermute(two[1], 'vol', back)]
    unnamed x68 -> x66, local copies, waits for them, and re-layouts: 4.51 us -> 3.05 us
    ppermute x1 -> x2, waiting for transfers between devices: 11.8 us -> 10.7 us  [to_member(): lax.ppermute(summed[m], 'img', flip(n_img, 2 * m))]
  transfers between devices with their start and end apart: 28 -> 35, of which waited for: 13 -> 21; matrix products, arithmetic and copies ran while one was open for 5% -> 5% of each run, Pallas kernels for 16% -> 7%
where the time goes in v6:
time: 185 us; the launch traced here: 184 us
  Pallas kernels  60.7 us (33%)
  waiting for transfers between devices  55.7 us (30%)
  starting transfers between devices  36.3 us (20%)
  between operations  14.4 us (8%)
  other arithmetic  8.48 us (5%)
  local copies, waits for them, and re-layouts  7.98 us (4%)
    pallas_call x1, Pallas kernels, extract(): pl.pallas_call(partial(extract_kernel, rows, planes_here), out_shape=[sha...  14.1 us
    ppermute x4, waiting for transfers between devices, ring_gather(): lax.ppermute(two[1], 'vol', back)  13.4 us
    pallas_call x1, Pallas kernels, project(): pl.pallas_call(project_kernel, grid=(rows // inner,), out_shape=[jax.Shap...  11.3 us
    ppermute x3, waiting for transfers between devices, to_pixel_rows(): lax.ppermute(sums_a[d], 'vol', along_z(n_vol, d))  10.7 us
    ppermute x2, waiting for transfers between devices, to_member(): lax.ppermute(summed[m], 'img', flip(n_img, 2 * m))  10.7 us
    pallas_call x1, Pallas kernels, insert(): pl.pallas_call(partial(insert_kernel, count), out_shape=jax.ShapeDtypeStr...  10.4 us
    pallas_call x1, Pallas kernels, candidate_logits(): pl.pallas_call(logits_kernel, grid=(rows // inner,), out_shape=jax.ShapeD...  8.6 us
    pallas_call x1, Pallas kernels, weigh(): pl.pallas_call(weigh_kernel, grid=(count // step,), out_shape=[jax.ShapeD...  8.42 us
  transfers between devices with their start and end apart: 35, of which 21 were waited for; matrix products, arithmetic and copies ran while one was open for 5% of the time, Pallas kernels for 7%

profile of v6, /device:TPU:12, one launch (start us, length us, event | category | flops | bytes accessed | tf_op | source)
XLA Modules:
  0.0 183.7 jit_solution(8070314624744296457)
XLA Ops:
  6.5 14.1 %extract.1 = (bf16[4,2,352,128]{3,2,1,0:T(8,128)(2,1)}, bf16[4,2,352,128]{3,2,1,0:T(8,128)(2,1)}, bf16[2,2,160,128]{3,2,1,0:T(8,128)(2,1)}, bf16[2,2,160,128]{3,...) custom-call(s32[64,256]{1,0:T(8,128)} %refs_0_.1, s32[64,256]{1,0:T(8,128)} %refs_1_.1, ...), custom_call_target="tpu_custom_call" | custom-call | bytes 40590000 | tf_op jit(solution)/shard_map/extract/pallas_call | solution.py:167
  20.9 1.8 collective-permute-start.3
  22.7 2.0 %collective-permute-start = (bf16[4,2,352,128]{3,2,1,0:T(8,128)(2,1)}, bf16[4,2,352,128]{3,2,1,0:T(8,128)(2,1)S(1)}, u32[]{:S(2)}, u32[]{:S(2)}) collective-permute-start(bf16[4,2,352,128]{3,2,1,0:T(8,128)(2,1)} %get-tuple-element.160), channel_id=1, source_target_pairs={{0,1},{1,0},{2,3},{3,2},{4,5},{5,4},{6,7},{7,6},{8,9},{9,8},{10,11... | collective-permute-start | bytes 2162696 | tf_op jit(solution)/shard_map/ppermute | solution.py:206
  24.8 1.5 multiply_cosine_fusion
  26.3 1.5 fusion.23
  27.9 8.4 %weigh.1 = (bf16[32,384,256]{2,1,0:T(8,128)(2,1)S(1)}, bf16[32,384,128]{2,1,0:T(8,128)(2,1)}) custom-call(bf16[2,384,32,128]{3,2,1,0:T(8,128)(2,1)} %img_ref.1, f32[384,32]{1,0:T(8,128)} %get-tuple-element.286.sa_ref, f32[384,32]{1,0:T(8,128)} %get-tuple-element.285.ca_ref, f32[384,128]{1,0:T(8,128)} %get-tuple-element.284.sx_ref, ...), custom_call_target="tpu_custom_call" | custom-call | bytes 44280000 | tf_op jit(solution)/shard_map/weigh/pallas_call | solution.py:269
  36.4 4.3 %collective-permute-done.got_a = bf16[4,2,352,128]{3,2,1,0:T(8,128)(2,1)S(1)} collective-permute-done((bf16[4,2,352,128]{3,2,1,0:T(8,128)(2,1)}, bf16[4,2,352,128]{3,2,1,0:T(8,128)(2,1)S(1)}, u32[]{:S(2)}, u32[]{:S(2)}) %collective-permute-start) | collective-permute-done | bytes 720928 | tf_op jit(solution)/shard_map/ppermute | solution.py:206
  40.8 0.9 copy-done.5
  41.6 2.7 %combine_first.1 = (bf16[2,352,128]{2,1,0:T(8,128)(2,1)}, bf16[2,352,128]{2,1,0:T(8,128)(2,1)}, bf16[2,352,128]{2,1,0:T(8,128)(2,1)}, bf16[2,352,128]{2,1,0:T(8,...) custom-call(bf16[4,2,352,128]{3,2,1,0:T(8,128)(2,1)} %get-tuple-element.159.keep_a, ...), custom_call_target="tpu_custom_call" | custom-call | bytes 11070000 | tf_op jit(solution)/shard_map/combine_first/pallas_call | solution.py:209
  44.3 1.7 collective-permute-start.7
  46.0 0.5 collective-permute-start.4
  46.5 4.4 %collective-permute-start.5 = (bf16[2,352,128]{2,1,0:T(8,128)(2,1)}, bf16[2,352,128]{2,1,0:T(8,128)(2,1)S(1)}, u32[]{:S(2)}, u32[]{:S(2)}) collective-permute-start(bf16[2,352,128]{2,1,0:T(8,128)(2,1)} %get-tuple-element.167), channel_id=1, source_target_pairs={{0,4},{1,5},{2,6},{3,7},{4,0},{5,1},{6,2},{7,3},{8,12},{9,13},{10,... | collective-permute-start | bytes 540680 | tf_op jit(solution)/shard_map/ppermute | solution.py:220
  51.0 0.9 add.185.rest_2_
  52.0 1.6 collective-permute-start.11
  53.6 0.6 collective-permute-done.4
  54.3 7.2 %collective-permute-done.5 = bf16[2,352,128]{2,1,0:T(8,128)(2,1)S(1)} collective-permute-done((bf16[2,352,128]{2,1,0:T(8,128)(2,1)}, bf16[2,352,128]{2,1,0:T(8,128)(2,1)S(1)}, u32[]{:S(2)}, u32[]{:S(2)}) %collective-permute-start.5) | collective-permute-done | bytes 180256 | tf_op jit(solution)/shard_map/ppermute | solution.py:220
  61.4 3.0 %collective-permute-done.6 = bf16[2,352,128]{2,1,0:T(8,128)(2,1)S(1)} collective-permute-done((bf16[2,352,128]{2,1,0:T(8,128)(2,1)}, bf16[2,352,128]{2,1,0:T(8,128)(2,1)S(1)}, u32[]{:S(2)}, u32[]{:S(2)}) %collective-permute-start.6) | collective-permute-done | bytes 180256 | tf_op jit(solution)/shard_map/ppermute | solution.py:220
  64.4 1.0 add_add_fusion.rest_1_
  65.5 0.7 collective-permute-start.10
  66.2 1.2 collective-permute-start.8
  67.3 0.3 fusion.25
  67.8 0.7 reshape.231.wgt_ref
  68.6 0.7 reshape.230.line_ref
  69.4 0.7 reshape.229.plane_ref
  70.1 5.3 %lists.1 = (s32[32,128]{1,0:T(8,128)}, s32[64,128]{1,0:T(8,128)S(1)}, f32[64,128]{1,0:T(8,128)}, s32[8,128]{1,0:T(8,128)}, s32[8,128]{1,0:T(8,128)}, /*index=5*/s32[8,128]{1,0:T(8,128)}) custom-call(s32[8,2048]{1,0:T(8,128)} %reshape.229.plane_ref, s32[8,2048]{1,0:T(8,128)} %reshape.230.line_ref, f32[8,2048]{1,0:T(8,128)} %reshape.231.wgt_ref), custom_call_target="tpu_custom_call" | custom-call | bytes 22140000 | tf_op jit(solution)/shard_map/lists/pallas_call | solution.py:724
  75.5 0.6 copy-done.31
  76.2 8.6 %logits.1 = f32[32,384]{1,0:T(8,128)} custom-call(bf16[32,384,256]{2,1,0:T(8,128)(2,1)} %copy-done, bf16[32,384,128]{2,1,0:T(8,128)(2,1)} %get-tuple-element.157.sq_ref, f32[4,32,128]{2,1,0:T(8,128)S(1)} %get-tuple-element.282.cos_ref, f32[4,32,128]{2,1,0:T(8,128)S(1)} %get-tuple-element.281.sin_ref, s32[8,384]{1,0:T(8,128)S(1)} %bitcast.101, ...), custom_call_target="tpu_custom_call" | custom-call | bytes 29520000 | tf_op jit(solution)/shard_map/logits/pallas_call | solution.py:361
  84.8 0.6 collective-permute-start.14
  85.4 3.7 %collective-permute-done.14 = f32[32,384]{1,0:T(8,128)S(1)} collective-permute-done((f32[32,384]{1,0:T(8,128)}, f32[32,384]{1,0:T(8,128)S(1)}, u32[]{:S(2)}, u32[]{:S(2)}) %collective-permute-start.14) | collective-permute-done | bytes 49184 | tf_op jit(solution)/shard_map/ppermute | solution.py:824
  89.1 0.8 add.186.rest_0_
  90.0 1.1 collective-permute-start.16
  91.1 2.5 %collective-permute-start.15 = (f32[32,384]{1,0:T(8,128)S(1)}, f32[32,384]{1,0:T(8,128)S(1)}, u32[]{:S(2)}, u32[]{:S(2)}) collective-permute-start(f32[32,384]{1,0:T(8,128)S(1)} %add.186.rest_0_), channel_id=1, source_target_pairs={{0,2},{1,3},{2,4},{3,5},{4,6},{5,7},{6,0},{7,1},{8,10},{9,11},{10,... | collective-permute-start | bytes 147464 | tf_op jit(solution)/shard_map/ppermute | solution.py:826
  93.6 0.5 collective-permute-done.17.rest_3_
  94.1 1.3 collective-permute-done.16.rest_2_
  95.4 0.6 collective-permute-done.15.rest_1_
  96.1 11.3 %project.1 = (bf16[2,3,608,128]{3,2,1,0:T(8,128)(2,1)}, bf16[2,3,608,128]{3,2,1,0:T(8,128)(2,1)}) custom-call(s32[4096]{0:T(1024)} %bitcast.108, s32[8,128]{1,0:T(8,128)} %get-tuple-element.174.len_s, s32[8,384]{1,0:T(8,128)S(1)} %bitcast.102, s32[1,384]{1,0:T(1,128)S(1)} %broadcast_in_dim.13.cnt_ref, bf16[32,384,256]{2,1,0:T(8,128)(2,1)S(1)} %bitcast.88, ...), custom_call_target="tpu_custom_call" | custom-call | bytes 44280000 | tf_op jit(solution)/shard_map/project/pallas_call | solution.py:466
  107.4 2.7 %collective-permute-done.18 = bf16[2,3,608,128]{3,2,1,0:T(8,128)(2,1)S(1)} collective-permute-done((bf16[2,3,608,128]{3,2,1,0:T(8,128)(2,1)}, bf16[2,3,608,128]{3,2,1,0:T(8,128)(2,1)S(1)}, u32[]{:S(2)}, u32[]{:S(2)}) %collective-permute-start.18) | collective-permute-done | bytes 933920 | tf_op jit(solution)/shard_map/ppermute | solution.py:495
  110.1 1.1 fusion.17
  111.3 1.2 collective-permute-start.20
  112.5 0.9 collective-permute-start.19
  113.4 6.5 %collective-permute-done.20 = bf16[3,304,128]{2,1,0:T(8,128)(2,1)S(1)} collective-permute-done((bf16[3,304,128]{2,1,0:T(8,128)(2,1)S(1)}, bf16[3,304,128]{2,1,0:T(8,128)(2,1)S(1)}, u32[]{:S(2)}, u32[]{:S(2)}) %collective-permute-start.20) | collective-permute-done | bytes 233504 | tf_op jit(solution)/shard_map/ppermute | solution.py:501
  119.9 4.2 %collective-permute-done.19 = bf16[3,304,128]{2,1,0:T(8,128)(2,1)S(1)} collective-permute-done((bf16[3,304,128]{2,1,0:T(8,128)(2,1)S(1)}, bf16[3,304,128]{2,1,0:T(8,128)(2,1)S(1)}, u32[]{:S(2)}, u32[]{:S(2)}) %collective-permute-start.19) | collective-permute-done | bytes 233504 | tf_op jit(solution)/shard_map/ppermute | solution.py:501
  124.1 1.1 fusion.19
  125.3 1.6 collective-permute-start.24
  126.8 1.8 collective-permute-start.21
  128.7 2.0 %collective-permute-start.22 = (bf16[3,304,128]{2,1,0:T(8,128)(2,1)S(1)}, bf16[3,304,128]{2,1,0:T(8,128)(2,1)S(1)}, u32[]{:S(2)}, u32[]{:S(2)}) collective-permute-start(bf16[3,304,128]{2,1,0:T(8,128)(2,1)S(1)} %get-tuple-element.277), channel_id=1, source_target_pairs={{0,2},{2,4},{4,6},{6,7},{7,5},{5,3},{3,1},{1,0},{8,10},{10,12},{12... | collective-permute-start | bytes 700424 | tf_op jit(solution)/shard_map/ppermute | solution.py:238
  130.7 4.5 %collective-permute-done.24 = bf16[3,304,128]{2,1,0:T(8,128)(2,1)S(1)} collective-permute-done((bf16[3,304,128]{2,1,0:T(8,128)(2,1)S(1)}, bf16[3,304,128]{2,1,0:T(8,128)(2,1)S(1)}, u32[]{:S(2)}, u32[]{:S(2)}) %collective-permute-start.24) | collective-permute-done | bytes 233504 | tf_op jit(solution)/shard_map/ppermute | solution.py:238
  135.5 1.8 %collective-permute-start.25 = (bf16[3,304,128]{2,1,0:T(8,128)(2,1)S(1)}, bf16[3,304,128]{2,1,0:T(8,128)(2,1)S(1)}, u32[]{:S(2)}, u32[]{:S(2)}) collective-permute-start(bf16[3,304,128]{2,1,0:T(8,128)(2,1)S(1)} %collective-permute-done.21), channel_id=1, source_target_pairs={{0,2},{2,4},{4,6},{6,7},{7,5},{5,3},{3,1},{1,0},{8,10},{10,12},{12... | collective-permute-start | bytes 700424 | tf_op jit(solution)/shard_map/ppermute | solution.py:237
  137.3 3.2 %collective-permute-done.22 = bf16[3,304,128]{2,1,0:T(8,128)(2,1)S(1)} collective-permute-done((bf16[3,304,128]{2,1,0:T(8,128)(2,1)S(1)}, bf16[3,304,128]{2,1,0:T(8,128)(2,1)S(1)}, u32[]{:S(2)}, u32[]{:S(2)}) %collective-permute-start.22) | collective-permute-done | bytes 233504 | tf_op jit(solution)/shard_map/ppermute | solution.py:238
  140.5 1.8 %collective-permute-start.26 = (bf16[3,304,128]{2,1,0:T(8,128)(2,1)S(1)}, bf16[3,304,128]{2,1,0:T(8,128)(2,1)S(1)}, u32[]{:S(2)}, u32[]{:S(2)}) collective-permute-start(bf16[3,304,128]{2,1,0:T(8,128)(2,1)S(1)} %collective-permute-done.22), channel_id=1, source_target_pairs={{0,2},{2,4},{4,6},{6,7},{7,5},{5,3},{3,1},{1,0},{8,10},{10,12},{12... | collective-permute-start | bytes 700424 | tf_op jit(solution)/shard_map/ppermute | solution.py:238
  142.6 2.6 %collective-permute-done.28 = bf16[3,304,128]{2,1,0:T(8,128)(2,1)S(1)} collective-permute-done((bf16[3,304,128]{2,1,0:T(8,128)(2,1)S(1)}, bf16[3,304,128]{2,1,0:T(8,128)(2,1)S(1)}, u32[]{:S(2)}, u32[]{:S(2)}) %collective-permute-start.28) | collective-permute-done | bytes 233504 | tf_op jit(solution)/shard_map/ppermute | solution.py:238
  145.5 1.9 %collective-permute-start.29 = (bf16[3,304,128]{2,1,0:T(8,128)(2,1)S(1)}, bf16[3,304,128]{2,1,0:T(8,128)(2,1)S(1)}, u32[]{:S(2)}, u32[]{:S(2)}) collective-permute-start(bf16[3,304,128]{2,1,0:T(8,128)(2,1)S(1)} %collective-permute-done.25), channel_id=1, source_target_pairs={{0,2},{2,4},{4,6},{6,7},{7,5},{5,3},{3,1},{1,0},{8,10},{10,12},{12... | collective-permute-start | bytes 700424 | tf_op jit(solution)/shard_map/ppermute | solution.py:237
  147.3 3.1 %collective-permute-done.26 = bf16[3,304,128]{2,1,0:T(8,128)(2,1)S(1)} collective-permute-done((bf16[3,304,128]{2,1,0:T(8,128)(2,1)S(1)}, bf16[3,304,128]{2,1,0:T(8,128)(2,1)S(1)}, u32[]{:S(2)}, u32[]{:S(2)}) %collective-permute-start.26) | collective-permute-done | bytes 233504 | tf_op jit(solution)/shard_map/ppermute | solution.py:238
  150.5 1.8 %collective-permute-start.30 = (bf16[3,304,128]{2,1,0:T(8,128)(2,1)S(1)}, bf16[3,304,128]{2,1,0:T(8,128)(2,1)S(1)}, u32[]{:S(2)}, u32[]{:S(2)}) collective-permute-start(bf16[3,304,128]{2,1,0:T(8,128)(2,1)S(1)} %collective-permute-done.26), channel_id=1, source_target_pairs={{0,2},{2,4},{4,6},{6,7},{7,5},{5,3},{3,1},{1,0},{8,10},{10,12},{12... | collective-permute-start | bytes 700424 | tf_op jit(solution)/shard_map/ppermute | solution.py:238
  152.5 3.5 %collective-permute-done.32 = bf16[3,304,128]{2,1,0:T(8,128)(2,1)S(1)} collective-permute-done((bf16[3,304,128]{2,1,0:T(8,128)(2,1)S(1)}, bf16[3,304,128]{2,1,0:T(8,128)(2,1)S(1)}, u32[]{:S(2)}, u32[]{:S(2)}) %collective-permute-start.32) | collective-permute-done | bytes 233504 | tf_op jit(solution)/shard_map/ppermute | solution.py:238
  156.0 2.0 %collective-permute-start.33 = (bf16[3,304,128]{2,1,0:T(8,128)(2,1)S(1)}, bf16[3,304,128]{2,1,0:T(8,128)(2,1)S(1)}, u32[]{:S(2)}, u32[]{:S(2)}) collective-permute-start(bf16[3,304,128]{2,1,0:T(8,128)(2,1)S(1)} %collective-permute-done.29), channel_id=1, source_target_pairs={{0,2},{2,4},{4,6},{6,7},{7,5},{5,3},{3,1},{1,0},{8,10},{10,12},{12... | collective-permute-start | bytes 700424 | tf_op jit(solution)/shard_map/ppermute | solution.py:241
  158.0 1.3 slice.45
  159.9 0.6 collective-permute-done.30
  160.5 0.5 collective-permute-done.31
  161.0 2.8 %collective-permute-done.34 = bf16[3,304,128]{2,1,0:T(8,128)(2,1)S(1)} collective-permute-done((bf16[3,304,128]{2,1,0:T(8,128)(2,1)S(1)}, bf16[3,304,128]{2,1,0:T(8,128)(2,1)S(1)}, u32[]{:S(2)}, u32[]{:S(2)}) %collective-permute-start.34) | collective-permute-done | bytes 233504 | tf_op jit(solution)/shard_map/ppermute | solution.py:241
  163.8 11.7 %conditional.1 = (f32[2,32,64,128]{3,2,1,0:T(8,128)S(1)}) conditional(s32[]{:T(128)} %bitcast.20, (s32[]{:T(128)}, s32[64,256]{1,0:T(8,128)}, s32[]{:T(128)}, s32[64,256]{1,0:T(8,128)}, f32[64,256]{1,0:T(8,128)}, /*index=5*/f32[4,32,128]{2,1,0:T(8,128)S(1)}, s32[8,384]{1,0:T(8,128)S(1)}, s32[1,384]{1,0:T(1,128)}, f32[32,384]{1,0:T(8,128)}, ...), branch_computations={%region_0.10_spmd, %region_10.11_spmd} | conditional | flops 1831321088 | bytes 333904320 | solution.py:844
  163.9 0.6 copy-done.20
  165.1 10.4 %insert.1 = f32[2,32,64,128]{3,2,1,0:T(8,128)S(1)} custom-call(s32[8,128]{1,0:T(8,128)} %get-tuple-element.113.len_s, s32[8192]{0:T(1024)S(1)} %bitcast.100, f32[8192]{0:T(1024)} %bitcast.107, f32[32,64,128]{2,1,0:T(8,128)S(1)} %get-tuple-element.116.reg_hbm, bf16[3,304,128]{2,1,0:T(8,128)(2,1)} %get-tuple-element.117.rest_0_, ...), custom_call_target="tpu_custom_call" | custom-call | bytes 33210000 | tf_op jit(solution)/shard_map/cond/branch_1_fun/insert/pallas_call | solution.py:600
  175.5 1.3 copy-done.3
  (120 shorter events, 2.9 us)
Async XLA Ops:
  6.5 18.3 %copy-start.40 = (f32[384]{0:T(512)S(1)}, f32[384]{0:T(512)}, u32[]{:S(2)}) copy-start(f32[384]{0:T(512)} %param.13) | copy-start | bytes 4612
  20.6 15.8 %collective-permute-start.1 = (bf16[2,2,160,128]{3,2,1,0:T(8,128)(2,1)}, bf16[2,2,160,128]{3,2,1,0:T(8,128)(2,1)S(1)}, u32[]{:S(2)}, u32[]{:S(2)}) collective-permute-start(bf16[2,2,160,128]{3,2,1,0:T(8,128)(2,1)} %get-tuple-element.162), channel_id=1, source_target_pairs={{0,2},{1,3},{2,4},{3,5},{4,6},{5,7},{6,0},{7,1},{8,10},{9,11},{10,... | collective-permute-start | bytes 491528 | tf_op jit(solution)/shard_map/ppermute | solution.py:205
  20.7 15.7 %collective-permute-start.2 = (bf16[2,2,160,128]{3,2,1,0:T(8,128)(2,1)}, bf16[2,2,160,128]{3,2,1,0:T(8,128)(2,1)S(1)}, u32[]{:S(2)}, u32[]{:S(2)}) collective-permute-start(bf16[2,2,160,128]{3,2,1,0:T(8,128)(2,1)} %get-tuple-element.163), channel_id=1, source_target_pairs={{0,4},{1,5},{2,6},{3,7},{4,0},{5,1},{6,2},{7,3},{8,12},{9,13},{10,... | collective-permute-start | bytes 491528 | tf_op jit(solution)/shard_map/ppermute | solution.py:205
  20.9 15.5 %collective-permute-start.3 = (bf16[2,2,160,128]{3,2,1,0:T(8,128)(2,1)}, bf16[2,2,160,128]{3,2,1,0:T(8,128)(2,1)S(1)}, u32[]{:S(2)}, u32[]{:S(2)}) collective-permute-start(bf16[2,2,160,128]{3,2,1,0:T(8,128)(2,1)} %get-tuple-element.164), channel_id=1, source_target_pairs={{0,6},{1,7},{2,0},{3,1},{4,2},{5,3},{6,4},{7,5},{8,14},{9,15},{10,... | collective-permute-start | bytes 491528 | tf_op jit(solution)/shard_map/ppermute | solution.py:205
  22.7 18.1 %collective-permute-start = (bf16[4,2,352,128]{3,2,1,0:T(8,128)(2,1)}, bf16[4,2,352,128]{3,2,1,0:T(8,128)(2,1)S(1)}, u32[]{:S(2)}, u32[]{:S(2)}) collective-permute-start(bf16[4,2,352,128]{3,2,1,0:T(8,128)(2,1)} %get-tuple-element.160), channel_id=1, source_target_pairs={{0,1},{1,0},{2,3},{3,2},{4,5},{5,4},{6,7},{7,6},{8,9},{9,8},{10,11... | collective-permute-start | bytes 2162696 | tf_op jit(solution)/shard_map/ppermute | solution.py:206
  36.3 4.4 %copy-start = (bf16[32,384,256]{2,1,0:T(8,128)(2,1)}, bf16[32,384,256]{2,1,0:T(8,128)(2,1)S(1)}, u32[]{:S(2)}) copy-start(bf16[32,384,256]{2,1,0:T(8,128)(2,1)S(1)} %get-tuple-element.156.rest_3_.wt_ref) | copy-start | bytes 18874372
  36.3 31.3 %copy-start.12 = (f32[64,256]{1,0:T(8,128)S(1)}, f32[64,256]{1,0:T(8,128)}, u32[]{:S(2)}) copy-start(f32[64,256]{1,0:T(8,128)} %refs_2_.1) | copy-start | bytes 196612
  36.3 32.2 %copy-start.10 = (s32[64,256]{1,0:T(8,128)S(1)}, s32[64,256]{1,0:T(8,128)}, u32[]{:S(2)}) copy-start(s32[64,256]{1,0:T(8,128)} %refs_1_.1) | copy-start | bytes 196612
  36.3 33.0 %copy-start.8 = (s32[64,256]{1,0:T(8,128)S(1)}, s32[64,256]{1,0:T(8,128)}, u32[]{:S(2)}) copy-start(s32[64,256]{1,0:T(8,128)} %refs_0_.1) | copy-start | bytes 196612
  36.3 39.9 %copy-start.37 = (s32[384,8]{0,1:T(8,128)S(1)}, s32[384,8]{0,1:T(8,128)}, u32[]{:S(2)}) copy-start(s32[384,8]{0,1:T(8,128)} %param.14) | copy-start | bytes 36868
  36.4 4.4 %copy-start.34 = (bf16[2,2,160,128]{3,2,1,0:T(8,128)(2,1)}, bf16[2,2,160,128]{3,2,1,0:T(8,128)(2,1)S(1)}, u32[]{:S(2)}) copy-start(bf16[2,2,160,128]{3,2,1,0:T(8,128)(2,1)S(1)} %collective-permute-done.1.rest_0_) | copy-start | bytes 491524
  36.4 4.4 %copy-start.35 = (bf16[2,2,160,128]{3,2,1,0:T(8,128)(2,1)}, bf16[2,2,160,128]{3,2,1,0:T(8,128)(2,1)S(1)}, u32[]{:S(2)}) copy-start(bf16[2,2,160,128]{3,2,1,0:T(8,128)(2,1)S(1)} %collective-permute-done.2.rest_1_) | copy-start | bytes 491524
  36.4 4.3 %copy-start.36 = (bf16[2,2,160,128]{3,2,1,0:T(8,128)(2,1)}, bf16[2,2,160,128]{3,2,1,0:T(8,128)(2,1)S(1)}, u32[]{:S(2)}) copy-start(bf16[2,2,160,128]{3,2,1,0:T(8,128)(2,1)S(1)} %collective-permute-done.3.rest_2_) | copy-start | bytes 491524
  44.3 6.7 %collective-permute-start.7 = (bf16[2,160,128]{2,1,0:T(8,128)(2,1)}, bf16[2,160,128]{2,1,0:T(8,128)(2,1)S(1)}, u32[]{:S(2)}, u32[]{:S(2)}) collective-permute-start(bf16[2,160,128]{2,1,0:T(8,128)(2,1)} %get-tuple-element.170), channel_id=1, source_target_pairs={{0,1},{1,0},{2,3},{3,2},{4,5},{5,4},{6,7},{7,6},{8,9},{9,8},{10,11... | collective-permute-start | bytes 245768 | tf_op jit(solution)/shard_map/ppermute | solution.py:219
  46.0 8.2 %collective-permute-start.4 = (bf16[2,352,128]{2,1,0:T(8,128)(2,1)}, bf16[2,352,128]{2,1,0:T(8,128)(2,1)S(1)}, u32[]{:S(2)}, u32[]{:S(2)}) collective-permute-start(bf16[2,352,128]{2,1,0:T(8,128)(2,1)} %get-tuple-element.166), channel_id=1, source_target_pairs={{0,2},{1,3},{2,4},{3,5},{4,6},{5,7},{6,0},{7,1},{8,10},{9,11},{10,... | collective-permute-start | bytes 540680 | tf_op jit(solution)/shard_map/ppermute | solution.py:220
  46.5 14.9 %collective-permute-start.5 = (bf16[2,352,128]{2,1,0:T(8,128)(2,1)}, bf16[2,352,128]{2,1,0:T(8,128)(2,1)S(1)}, u32[]{:S(2)}, u32[]{:S(2)}) collective-permute-start(bf16[2,352,128]{2,1,0:T(8,128)(2,1)} %get-tuple-element.167), channel_id=1, source_target_pairs={{0,4},{1,5},{2,6},{3,7},{4,0},{5,1},{6,2},{7,3},{8,12},{9,13},{10,... | collective-permute-start | bytes 540680 | tf_op jit(solution)/shard_map/ppermute | solution.py:220
  51.0 13.4 %collective-permute-start.6 = (bf16[2,352,128]{2,1,0:T(8,128)(2,1)}, bf16[2,352,128]{2,1,0:T(8,128)(2,1)S(1)}, u32[]{:S(2)}, u32[]{:S(2)}) collective-permute-start(bf16[2,352,128]{2,1,0:T(8,128)(2,1)} %get-tuple-element.168), channel_id=1, source_target_pairs={{0,6},{1,7},{2,0},{3,1},{4,2},{5,3},{6,4},{7,5},{8,14},{9,15},{10,... | collective-permute-start | bytes 540680 | tf_op jit(solution)/shard_map/ppermute | solution.py:220
  52.0 23.5 %copy-start.13 = (bf16[2,160,128]{2,1,0:T(8,128)(2,1)}, bf16[2,160,128]{2,1,0:T(8,128)(2,1)S(1)}, u32[]{:S(2)}) copy-start(bf16[2,160,128]{2,1,0:T(8,128)(2,1)S(1)} %add.185.rest_2_) | copy-start | bytes 245764
  52.0 14.2 %collective-permute-start.13 = (bf16[2,160,128]{2,1,0:T(8,128)(2,1)S(1)}, bf16[2,160,128]{2,1,0:T(8,128)(2,1)S(1)}, u32[]{:S(2)}, u32[]{:S(2)}) collective-permute-start(bf16[2,160,128]{2,1,0:T(8,128)(2,1)S(1)} %add.185.rest_2_), channel_id=1, source_target_pairs={{0,24},{8,16},{16,8},{24,0},{1,25},{9,17},{17,9},{25,1},{2,26},{10... | collective-permute-start | bytes 245768 | tf_op jit(solution)/shard_map/ppermute | solution.py:227
  52.0 23.3 %collective-permute-start.11 = (bf16[2,160,128]{2,1,0:T(8,128)(2,1)S(1)}, bf16[2,160,128]{2,1,0:T(8,128)(2,1)}, u32[]{:S(2)}, u32[]{:S(2)}) collective-permute-start(bf16[2,160,128]{2,1,0:T(8,128)(2,1)S(1)} %add.185.rest_2_), channel_id=1, source_target_pairs={{0,16},{8,24},{16,0},{24,8},{1,17},{9,25},{17,1},{25,9},{2,18},{10... | collective-permute-start | bytes 245768 | tf_op jit(solution)/shard_map/ppermute | solution.py:227
  54.3 21.1 %collective-permute-start.9 = (bf16[2,160,128]{2,1,0:T(8,128)(2,1)S(1)}, bf16[2,160,128]{2,1,0:T(8,128)(2,1)}, u32[]{:S(2)}, u32[]{:S(2)}) collective-permute-start(bf16[2,160,128]{2,1,0:T(8,128)(2,1)S(1)} %add.185.rest_2_), channel_id=1, source_target_pairs={{0,8},{8,0},{16,24},{24,16},{1,9},{9,1},{17,25},{25,17},{2,10},{10... | collective-permute-start | bytes 245768 | tf_op jit(solution)/shard_map/ppermute | solution.py:227
  65.4 10.1 %copy-start.6 = (bf16[2,352,128]{2,1,0:T(8,128)(2,1)}, bf16[2,352,128]{2,1,0:T(8,128)(2,1)S(1)}, u32[]{:S(2)}) copy-start(bf16[2,352,128]{2,1,0:T(8,128)(2,1)S(1)} %add_add_fusion.rest_1_) | copy-start | bytes 540676
  65.4 28.2 %copy-start.41 = (s32[384]{0:T(512)S(1)}, s32[384]{0:T(512)}, u32[]{:S(2)}) copy-start(s32[384]{0:T(512)} %param.15) | copy-start | bytes 4612
  65.4 30.7 %slice-start = ((s8[6291456]{0:T(1024)(128)(4,1)}), s8[2097152]{0:T(1024)(128)(4,1)S(1)}, s32[]{:S(2)}) async-start(s8[6291456]{0:T(1024)(128)(4,1)} %bitcast.87), calls=%async_computation.5 | async-start | bytes 4194304
  65.4 10.0 %collective-permute-start.12 = (bf16[2,352,128]{2,1,0:T(8,128)(2,1)S(1)}, bf16[2,352,128]{2,1,0:T(8,128)(2,1)S(1)}, u32[]{:S(2)}, u32[]{:S(2)}) collective-permute-start(bf16[2,352,128]{2,1,0:T(8,128)(2,1)S(1)} %add_add_fusion.rest_1_), channel_id=1, source_target_pairs={{0,24},{8,16},{16,8},{24,0},{1,25},{9,17},{17,9},{25,1},{2,26},{10... | collective-permute-start | bytes 540680 | tf_op jit(solution)/shard_map/ppermute | solution.py:227
  65.5 9.9 %collective-permute-start.10 = (bf16[2,352,128]{2,1,0:T(8,128)(2,1)S(1)}, bf16[2,352,128]{2,1,0:T(8,128)(2,1)S(1)}, u32[]{:S(2)}, u32[]{:S(2)}) collective-permute-start(bf16[2,352,128]{2,1,0:T(8,128)(2,1)S(1)} %add_add_fusion.rest_1_), channel_id=1, source_target_pairs={{0,16},{8,24},{16,0},{24,8},{1,17},{9,25},{17,1},{25,9},{2,18},{10... | collective-permute-start | bytes 540680 | tf_op jit(solution)/shard_map/ppermute | solution.py:227
  66.1 9.3 %copy-start.38 = (bf16[2,160,128]{2,1,0:T(8,128)(2,1)}, bf16[2,160,128]{2,1,0:T(8,128)(2,1)S(1)}, u32[]{:S(2)}) copy-start(bf16[2,160,128]{2,1,0:T(8,128)(2,1)S(1)} %collective-permute-done.13.rest_8_) | copy-start | bytes 245764
  66.2 9.3 %collective-permute-start.8 = (bf16[2,352,128]{2,1,0:T(8,128)(2,1)S(1)}, bf16[2,352,128]{2,1,0:T(8,128)(2,1)S(1)}, u32[]{:S(2)}, u32[]{:S(2)}) collective-permute-start(bf16[2,352,128]{2,1,0:T(8,128)(2,1)S(1)} %add_add_fusion.rest_1_), channel_id=1, source_target_pairs={{0,8},{8,0},{16,24},{24,16},{1,9},{9,1},{17,25},{25,17},{2,10},{10... | collective-permute-start | bytes 540680 | tf_op jit(solution)/shard_map/ppermute | solution.py:227
  76.2 19.9 %slice-start.1 = ((s8[6291456]{0:T(1024)(128)(4,1)}), s8[4194304]{0:T(1024)(128)(4,1)S(1)}, s32[]{:S(2)}) async-start(s8[6291456]{0:T(1024)(128)(4,1)} %bitcast.87), calls=%async_computation.6 | async-start | bytes 8388608
  84.8 4.3 %collective-permute-start.14 = (f32[32,384]{1,0:T(8,128)}, f32[32,384]{1,0:T(8,128)S(1)}, u32[]{:S(2)}, u32[]{:S(2)}) collective-permute-start(f32[32,384]{1,0:T(8,128)} %logits.1), channel_id=1, source_target_pairs={{0,1},{1,0},{2,3},{3,2},{4,5},{5,4},{6,7},{7,6},{8,9},{9,8},{10,11... | collective-permute-start | bytes 147464 | tf_op jit(solution)/shard_map/ppermute | solution.py:824
  89.9 35.3 %copy-start.7 = (f32[32,384]{1,0:T(8,128)}, f32[32,384]{1,0:T(8,128)S(1)}, u32[]{:S(2)}) copy-start(f32[32,384]{1,0:T(8,128)S(1)} %add.186.rest_0_) | copy-start | bytes 147460
  89.9 4.1 %collective-permute-start.17 = (f32[32,384]{1,0:T(8,128)S(1)}, f32[32,384]{1,0:T(8,128)S(1)}, u32[]{:S(2)}, u32[]{:S(2)}) collective-permute-start(f32[32,384]{1,0:T(8,128)S(1)} %add.186.rest_0_), channel_id=1, source_target_pairs={{0,6},{1,7},{2,0},{3,1},{4,2},{5,3},{6,4},{7,5},{8,14},{9,15},{10,... | collective-permute-start | bytes 147464 | tf_op jit(solution)/shard_map/ppermute | solution.py:826
  90.0 5.4 %collective-permute-start.16 = (f32[32,384]{1,0:T(8,128)S(1)}, f32[32,384]{1,0:T(8,128)S(1)}, u32[]{:S(2)}, u32[]{:S(2)}) collective-permute-start(f32[32,384]{1,0:T(8,128)S(1)} %add.186.rest_0_), channel_id=1, source_target_pairs={{0,4},{1,5},{2,6},{3,7},{4,0},{5,1},{6,2},{7,3},{8,12},{9,13},{10,... | collective-permute-start | bytes 147464 | tf_op jit(solution)/shard_map/ppermute | solution.py:826
  91.1 5.0 %collective-permute-start.15 = (f32[32,384]{1,0:T(8,128)S(1)}, f32[32,384]{1,0:T(8,128)S(1)}, u32[]{:S(2)}, u32[]{:S(2)}) collective-permute-start(f32[32,384]{1,0:T(8,128)S(1)} %add.186.rest_0_), channel_id=1, source_target_pairs={{0,2},{1,3},{2,4},{3,5},{4,6},{5,7},{6,0},{7,1},{8,10},{9,11},{10,... | collective-permute-start | bytes 147464 | tf_op jit(solution)/shard_map/ppermute | solution.py:826
  93.6 26.3 %copy-start.39 = (s32[1,384]{1,0:T(1,128)}, s32[1,384]{1,0:T(1,128)S(1)}, u32[]{:S(2)}) copy-start(s32[1,384]{1,0:T(1,128)S(1)} %broadcast_in_dim.13.cnt_ref) | copy-start | bytes 4612
  94.1 17.2 %copy-start.28 = (f32[32,384]{1,0:T(8,128)}, f32[32,384]{1,0:T(8,128)S(1)}, u32[]{:S(2)}) copy-start(f32[32,384]{1,0:T(8,128)S(1)} %collective-permute-done.17.rest_3_) | copy-start | bytes 147460
  95.4 15.8 %copy-start.29 = (f32[32,384]{1,0:T(8,128)}, f32[32,384]{1,0:T(8,128)S(1)}, u32[]{:S(2)}) copy-start(f32[32,384]{1,0:T(8,128)S(1)} %collective-permute-done.16.rest_2_) | copy-start | bytes 147460
  96.1 15.2 %copy-start.30 = (f32[32,384]{1,0:T(8,128)}, f32[32,384]{1,0:T(8,128)S(1)}, u32[]{:S(2)}) copy-start(f32[32,384]{1,0:T(8,128)S(1)} %collective-permute-done.15.rest_1_) | copy-start | bytes 147460
  96.1 67.7 %copy-start.2 = (f32[32,64,128]{2,1,0:T(8,128)S(1)}, f32[32,64,128]{2,1,0:T(8,128)}, u32[]{:S(2)}) copy-start(f32[32,64,128]{2,1,0:T(8,128)} %param.21) | copy-start | bytes 3145732
  107.4 2.7 %collective-permute-start.18 = (bf16[2,3,608,128]{3,2,1,0:T(8,128)(2,1)}, bf16[2,3,608,128]{3,2,1,0:T(8,128)(2,1)S(1)}, u32[]{:S(2)}, u32[]{:S(2)}) collective-permute-start(bf16[2,3,608,128]{3,2,1,0:T(8,128)(2,1)} %get-tuple-element.176), channel_id=1, source_target_pairs={{0,8},{8,0},{16,24},{24,16},{1,9},{9,1},{17,25},{25,17},{2,10},{10... | collective-permute-start | bytes 2801672 | tf_op jit(solution)/shard_map/ppermute | solution.py:495
  111.3 8.6 %collective-permute-start.20 = (bf16[3,304,128]{2,1,0:T(8,128)(2,1)S(1)}, bf16[3,304,128]{2,1,0:T(8,128)(2,1)S(1)}, u32[]{:S(2)}, u32[]{:S(2)}) collective-permute-start(bf16[3,304,128]{2,1,0:T(8,128)(2,1)S(1)} %get-tuple-element.279), channel_id=1, source_target_pairs={{0,16},{8,24},{16,0},{24,8},{1,17},{9,25},{17,1},{25,9},{2,18},{10... | collective-permute-start | bytes 700424 | tf_op jit(solution)/shard_map/ppermute | solution.py:501
  112.5 11.6 %collective-permute-start.19 = (bf16[3,304,128]{2,1,0:T(8,128)(2,1)S(1)}, bf16[3,304,128]{2,1,0:T(8,128)(2,1)S(1)}, u32[]{:S(2)}, u32[]{:S(2)}) collective-permute-start(bf16[3,304,128]{2,1,0:T(8,128)(2,1)S(1)} %get-tuple-element.280), channel_id=1, source_target_pairs={{0,16},{8,24},{16,0},{24,8},{1,17},{9,25},{17,1},{25,9},{2,18},{10... | collective-permute-start | bytes 700424 | tf_op jit(solution)/shard_map/ppermute | solution.py:501
  125.2 15.2 %copy-start.4 = (bf16[3,304,128]{2,1,0:T(8,128)(2,1)}, bf16[3,304,128]{2,1,0:T(8,128)(2,1)S(1)}, u32[]{:S(2)}) copy-start(bf16[3,304,128]{2,1,0:T(8,128)(2,1)S(1)} %get-tuple-element.278) | copy-start | bytes 700420
  125.3 9.9 %collective-permute-start.24 = (bf16[3,304,128]{2,1,0:T(8,128)(2,1)S(1)}, bf16[3,304,128]{2,1,0:T(8,128)(2,1)S(1)}, u32[]{:S(2)}, u32[]{:S(2)}) collective-permute-start(bf16[3,304,128]{2,1,0:T(8,128)(2,1)S(1)} %get-tuple-element.277), channel_id=1, source_target_pairs={{2,0},{4,2},{6,4},{7,6},{5,7},{3,5},{1,3},{0,1},{10,8},{12,10},{14... | collective-permute-start | bytes 700424 | tf_op jit(solution)/shard_map/ppermute | solution.py:238
  126.8 8.6 %collective-permute-start.21 = (bf16[3,304,128]{2,1,0:T(8,128)(2,1)S(1)}, bf16[3,304,128]{2,1,0:T(8,128)(2,1)S(1)}, u32[]{:S(2)}, u32[]{:S(2)}) collective-permute-start(bf16[3,304,128]{2,1,0:T(8,128)(2,1)S(1)} %get-tuple-element.278), channel_id=1, source_target_pairs={{0,2},{2,4},{4,6},{6,7},{7,5},{5,3},{3,1},{1,0},{8,10},{10,12},{12... | collective-permute-start | bytes 700424 | tf_op jit(solution)/shard_map/ppermute | solution.py:237
  128.7 11.8 %collective-permute-start.22 = (bf16[3,304,128]{2,1,0:T(8,128)(2,1)S(1)}, bf16[3,304,128]{2,1,0:T(8,128)(2,1)S(1)}, u32[]{:S(2)}, u32[]{:S(2)}) collective-permute-start(bf16[3,304,128]{2,1,0:T(8,128)(2,1)S(1)} %get-tuple-element.277), channel_id=1, source_target_pairs={{0,2},{2,4},{4,6},{6,7},{7,5},{5,3},{3,1},{1,0},{8,10},{10,12},{12... | collective-permute-start | bytes 700424 | tf_op jit(solution)/shard_map/ppermute | solution.py:238
  130.6 11.7 %collective-permute-start.23 = (bf16[3,304,128]{2,1,0:T(8,128)(2,1)S(1)}, bf16[3,304,128]{2,1,0:T(8,128)(2,1)S(1)}, u32[]{:S(2)}, u32[]{:S(2)}) collective-permute-start(bf16[3,304,128]{2,1,0:T(8,128)(2,1)S(1)} %get-tuple-element.278), channel_id=1, source_target_pairs={{2,0},{4,2},{6,4},{7,6},{5,7},{3,5},{1,3},{0,1},{10,8},{12,10},{14... | collective-permute-start | bytes 700424 | tf_op jit(solution)/shard_map/ppermute | solution.py:237
  135.2 7.1 %copy-start.14 = (bf16[3,304,128]{2,1,0:T(8,128)(2,1)}, bf16[3,304,128]{2,1,0:T(8,128)(2,1)S(1)}, u32[]{:S(2)}) copy-start(bf16[3,304,128]{2,1,0:T(8,128)(2,1)S(1)} %collective-permute-done.24) | copy-start | bytes 700420
  135.2 10.0 %collective-permute-start.28 = (bf16[3,304,128]{2,1,0:T(8,128)(2,1)S(1)}, bf16[3,304,128]{2,1,0:T(8,128)(2,1)S(1)}, u32[]{:S(2)}, u32[]{:S(2)}) collective-permute-start(bf16[3,304,128]{2,1,0:T(8,128)(2,1)S(1)} %collective-permute-done.24), channel_id=1, source_target_pairs={{2,0},{4,2},{6,4},{7,6},{5,7},{3,5},{1,3},{0,1},{10,8},{12,10},{14... | collective-permute-start | bytes 700424 | tf_op jit(solution)/shard_map/ppermute | solution.py:238
  135.5 9.7 %copy-start.15 = (bf16[3,304,128]{2,1,0:T(8,128)(2,1)}, bf16[3,304,128]{2,1,0:T(8,128)(2,1)S(1)}, u32[]{:S(2)}) copy-start(bf16[3,304,128]{2,1,0:T(8,128)(2,1)S(1)} %collective-permute-done.21) | copy-start | bytes 700420
  135.5 10.0 %collective-permute-start.25 = (bf16[3,304,128]{2,1,0:T(8,128)(2,1)S(1)}, bf16[3,304,128]{2,1,0:T(8,128)(2,1)S(1)}, u32[]{:S(2)}, u32[]{:S(2)}) collective-permute-start(bf16[3,304,128]{2,1,0:T(8,128)(2,1)S(1)} %collective-permute-done.21), channel_id=1, source_target_pairs={{0,2},{2,4},{4,6},{6,7},{7,5},{5,3},{3,1},{1,0},{8,10},{10,12},{12... | collective-permute-start | bytes 700424 | tf_op jit(solution)/shard_map/ppermute | solution.py:237
  140.5 5.0 %copy-start.16 = (bf16[3,304,128]{2,1,0:T(8,128)(2,1)}, bf16[3,304,128]{2,1,0:T(8,128)(2,1)S(1)}, u32[]{:S(2)}) copy-start(bf16[3,304,128]{2,1,0:T(8,128)(2,1)S(1)} %collective-permute-done.22) | copy-start | bytes 700420
  140.5 10.0 %collective-permute-start.26 = (bf16[3,304,128]{2,1,0:T(8,128)(2,1)S(1)}, bf16[3,304,128]{2,1,0:T(8,128)(2,1)S(1)}, u32[]{:S(2)}, u32[]{:S(2)}) collective-permute-start(bf16[3,304,128]{2,1,0:T(8,128)(2,1)S(1)} %collective-permute-done.22), channel_id=1, source_target_pairs={{0,2},{2,4},{4,6},{6,7},{7,5},{5,3},{3,1},{1,0},{8,10},{10,12},{12... | collective-permute-start | bytes 700424 | tf_op jit(solution)/shard_map/ppermute | solution.py:238
  142.3 8.2 %copy-start.17 = (bf16[3,304,128]{2,1,0:T(8,128)(2,1)}, bf16[3,304,128]{2,1,0:T(8,128)(2,1)S(1)}, u32[]{:S(2)}) copy-start(bf16[3,304,128]{2,1,0:T(8,128)(2,1)S(1)} %collective-permute-done.23) | copy-start | bytes 700420
  142.3 10.0 %collective-permute-start.27 = (bf16[3,304,128]{2,1,0:T(8,128)(2,1)S(1)}, bf16[3,304,128]{2,1,0:T(8,128)(2,1)S(1)}, u32[]{:S(2)}, u32[]{:S(2)}) collective-permute-start(bf16[3,304,128]{2,1,0:T(8,128)(2,1)S(1)} %collective-permute-done.23), channel_id=1, source_target_pairs={{2,0},{4,2},{6,4},{7,6},{5,7},{3,5},{1,3},{0,1},{10,8},{12,10},{14... | collective-permute-start | bytes 700424 | tf_op jit(solution)/shard_map/ppermute | solution.py:237
  145.2 7.1 %copy-start.18 = (bf16[3,304,128]{2,1,0:T(8,128)(2,1)}, bf16[3,304,128]{2,1,0:T(8,128)(2,1)S(1)}, u32[]{:S(2)}) copy-start(bf16[3,304,128]{2,1,0:T(8,128)(2,1)S(1)} %collective-permute-done.28) | copy-start | bytes 700420
  145.2 10.8 %collective-permute-start.32 = (bf16[3,304,128]{2,1,0:T(8,128)(2,1)S(1)}, bf16[3,304,128]{2,1,0:T(8,128)(2,1)S(1)}, u32[]{:S(2)}, u32[]{:S(2)}) collective-permute-start(bf16[3,304,128]{2,1,0:T(8,128)(2,1)S(1)} %collective-permute-done.28), channel_id=1, source_target_pairs={{2,0},{4,2},{6,4},{7,6},{5,7},{3,5},{1,3},{0,1},{10,8},{12,10},{14... | collective-permute-start | bytes 700424 | tf_op jit(solution)/shard_map/ppermute | solution.py:238
  145.5 10.5 %copy-start.19 = (bf16[3,304,128]{2,1,0:T(8,128)(2,1)}, bf16[3,304,128]{2,1,0:T(8,128)(2,1)S(1)}, u32[]{:S(2)}) copy-start(bf16[3,304,128]{2,1,0:T(8,128)(2,1)S(1)} %collective-permute-done.25) | copy-start | bytes 700420
  145.5 10.5 %collective-permute-start.29 = (bf16[3,304,128]{2,1,0:T(8,128)(2,1)S(1)}, bf16[3,304,128]{2,1,0:T(8,128)(2,1)S(1)}, u32[]{:S(2)}, u32[]{:S(2)}) collective-permute-start(bf16[3,304,128]{2,1,0:T(8,128)(2,1)S(1)} %collective-permute-done.25), channel_id=1, source_target_pairs={{0,2},{2,4},{4,6},{6,7},{7,5},{5,3},{3,1},{1,0},{8,10},{10,12},{12... | collective-permute-start | bytes 700424 | tf_op jit(solution)/shard_map/ppermute | solution.py:237
  150.5 10.0 %collective-permute-start.30 = (bf16[3,304,128]{2,1,0:T(8,128)(2,1)S(1)}, bf16[3,304,128]{2,1,0:T(8,128)(2,1)S(1)}, u32[]{:S(2)}, u32[]{:S(2)}) collective-permute-start(bf16[3,304,128]{2,1,0:T(8,128)(2,1)S(1)} %collective-permute-done.26), channel_id=1, source_target_pairs={{0,2},{2,4},{4,6},{6,7},{7,5},{5,3},{3,1},{1,0},{8,10},{10,12},{12... | collective-permute-start | bytes 700424 | tf_op jit(solution)/shard_map/ppermute | solution.py:238
  152.3 8.7 %collective-permute-start.31 = (bf16[3,304,128]{2,1,0:T(8,128)(2,1)S(1)}, bf16[3,304,128]{2,1,0:T(8,128)(2,1)S(1)}, u32[]{:S(2)}, u32[]{:S(2)}) collective-permute-start(bf16[3,304,128]{2,1,0:T(8,128)(2,1)S(1)} %collective-permute-done.27), channel_id=1, source_target_pairs={{2,0},{4,2},{6,4},{7,6},{5,7},{3,5},{1,3},{0,1},{10,8},{12,10},{14... | collective-permute-start | bytes 700424 | tf_op jit(solution)/shard_map/ppermute | solution.py:237
  156.0 7.8 %collective-permute-start.34 = (bf16[3,304,128]{2,1,0:T(8,128)(2,1)S(1)}, bf16[3,304,128]{2,1,0:T(8,128)(2,1)S(1)}, u32[]{:S(2)}, u32[]{:S(2)}) collective-permute-start(bf16[3,304,128]{2,1,0:T(8,128)(2,1)S(1)} %collective-permute-done.32), channel_id=1, source_target_pairs={{2,0},{4,2},{6,4},{7,6},{5,7},{3,5},{1,3},{0,1},{10,8},{12,10},{14... | collective-permute-start | bytes 700424 | tf_op jit(solution)/shard_map/ppermute | solution.py:241
  156.0 7.8 %collective-permute-start.33 = (bf16[3,304,128]{2,1,0:T(8,128)(2,1)S(1)}, bf16[3,304,128]{2,1,0:T(8,128)(2,1)S(1)}, u32[]{:S(2)}, u32[]{:S(2)}) collective-permute-start(bf16[3,304,128]{2,1,0:T(8,128)(2,1)S(1)} %collective-permute-done.29), channel_id=1, source_target_pairs={{0,2},{2,4},{4,6},{6,7},{7,5},{5,3},{3,1},{1,0},{8,10},{10,12},{12... | collective-permute-start | bytes 700424 | tf_op jit(solution)/shard_map/ppermute | solution.py:241
  175.5 1.3 copy-start.3
  (12 other events, 10.9 us)

commit v7 on v6

--- a/solution.py
+++ b/solution.py
@@ -101,8 +101,17 @@
         lax.broadcasted_iota(jnp.int32, (ROWS, COLS), 0) >> 3
         == lax.broadcasted_iota(jnp.int32, (ROWS, COLS), 1)
     )
+    held = jnp.dot(
+        owned.astype(F32).astype(BF16), eights.astype(F32).astype(BF16), preferred_element_type=F32
+    )
+    eight = lax.broadcasted_iota(jnp.int32, (COLS, COLS), 0)
+    bits = jnp.where(
+        eight >> 4 == lax.broadcasted_iota(jnp.int32, (COLS, COLS), 1), 1 << (eight & 15), 0
+    )
     flag_v[...] = jnp.dot(
-        owned.astype(F32).astype(BF16), eights.astype(F32).astype(BF16), preferred_element_type=F32
+        (held > 0.0).astype(F32).astype(BF16),
+        bits.astype(F32).astype(BF16),
+        preferred_element_type=F32,
     ).astype(jnp.int32)
     to_idx = pltpu.make_async_copy(idx_v, idx_s, sem.at[2])
     to_flag = pltpu.make_async_copy(flag_v, flag_s, sem.at[3])
@@ -117,45 +126,50 @@
         copy.wait()
     load.wait()
     lower_row = lax.broadcasted_iota(jnp.int32, (2, COLS), 0) == 0
-    shift = rows.bit_length() - 1
-
-    def fill(out, lead, block, skip, groups):
-        def one_group(g):
-            base = pl.multiple_of(g * 16, 16)
-            at = []
-            for h in range(2):
-                n = (skip + g) * 16 + 8 * h
-                at.append((n >> shift, block * rows + (n & (rows - 1))))
-            hits = flag_s[at[0][0], at[0][1] >> 3] + flag_s[at[1][0], at[1][1] >> 3]
-
-            @pl.when(hits > 0)
-            def _():
-                spot = [(k + share * (r >> 7), r & (COLS - 1)) for k, r in at]
-                for u in range(16):
-                    line, lane = spot[u // 8]
-                    i = idx_s[line, lane + u % 8]
-                    w = w_s[line, lane + u % 8]
-                    both = jnp.where(lower_row, w, 1.0 - w)
-                    for j in range(2):
-                        pair[j, 2 * u : 2 * u + 2, :] = both * vol[j, pl.ds(i, 2), :]
+    per_k = max(1, 16 // rows)
+    per_block = max(1, rows // 16)
+    run = min(rows, 16)
+
+    def message(out, lead, k, words, r0, base):
+        word = jnp.where(r0 >= COLS, words[1], words[0])
+        lane = r0 & (COLS - 1)
+        hits = (word >> (lane >> 3)) & ((1 << (run // 8)) - 1)
+
+        @pl.when(hits > 0)
+        def _():
+            line = k + share * (r0 >> 7)
+            for u in range(16):
+                i = idx_s[line + u // run, lane + u % run]
+                w = w_s[line + u // run, lane + u % run]
+                both = jnp.where(lower_row, w, 1.0 - w)
                 for j in range(2):
-                    value = pair[j, pl.ds(0, 16, stride=2), :] + pair[j, pl.ds(1, 16, stride=2), :]
-                    out[lead, j, pl.ds(base, 16), :] = value.astype(BF16)
-
-        def turn(g, carry):
-            for i in range(per_turn):
-                one_group(g * per_turn + i)
-            return carry
-
-        per_turn = 2 if groups % 2 == 0 else 1
-        lax.fori_loop(0, groups // per_turn, turn, 0)
-
+                    pair[j, 2 * u : 2 * u + 2, :] = both * vol[j, pl.ds(i, 2), :]
+            for j in range(2):
+                value = pair[j, pl.ds(0, 16, stride=2), :] + pair[j, pl.ds(1, 16, stride=2), :]
+                out[lead, j, pl.ds(base, 16), :] = value.astype(BF16)
+
+    places = []
     for dz in range(count_z):
         for dy in range(2):
             z = (slab >> 1) + dz
             block = jnp.where(z >= count_z, z - count_z, z) * 2 + ((slab + dy) & 1)
-            fill((keep_a, send_a)[dy], dz, block, 0, groups_a)
-            fill(parts_b[dz], dy, block, groups_a, groups_b)
+            places.append((dz, dy, block))
+    share_a = keep_a.shape[2] // rows
+    for k0, count in ((0, share_a), (share_a, share - share_a)):
+
+        def turn(t, carry, k0=k0):
+            k = k0 + t * per_k
+            words = [flag_s[k, 0], flag_s[k, 1]]
+            for i in range(1, per_k):
+                words = [words[0] | flag_s[k + i, 0], words[1] | flag_s[k + i, 1]]
+            for dz, dy, block in places:
+                out, lead = ((keep_a, send_a)[dy], dz) if k0 == 0 else (parts_b[dz], dy)
+                for g in range(per_block):
+                    base = pl.multiple_of((t * per_block + g) * 16, 16)
+                    message(out, lead, k, words, block * rows + 16 * g, base)
+            return carry
+
+        lax.fori_loop(0, count // per_k, turn, 0)
 
 
 def extract(volume, row_plane, row_line, row_weight, n_vol, share, share_a):
@@ -499,8 +513,27 @@
         cut = slice(h * half, (h + 1) * half)
         summed = [keep[m, :, cut] + got[m, :, cut] for m in range(n_img // 2)]
         moved = [lax.ppermute(summed[m], "img", flip(n_img, 2 * m)) for m in range(1, n_img // 2)]
-        owns.append(sum(moved, summed[0]))
+        owns.append(added(summed[0], *moved))
     return owns
+
+
+def added_kernel(*refs):
+    total = refs[0][...]
+    for ref in refs[1:-1]:
+        total = total + ref[...]
+    refs[-1][...] = total
+
+
+def added(*terms):
+    return pl.pallas_call(
+        added_kernel,
+        out_shape=jax.ShapeDtypeStruct(terms[0].shape, terms[0].dtype),
+        in_specs=[vmem()] * len(terms),
+        out_specs=vmem(),
+        compiler_params=pltpu.CompilerParams(vmem_limit_bytes=VMEM_LIMIT),
+        cost_estimate=cost(1),
+        name="added",
+    )(*terms)
 
 
 HEAD = 8

time: 185 us -> 184 us (level)
  waiting for transfers between devices: 55.7 us -> 45.6 us
  starting transfers between devices: 36.3 us -> 43 us
  Pallas kernels: 60.7 us -> 62.6 us
    ppermute x4, waiting for transfers between devices: 13.4 us -> 1.49 us  [ring_gather(): lax.ppermute(two[1], 'vol', back)]
    ppermute x4, waiting for transfers between devices: 0.18 us -> 9.21 us  [ring_gather(): lax.ppermute(one[0], 'vol', ahead)]
    ppermute x2, waiting for transfers between devices: 10.7 us -> 6.81 us  [to_member(): lax.ppermute(summed[m], 'img', flip(n_img, 2 * m))]
    ppermute x4, starting transfers between devices: 7.56 us -> 10.8 us  [ring_gather(): lax.ppermute(one[0], 'vol', ahead)]
    pallas_call x0 -> x2, Pallas kernels: none -> 2.21 us  [added(): pl.pallas_call(added_kernel, out_shape=jax.ShapeDtypeStruct(terms[0].shap...]
    unnamed x66 -> x70, local copies, waits for them, and re-layouts: 3.05 us -> 4.39 us
  transfers between devices with their start and end apart: 35 -> 35, of which waited for: 21 -> 20; matrix products, arithmetic and copies ran while one was open for 5% -> 5% of each run, Pallas kernels for 7% -> 9%
where the time goes in v7:
time: 184 us; the launch traced here: 183 us
  Pallas kernels  62.6 us (34%)
  waiting for transfers between devices  45.6 us (25%)
  starting transfers between devices  43 us (23%)
  between operations  14.4 us (8%)
  local copies, waits for them, and re-layouts  9.31 us (5%)
  other arithmetic  8.38 us (5%)
    pallas_call x1, Pallas kernels, extract(): pl.pallas_call(partial(extract_kernel, rows, planes_here), out_shape=[sha...  12.9 us
    pallas_call x1, Pallas kernels, project(): pl.pallas_call(project_kernel, grid=(rows // inner,), out_shape=[jax.Shap...  11.3 us
    pallas_call x1, Pallas kernels, insert(): pl.pallas_call(partial(insert_kernel, count), out_shape=jax.ShapeDtypeStr...  11.2 us
    ppermute x4, starting transfers between devices, ring_gather(): lax.ppermute(one[0], 'vol', ahead)  10.8 us
    ppermute x3, waiting for transfers between devices, to_pixel_rows(): lax.ppermute(sums_a[d], 'vol', along_z(n_vol, d))  9.72 us
    ppermute x4, waiting for transfers between devices, ring_gather(): lax.ppermute(one[0], 'vol', ahead)  9.21 us
    pallas_call x1, Pallas kernels, candidate_logits(): pl.pallas_call(logits_kernel, grid=(rows // inner,), out_shape=jax.ShapeD...  8.61 us
    pallas_call x1, Pallas kernels, weigh(): pl.pallas_call(weigh_kernel, grid=(count // step,), out_shape=[jax.ShapeD...  8.42 us
  transfers between devices with their start and end apart: 35, of which 20 were waited for; matrix products, arithmetic and copies ran while one was open for 5% of the time, Pallas kernels for 9%

profile of v7, /device:TPU:12, one launch (start us, length us, event | category | flops | bytes accessed | tf_op | source)
XLA Modules:
  0.0 183.3 jit_solution(11917547686306116149)
XLA Ops:
  6.5 12.9 %extract.1 = (bf16[4,2,352,128]{3,2,1,0:T(8,128)(2,1)}, bf16[4,2,352,128]{3,2,1,0:T(8,128)(2,1)}, bf16[2,2,160,128]{3,2,1,0:T(8,128)(2,1)}, bf16[2,2,160,128]{3,...) custom-call(s32[64,256]{1,0:T(8,128)} %refs_0_.1, s32[64,256]{1,0:T(8,128)} %refs_1_.1, ...), custom_call_target="tpu_custom_call" | custom-call | bytes 40590000 | tf_op jit(solution)/shard_map/extract/pallas_call | solution.py:181
  19.5 1.9 %collective-permute-start.3 = (bf16[2,2,160,128]{3,2,1,0:T(8,128)(2,1)}, bf16[2,2,160,128]{3,2,1,0:T(8,128)(2,1)S(1)}, u32[]{:S(2)}, u32[]{:S(2)}) collective-permute-start(bf16[2,2,160,128]{3,2,1,0:T(8,128)(2,1)} %get-tuple-element.164), channel_id=1, source_target_pairs={{0,6},{1,7},{2,0},{3,1},{4,2},{5,3},{6,4},{7,5},{8,14},{9,15},{10,... | collective-permute-start | bytes 491528 | tf_op jit(solution)/shard_map/ppermute | solution.py:219
  21.5 2.0 %collective-permute-start = (bf16[4,2,352,128]{3,2,1,0:T(8,128)(2,1)}, bf16[4,2,352,128]{3,2,1,0:T(8,128)(2,1)S(1)}, u32[]{:S(2)}, u32[]{:S(2)}) collective-permute-start(bf16[4,2,352,128]{3,2,1,0:T(8,128)(2,1)} %get-tuple-element.160), channel_id=1, source_target_pairs={{0,1},{1,0},{2,3},{3,2},{4,5},{5,4},{6,7},{7,6},{8,9},{9,8},{10,11... | collective-permute-start | bytes 2162696 | tf_op jit(solution)/shard_map/ppermute | solution.py:220
  23.6 1.5 multiply_cosine_fusion
  25.1 1.5 fusion.21
  26.7 8.4 %weigh.1 = (bf16[32,384,256]{2,1,0:T(8,128)(2,1)S(1)}, bf16[32,384,128]{2,1,0:T(8,128)(2,1)}) custom-call(bf16[2,384,32,128]{3,2,1,0:T(8,128)(2,1)} %img_ref.1, f32[384,32]{1,0:T(8,128)} %get-tuple-element.286.sa_ref, f32[384,32]{1,0:T(8,128)} %get-tuple-element.285.ca_ref, f32[384,128]{1,0:T(8,128)} %get-tuple-element.284.sx_ref, ...), custom_call_target="tpu_custom_call" | custom-call | bytes 44280000 | tf_op jit(solution)/shard_map/weigh/pallas_call | solution.py:283
  35.2 3.6 %collective-permute-done.got_a = bf16[4,2,352,128]{3,2,1,0:T(8,128)(2,1)S(1)} collective-permute-done((bf16[4,2,352,128]{3,2,1,0:T(8,128)(2,1)}, bf16[4,2,352,128]{3,2,1,0:T(8,128)(2,1)S(1)}, u32[]{:S(2)}, u32[]{:S(2)}) %collective-permute-start) | collective-permute-done | bytes 720928 | tf_op jit(solution)/shard_map/ppermute | solution.py:220
  38.8 0.9 copy-done.5
  39.7 2.7 %combine_first.1 = (bf16[2,352,128]{2,1,0:T(8,128)(2,1)}, bf16[2,352,128]{2,1,0:T(8,128)(2,1)}, bf16[2,352,128]{2,1,0:T(8,128)(2,1)}, bf16[2,352,128]{2,1,0:T(8,...) custom-call(bf16[4,2,352,128]{3,2,1,0:T(8,128)(2,1)} %get-tuple-element.159.keep_a, ...), custom_call_target="tpu_custom_call" | custom-call | bytes 11070000 | tf_op jit(solution)/shard_map/combine_first/pallas_call | solution.py:223
  42.3 1.7 collective-permute-start.7
  44.6 4.4 %collective-permute-start.5 = (bf16[2,352,128]{2,1,0:T(8,128)(2,1)}, bf16[2,352,128]{2,1,0:T(8,128)(2,1)S(1)}, u32[]{:S(2)}, u32[]{:S(2)}) collective-permute-start(bf16[2,352,128]{2,1,0:T(8,128)(2,1)} %get-tuple-element.167), channel_id=1, source_target_pairs={{0,4},{1,5},{2,6},{3,7},{4,0},{5,1},{6,2},{7,3},{8,12},{9,13},{10,... | collective-permute-start | bytes 540680 | tf_op jit(solution)/shard_map/ppermute | solution.py:234
  49.1 0.9 add.177.rest_2_
  50.1 1.9 %collective-permute-start.11 = (bf16[2,160,128]{2,1,0:T(8,128)(2,1)S(1)}, bf16[2,160,128]{2,1,0:T(8,128)(2,1)}, u32[]{:S(2)}, u32[]{:S(2)}) collective-permute-start(bf16[2,160,128]{2,1,0:T(8,128)(2,1)S(1)} %add.177.rest_2_), channel_id=1, source_target_pairs={{0,16},{8,24},{16,0},{24,8},{1,17},{9,25},{17,1},{25,9},{2,18},{10... | collective-permute-start | bytes 245768 | tf_op jit(solution)/shard_map/ppermute | solution.py:241
  51.9 5.5 %collective-permute-done.4 = bf16[2,352,128]{2,1,0:T(8,128)(2,1)S(1)} collective-permute-done((bf16[2,352,128]{2,1,0:T(8,128)(2,1)}, bf16[2,352,128]{2,1,0:T(8,128)(2,1)S(1)}, u32[]{:S(2)}, u32[]{:S(2)}) %collective-permute-start.4) | collective-permute-done | bytes 180256 | tf_op jit(solution)/shard_map/ppermute | solution.py:234
  57.4 2.0 %collective-permute-done.5 = bf16[2,352,128]{2,1,0:T(8,128)(2,1)S(1)} collective-permute-done((bf16[2,352,128]{2,1,0:T(8,128)(2,1)}, bf16[2,352,128]{2,1,0:T(8,128)(2,1)S(1)}, u32[]{:S(2)}, u32[]{:S(2)}) %collective-permute-start.5) | collective-permute-done | bytes 180256 | tf_op jit(solution)/shard_map/ppermute | solution.py:234
  59.5 2.2 %collective-permute-done.6 = bf16[2,352,128]{2,1,0:T(8,128)(2,1)S(1)} collective-permute-done((bf16[2,352,128]{2,1,0:T(8,128)(2,1)}, bf16[2,352,128]{2,1,0:T(8,128)(2,1)S(1)}, u32[]{:S(2)}, u32[]{:S(2)}) %collective-permute-start.6) | collective-permute-done | bytes 180256 | tf_op jit(solution)/shard_map/ppermute | solution.py:234
  61.7 1.0 add_add_fusion.rest_1_
  62.7 0.6 collective-permute-start.12
  63.3 1.4 collective-permute-start.10
  65.2 0.7 reshape.231.wgt_ref
  66.0 0.7 reshape.230.line_ref
  66.9 0.7 reshape.229.plane_ref
  67.6 5.3 %lists.1 = (s32[32,128]{1,0:T(8,128)}, s32[64,128]{1,0:T(8,128)S(1)}, f32[64,128]{1,0:T(8,128)}, s32[8,128]{1,0:T(8,128)}, s32[8,128]{1,0:T(8,128)}, /*index=5*/s32[8,128]{1,0:T(8,128)}) custom-call(s32[8,2048]{1,0:T(8,128)} %reshape.229.plane_ref, s32[8,2048]{1,0:T(8,128)} %reshape.230.line_ref, f32[8,2048]{1,0:T(8,128)} %reshape.231.wgt_ref), custom_call_target="tpu_custom_call" | custom-call | bytes 22140000 | tf_op jit(solution)/shard_map/lists/pallas_call | solution.py:757
  72.9 0.6 collective-permute-done.10.rest_5_
  73.5 0.6 copy-done.34
  74.2 8.6 %logits.1 = f32[32,384]{1,0:T(8,128)} custom-call(bf16[32,384,256]{2,1,0:T(8,128)(2,1)} %copy-done, bf16[32,384,128]{2,1,0:T(8,128)(2,1)} %get-tuple-element.157.sq_ref, f32[4,32,128]{2,1,0:T(8,128)S(1)} %get-tuple-element.282.cos_ref, f32[4,32,128]{2,1,0:T(8,128)S(1)} %get-tuple-element.281.sin_ref, s32[8,384]{1,0:T(8,128)S(1)} %bitcast.97, ...), custom_call_target="tpu_custom_call" | custom-call | bytes 29520000 | tf_op jit(solution)/shard_map/logits/pallas_call | solution.py:375
  83.3 3.7 %collective-permute-done.14 = f32[32,384]{1,0:T(8,128)S(1)} collective-permute-done((f32[32,384]{1,0:T(8,128)}, f32[32,384]{1,0:T(8,128)S(1)}, u32[]{:S(2)}, u32[]{:S(2)}) %collective-permute-start.14) | collective-permute-done | bytes 49184 | tf_op jit(solution)/shard_map/ppermute | solution.py:857
  87.1 0.8 add.178.rest_0_
  88.0 1.2 collective-permute-start.16
  89.1 2.8 %collective-permute-start.15 = (f32[32,384]{1,0:T(8,128)S(1)}, f32[32,384]{1,0:T(8,128)S(1)}, u32[]{:S(2)}, u32[]{:S(2)}) collective-permute-start(f32[32,384]{1,0:T(8,128)S(1)} %add.178.rest_0_), channel_id=1, source_target_pairs={{0,2},{1,3},{2,4},{3,5},{4,6},{5,7},{6,0},{7,1},{8,10},{9,11},{10,... | collective-permute-start | bytes 147464 | tf_op jit(solution)/shard_map/ppermute | solution.py:859
  92.0 1.4 collective-permute-done.16.rest_2_
  94.1 11.3 %project.1 = (bf16[2,3,608,128]{3,2,1,0:T(8,128)(2,1)}, bf16[2,3,608,128]{3,2,1,0:T(8,128)(2,1)}) custom-call(s32[4096]{0:T(1024)} %bitcast.104, s32[8,128]{1,0:T(8,128)} %get-tuple-element.174.len_s, s32[8,384]{1,0:T(8,128)S(1)} %bitcast.98, s32[1,384]{1,0:T(1,128)S(1)} %broadcast_in_dim.13.cnt_ref, bf16[32,384,256]{2,1,0:T(8,128)(2,1)S(1)} %bitcast.84, ...), custom_call_target="tpu_custom_call" | custom-call | bytes 44280000 | tf_op jit(solution)/shard_map/project/pallas_call | solution.py:480
  105.4 2.7 %collective-permute-done.18 = bf16[2,3,608,128]{3,2,1,0:T(8,128)(2,1)S(1)} collective-permute-done((bf16[2,3,608,128]{3,2,1,0:T(8,128)(2,1)}, bf16[2,3,608,128]{3,2,1,0:T(8,128)(2,1)S(1)}, u32[]{:S(2)}, u32[]{:S(2)}) %collective-permute-start.18) | collective-permute-done | bytes 933920 | tf_op jit(solution)/shard_map/ppermute | solution.py:509
  108.1 2.2 %fusion.17 = (bf16[3,304,128]{2,1,0:T(8,128)(2,1)S(1)}, bf16[3,304,128]{2,1,0:T(8,128)(2,1)}, bf16[3,304,128]{2,1,0:T(8,128)(2,1)S(1)}, bf16[3,304,128]{2,1,0:T(8,128)(2,1)}) fusion(bf16[2,3,608,128]{3,2,1,0:T(8,128)(2,1)S(1)} %collective-permute-done.18, bf16[2,3,608,128]{3,2,1,0:T(8,128)(2,1)} %get-tuple-element.175), kind=kLoop, calls=%fused_computation.49 | loop fusion | flops 466944 | bytes 2801664 | tf_op jit(solution)/shard_map/add | solution.py:514
  110.3 1.2 collective-permute-start.20
  111.5 0.9 collective-permute-start.19
  112.4 6.5 %collective-permute-done.20.refs_1_ = bf16[3,304,128]{2,1,0:T(8,128)(2,1)S(1)} collective-permute-done((bf16[3,304,128]{2,1,0:T(8,128)(2,1)S(1)}, bf16[3,304,128]{2,1,0:T(8,128)(2,1)S(1)}, u32[]{:S(2)}, u32[]{:S(2)}) %collective-permute-start.20) | collective-permute-done | bytes 233504 | tf_op jit(solution)/shard_map/ppermute | solution.py:515
  118.9 0.7 copy-done.29
  119.6 1.1 added.3
  120.7 2.1 %collective-permute-start.24 = (bf16[3,304,128]{2,1,0:T(8,128)(2,1)S(1)}, bf16[3,304,128]{2,1,0:T(8,128)(2,1)S(1)}, u32[]{:S(2)}, u32[]{:S(2)}) collective-permute-start(bf16[3,304,128]{2,1,0:T(8,128)(2,1)S(1)} %added.3), channel_id=1, source_target_pairs={{2,0},{4,2},{6,4},{7,6},{5,7},{3,5},{1,3},{0,1},{10,8},{12,10},{14... | collective-permute-start | bytes 700424 | tf_op jit(solution)/shard_map/ppermute | solution.py:252
  123.1 0.7 copy-done.28
  123.8 1.1 added.2
  124.9 3.4 %collective-permute-start.21 = (bf16[3,304,128]{2,1,0:T(8,128)(2,1)S(1)}, bf16[3,304,128]{2,1,0:T(8,128)(2,1)S(1)}, u32[]{:S(2)}, u32[]{:S(2)}) collective-permute-start(bf16[3,304,128]{2,1,0:T(8,128)(2,1)S(1)} %added.2), channel_id=1, source_target_pairs={{0,2},{2,4},{4,6},{6,7},{7,5},{5,3},{3,1},{1,0},{8,10},{10,12},{12... | collective-permute-start | bytes 700424 | tf_op jit(solution)/shard_map/ppermute | solution.py:251
  128.8 1.5 collective-permute-start.23
  130.3 4.1 %collective-permute-done.21 = bf16[3,304,128]{2,1,0:T(8,128)(2,1)S(1)} collective-permute-done((bf16[3,304,128]{2,1,0:T(8,128)(2,1)S(1)}, bf16[3,304,128]{2,1,0:T(8,128)(2,1)S(1)}, u32[]{:S(2)}, u32[]{:S(2)}) %collective-permute-start.21) | collective-permute-done | bytes 233504 | tf_op jit(solution)/shard_map/ppermute | solution.py:251
  134.4 2.5 %collective-permute-start.25 = (bf16[3,304,128]{2,1,0:T(8,128)(2,1)S(1)}, bf16[3,304,128]{2,1,0:T(8,128)(2,1)S(1)}, u32[]{:S(2)}, u32[]{:S(2)}) collective-permute-start(bf16[3,304,128]{2,1,0:T(8,128)(2,1)S(1)} %collective-permute-done.21), channel_id=1, source_target_pairs={{0,2},{2,4},{4,6},{6,7},{7,5},{5,3},{3,1},{1,0},{8,10},{10,12},{12... | collective-permute-start | bytes 700424 | tf_op jit(solution)/shard_map/ppermute | solution.py:251
  136.9 2.5 %collective-permute-done.22 = bf16[3,304,128]{2,1,0:T(8,128)(2,1)S(1)} collective-permute-done((bf16[3,304,128]{2,1,0:T(8,128)(2,1)S(1)}, bf16[3,304,128]{2,1,0:T(8,128)(2,1)S(1)}, u32[]{:S(2)}, u32[]{:S(2)}) %collective-permute-start.22) | collective-permute-done | bytes 233504 | tf_op jit(solution)/shard_map/ppermute | solution.py:252
  139.4 2.5 %collective-permute-start.26 = (bf16[3,304,128]{2,1,0:T(8,128)(2,1)S(1)}, bf16[3,304,128]{2,1,0:T(8,128)(2,1)S(1)}, u32[]{:S(2)}, u32[]{:S(2)}) collective-permute-start(bf16[3,304,128]{2,1,0:T(8,128)(2,1)S(1)} %collective-permute-done.22), channel_id=1, source_target_pairs={{0,2},{2,4},{4,6},{6,7},{7,5},{5,3},{3,1},{1,0},{8,10},{10,12},{12... | collective-permute-start | bytes 700424 | tf_op jit(solution)/shard_map/ppermute | solution.py:252
  142.0 0.8 collective-permute-start.32
  142.7 1.6 collective-permute-done.25
  144.4 2.5 %collective-permute-start.29 = (bf16[3,304,128]{2,1,0:T(8,128)(2,1)S(1)}, bf16[3,304,128]{2,1,0:T(8,128)(2,1)S(1)}, u32[]{:S(2)}, u32[]{:S(2)}) collective-permute-start(bf16[3,304,128]{2,1,0:T(8,128)(2,1)S(1)} %collective-permute-done.25), channel_id=1, source_target_pairs={{0,2},{2,4},{4,6},{6,7},{7,5},{5,3},{3,1},{1,0},{8,10},{10,12},{12... | collective-permute-start | bytes 700424 | tf_op jit(solution)/shard_map/ppermute | solution.py:251
  146.9 2.5 %collective-permute-done.26 = bf16[3,304,128]{2,1,0:T(8,128)(2,1)S(1)} collective-permute-done((bf16[3,304,128]{2,1,0:T(8,128)(2,1)S(1)}, bf16[3,304,128]{2,1,0:T(8,128)(2,1)S(1)}, u32[]{:S(2)}, u32[]{:S(2)}) %collective-permute-start.26) | collective-permute-done | bytes 233504 | tf_op jit(solution)/shard_map/ppermute | solution.py:252
  149.4 2.5 %collective-permute-start.30 = (bf16[3,304,128]{2,1,0:T(8,128)(2,1)S(1)}, bf16[3,304,128]{2,1,0:T(8,128)(2,1)S(1)}, u32[]{:S(2)}, u32[]{:S(2)}) collective-permute-start(bf16[3,304,128]{2,1,0:T(8,128)(2,1)S(1)} %collective-permute-done.26), channel_id=1, source_target_pairs={{0,2},{2,4},{4,6},{6,7},{7,5},{5,3},{3,1},{1,0},{8,10},{10,12},{12... | collective-permute-start | bytes 700424 | tf_op jit(solution)/shard_map/ppermute | solution.py:252
  151.9 0.7 collective-permute-start.34
  152.7 1.7 collective-permute-done.29
  154.4 2.5 %collective-permute-start.33 = (bf16[3,304,128]{2,1,0:T(8,128)(2,1)S(1)}, bf16[3,304,128]{2,1,0:T(8,128)(2,1)S(1)}, u32[]{:S(2)}, u32[]{:S(2)}) collective-permute-start(bf16[3,304,128]{2,1,0:T(8,128)(2,1)S(1)} %collective-permute-done.29), channel_id=1, source_target_pairs={{0,2},{2,4},{4,6},{6,7},{7,5},{5,3},{3,1},{1,0},{8,10},{10,12},{12... | collective-permute-start | bytes 700424 | tf_op jit(solution)/shard_map/ppermute | solution.py:255
  156.9 1.2 slice.45
  158.7 0.7 collective-permute-done.30
  159.4 1.5 collective-permute-done.34
  160.9 1.8 collective-permute-done.33
  162.7 12.5 %conditional.1 = (f32[2,32,64,128]{3,2,1,0:T(8,128)S(1)}) conditional(s32[]{:T(128)} %bitcast.20, (s32[]{:T(128)}, s32[64,256]{1,0:T(8,128)}, s32[]{:T(128)}, s32[64,256]{1,0:T(8,128)}, f32[64,256]{1,0:T(8,128)}, /*index=5*/f32[4,32,128]{2,1,0:T(8,128)S(1)}, s32[8,384]{1,0:T(8,128)S(1)}, s32[1,384]{1,0:T(1,128)}, f32[32,384]{1,0:T(8,128)}, ...), branch_computations={%region_0.10_spmd, %region_10.11_spmd} | conditional | flops 1831321088 | bytes 333904320 | solution.py:877
  162.7 0.6 copy-done.20
  164.0 11.2 %insert.1 = f32[2,32,64,128]{3,2,1,0:T(8,128)S(1)} custom-call(s32[8,128]{1,0:T(8,128)} %get-tuple-element.113.len_s, s32[8192]{0:T(1024)S(1)} %bitcast.96, f32[8192]{0:T(1024)} %bitcast.103, f32[32,64,128]{2,1,0:T(8,128)S(1)} %get-tuple-element.116.reg_hbm, bf16[3,304,128]{2,1,0:T(8,128)(2,1)} %get-tuple-element.117.rest_0_, ...), custom_call_target="tpu_custom_call" | custom-call | bytes 33210000 | tf_op jit(solution)/shard_map/cond/branch_1_fun/insert/pallas_call | solution.py:633
  175.2 1.3 copy-done.3
  (125 shorter events, 4.7 us)
Async XLA Ops:
  6.5 17.1 %copy-start.42 = (f32[384]{0:T(512)S(1)}, f32[384]{0:T(512)}, u32[]{:S(2)}) copy-start(f32[384]{0:T(512)} %param.13) | copy-start | bytes 4612
  19.4 15.7 %collective-permute-start.1 = (bf16[2,2,160,128]{3,2,1,0:T(8,128)(2,1)}, bf16[2,2,160,128]{3,2,1,0:T(8,128)(2,1)S(1)}, u32[]{:S(2)}, u32[]{:S(2)}) collective-permute-start(bf16[2,2,160,128]{3,2,1,0:T(8,128)(2,1)} %get-tuple-element.162), channel_id=1, source_target_pairs={{0,2},{1,3},{2,4},{3,5},{4,6},{5,7},{6,0},{7,1},{8,10},{9,11},{10,... | collective-permute-start | bytes 491528 | tf_op jit(solution)/shard_map/ppermute | solution.py:219
  19.5 15.7 %collective-permute-start.2 = (bf16[2,2,160,128]{3,2,1,0:T(8,128)(2,1)}, bf16[2,2,160,128]{3,2,1,0:T(8,128)(2,1)S(1)}, u32[]{:S(2)}, u32[]{:S(2)}) collective-permute-start(bf16[2,2,160,128]{3,2,1,0:T(8,128)(2,1)} %get-tuple-element.163), channel_id=1, source_target_pairs={{0,4},{1,5},{2,6},{3,7},{4,0},{5,1},{6,2},{7,3},{8,12},{9,13},{10,... | collective-permute-start | bytes 491528 | tf_op jit(solution)/shard_map/ppermute | solution.py:219
  19.5 15.6 %collective-permute-start.3 = (bf16[2,2,160,128]{3,2,1,0:T(8,128)(2,1)}, bf16[2,2,160,128]{3,2,1,0:T(8,128)(2,1)S(1)}, u32[]{:S(2)}, u32[]{:S(2)}) collective-permute-start(bf16[2,2,160,128]{3,2,1,0:T(8,128)(2,1)} %get-tuple-element.164), channel_id=1, source_target_pairs={{0,6},{1,7},{2,0},{3,1},{4,2},{5,3},{6,4},{7,5},{8,14},{9,15},{10,... | collective-permute-start | bytes 491528 | tf_op jit(solution)/shard_map/ppermute | solution.py:219
  21.5 17.3 %collective-permute-start = (bf16[4,2,352,128]{3,2,1,0:T(8,128)(2,1)}, bf16[4,2,352,128]{3,2,1,0:T(8,128)(2,1)S(1)}, u32[]{:S(2)}, u32[]{:S(2)}) collective-permute-start(bf16[4,2,352,128]{3,2,1,0:T(8,128)(2,1)} %get-tuple-element.160), channel_id=1, source_target_pairs={{0,1},{1,0},{2,3},{3,2},{4,5},{5,4},{6,7},{7,6},{8,9},{9,8},{10,11... | collective-permute-start | bytes 2162696 | tf_op jit(solution)/shard_map/ppermute | solution.py:220
  35.1 3.7 %copy-start = (bf16[32,384,256]{2,1,0:T(8,128)(2,1)}, bf16[32,384,256]{2,1,0:T(8,128)(2,1)S(1)}, u32[]{:S(2)}) copy-start(bf16[32,384,256]{2,1,0:T(8,128)(2,1)S(1)} %get-tuple-element.156.rest_3_.wt_ref) | copy-start | bytes 18874372
  35.1 30.0 %copy-start.12 = (f32[64,256]{1,0:T(8,128)S(1)}, f32[64,256]{1,0:T(8,128)}, u32[]{:S(2)}) copy-start(f32[64,256]{1,0:T(8,128)} %refs_2_.1) | copy-start | bytes 196612
  35.1 30.9 %copy-start.10 = (s32[64,256]{1,0:T(8,128)S(1)}, s32[64,256]{1,0:T(8,128)}, u32[]{:S(2)}) copy-start(s32[64,256]{1,0:T(8,128)} %refs_1_.1) | copy-start | bytes 196612
  35.1 31.7 %copy-start.8 = (s32[64,256]{1,0:T(8,128)S(1)}, s32[64,256]{1,0:T(8,128)}, u32[]{:S(2)}) copy-start(s32[64,256]{1,0:T(8,128)} %refs_0_.1) | copy-start | bytes 196612
  35.1 39.1 %copy-start.39 = (s32[384,8]{0,1:T(8,128)S(1)}, s32[384,8]{0,1:T(8,128)}, u32[]{:S(2)}) copy-start(s32[384,8]{0,1:T(8,128)} %param.14) | copy-start | bytes 36868
  35.1 3.6 %copy-start.36 = (bf16[2,2,160,128]{3,2,1,0:T(8,128)(2,1)}, bf16[2,2,160,128]{3,2,1,0:T(8,128)(2,1)S(1)}, u32[]{:S(2)}) copy-start(bf16[2,2,160,128]{3,2,1,0:T(8,128)(2,1)S(1)} %collective-permute-done.1.rest_0_) | copy-start | bytes 491524
  35.2 3.6 %copy-start.37 = (bf16[2,2,160,128]{3,2,1,0:T(8,128)(2,1)}, bf16[2,2,160,128]{3,2,1,0:T(8,128)(2,1)S(1)}, u32[]{:S(2)}) copy-start(bf16[2,2,160,128]{3,2,1,0:T(8,128)(2,1)S(1)} %collective-permute-done.2.rest_1_) | copy-start | bytes 491524
  35.2 3.6 %copy-start.38 = (bf16[2,2,160,128]{3,2,1,0:T(8,128)(2,1)}, bf16[2,2,160,128]{3,2,1,0:T(8,128)(2,1)S(1)}, u32[]{:S(2)}) copy-start(bf16[2,2,160,128]{3,2,1,0:T(8,128)(2,1)S(1)} %collective-permute-done.3.rest_2_) | copy-start | bytes 491524
  42.3 6.7 %collective-permute-start.7 = (bf16[2,160,128]{2,1,0:T(8,128)(2,1)}, bf16[2,160,128]{2,1,0:T(8,128)(2,1)S(1)}, u32[]{:S(2)}, u32[]{:S(2)}) collective-permute-start(bf16[2,160,128]{2,1,0:T(8,128)(2,1)} %get-tuple-element.170), channel_id=1, source_target_pairs={{0,1},{1,0},{2,3},{3,2},{4,5},{5,4},{6,7},{7,6},{8,9},{9,8},{10,11... | collective-permute-start | bytes 245768 | tf_op jit(solution)/shard_map/ppermute | solution.py:233
  44.1 13.4 %collective-permute-start.4 = (bf16[2,352,128]{2,1,0:T(8,128)(2,1)}, bf16[2,352,128]{2,1,0:T(8,128)(2,1)S(1)}, u32[]{:S(2)}, u32[]{:S(2)}) collective-permute-start(bf16[2,352,128]{2,1,0:T(8,128)(2,1)} %get-tuple-element.166), channel_id=1, source_target_pairs={{0,2},{1,3},{2,4},{3,5},{4,6},{5,7},{6,0},{7,1},{8,10},{9,11},{10,... | collective-permute-start | bytes 540680 | tf_op jit(solution)/shard_map/ppermute | solution.py:234
  44.6 14.9 %collective-permute-start.5 = (bf16[2,352,128]{2,1,0:T(8,128)(2,1)}, bf16[2,352,128]{2,1,0:T(8,128)(2,1)S(1)}, u32[]{:S(2)}, u32[]{:S(2)}) collective-permute-start(bf16[2,352,128]{2,1,0:T(8,128)(2,1)} %get-tuple-element.167), channel_id=1, source_target_pairs={{0,4},{1,5},{2,6},{3,7},{4,0},{5,1},{6,2},{7,3},{8,12},{9,13},{10,... | collective-permute-start | bytes 540680 | tf_op jit(solution)/shard_map/ppermute | solution.py:234
  49.0 12.7 %collective-permute-start.6 = (bf16[2,352,128]{2,1,0:T(8,128)(2,1)}, bf16[2,352,128]{2,1,0:T(8,128)(2,1)S(1)}, u32[]{:S(2)}, u32[]{:S(2)}) collective-permute-start(bf16[2,352,128]{2,1,0:T(8,128)(2,1)} %get-tuple-element.168), channel_id=1, source_target_pairs={{0,6},{1,7},{2,0},{3,1},{4,2},{5,3},{6,4},{7,5},{8,14},{9,15},{10,... | collective-permute-start | bytes 540680 | tf_op jit(solution)/shard_map/ppermute | solution.py:234
  50.0 23.5 %copy-start.13 = (bf16[2,160,128]{2,1,0:T(8,128)(2,1)}, bf16[2,160,128]{2,1,0:T(8,128)(2,1)S(1)}, u32[]{:S(2)}) copy-start(bf16[2,160,128]{2,1,0:T(8,128)(2,1)S(1)} %add.177.rest_2_) | copy-start | bytes 245764
  50.0 14.7 %collective-permute-start.13 = (bf16[2,160,128]{2,1,0:T(8,128)(2,1)S(1)}, bf16[2,160,128]{2,1,0:T(8,128)(2,1)S(1)}, u32[]{:S(2)}, u32[]{:S(2)}) collective-permute-start(bf16[2,160,128]{2,1,0:T(8,128)(2,1)S(1)} %add.177.rest_2_), channel_id=1, source_target_pairs={{0,24},{8,16},{16,8},{24,0},{1,25},{9,17},{17,9},{25,1},{2,26},{10... | collective-permute-start | bytes 245768 | tf_op jit(solution)/shard_map/ppermute | solution.py:241
  50.1 22.8 %collective-permute-start.11 = (bf16[2,160,128]{2,1,0:T(8,128)(2,1)S(1)}, bf16[2,160,128]{2,1,0:T(8,128)(2,1)}, u32[]{:S(2)}, u32[]{:S(2)}) collective-permute-start(bf16[2,160,128]{2,1,0:T(8,128)(2,1)S(1)} %add.177.rest_2_), channel_id=1, source_target_pairs={{0,16},{8,24},{16,0},{24,8},{1,17},{9,25},{17,1},{25,9},{2,18},{10... | collective-permute-start | bytes 245768 | tf_op jit(solution)/shard_map/ppermute | solution.py:241
  57.4 15.4 %collective-permute-start.9 = (bf16[2,160,128]{2,1,0:T(8,128)(2,1)S(1)}, bf16[2,160,128]{2,1,0:T(8,128)(2,1)}, u32[]{:S(2)}, u32[]{:S(2)}) collective-permute-start(bf16[2,160,128]{2,1,0:T(8,128)(2,1)S(1)} %add.177.rest_2_), channel_id=1, source_target_pairs={{0,8},{8,0},{16,24},{24,16},{1,9},{9,1},{17,25},{25,17},{2,10},{10... | collective-permute-start | bytes 245768 | tf_op jit(solution)/shard_map/ppermute | solution.py:241
  62.6 10.8 %copy-start.6 = (bf16[2,352,128]{2,1,0:T(8,128)(2,1)}, bf16[2,352,128]{2,1,0:T(8,128)(2,1)S(1)}, u32[]{:S(2)}) copy-start(bf16[2,352,128]{2,1,0:T(8,128)(2,1)S(1)} %add_add_fusion.rest_1_) | copy-start | bytes 540676
  62.6 29.3 %copy-start.43 = (s32[384]{0:T(512)S(1)}, s32[384]{0:T(512)}, u32[]{:S(2)}) copy-start(s32[384]{0:T(512)} %param.15) | copy-start | bytes 4612
  62.6 31.4 %slice-start = ((s8[6291456]{0:T(1024)(128)(4,1)}), s8[2097152]{0:T(1024)(128)(4,1)S(1)}, s32[]{:S(2)}) async-start(s8[6291456]{0:T(1024)(128)(4,1)} %bitcast.83), calls=%async_computation.5 | async-start | bytes 4194304
  62.7 10.2 %collective-permute-start.12 = (bf16[2,352,128]{2,1,0:T(8,128)(2,1)S(1)}, bf16[2,352,128]{2,1,0:T(8,128)(2,1)S(1)}, u32[]{:S(2)}, u32[]{:S(2)}) collective-permute-start(bf16[2,352,128]{2,1,0:T(8,128)(2,1)S(1)} %add_add_fusion.rest_1_), channel_id=1, source_target_pairs={{0,24},{8,16},{16,8},{24,0},{1,25},{9,17},{17,9},{25,1},{2,26},{10... | collective-permute-start | bytes 540680 | tf_op jit(solution)/shard_map/ppermute | solution.py:241
  63.3 10.2 %collective-permute-start.10 = (bf16[2,352,128]{2,1,0:T(8,128)(2,1)S(1)}, bf16[2,352,128]{2,1,0:T(8,128)(2,1)S(1)}, u32[]{:S(2)}, u32[]{:S(2)}) collective-permute-start(bf16[2,352,128]{2,1,0:T(8,128)(2,1)S(1)} %add_add_fusion.rest_1_), channel_id=1, source_target_pairs={{0,16},{8,24},{16,0},{24,8},{1,17},{9,25},{17,1},{25,9},{2,18},{10... | collective-permute-start | bytes 540680 | tf_op jit(solution)/shard_map/ppermute | solution.py:241
  64.7 8.8 %copy-start.40 = (bf16[2,160,128]{2,1,0:T(8,128)(2,1)}, bf16[2,160,128]{2,1,0:T(8,128)(2,1)S(1)}, u32[]{:S(2)}) copy-start(bf16[2,160,128]{2,1,0:T(8,128)(2,1)S(1)} %collective-permute-done.13.rest_8_) | copy-start | bytes 245764
  64.7 8.7 %collective-permute-start.8 = (bf16[2,352,128]{2,1,0:T(8,128)(2,1)S(1)}, bf16[2,352,128]{2,1,0:T(8,128)(2,1)S(1)}, u32[]{:S(2)}, u32[]{:S(2)}) collective-permute-start(bf16[2,352,128]{2,1,0:T(8,128)(2,1)S(1)} %add_add_fusion.rest_1_), channel_id=1, source_target_pairs={{0,8},{8,0},{16,24},{24,16},{1,9},{9,1},{17,25},{25,17},{2,10},{10... | collective-permute-start | bytes 540680 | tf_op jit(solution)/shard_map/ppermute | solution.py:241
  74.2 19.9 %slice-start.1 = ((s8[6291456]{0:T(1024)(128)(4,1)}), s8[4194304]{0:T(1024)(128)(4,1)S(1)}, s32[]{:S(2)}) async-start(s8[6291456]{0:T(1024)(128)(4,1)} %bitcast.83), calls=%async_computation.6 | async-start | bytes 8388608
  82.8 4.3 %collective-permute-start.14 = (f32[32,384]{1,0:T(8,128)}, f32[32,384]{1,0:T(8,128)S(1)}, u32[]{:S(2)}, u32[]{:S(2)}) collective-permute-start(f32[32,384]{1,0:T(8,128)} %logits.1), channel_id=1, source_target_pairs={{0,1},{1,0},{2,3},{3,2},{4,5},{5,4},{6,7},{7,6},{8,9},{9,8},{10,11... | collective-permute-start | bytes 147464 | tf_op jit(solution)/shard_map/ppermute | solution.py:857
  87.9 22.4 %copy-start.7 = (f32[32,384]{1,0:T(8,128)}, f32[32,384]{1,0:T(8,128)S(1)}, u32[]{:S(2)}) copy-start(f32[32,384]{1,0:T(8,128)S(1)} %add.178.rest_0_) | copy-start | bytes 147460
  87.9 4.1 %collective-permute-start.17 = (f32[32,384]{1,0:T(8,128)S(1)}, f32[32,384]{1,0:T(8,128)S(1)}, u32[]{:S(2)}, u32[]{:S(2)}) collective-permute-start(f32[32,384]{1,0:T(8,128)S(1)} %add.178.rest_0_), channel_id=1, source_target_pairs={{0,6},{1,7},{2,0},{3,1},{4,2},{5,3},{6,4},{7,5},{8,14},{9,15},{10,... | collective-permute-start | bytes 147464 | tf_op jit(solution)/shard_map/ppermute | solution.py:859
  88.0 5.5 %collective-permute-start.16 = (f32[32,384]{1,0:T(8,128)S(1)}, f32[32,384]{1,0:T(8,128)S(1)}, u32[]{:S(2)}, u32[]{:S(2)}) collective-permute-start(f32[32,384]{1,0:T(8,128)S(1)} %add.178.rest_0_), channel_id=1, source_target_pairs={{0,4},{1,5},{2,6},{3,7},{4,0},{5,1},{6,2},{7,3},{8,12},{9,13},{10,... | collective-permute-start | bytes 147464 | tf_op jit(solution)/shard_map/ppermute | solution.py:859
  89.1 4.9 %collective-permute-start.15 = (f32[32,384]{1,0:T(8,128)S(1)}, f32[32,384]{1,0:T(8,128)S(1)}, u32[]{:S(2)}, u32[]{:S(2)}) collective-permute-start(f32[32,384]{1,0:T(8,128)S(1)} %add.178.rest_0_), channel_id=1, source_target_pairs={{0,2},{1,3},{2,4},{3,5},{4,6},{5,7},{6,0},{7,1},{8,10},{9,11},{10,... | collective-permute-start | bytes 147464 | tf_op jit(solution)/shard_map/ppermute | solution.py:859
  92.0 18.3 %copy-start.41 = (s32[1,384]{1,0:T(1,128)}, s32[1,384]{1,0:T(1,128)S(1)}, u32[]{:S(2)}) copy-start(s32[1,384]{1,0:T(1,128)S(1)} %broadcast_in_dim.13.cnt_ref) | copy-start | bytes 4612
  92.0 16.1 %copy-start.30 = (f32[32,384]{1,0:T(8,128)}, f32[32,384]{1,0:T(8,128)S(1)}, u32[]{:S(2)}) copy-start(f32[32,384]{1,0:T(8,128)S(1)} %collective-permute-done.17.rest_3_) | copy-start | bytes 147460
  93.5 14.6 %copy-start.31 = (f32[32,384]{1,0:T(8,128)}, f32[32,384]{1,0:T(8,128)S(1)}, u32[]{:S(2)}) copy-start(f32[32,384]{1,0:T(8,128)S(1)} %collective-permute-done.16.rest_2_) | copy-start | bytes 147460
  94.0 14.1 %copy-start.32 = (f32[32,384]{1,0:T(8,128)}, f32[32,384]{1,0:T(8,128)S(1)}, u32[]{:S(2)}) copy-start(f32[32,384]{1,0:T(8,128)S(1)} %collective-permute-done.15.rest_1_) | copy-start | bytes 147460
  94.0 68.6 %copy-start.2 = (f32[32,64,128]{2,1,0:T(8,128)S(1)}, f32[32,64,128]{2,1,0:T(8,128)}, u32[]{:S(2)}) copy-start(f32[32,64,128]{2,1,0:T(8,128)} %param.21) | copy-start | bytes 3145732
  105.4 2.7 %collective-permute-start.18 = (bf16[2,3,608,128]{3,2,1,0:T(8,128)(2,1)}, bf16[2,3,608,128]{3,2,1,0:T(8,128)(2,1)S(1)}, u32[]{:S(2)}, u32[]{:S(2)}) collective-permute-start(bf16[2,3,608,128]{3,2,1,0:T(8,128)(2,1)} %get-tuple-element.176), channel_id=1, source_target_pairs={{0,8},{8,0},{16,24},{24,16},{1,9},{9,1},{17,25},{25,17},{2,10},{10... | collective-permute-start | bytes 2801672 | tf_op jit(solution)/shard_map/ppermute | solution.py:509
  110.3 8.6 %collective-permute-start.20 = (bf16[3,304,128]{2,1,0:T(8,128)(2,1)S(1)}, bf16[3,304,128]{2,1,0:T(8,128)(2,1)S(1)}, u32[]{:S(2)}, u32[]{:S(2)}) collective-permute-start(bf16[3,304,128]{2,1,0:T(8,128)(2,1)S(1)} %get-tuple-element.277), channel_id=1, source_target_pairs={{0,16},{8,24},{16,0},{24,8},{1,17},{9,25},{17,1},{25,9},{2,18},{10... | collective-permute-start | bytes 700424 | tf_op jit(solution)/shard_map/ppermute | solution.py:515
  111.5 11.6 %collective-permute-start.19 = (bf16[3,304,128]{2,1,0:T(8,128)(2,1)S(1)}, bf16[3,304,128]{2,1,0:T(8,128)(2,1)S(1)}, u32[]{:S(2)}, u32[]{:S(2)}) collective-permute-start(bf16[3,304,128]{2,1,0:T(8,128)(2,1)S(1)} %get-tuple-element.279), channel_id=1, source_target_pairs={{0,16},{8,24},{16,0},{24,8},{1,17},{9,25},{17,1},{25,9},{2,18},{10... | collective-permute-start | bytes 700424 | tf_op jit(solution)/shard_map/ppermute | solution.py:515
  120.7 9.6 %collective-permute-start.24 = (bf16[3,304,128]{2,1,0:T(8,128)(2,1)S(1)}, bf16[3,304,128]{2,1,0:T(8,128)(2,1)S(1)}, u32[]{:S(2)}, u32[]{:S(2)}) collective-permute-start(bf16[3,304,128]{2,1,0:T(8,128)(2,1)S(1)} %added.3), channel_id=1, source_target_pairs={{2,0},{4,2},{6,4},{7,6},{5,7},{3,5},{1,3},{0,1},{10,8},{12,10},{14... | collective-permute-start | bytes 700424 | tf_op jit(solution)/shard_map/ppermute | solution.py:252
  124.9 14.5 %copy-start.4 = (bf16[3,304,128]{2,1,0:T(8,128)(2,1)}, bf16[3,304,128]{2,1,0:T(8,128)(2,1)S(1)}, u32[]{:S(2)}) copy-start(bf16[3,304,128]{2,1,0:T(8,128)(2,1)S(1)} %added.2) | copy-start | bytes 700420
  124.9 9.5 %collective-permute-start.21 = (bf16[3,304,128]{2,1,0:T(8,128)(2,1)S(1)}, bf16[3,304,128]{2,1,0:T(8,128)(2,1)S(1)}, u32[]{:S(2)}, u32[]{:S(2)}) collective-permute-start(bf16[3,304,128]{2,1,0:T(8,128)(2,1)S(1)} %added.2), channel_id=1, source_target_pairs={{0,2},{2,4},{4,6},{6,7},{7,5},{5,3},{3,1},{1,0},{8,10},{10,12},{12... | collective-permute-start | bytes 700424 | tf_op jit(solution)/shard_map/ppermute | solution.py:251
  128.2 11.1 %collective-permute-start.22 = (bf16[3,304,128]{2,1,0:T(8,128)(2,1)S(1)}, bf16[3,304,128]{2,1,0:T(8,128)(2,1)S(1)}, u32[]{:S(2)}, u32[]{:S(2)}) collective-permute-start(bf16[3,304,128]{2,1,0:T(8,128)(2,1)S(1)} %added.3), channel_id=1, source_target_pairs={{0,2},{2,4},{4,6},{6,7},{7,5},{5,3},{3,1},{1,0},{8,10},{10,12},{12... | collective-permute-start | bytes 700424 | tf_op jit(solution)/shard_map/ppermute | solution.py:252
  128.8 13.1 %collective-permute-start.23 = (bf16[3,304,128]{2,1,0:T(8,128)(2,1)S(1)}, bf16[3,304,128]{2,1,0:T(8,128)(2,1)S(1)}, u32[]{:S(2)}, u32[]{:S(2)}) collective-permute-start(bf16[3,304,128]{2,1,0:T(8,128)(2,1)S(1)} %added.2), channel_id=1, source_target_pairs={{2,0},{4,2},{6,4},{7,6},{5,7},{3,5},{1,3},{0,1},{10,8},{12,10},{14... | collective-permute-start | bytes 700424 | tf_op jit(solution)/shard_map/ppermute | solution.py:251
  130.3 11.6 %copy-start.14 = (bf16[3,304,128]{2,1,0:T(8,128)(2,1)}, bf16[3,304,128]{2,1,0:T(8,128)(2,1)S(1)}, u32[]{:S(2)}) copy-start(bf16[3,304,128]{2,1,0:T(8,128)(2,1)S(1)} %collective-permute-done.24) | copy-start | bytes 700420
  130.3 11.7 %collective-permute-start.28 = (bf16[3,304,128]{2,1,0:T(8,128)(2,1)S(1)}, bf16[3,304,128]{2,1,0:T(8,128)(2,1)S(1)}, u32[]{:S(2)}, u32[]{:S(2)}) collective-permute-start(bf16[3,304,128]{2,1,0:T(8,128)(2,1)S(1)} %collective-permute-done.24), channel_id=1, source_target_pairs={{2,0},{4,2},{6,4},{7,6},{5,7},{3,5},{1,3},{0,1},{10,8},{12,10},{14... | collective-permute-start | bytes 700424 | tf_op jit(solution)/shard_map/ppermute | solution.py:252
  134.4 7.6 %copy-start.15 = (bf16[3,304,128]{2,1,0:T(8,128)(2,1)}, bf16[3,304,128]{2,1,0:T(8,128)(2,1)S(1)}, u32[]{:S(2)}) copy-start(bf16[3,304,128]{2,1,0:T(8,128)(2,1)S(1)} %collective-permute-done.21) | copy-start | bytes 700420
  134.4 10.0 %collective-permute-start.25 = (bf16[3,304,128]{2,1,0:T(8,128)(2,1)S(1)}, bf16[3,304,128]{2,1,0:T(8,128)(2,1)S(1)}, u32[]{:S(2)}, u32[]{:S(2)}) collective-permute-start(bf16[3,304,128]{2,1,0:T(8,128)(2,1)S(1)} %collective-permute-done.21), channel_id=1, source_target_pairs={{0,2},{2,4},{4,6},{6,7},{7,5},{5,3},{3,1},{1,0},{8,10},{10,12},{12... | collective-permute-start | bytes 700424 | tf_op jit(solution)/shard_map/ppermute | solution.py:251
  139.4 5.0 %copy-start.16 = (bf16[3,304,128]{2,1,0:T(8,128)(2,1)}, bf16[3,304,128]{2,1,0:T(8,128)(2,1)S(1)}, u32[]{:S(2)}) copy-start(bf16[3,304,128]{2,1,0:T(8,128)(2,1)S(1)} %collective-permute-done.22) | copy-start | bytes 700420
  139.4 10.0 %collective-permute-start.26 = (bf16[3,304,128]{2,1,0:T(8,128)(2,1)S(1)}, bf16[3,304,128]{2,1,0:T(8,128)(2,1)S(1)}, u32[]{:S(2)}, u32[]{:S(2)}) collective-permute-start(bf16[3,304,128]{2,1,0:T(8,128)(2,1)S(1)} %collective-permute-done.22), channel_id=1, source_target_pairs={{0,2},{2,4},{4,6},{6,7},{7,5},{5,3},{3,1},{1,0},{8,10},{10,12},{12... | collective-permute-start | bytes 700424 | tf_op jit(solution)/shard_map/ppermute | solution.py:252
  141.9 7.5 %copy-start.17 = (bf16[3,304,128]{2,1,0:T(8,128)(2,1)}, bf16[3,304,128]{2,1,0:T(8,128)(2,1)S(1)}, u32[]{:S(2)}) copy-start(bf16[3,304,128]{2,1,0:T(8,128)(2,1)S(1)} %collective-permute-done.23) | copy-start | bytes 700420
  141.9 10.0 %collective-permute-start.27 = (bf16[3,304,128]{2,1,0:T(8,128)(2,1)S(1)}, bf16[3,304,128]{2,1,0:T(8,128)(2,1)S(1)}, u32[]{:S(2)}, u32[]{:S(2)}) collective-permute-start(bf16[3,304,128]{2,1,0:T(8,128)(2,1)S(1)} %collective-permute-done.23), channel_id=1, source_target_pairs={{2,0},{4,2},{6,4},{7,6},{5,7},{3,5},{1,3},{0,1},{10,8},{12,10},{14... | collective-permute-start | bytes 700424 | tf_op jit(solution)/shard_map/ppermute | solution.py:251
  142.0 9.9 %copy-start.18 = (bf16[3,304,128]{2,1,0:T(8,128)(2,1)}, bf16[3,304,128]{2,1,0:T(8,128)(2,1)S(1)}, u32[]{:S(2)}) copy-start(bf16[3,304,128]{2,1,0:T(8,128)(2,1)S(1)} %collective-permute-done.28) | copy-start | bytes 700420
  142.0 9.9 %collective-permute-start.32 = (bf16[3,304,128]{2,1,0:T(8,128)(2,1)S(1)}, bf16[3,304,128]{2,1,0:T(8,128)(2,1)S(1)}, u32[]{:S(2)}, u32[]{:S(2)}) collective-permute-start(bf16[3,304,128]{2,1,0:T(8,128)(2,1)S(1)} %collective-permute-done.28), channel_id=1, source_target_pairs={{2,0},{4,2},{6,4},{7,6},{5,7},{3,5},{1,3},{0,1},{10,8},{12,10},{14... | collective-permute-start | bytes 700424 | tf_op jit(solution)/shard_map/ppermute | solution.py:252
  144.4 7.5 %copy-start.19 = (bf16[3,304,128]{2,1,0:T(8,128)(2,1)}, bf16[3,304,128]{2,1,0:T(8,128)(2,1)S(1)}, u32[]{:S(2)}) copy-start(bf16[3,304,128]{2,1,0:T(8,128)(2,1)S(1)} %collective-permute-done.25) | copy-start | bytes 700420
  144.4 10.0 %collective-permute-start.29 = (bf16[3,304,128]{2,1,0:T(8,128)(2,1)S(1)}, bf16[3,304,128]{2,1,0:T(8,128)(2,1)S(1)}, u32[]{:S(2)}, u32[]{:S(2)}) collective-permute-start(bf16[3,304,128]{2,1,0:T(8,128)(2,1)S(1)} %collective-permute-done.25), channel_id=1, source_target_pairs={{0,2},{2,4},{4,6},{6,7},{7,5},{5,3},{3,1},{1,0},{8,10},{10,12},{12... | collective-permute-start | bytes 700424 | tf_op jit(solution)/shard_map/ppermute | solution.py:251
  149.4 10.0 %collective-permute-start.30 = (bf16[3,304,128]{2,1,0:T(8,128)(2,1)S(1)}, bf16[3,304,128]{2,1,0:T(8,128)(2,1)S(1)}, u32[]{:S(2)}, u32[]{:S(2)}) collective-permute-start(bf16[3,304,128]{2,1,0:T(8,128)(2,1)S(1)} %collective-permute-done.26), channel_id=1, source_target_pairs={{0,2},{2,4},{4,6},{6,7},{7,5},{5,3},{3,1},{1,0},{8,10},{10,12},{12... | collective-permute-start | bytes 700424 | tf_op jit(solution)/shard_map/ppermute | solution.py:252
  151.9 7.5 %collective-permute-start.31 = (bf16[3,304,128]{2,1,0:T(8,128)(2,1)S(1)}, bf16[3,304,128]{2,1,0:T(8,128)(2,1)S(1)}, u32[]{:S(2)}, u32[]{:S(2)}) collective-permute-start(bf16[3,304,128]{2,1,0:T(8,128)(2,1)S(1)} %collective-permute-done.27), channel_id=1, source_target_pairs={{2,0},{4,2},{6,4},{7,6},{5,7},{3,5},{1,3},{0,1},{10,8},{12,10},{14... | collective-permute-start | bytes 700424 | tf_op jit(solution)/shard_map/ppermute | solution.py:251
  151.9 9.0 %collective-permute-start.34 = (bf16[3,304,128]{2,1,0:T(8,128)(2,1)S(1)}, bf16[3,304,128]{2,1,0:T(8,128)(2,1)S(1)}, u32[]{:S(2)}, u32[]{:S(2)}) collective-permute-start(bf16[3,304,128]{2,1,0:T(8,128)(2,1)S(1)} %collective-permute-done.32), channel_id=1, source_target_pairs={{2,0},{4,2},{6,4},{7,6},{5,7},{3,5},{1,3},{0,1},{10,8},{12,10},{14... | collective-permute-start | bytes 700424 | tf_op jit(solution)/shard_map/ppermute | solution.py:255
  154.4 8.3 %collective-permute-start.33 = (bf16[3,304,128]{2,1,0:T(8,128)(2,1)S(1)}, bf16[3,304,128]{2,1,0:T(8,128)(2,1)S(1)}, u32[]{:S(2)}, u32[]{:S(2)}) collective-permute-start(bf16[3,304,128]{2,1,0:T(8,128)(2,1)S(1)} %collective-permute-done.29), channel_id=1, source_target_pairs={{0,2},{2,4},{4,6},{6,7},{7,5},{5,3},{3,1},{1,0},{8,10},{10,12},{12... | collective-permute-start | bytes 700424 | tf_op jit(solution)/shard_map/ppermute | solution.py:255
  175.2 1.3 copy-start.3
  (14 other events, 12.4 us)

commit v8 on v7

--- a/solution.py
+++ b/solution.py
@@ -70,16 +70,15 @@
 
 
 def extract_kernel(rows, planes_here, *refs):
-    plane_ref, line_ref, weight_hbm, vol_hbm, keep_a, send_a = refs[:6]
+    plane_ref, line_ref, weight_hbm, vol_hbm = refs[:4]
+    parts_a = (refs[4:6], refs[6:8])
     vol, pair, idx_v, flag_v, idx_s, flag_s, w_s, sem = refs[-8:]
-    parts_b = refs[6:-8]
+    parts_b = refs[8:-8]
     slab = lax.axis_index("vol")
     share = idx_v.shape[0] // 2
     first = lax.axis_index("img") * share
     height = planes_here * ROWS
-    count_z = keep_a.shape[0]
-    groups_a = keep_a.shape[2] // 16
-    groups_b = parts_b[0].shape[2] // 16
+    count_z = len(parts_b)
     load = pltpu.make_async_copy(vol_hbm, vol.at[:, :height, :], sem.at[0])
     load.start()
     loads_w = [
@@ -118,7 +117,7 @@
     to_idx.start()
     to_flag.start()
     vol[:, height : height + 8, :] = jnp.zeros((2, 8, COLS), F32)
-    for ref in (keep_a, send_a) + parts_b:
+    for ref in refs[4:-8]:
         ref[...] = jnp.zeros_like(ref)
     to_idx.wait()
     to_flag.wait()
@@ -154,35 +153,40 @@
             z = (slab >> 1) + dz
             block = jnp.where(z >= count_z, z - count_z, z) * 2 + ((slab + dy) & 1)
             places.append((dz, dy, block))
-    share_a = keep_a.shape[2] // rows
-    for k0, count in ((0, share_a), (share_a, share - share_a)):
-
-        def turn(t, carry, k0=k0):
+    k0 = 0
+    for part in range(3):
+        count = (parts_a + (parts_b,))[part][0].shape[2] // rows
+
+        def turn(t, carry, k0=k0, part=part):
             k = k0 + t * per_k
             words = [flag_s[k, 0], flag_s[k, 1]]
             for i in range(1, per_k):
                 words = [words[0] | flag_s[k + i, 0], words[1] | flag_s[k + i, 1]]
             for dz, dy, block in places:
-                out, lead = ((keep_a, send_a)[dy], dz) if k0 == 0 else (parts_b[dz], dy)
+                out, lead = (parts_a[part][dy], dz) if part < 2 else (parts_b[dz], dy)
                 for g in range(per_block):
                     base = pl.multiple_of((t * per_block + g) * 16, 16)
                     message(out, lead, k, words, block * rows + 16 * g, base)
             return carry
 
         lax.fori_loop(0, count // per_k, turn, 0)
-
-
-def extract(volume, row_plane, row_line, row_weight, n_vol, share, share_a):
+        k0 += count
+
+
+def extract(volume, row_plane, row_line, row_weight, n_vol, shares):
     planes_here = volume.shape[1]
     rows = ROWS // n_vol
     count_z = n_vol // 2
-    shape_a = jax.ShapeDtypeStruct((count_z, 2, share_a * rows, COLS), BF16)
-    shape_b = jax.ShapeDtypeStruct((2, 2, (share - share_a) * rows, COLS), BF16)
+    share = sum(shares)
+    shape_a, shape_c = [
+        jax.ShapeDtypeStruct((count_z, 2, n * rows, COLS), BF16) for n in shares[:2]
+    ]
+    shape_b = jax.ShapeDtypeStruct((2, 2, shares[2] * rows, COLS), BF16)
     return pl.pallas_call(
         partial(extract_kernel, rows, planes_here),
-        out_shape=[shape_a, shape_a] + [shape_b] * count_z,
+        out_shape=[shape_a, shape_a, shape_c, shape_c] + [shape_b] * count_z,
         in_specs=[vmem(), vmem(), hbm(), hbm()],
-        out_specs=[vmem()] * (2 + count_z),
+        out_specs=[vmem()] * (4 + count_z),
         scratch_shapes=[
             pltpu.VMEM((2, planes_here * ROWS + 8, COLS), F32),
             pltpu.VMEM((2, 32, COLS), F32),
@@ -199,60 +203,61 @@
     )(row_plane, row_line, row_weight, volume.reshape(2, planes_here * ROWS, COLS))
 
 
-def combine_first_kernel(keep_a, got_a, keep_b, *rest):
-    count_z = keep_a.shape[0]
-    got_b = rest[: count_z - 1]
-    out_a = rest[count_z : 2 * count_z]
-    out_b = rest[2 * count_z :]
-    for d in range(count_z):
-        out_a[d][...] = keep_a[d] + got_a[d]
-    for d in range(2):
-        total = keep_b[d]
-        for ref in got_b:
+def combine_kernel(count, *refs):
+    outs = refs[count + 1 :]
+    for d, out in enumerate(outs):
+        total = refs[0][d]
+        for ref in refs[1:count]:
             total = total + ref[d]
-        out_b[d][...] = total
+        out[...] = total
+
+
+def combine(terms, after):
+    shape = terms[0].shape
+    return pl.pallas_call(
+        partial(combine_kernel, len(terms)),
+        out_shape=[jax.ShapeDtypeStruct(shape[1:], BF16)] * shape[0],
+        in_specs=[vmem()] * len(terms) + [hbm()],
+        out_specs=[vmem()] * shape[0],
+        compiler_params=pltpu.CompilerParams(vmem_limit_bytes=VMEM_LIMIT),
+        cost_estimate=cost(2),
+        name="combine",
+    )(*terms, after)
 
 
 def to_pixel_rows(messages, n_vol, first_with):
-    keep_a, send_a, keep_b = messages[:3]
+    keep_1, send_1, keep_2, send_2, keep_b = messages[:5]
     count_z = n_vol // 2
-    got_b = [lax.ppermute(m, "vol", along_z(n_vol, d + 1)) for d, m in enumerate(messages[3:])]
-    got_a = lax.ppermute(send_a, "vol", flip(n_vol, 1))
-    shape_a = jax.ShapeDtypeStruct(keep_a.shape[1:], BF16)
-    shape_b = jax.ShapeDtypeStruct(keep_b.shape[1:], BF16)
-    sums = pl.pallas_call(
-        combine_first_kernel,
-        out_shape=[shape_a] * count_z + [shape_b] * 2,
-        in_specs=[vmem()] * (2 + count_z) + [hbm()],
-        out_specs=[vmem()] * (count_z + 2),
-        compiler_params=pltpu.CompilerParams(vmem_limit_bytes=VMEM_LIMIT),
-        cost_estimate=cost(3),
-        name="combine_first",
-    )(keep_a, got_a, keep_b, *got_b, first_with)
-    sums_a, sums_b = sums[:count_z], sums[count_z:]
+    got_1 = lax.ppermute(send_1, "vol", flip(n_vol, 1))
+    got_b = [lax.ppermute(m, "vol", along_z(n_vol, d + 1)) for d, m in enumerate(messages[5:])]
+    got_2 = lax.ppermute(send_2, "vol", flip(n_vol, 1))
+    sums_1 = combine([keep_1, got_1], first_with)
+    moved_1 = [lax.ppermute(sums_1[d], "vol", along_z(n_vol, d)) for d in range(1, count_z)]
+    sums_b = combine([keep_b, *got_b], sums_1[0])
     moved_b = lax.ppermute(sums_b[1], "vol", flip(n_vol, 1))
-    moved = [lax.ppermute(sums_a[d], "vol", along_z(n_vol, d)) for d in range(1, count_z)]
-    out_b = sums_b[0] + moved_b
-    out_a = sum(moved, sums_a[0])
-    return out_a, out_b
+    sums_2 = combine([keep_2, got_2], sums_b[0])
+    moved_2 = [lax.ppermute(sums_2[d], "vol", along_z(n_vol, d)) for d in range(1, count_z)]
+    return [added(sums_1[0], *moved_1), added(sums_2[0], *moved_2), added(sums_b[0], moved_b)]
 
 
 def from_partners(x, n_img):
     return [x] + [lax.ppermute(x, "img", flip(n_img, m)) for m in range(1, n_img)]
 
 
-def ring_gather(low, high, n_vol):
+def ring_gather(low, high_terms, n_vol):
     ring = ring_of(n_vol)
     ahead = [(ring[p], ring[(p + 1) % n_vol]) for p in range(n_vol)]
     back = [(b, a) for a, b in ahead]
+    one_low, two_low = lax.ppermute(low, "vol", ahead), lax.ppermute(low, "vol", back)
+    high = added(*high_terms, after=[one_low, two_low])
     pieces = [low, high]
-    one = two = (low, high)
-    for _ in range(1, n_vol // 2):
-        one_low, two_low = lax.ppermute(one[0], "vol", ahead), lax.ppermute(two[0], "vol", back)
-        one_high, two_high = lax.ppermute(one[1], "vol", ahead), lax.ppermute(two[1], "vol", back)
-        one, two = (one_low, one_high), (two_low, two_high)
-        pieces += [*one, *two]
-    return pieces + [lax.ppermute(one[0], "vol", ahead), lax.ppermute(two[1], "vol", back)]
+    one_high, two_high = high, high
+    for d in range(1, n_vol // 2):
+        if d > 1:
+            one_low, two_low = lax.ppermute(one_low, "vol", ahead), lax.ppermute(two_low, "vol", back)
+        one_high, two_high = lax.ppermute(one_high, "vol", ahead), lax.ppermute(two_high, "vol", back)
+        pieces += [one_low, one_high, two_low, two_high]
+    return pieces + [lax.ppermute(one_low, "vol", ahead), lax.ppermute(two_high, "vol", back)]
 
 
 def weigh_kernel(img_ref, sa_ref, ca_ref, sx_ref, cx_ref, nw_ref, wt_ref, sq_ref, buf):
@@ -317,7 +322,7 @@
     sl_refs = rest[1:-4]
     out_ref, part, acc, quad = rest[-4:]
     step = pl.program_id(0)
-    groups = len(sl_refs) // 2
+    groups = len(sl_refs) // 3
     rows = part.shape[1] // K - 1
     share = K // groups
     pitch = rows + 1
@@ -327,7 +332,7 @@
     def _():
         for m in range(groups):
             at = m * share
-            for ref in sl_refs[2 * m : 2 * m + 2]:
+            for ref in sl_refs[3 * m : 3 * m + 3]:
                 for j in range(2):
                     for k in range(ref.shape[1] // rows):
                         row = (at + k) * pitch
@@ -508,32 +513,32 @@
 def to_member(keep, send, n_img):
     got = lax.ppermute(send, "img", flip(n_img, 1))
     half = keep.shape[2] // 2
-    owns = []
+    terms = []
     for h in range(2):
         cut = slice(h * half, (h + 1) * half)
         summed = [keep[m, :, cut] + got[m, :, cut] for m in range(n_img // 2)]
         moved = [lax.ppermute(summed[m], "img", flip(n_img, 2 * m)) for m in range(1, n_img // 2)]
-        owns.append(added(summed[0], *moved))
-    return owns
-
-
-def added_kernel(*refs):
+        terms.append([summed[0], *moved])
+    return terms
+
+
+def added_kernel(count, *refs):
     total = refs[0][...]
-    for ref in refs[1:-1]:
+    for ref in refs[1:count]:
         total = total + ref[...]
     refs[-1][...] = total
 
 
-def added(*terms):
+def added(*terms, after=()):
     return pl.pallas_call(
-        added_kernel,
+        partial(added_kernel, len(terms)),
         out_shape=jax.ShapeDtypeStruct(terms[0].shape, terms[0].dtype),
-        in_specs=[vmem()] * len(terms),
+        in_specs=[vmem()] * len(terms) + [hbm()] * len(after),
         out_specs=vmem(),
         compiler_params=pltpu.CompilerParams(vmem_limit_bytes=VMEM_LIMIT),
         cost_estimate=cost(1),
         name="added",
-    )(*terms)
+    )(*terms, *after)
 
 
 HEAD = 8
@@ -583,8 +588,8 @@
         )
 
         def group_step(g, carry, block=block):
-            at = block * lead + g * 4
-            for u in range(4):
+            at = block * lead + g * 8
+            for u in range(8):
                 code = code_s[at + u]
                 s = code & 1023
                 to = code >> 10
@@ -596,7 +601,7 @@
                     into[c, pl.ds(to, 2), :] = into[c, pl.ds(to, 2), :] + both * row
             return carry
 
-        lax.fori_loop(0, (jnp.minimum(len_s[block, 0], cap) + 3) // 4, group_step, 0)
+        lax.fori_loop(0, (jnp.minimum(len_s[block, 0], cap) + 7) // 8, group_step, 0)
 
     prior.wait()
     chunks = sem_out.shape[0]
@@ -838,8 +843,10 @@
     weight_share = lax.dynamic_slice_in_dim(row_weight, first, share, 0)
 
     aligned = max(1, 16 // rows)
-    share_a = share * 11 // 16 // aligned * aligned
-    messages = extract(volume, row_plane, row_line, row_weight, n_vol, share, share_a)
+    share_b = max(1, share * 5 // 16 // aligned) * aligned
+    share_2 = max(1, (share - share_b) // 2 // aligned) * aligned
+    shares = (share - share_b - share_2, share_2, share_b)
+    messages = extract(volume, row_plane, row_line, row_weight, n_vol, shares)
     cosine, sine = shift_phases(row_freq, col_freq, TRANS)
     weighted, squared = weigh(images, defocus, noise_weight, row_freq, col_freq)
     mean = rows * K // n_img
@@ -847,10 +854,10 @@
     src, code, wgt, send_len, recv_len, longest = lists(
         row_plane, row_line, row_weight, n_vol, n_img, planes_here, lines_here, cap
     )
-    own_a, own_b = to_pixel_rows(messages, n_vol, weighted)
-    slices_b = from_partners(own_b, n_img)
-    slices_a = from_partners(own_a, n_img)
-    slices = [x for both in zip(slices_a, slices_b) for x in both]
+    owns = to_pixel_rows(messages, n_vol, weighted)
+    parts = [from_partners(own, n_img) for own in (owns[2], owns[0], owns[1])]
+    slices = [x for three in zip(parts[1], parts[2], parts[0]) for x in three]
+
     cand = candidates.T
     count_row = counts[None, :]
     partial_logits = candidate_logits(code, slices, weighted, squared, cosine, sine, cand)
@@ -862,8 +869,8 @@
     keep, send = project(
         src.reshape(-1), send_len, n_img, logits, cand, count_row, weighted, squared, cosine, sine, cap
     )
-    low, high = to_member(keep, send, n_img)
-    pieces = ring_gather(low, high, n_vol)
+    low_terms, high_terms = to_member(keep, send, n_img)
+    pieces = ring_gather(added(*low_terms), high_terms, n_vol)
 
     def listed():
         return insert(recv_len, code.reshape(-1), wgt.reshape(-1), pieces, regularizer)

time: 184 us -> 191 us (1.038)
  Pallas kernels: 62.6 us -> 68.7 us
  starting transfers between devices: 43 us -> 48.5 us
  waiting for transfers between devices: 45.6 us -> 41.4 us
  other arithmetic: 8.38 us -> 6.47 us
    pallas_call x3 -> x8, Pallas kernels: 4.88 us -> 13 us  [the longest x5 7.31 us: added(): pl.pallas_call(partial(added_kernel, len(terms)), out_shape=jax.ShapeDtyp...]
    ppermute x6 -> x9, starting transfers between devices: 4.06 us -> 10.8 us  [from_partners(): lax.ppermute(x, 'img', flip(n_img, m))]
    ppermute x18 -> x22, waiting for transfers between devices: 29.7 us -> 25.2 us  [the longest x3 7.09 us: ring_gather(): lax.ppermute(one_low, 'vol', ahead)]
    pallas_call x1, Pallas kernels: 11.2 us -> 9.03 us  [insert(): pl.pallas_call(partial(insert_kernel, count), out_shape=jax.ShapeDtypeStr...]
    ppermute x3, waiting for transfers between devices: 2.05 us -> 4.04 us  [body(): lax.ppermute(pair_logits, 'vol', along_z(n_vol, d))]
    ppermute x3, starting transfers between devices: 4.06 us -> 2.07 us  [body(): lax.ppermute(pair_logits, 'vol', along_z(n_vol, d))]
    unnamed x70 -> x92, local copies, waits for them, and re-layouts: 4.39 us -> 5.64 us
    ppermute x18 -> x22, starting transfers between devices: 28.5 us -> 28.2 us  [the longest x3 4.93 us: to_pixel_rows(): lax.ppermute(sums_2[d], 'vol', along_z(n_vol, d))]
  transfers between devices with their start and end apart: 35 -> 42, of which waited for: 20 -> 18; matrix products, arithmetic and copies ran while one was open for 5% -> 4% of each run, Pallas kernels for 9% -> 12%
where the time goes in v8:
time: 191 us; the launch traced here: 190 us
  Pallas kernels  68.7 us (36%)
  starting transfers between devices  48.5 us (25%)
  waiting for transfers between devices  41.4 us (22%)
  between operations  14.4 us (8%)
  local copies, waits for them, and re-layouts  10.6 us (6%)
  other arithmetic  6.47 us (3%)
    pallas_call x1, Pallas kernels, extract(): pl.pallas_call(partial(extract_kernel, rows, planes_here), out_shape=[sha...  13.1 us
    pallas_call x1, Pallas kernels, project(): pl.pallas_call(project_kernel, grid=(rows // inner,), out_shape=[jax.Shap...  11.3 us
    ppermute x9, starting transfers between devices, from_partners(): lax.ppermute(x, 'img', flip(n_img, m))  10.8 us
    pallas_call x1, Pallas kernels, insert(): pl.pallas_call(partial(insert_kernel, count), out_shape=jax.ShapeDtypeStr...  9.03 us
    pallas_call x1, Pallas kernels, candidate_logits(): pl.pallas_call(logits_kernel, grid=(rows // inner,), out_shape=jax.ShapeD...  8.63 us
    pallas_call x1, Pallas kernels, weigh(): pl.pallas_call(weigh_kernel, grid=(count // step,), out_shape=[jax.ShapeD...  8.39 us
    pallas_call x5, Pallas kernels, added(): pl.pallas_call(partial(added_kernel, len(terms)), out_shape=jax.ShapeDtyp...  7.31 us
    ppermute x3, waiting for transfers between devices, ring_gather(): lax.ppermute(one_low, 'vol', ahead)  7.09 us
  transfers between devices with their start and end apart: 42, of which 18 were waited for; matrix products, arithmetic and copies ran while one was open for 4% of the time, Pallas kernels for 12%

profile of v8, /device:TPU:12, one launch (start us, length us, event | category | flops | bytes accessed | tf_op | source)
XLA Modules:
  0.0 190.1 jit_solution(9875448393444144192)
XLA Ops:
  6.5 13.1 %extract.1 = (bf16[4,2,192,128]{3,2,1,0:T(8,128)(2,1)}, bf16[4,2,192,128]{3,2,1,0:T(8,128)(2,1)}, bf16[4,2,160,128]{3,2,1,0:T(8,128)(2,1)}, bf16[4,2,160,128]{3,...) custom-call(s32[64,256]{1,0:T(8,128)} %refs_0_.1, ...), custom_call_target="tpu_custom_call" | custom-call | bytes 40590000 | tf_op jit(solution)/shard_map/extract/pallas_call | solution.py:185
  19.7 1.9 %collective-permute-start.7 = (bf16[2,2,160,128]{3,2,1,0:T(8,128)(2,1)}, bf16[2,2,160,128]{3,2,1,0:T(8,128)(2,1)S(1)}, u32[]{:S(2)}, u32[]{:S(2)}) collective-permute-start(bf16[2,2,160,128]{3,2,1,0:T(8,128)(2,1)} %get-tuple-element.176), channel_id=1, source_target_pairs={{0,6},{1,7},{2,0},{3,1},{4,2},{5,3},{6,4},{7,5},{8,14},{9,15},{10,... | collective-permute-start | bytes 491528 | tf_op jit(solution)/shard_map/ppermute | solution.py:232
  21.7 2.2 %collective-permute-start.4 = (bf16[4,2,160,128]{3,2,1,0:T(8,128)(2,1)}, bf16[4,2,160,128]{3,2,1,0:T(8,128)(2,1)S(1)}, u32[]{:S(2)}, u32[]{:S(2)}) collective-permute-start(bf16[4,2,160,128]{3,2,1,0:T(8,128)(2,1)} %get-tuple-element.172), channel_id=1, source_target_pairs={{0,1},{1,0},{2,3},{3,2},{4,5},{5,4},{6,7},{7,6},{8,9},{9,8},{10,11... | collective-permute-start | bytes 983048 | tf_op jit(solution)/shard_map/ppermute | solution.py:233
  23.9 1.5 multiply_cosine_fusion
  25.4 1.5 fusion.21
  26.9 8.4 %weigh.1 = (bf16[32,384,256]{2,1,0:T(8,128)(2,1)S(1)}, bf16[32,384,128]{2,1,0:T(8,128)(2,1)}) custom-call(bf16[2,384,32,128]{3,2,1,0:T(8,128)(2,1)} %img_ref.1, f32[384,32]{1,0:T(8,128)} %get-tuple-element.298.sa_ref, f32[384,32]{1,0:T(8,128)} %get-tuple-element.297.ca_ref, f32[384,128]{1,0:T(8,128)} %get-tuple-element.296.sx_ref, ...), custom_call_target="tpu_custom_call" | custom-call | bytes 44280000 | tf_op jit(solution)/shard_map/weigh/pallas_call | solution.py:288
  35.5 3.1 %collective-permute-done.refs_1_ = bf16[4,2,192,128]{3,2,1,0:T(8,128)(2,1)S(1)} collective-permute-done((bf16[4,2,192,128]{3,2,1,0:T(8,128)(2,1)}, bf16[4,2,192,128]{3,2,1,0:T(8,128)(2,1)S(1)}, u32[]{:S(2)}, u32[]{:S(2)}) %collective-permute-start) | collective-permute-done | bytes 393248 | tf_op jit(solution)/shard_map/ppermute | solution.py:231
  39.3 2.0 %combine.3 = (bf16[2,192,128]{2,1,0:T(8,128)(2,1)}, bf16[2,192,128]{2,1,0:T(8,128)(2,1)}, bf16[2,192,128]{2,1,0:T(8,128)(2,1)}, bf16[2,192,128]{2,1,0:T(8,128)(2,1)}) custom-call(bf16[4,2,192,128]{3,2,1,0:T(8,128)(2,1)} %get-tuple-element.165.refs_0_, bf16[4,2,192,128]{3,2,1,0:T(8,128)(2,1)} %copy-done.12, ...), custom_call_target="tpu_custom_call" | custom-call | bytes 7380000 | tf_op jit(solution)/shard_map/combine/pallas_call | solution.py:217
  42.0 1.9 combine.4
  44.6 1.9 combine.5
  46.5 1.2 collective-permute-start.8
  47.7 3.7 %collective-permute-start.9 = (bf16[2,160,128]{2,1,0:T(8,128)(2,1)}, bf16[2,160,128]{2,1,0:T(8,128)(2,1)S(1)}, u32[]{:S(2)}, u32[]{:S(2)}) collective-permute-start(bf16[2,160,128]{2,1,0:T(8,128)(2,1)} %get-tuple-element.180), channel_id=1, source_target_pairs={{0,4},{1,5},{2,6},{3,7},{4,0},{5,1},{6,2},{7,3},{8,12},{9,13},{10,... | collective-permute-start | bytes 245768 | tf_op jit(solution)/shard_map/ppermute | solution.py:239
  51.4 1.7 collective-permute-start.11
  53.2 2.0 %collective-permute-start.1 = (bf16[2,192,128]{2,1,0:T(8,128)(2,1)}, bf16[2,192,128]{2,1,0:T(8,128)(2,1)S(1)}, u32[]{:S(2)}, u32[]{:S(2)}) collective-permute-start(bf16[2,192,128]{2,1,0:T(8,128)(2,1)} %get-tuple-element.168), channel_id=1, source_target_pairs={{0,2},{1,3},{2,4},{3,5},{4,6},{5,7},{6,0},{7,1},{8,10},{9,11},{10,... | collective-permute-start | bytes 294920 | tf_op jit(solution)/shard_map/ppermute | solution.py:235
  55.2 1.8 collective-permute-start.2
  57.0 0.9 collective-permute-done.9.refs_2_
  57.9 1.1 collective-permute-done.10.refs_3_
  59.6 1.7 added.6.rest_2_
  61.3 2.4 %collective-permute-start.19 = (bf16[2,160,128]{2,1,0:T(8,128)(2,1)}, bf16[2,160,128]{2,1,0:T(8,128)(2,1)S(1)}, u32[]{:S(2)}, u32[]{:S(2)}) collective-permute-start(bf16[2,160,128]{2,1,0:T(8,128)(2,1)} %added.6.rest_2_), channel_id=1, source_target_pairs={{0,24},{8,16},{16,8},{24,0},{1,25},{9,17},{17,9},{25,1},{2,26},{10... | collective-permute-start | bytes 245768 | tf_op jit(solution)/shard_map/ppermute | solution.py:244
  63.7 3.9 %collective-permute-start.16 = (bf16[2,160,128]{2,1,0:T(8,128)(2,1)}, bf16[2,160,128]{2,1,0:T(8,128)(2,1)S(1)}, u32[]{:S(2)}, u32[]{:S(2)}) collective-permute-start(bf16[2,160,128]{2,1,0:T(8,128)(2,1)} %added.6.rest_2_), channel_id=1, source_target_pairs={{0,16},{8,24},{16,0},{24,8},{1,17},{9,25},{17,1},{25,9},{2,18},{10... | collective-permute-start | bytes 245768 | tf_op jit(solution)/shard_map/ppermute | solution.py:244
  67.5 1.6 added.7.rest_3_
  69.8 0.8 collective-permute-start.20
  70.7 0.9 collective-permute-start.17
  71.6 1.7 added.5.rest_1_
  73.5 1.1 collective-permute-start.18
  74.6 0.9 collective-permute-start.15
  78.3 5.3 %lists.1 = (s32[32,128]{1,0:T(8,128)}, s32[64,128]{1,0:T(8,128)S(1)}, f32[64,128]{1,0:T(8,128)}, s32[8,128]{1,0:T(8,128)}, s32[8,128]{1,0:T(8,128)}, /*index=5*/s32[8,128]{1,0:T(8,128)}) custom-call(s32[8,2048]{1,0:T(8,128)} %reshape.229.plane_ref, s32[8,2048]{1,0:T(8,128)} %reshape.230.line_ref, f32[8,2048]{1,0:T(8,128)} %reshape.231.wgt_ref), custom_call_target="tpu_custom_call" | custom-call | bytes 22140000 | tf_op jit(solution)/shard_map/lists/pallas_call | solution.py:762
  84.3 8.6 %logits.1 = f32[32,384]{1,0:T(8,128)} custom-call(bf16[32,384,256]{2,1,0:T(8,128)(2,1)} %copy-done, bf16[32,384,128]{2,1,0:T(8,128)(2,1)} %get-tuple-element.163.sq_ref, f32[4,32,128]{2,1,0:T(8,128)S(1)} %get-tuple-element.294.cos_ref, f32[4,32,128]{2,1,0:T(8,128)S(1)} %get-tuple-element.293.sin_ref, s32[8,384]{1,0:T(8,128)S(1)} %bitcast.97, ...), custom_call_target="tpu_custom_call" | custom-call | bytes 29520000 | tf_op jit(solution)/shard_map/logits/pallas_call | solution.py:380
  93.0 1.4 collective-permute-start.21
  94.4 2.9 %collective-permute-done.21 = f32[32,384]{1,0:T(8,128)S(1)} collective-permute-done((f32[32,384]{1,0:T(8,128)}, f32[32,384]{1,0:T(8,128)S(1)}, u32[]{:S(2)}, u32[]{:S(2)}) %collective-permute-start.21) | collective-permute-done | bytes 49184 | tf_op jit(solution)/shard_map/ppermute | solution.py:864
  97.3 0.8 add.162.rest_0_
  98.2 1.0 collective-permute-start.23
  99.2 1.1 collective-permute-start.22
  100.2 2.4 %collective-permute-done.24.rest_3_ = f32[32,384]{1,0:T(8,128)S(1)} collective-permute-done((f32[32,384]{1,0:T(8,128)S(1)}, f32[32,384]{1,0:T(8,128)S(1)}, u32[]{:S(2)}, u32[]{:S(2)}) %collective-permute-start.24) | collective-permute-done | bytes 49184 | tf_op jit(solution)/shard_map/ppermute | solution.py:866
  103.4 0.9 collective-permute-done.22.rest_1_
  104.3 11.3 %project.1 = (bf16[2,3,608,128]{3,2,1,0:T(8,128)(2,1)}, bf16[2,3,608,128]{3,2,1,0:T(8,128)(2,1)}) custom-call(s32[4096]{0:T(1024)} %bitcast.104, s32[8,128]{1,0:T(8,128)} %get-tuple-element.186.len_s, s32[8,384]{1,0:T(8,128)S(1)} %bitcast.98, s32[1,384]{1,0:T(1,128)S(1)} %broadcast_in_dim.13.cnt_ref, bf16[32,384,256]{2,1,0:T(8,128)(2,1)S(1)} %bitcast.84, ...), custom_call_target="tpu_custom_call" | custom-call | bytes 44280000 | tf_op jit(solution)/shard_map/project/pallas_call | solution.py:485
  115.6 2.7 %collective-permute-done.25 = bf16[2,3,608,128]{3,2,1,0:T(8,128)(2,1)S(1)} collective-permute-done((bf16[2,3,608,128]{3,2,1,0:T(8,128)(2,1)}, bf16[2,3,608,128]{3,2,1,0:T(8,128)(2,1)S(1)}, u32[]{:S(2)}, u32[]{:S(2)}) %collective-permute-start.25) | collective-permute-done | bytes 933920 | tf_op jit(solution)/shard_map/ppermute | solution.py:514
  118.4 2.2 %fusion.17 = (bf16[3,304,128]{2,1,0:T(8,128)(2,1)S(1)}, bf16[3,304,128]{2,1,0:T(8,128)(2,1)}, bf16[3,304,128]{2,1,0:T(8,128)(2,1)S(1)}, bf16[3,304,128]{2,1,0:T(8,128)(2,1)}) fusion(bf16[2,3,608,128]{3,2,1,0:T(8,128)(2,1)S(1)} %collective-permute-done.25, bf16[2,3,608,128]{3,2,1,0:T(8,128)(2,1)} %get-tuple-element.187), kind=kLoop, calls=%fused_computation.49 | loop fusion | flops 466944 | bytes 2801664 | tf_op jit(solution)/shard_map/add | solution.py:519
  120.5 1.2 collective-permute-start.26
  121.7 0.9 collective-permute-start.27
  122.6 6.5 %collective-permute-done.26.refs_1_ = bf16[3,304,128]{2,1,0:T(8,128)(2,1)S(1)} collective-permute-done((bf16[3,304,128]{2,1,0:T(8,128)(2,1)S(1)}, bf16[3,304,128]{2,1,0:T(8,128)(2,1)S(1)}, u32[]{:S(2)}, u32[]{:S(2)}) %collective-permute-start.26) | collective-permute-done | bytes 233504 | tf_op jit(solution)/shard_map/ppermute | solution.py:520
  129.8 1.1 added.8
  130.9 1.0 collective-permute-start.29
  131.9 2.3 %collective-permute-start.28 = (bf16[3,304,128]{2,1,0:T(8,128)(2,1)S(1)}, bf16[3,304,128]{2,1,0:T(8,128)(2,1)S(1)}, u32[]{:S(2)}, u32[]{:S(2)}) collective-permute-start(bf16[3,304,128]{2,1,0:T(8,128)(2,1)S(1)} %added.8), channel_id=1, source_target_pairs={{0,2},{2,4},{4,6},{6,7},{7,5},{5,3},{3,1},{1,0},{8,10},{10,12},{12... | collective-permute-start | bytes 700424 | tf_op jit(solution)/shard_map/ppermute | solution.py:251
  134.3 4.3 %collective-permute-done.29.refs_3_ = bf16[3,304,128]{2,1,0:T(8,128)(2,1)S(1)} collective-permute-done((bf16[3,304,128]{2,1,0:T(8,128)(2,1)S(1)}, bf16[3,304,128]{2,1,0:T(8,128)(2,1)S(1)}, u32[]{:S(2)}, u32[]{:S(2)}) %collective-permute-start.29) | collective-permute-done | bytes 233504 | tf_op jit(solution)/shard_map/ppermute | solution.py:251
  138.5 1.3 added.9
  140.4 1.5 collective-permute-start.30
  141.9 1.7 collective-permute-start.32
  143.6 3.0 %collective-permute-done.31 = bf16[3,304,128]{2,1,0:T(8,128)(2,1)S(1)} collective-permute-done((bf16[3,304,128]{2,1,0:T(8,128)(2,1)S(1)}, bf16[3,304,128]{2,1,0:T(8,128)(2,1)S(1)}, u32[]{:S(2)}, u32[]{:S(2)}) %collective-permute-start.31) | collective-permute-done | bytes 233504 | tf_op jit(solution)/shard_map/ppermute | solution.py:258
  147.4 1.6 collective-permute-start.34
  149.1 1.5 collective-permute-start.33
  150.5 3.5 %collective-permute-done.32 = bf16[3,304,128]{2,1,0:T(8,128)(2,1)S(1)} collective-permute-done((bf16[3,304,128]{2,1,0:T(8,128)(2,1)S(1)}, bf16[3,304,128]{2,1,0:T(8,128)(2,1)S(1)}, u32[]{:S(2)}, u32[]{:S(2)}) %collective-permute-start.32) | collective-permute-done | bytes 233504 | tf_op jit(solution)/shard_map/ppermute | solution.py:257
  154.1 1.5 collective-permute-start.36
  156.1 4.1 %collective-permute-done.34 = bf16[3,304,128]{2,1,0:T(8,128)(2,1)S(1)} collective-permute-done((bf16[3,304,128]{2,1,0:T(8,128)(2,1)S(1)}, bf16[3,304,128]{2,1,0:T(8,128)(2,1)S(1)}, u32[]{:S(2)}, u32[]{:S(2)}) %collective-permute-start.34) | collective-permute-done | bytes 233504 | tf_op jit(solution)/shard_map/ppermute | solution.py:257
  160.2 0.8 collective-permute-start.38
  161.1 1.4 collective-permute-start.37
  162.4 1.6 collective-permute-done.36
  164.1 1.5 collective-permute-start.40
  166.1 1.3 slice.45
  168.5 1.9 %collective-permute-done.40 = bf16[3,304,128]{2,1,0:T(8,128)(2,1)S(1)} collective-permute-done((bf16[3,304,128]{2,1,0:T(8,128)(2,1)S(1)}, bf16[3,304,128]{2,1,0:T(8,128)(2,1)S(1)}, u32[]{:S(2)}, u32[]{:S(2)}) %collective-permute-start.40) | collective-permute-done | bytes 233504 | tf_op jit(solution)/shard_map/ppermute | solution.py:260
  170.4 1.2 collective-permute-done.41
  171.6 10.3 %conditional.1 = (f32[2,32,64,128]{3,2,1,0:T(8,128)S(1)}) conditional(s32[]{:T(128)} %bitcast.20, (s32[]{:T(128)}, s32[64,256]{1,0:T(8,128)}, s32[]{:T(128)}, s32[64,256]{1,0:T(8,128)}, f32[64,256]{1,0:T(8,128)}, /*index=5*/f32[4,32,128]{2,1,0:T(8,128)S(1)}, s32[8,384]{1,0:T(8,128)S(1)}, s32[1,384]{1,0:T(1,128)}, f32[32,384]{1,0:T(8,128)}, ...), branch_computations={%region_0.10_spmd, %region_10.11_spmd} | conditional | flops 1831321088 | bytes 333904320 | solution.py:884
  172.9 9.0 %insert.1 = f32[2,32,64,128]{3,2,1,0:T(8,128)S(1)} custom-call(s32[8,128]{1,0:T(8,128)} %get-tuple-element.113.len_s, s32[8192]{0:T(1024)S(1)} %bitcast.96, f32[8192]{0:T(1024)} %bitcast.103, f32[32,64,128]{2,1,0:T(8,128)S(1)} %get-tuple-element.116.reg_hbm, bf16[3,304,128]{2,1,0:T(8,128)(2,1)S(1)} %get-tuple-element.117.rest_0_, ...), custom_call_target="tpu_custom_call" | custom-call | bytes 33210000 | tf_op jit(solution)/shard_map/cond/branch_1_fun/insert/pallas_call | solution.py:638
  181.9 1.3 copy-done.3
  (164 shorter events, 13.4 us)
Async XLA Ops:
  6.5 17.4 %copy-start.53 = (f32[384]{0:T(512)S(1)}, f32[384]{0:T(512)}, u32[]{:S(2)}) copy-start(f32[384]{0:T(512)} %param.13) | copy-start | bytes 4612
  19.6 21.7 %collective-permute-start.5 = (bf16[2,2,160,128]{3,2,1,0:T(8,128)(2,1)}, bf16[2,2,160,128]{3,2,1,0:T(8,128)(2,1)S(1)}, u32[]{:S(2)}, u32[]{:S(2)}) collective-permute-start(bf16[2,2,160,128]{3,2,1,0:T(8,128)(2,1)} %get-tuple-element.174), channel_id=1, source_target_pairs={{0,2},{1,3},{2,4},{3,5},{4,6},{5,7},{6,0},{7,1},{8,10},{9,11},{10,... | collective-permute-start | bytes 491528 | tf_op jit(solution)/shard_map/ppermute | solution.py:232
  19.7 21.6 %collective-permute-start.6 = (bf16[2,2,160,128]{3,2,1,0:T(8,128)(2,1)}, bf16[2,2,160,128]{3,2,1,0:T(8,128)(2,1)S(1)}, u32[]{:S(2)}, u32[]{:S(2)}) collective-permute-start(bf16[2,2,160,128]{3,2,1,0:T(8,128)(2,1)} %get-tuple-element.175), channel_id=1, source_target_pairs={{0,4},{1,5},{2,6},{3,7},{4,0},{5,1},{6,2},{7,3},{8,12},{9,13},{10,... | collective-permute-start | bytes 491528 | tf_op jit(solution)/shard_map/ppermute | solution.py:232
  19.7 21.5 %collective-permute-start.7 = (bf16[2,2,160,128]{3,2,1,0:T(8,128)(2,1)}, bf16[2,2,160,128]{3,2,1,0:T(8,128)(2,1)S(1)}, u32[]{:S(2)}, u32[]{:S(2)}) collective-permute-start(bf16[2,2,160,128]{3,2,1,0:T(8,128)(2,1)} %get-tuple-element.176), channel_id=1, source_target_pairs={{0,6},{1,7},{2,0},{3,1},{4,2},{5,3},{6,4},{7,5},{8,14},{9,15},{10,... | collective-permute-start | bytes 491528 | tf_op jit(solution)/shard_map/ppermute | solution.py:232
  21.7 22.2 %collective-permute-start.4 = (bf16[4,2,160,128]{3,2,1,0:T(8,128)(2,1)}, bf16[4,2,160,128]{3,2,1,0:T(8,128)(2,1)S(1)}, u32[]{:S(2)}, u32[]{:S(2)}) collective-permute-start(bf16[4,2,160,128]{3,2,1,0:T(8,128)(2,1)} %get-tuple-element.172), channel_id=1, source_target_pairs={{0,1},{1,0},{2,3},{3,2},{4,5},{5,4},{6,7},{7,6},{8,9},{9,8},{10,11... | collective-permute-start | bytes 983048 | tf_op jit(solution)/shard_map/ppermute | solution.py:233
  23.9 14.7 %collective-permute-start = (bf16[4,2,192,128]{3,2,1,0:T(8,128)(2,1)}, bf16[4,2,192,128]{3,2,1,0:T(8,128)(2,1)S(1)}, u32[]{:S(2)}, u32[]{:S(2)}) collective-permute-start(bf16[4,2,192,128]{3,2,1,0:T(8,128)(2,1)} %get-tuple-element.166), channel_id=1, source_target_pairs={{0,1},{1,0},{2,3},{3,2},{4,5},{5,4},{6,7},{7,6},{8,9},{9,8},{10,11... | collective-permute-start | bytes 1179656 | tf_op jit(solution)/shard_map/ppermute | solution.py:231
  35.3 40.5 %copy-start.13 = (f32[64,256]{1,0:T(8,128)S(1)}, f32[64,256]{1,0:T(8,128)}, u32[]{:S(2)}) copy-start(f32[64,256]{1,0:T(8,128)} %refs_2_.1) | copy-start | bytes 196612
  35.3 41.3 %copy-start.10 = (s32[64,256]{1,0:T(8,128)S(1)}, s32[64,256]{1,0:T(8,128)}, u32[]{:S(2)}) copy-start(s32[64,256]{1,0:T(8,128)} %refs_1_.1) | copy-start | bytes 196612
  35.4 42.1 %copy-start.8 = (s32[64,256]{1,0:T(8,128)S(1)}, s32[64,256]{1,0:T(8,128)}, u32[]{:S(2)}) copy-start(s32[64,256]{1,0:T(8,128)} %refs_0_.1) | copy-start | bytes 196612
  35.4 49.0 %copy-start.35 = (s32[384,8]{0,1:T(8,128)S(1)}, s32[384,8]{0,1:T(8,128)}, u32[]{:S(2)}) copy-start(s32[384,8]{0,1:T(8,128)} %param.14) | copy-start | bytes 36868
  46.5 8.7 %collective-permute-start.8 = (bf16[2,160,128]{2,1,0:T(8,128)(2,1)}, bf16[2,160,128]{2,1,0:T(8,128)(2,1)S(1)}, u32[]{:S(2)}, u32[]{:S(2)}) collective-permute-start(bf16[2,160,128]{2,1,0:T(8,128)(2,1)} %get-tuple-element.179), channel_id=1, source_target_pairs={{0,2},{1,3},{2,4},{3,5},{4,6},{5,7},{6,0},{7,1},{8,10},{9,11},{10,... | collective-permute-start | bytes 245768 | tf_op jit(solution)/shard_map/ppermute | solution.py:239
  47.7 10.2 %collective-permute-start.9 = (bf16[2,160,128]{2,1,0:T(8,128)(2,1)}, bf16[2,160,128]{2,1,0:T(8,128)(2,1)S(1)}, u32[]{:S(2)}, u32[]{:S(2)}) collective-permute-start(bf16[2,160,128]{2,1,0:T(8,128)(2,1)} %get-tuple-element.180), channel_id=1, source_target_pairs={{0,4},{1,5},{2,6},{3,7},{4,0},{5,1},{6,2},{7,3},{8,12},{9,13},{10,... | collective-permute-start | bytes 245768 | tf_op jit(solution)/shard_map/ppermute | solution.py:239
  51.4 7.5 %collective-permute-start.10 = (bf16[2,160,128]{2,1,0:T(8,128)(2,1)}, bf16[2,160,128]{2,1,0:T(8,128)(2,1)S(1)}, u32[]{:S(2)}, u32[]{:S(2)}) collective-permute-start(bf16[2,160,128]{2,1,0:T(8,128)(2,1)} %get-tuple-element.181), channel_id=1, source_target_pairs={{0,6},{1,7},{2,0},{3,1},{4,2},{5,3},{6,4},{7,5},{8,14},{9,15},{10,... | collective-permute-start | bytes 245768 | tf_op jit(solution)/shard_map/ppermute | solution.py:239
  51.4 12.2 %collective-permute-start.11 = (bf16[2,160,128]{2,1,0:T(8,128)(2,1)}, bf16[2,160,128]{2,1,0:T(8,128)(2,1)S(1)}, u32[]{:S(2)}, u32[]{:S(2)}) collective-permute-start(bf16[2,160,128]{2,1,0:T(8,128)(2,1)} %get-tuple-element.182), channel_id=1, source_target_pairs={{0,1},{1,0},{2,3},{3,2},{4,5},{5,4},{6,7},{7,6},{8,9},{9,8},{10,11... | collective-permute-start | bytes 245768 | tf_op jit(solution)/shard_map/ppermute | solution.py:237
  53.2 15.9 %collective-permute-start.1 = (bf16[2,192,128]{2,1,0:T(8,128)(2,1)}, bf16[2,192,128]{2,1,0:T(8,128)(2,1)S(1)}, u32[]{:S(2)}, u32[]{:S(2)}) collective-permute-start(bf16[2,192,128]{2,1,0:T(8,128)(2,1)} %get-tuple-element.168), channel_id=1, source_target_pairs={{0,2},{1,3},{2,4},{3,5},{4,6},{5,7},{6,0},{7,1},{8,10},{9,11},{10,... | collective-permute-start | bytes 294920 | tf_op jit(solution)/shard_map/ppermute | solution.py:235
  55.2 14.6 %collective-permute-start.2 = (bf16[2,192,128]{2,1,0:T(8,128)(2,1)}, bf16[2,192,128]{2,1,0:T(8,128)(2,1)S(1)}, u32[]{:S(2)}, u32[]{:S(2)}) collective-permute-start(bf16[2,192,128]{2,1,0:T(8,128)(2,1)} %get-tuple-element.169), channel_id=1, source_target_pairs={{0,4},{1,5},{2,6},{3,7},{4,0},{5,1},{6,2},{7,3},{8,12},{9,13},{10,... | collective-permute-start | bytes 294920 | tf_op jit(solution)/shard_map/ppermute | solution.py:235
  57.9 12.7 %collective-permute-start.3 = (bf16[2,192,128]{2,1,0:T(8,128)(2,1)}, bf16[2,192,128]{2,1,0:T(8,128)(2,1)S(1)}, u32[]{:S(2)}, u32[]{:S(2)}) collective-permute-start(bf16[2,192,128]{2,1,0:T(8,128)(2,1)} %get-tuple-element.170), channel_id=1, source_target_pairs={{0,6},{1,7},{2,0},{3,1},{4,2},{5,3},{6,4},{7,5},{8,14},{9,15},{10,... | collective-permute-start | bytes 294920 | tf_op jit(solution)/shard_map/ppermute | solution.py:235
  61.3 12.0 %collective-permute-start.19 = (bf16[2,160,128]{2,1,0:T(8,128)(2,1)}, bf16[2,160,128]{2,1,0:T(8,128)(2,1)S(1)}, u32[]{:S(2)}, u32[]{:S(2)}) collective-permute-start(bf16[2,160,128]{2,1,0:T(8,128)(2,1)} %added.6.rest_2_), channel_id=1, source_target_pairs={{0,24},{8,16},{16,8},{24,0},{1,25},{9,17},{17,9},{25,1},{2,26},{10... | collective-permute-start | bytes 245768 | tf_op jit(solution)/shard_map/ppermute | solution.py:244
  63.7 9.9 %collective-permute-start.16 = (bf16[2,160,128]{2,1,0:T(8,128)(2,1)}, bf16[2,160,128]{2,1,0:T(8,128)(2,1)S(1)}, u32[]{:S(2)}, u32[]{:S(2)}) collective-permute-start(bf16[2,160,128]{2,1,0:T(8,128)(2,1)} %added.6.rest_2_), channel_id=1, source_target_pairs={{0,16},{8,24},{16,0},{24,8},{1,17},{9,25},{17,1},{25,9},{2,18},{10... | collective-permute-start | bytes 245768 | tf_op jit(solution)/shard_map/ppermute | solution.py:244
  69.1 5.5 %collective-permute-start.13 = (bf16[2,160,128]{2,1,0:T(8,128)(2,1)}, bf16[2,160,128]{2,1,0:T(8,128)(2,1)S(1)}, u32[]{:S(2)}, u32[]{:S(2)}) collective-permute-start(bf16[2,160,128]{2,1,0:T(8,128)(2,1)} %added.6.rest_2_), channel_id=1, source_target_pairs={{0,8},{8,0},{16,24},{24,16},{1,9},{9,1},{17,25},{25,17},{2,10},{10... | collective-permute-start | bytes 245768 | tf_op jit(solution)/shard_map/ppermute | solution.py:244
  69.8 5.8 %collective-permute-start.20 = (bf16[2,160,128]{2,1,0:T(8,128)(2,1)}, bf16[2,160,128]{2,1,0:T(8,128)(2,1)S(1)}, u32[]{:S(2)}, u32[]{:S(2)}) collective-permute-start(bf16[2,160,128]{2,1,0:T(8,128)(2,1)} %added.7.rest_3_), channel_id=1, source_target_pairs={{0,24},{8,16},{16,8},{24,0},{1,25},{9,17},{17,9},{25,1},{2,26},{10... | collective-permute-start | bytes 245768 | tf_op jit(solution)/shard_map/ppermute | solution.py:244
  70.7 12.9 %collective-permute-start.17 = (bf16[2,160,128]{2,1,0:T(8,128)(2,1)}, bf16[2,160,128]{2,1,0:T(8,128)(2,1)S(1)}, u32[]{:S(2)}, u32[]{:S(2)}) collective-permute-start(bf16[2,160,128]{2,1,0:T(8,128)(2,1)} %added.7.rest_3_), channel_id=1, source_target_pairs={{0,16},{8,24},{16,0},{24,8},{1,17},{9,25},{17,1},{25,9},{2,18},{10... | collective-permute-start | bytes 245768 | tf_op jit(solution)/shard_map/ppermute | solution.py:244
  73.3 26.9 %copy-start.54 = (s32[384]{0:T(512)S(1)}, s32[384]{0:T(512)}, u32[]{:S(2)}) copy-start(s32[384]{0:T(512)} %param.15) | copy-start | bytes 4612
  73.3 31.0 %slice-start = ((s8[6291456]{0:T(1024)(128)(4,1)}), s8[2097152]{0:T(1024)(128)(4,1)S(1)}, s32[]{:S(2)}) async-start(s8[6291456]{0:T(1024)(128)(4,1)} %bitcast.83), calls=%async_computation.5 | async-start | bytes 4194304
  73.3 10.4 %copy-start.42 = (bf16[2,160,128]{2,1,0:T(8,128)(2,1)}, bf16[2,160,128]{2,1,0:T(8,128)(2,1)S(1)}, u32[]{:S(2)}) copy-start(bf16[2,160,128]{2,1,0:T(8,128)(2,1)S(1)} %collective-permute-done.19.rest_11_) | copy-start | bytes 245764
  73.3 10.3 %collective-permute-start.14 = (bf16[2,160,128]{2,1,0:T(8,128)(2,1)}, bf16[2,160,128]{2,1,0:T(8,128)(2,1)S(1)}, u32[]{:S(2)}, u32[]{:S(2)}) collective-permute-start(bf16[2,160,128]{2,1,0:T(8,128)(2,1)} %added.7.rest_3_), channel_id=1, source_target_pairs={{0,8},{8,0},{16,24},{24,16},{1,9},{9,1},{17,25},{25,17},{2,10},{10... | collective-permute-start | bytes 245768 | tf_op jit(solution)/shard_map/ppermute | solution.py:244
  73.5 10.1 %copy-start.43 = (bf16[2,160,128]{2,1,0:T(8,128)(2,1)}, bf16[2,160,128]{2,1,0:T(8,128)(2,1)S(1)}, u32[]{:S(2)}) copy-start(bf16[2,160,128]{2,1,0:T(8,128)(2,1)S(1)} %collective-permute-done.16.rest_8_) | copy-start | bytes 245764
  73.5 10.1 %collective-permute-start.18 = (bf16[2,192,128]{2,1,0:T(8,128)(2,1)}, bf16[2,192,128]{2,1,0:T(8,128)(2,1)S(1)}, u32[]{:S(2)}, u32[]{:S(2)}) collective-permute-start(bf16[2,192,128]{2,1,0:T(8,128)(2,1)} %added.5.rest_1_), channel_id=1, source_target_pairs={{0,24},{8,16},{16,8},{24,0},{1,25},{9,17},{17,9},{25,1},{2,26},{10... | collective-permute-start | bytes 294920 | tf_op jit(solution)/shard_map/ppermute | solution.py:244
  74.6 9.0 %collective-permute-start.15 = (bf16[2,192,128]{2,1,0:T(8,128)(2,1)}, bf16[2,192,128]{2,1,0:T(8,128)(2,1)S(1)}, u32[]{:S(2)}, u32[]{:S(2)}) collective-permute-start(bf16[2,192,128]{2,1,0:T(8,128)(2,1)} %added.5.rest_1_), channel_id=1, source_target_pairs={{0,16},{8,24},{16,0},{24,8},{1,17},{9,25},{17,1},{25,9},{2,18},{10... | collective-permute-start | bytes 294920 | tf_op jit(solution)/shard_map/ppermute | solution.py:244
  75.5 8.1 %collective-permute-start.12 = (bf16[2,192,128]{2,1,0:T(8,128)(2,1)}, bf16[2,192,128]{2,1,0:T(8,128)(2,1)S(1)}, u32[]{:S(2)}, u32[]{:S(2)}) collective-permute-start(bf16[2,192,128]{2,1,0:T(8,128)(2,1)} %added.5.rest_1_), channel_id=1, source_target_pairs={{0,8},{8,0},{16,24},{24,16},{1,9},{9,1},{17,25},{25,17},{2,10},{10... | collective-permute-start | bytes 294920 | tf_op jit(solution)/shard_map/ppermute | solution.py:244
  84.3 19.9 %slice-start.1 = ((s8[6291456]{0:T(1024)(128)(4,1)}), s8[4194304]{0:T(1024)(128)(4,1)S(1)}, s32[]{:S(2)}) async-start(s8[6291456]{0:T(1024)(128)(4,1)} %bitcast.83), calls=%async_computation.6 | async-start | bytes 8388608
  93.0 4.4 %collective-permute-start.21 = (f32[32,384]{1,0:T(8,128)}, f32[32,384]{1,0:T(8,128)S(1)}, u32[]{:S(2)}, u32[]{:S(2)}) collective-permute-start(f32[32,384]{1,0:T(8,128)} %logits.1), channel_id=1, source_target_pairs={{0,1},{1,0},{2,3},{3,2},{4,5},{5,4},{6,7},{7,6},{8,9},{9,8},{10,11... | collective-permute-start | bytes 147464 | tf_op jit(solution)/shard_map/ppermute | solution.py:864
  98.1 22.4 %copy-start.7 = (f32[32,384]{1,0:T(8,128)}, f32[32,384]{1,0:T(8,128)S(1)}, u32[]{:S(2)}) copy-start(f32[32,384]{1,0:T(8,128)S(1)} %add.162.rest_0_) | copy-start | bytes 147460
  98.1 4.5 %collective-permute-start.24 = (f32[32,384]{1,0:T(8,128)S(1)}, f32[32,384]{1,0:T(8,128)S(1)}, u32[]{:S(2)}, u32[]{:S(2)}) collective-permute-start(f32[32,384]{1,0:T(8,128)S(1)} %add.162.rest_0_), channel_id=1, source_target_pairs={{0,6},{1,7},{2,0},{3,1},{4,2},{5,3},{6,4},{7,5},{8,14},{9,15},{10,... | collective-permute-start | bytes 147464 | tf_op jit(solution)/shard_map/ppermute | solution.py:866
  98.2 5.2 %collective-permute-start.23 = (f32[32,384]{1,0:T(8,128)S(1)}, f32[32,384]{1,0:T(8,128)S(1)}, u32[]{:S(2)}, u32[]{:S(2)}) collective-permute-start(f32[32,384]{1,0:T(8,128)S(1)} %add.162.rest_0_), channel_id=1, source_target_pairs={{0,4},{1,5},{2,6},{3,7},{4,0},{5,1},{6,2},{7,3},{8,12},{9,13},{10,... | collective-permute-start | bytes 147464 | tf_op jit(solution)/shard_map/ppermute | solution.py:866
  99.2 5.1 %collective-permute-start.22 = (f32[32,384]{1,0:T(8,128)S(1)}, f32[32,384]{1,0:T(8,128)S(1)}, u32[]{:S(2)}, u32[]{:S(2)}) collective-permute-start(f32[32,384]{1,0:T(8,128)S(1)} %add.162.rest_0_), channel_id=1, source_target_pairs={{0,2},{1,3},{2,4},{3,5},{4,6},{5,7},{6,0},{7,1},{8,10},{9,11},{10,... | collective-permute-start | bytes 147464 | tf_op jit(solution)/shard_map/ppermute | solution.py:866
  100.2 20.3 %copy-start.52 = (s32[1,384]{1,0:T(1,128)}, s32[1,384]{1,0:T(1,128)S(1)}, u32[]{:S(2)}) copy-start(s32[1,384]{1,0:T(1,128)S(1)} %broadcast_in_dim.13.cnt_ref) | copy-start | bytes 4612
  102.6 15.7 %copy-start.29 = (f32[32,384]{1,0:T(8,128)}, f32[32,384]{1,0:T(8,128)S(1)}, u32[]{:S(2)}) copy-start(f32[32,384]{1,0:T(8,128)S(1)} %collective-permute-done.24.rest_3_) | copy-start | bytes 147460
  103.4 15.0 %copy-start.30 = (f32[32,384]{1,0:T(8,128)}, f32[32,384]{1,0:T(8,128)S(1)}, u32[]{:S(2)}) copy-start(f32[32,384]{1,0:T(8,128)S(1)} %collective-permute-done.23.rest_2_) | copy-start | bytes 147460
  104.3 14.1 %copy-start.31 = (f32[32,384]{1,0:T(8,128)}, f32[32,384]{1,0:T(8,128)S(1)}, u32[]{:S(2)}) copy-start(f32[32,384]{1,0:T(8,128)S(1)} %collective-permute-done.22.rest_1_) | copy-start | bytes 147460
  104.3 67.3 %copy-start.2 = (f32[32,64,128]{2,1,0:T(8,128)S(1)}, f32[32,64,128]{2,1,0:T(8,128)}, u32[]{:S(2)}) copy-start(f32[32,64,128]{2,1,0:T(8,128)} %param.21) | copy-start | bytes 3145732
  115.6 2.7 %collective-permute-start.25 = (bf16[2,3,608,128]{3,2,1,0:T(8,128)(2,1)}, bf16[2,3,608,128]{3,2,1,0:T(8,128)(2,1)S(1)}, u32[]{:S(2)}, u32[]{:S(2)}) collective-permute-start(bf16[2,3,608,128]{3,2,1,0:T(8,128)(2,1)} %get-tuple-element.188), channel_id=1, source_target_pairs={{0,8},{8,0},{16,24},{24,16},{1,9},{9,1},{17,25},{25,17},{2,10},{10... | collective-permute-start | bytes 2801672 | tf_op jit(solution)/shard_map/ppermute | solution.py:514
  120.5 8.6 %collective-permute-start.26 = (bf16[3,304,128]{2,1,0:T(8,128)(2,1)S(1)}, bf16[3,304,128]{2,1,0:T(8,128)(2,1)S(1)}, u32[]{:S(2)}, u32[]{:S(2)}) collective-permute-start(bf16[3,304,128]{2,1,0:T(8,128)(2,1)S(1)} %get-tuple-element.291), channel_id=1, source_target_pairs={{0,16},{8,24},{16,0},{24,8},{1,17},{9,25},{17,1},{25,9},{2,18},{10... | collective-permute-start | bytes 700424 | tf_op jit(solution)/shard_map/ppermute | solution.py:520
  121.7 12.6 %collective-permute-start.27 = (bf16[3,304,128]{2,1,0:T(8,128)(2,1)S(1)}, bf16[3,304,128]{2,1,0:T(8,128)(2,1)S(1)}, u32[]{:S(2)}, u32[]{:S(2)}) collective-permute-start(bf16[3,304,128]{2,1,0:T(8,128)(2,1)S(1)} %get-tuple-element.289), channel_id=1, source_target_pairs={{0,16},{8,24},{16,0},{24,8},{1,17},{9,25},{17,1},{25,9},{2,18},{10... | collective-permute-start | bytes 700424 | tf_op jit(solution)/shard_map/ppermute | solution.py:520
  130.9 7.6 %collective-permute-start.29 = (bf16[3,304,128]{2,1,0:T(8,128)(2,1)S(1)}, bf16[3,304,128]{2,1,0:T(8,128)(2,1)S(1)}, u32[]{:S(2)}, u32[]{:S(2)}) collective-permute-start(bf16[3,304,128]{2,1,0:T(8,128)(2,1)S(1)} %added.8), channel_id=1, source_target_pairs={{2,0},{4,2},{6,4},{7,6},{5,7},{3,5},{1,3},{0,1},{10,8},{12,10},{14... | collective-permute-start | bytes 700424 | tf_op jit(solution)/shard_map/ppermute | solution.py:251
  131.9 6.6 %collective-permute-start.28 = (bf16[3,304,128]{2,1,0:T(8,128)(2,1)S(1)}, bf16[3,304,128]{2,1,0:T(8,128)(2,1)S(1)}, u32[]{:S(2)}, u32[]{:S(2)}) collective-permute-start(bf16[3,304,128]{2,1,0:T(8,128)(2,1)S(1)} %added.8), channel_id=1, source_target_pairs={{0,2},{2,4},{4,6},{6,7},{7,5},{5,3},{3,1},{1,0},{8,10},{10,12},{12... | collective-permute-start | bytes 700424 | tf_op jit(solution)/shard_map/ppermute | solution.py:251
  138.5 21.7 %copy-start.5 = (bf16[3,304,128]{2,1,0:T(8,128)(2,1)}, bf16[3,304,128]{2,1,0:T(8,128)(2,1)S(1)}, u32[]{:S(2)}) copy-start(bf16[3,304,128]{2,1,0:T(8,128)(2,1)S(1)} %collective-permute-done.28.refs_2_) | copy-start | bytes 700420
  139.8 21.2 %copy-start.6 = (bf16[3,304,128]{2,1,0:T(8,128)(2,1)}, bf16[3,304,128]{2,1,0:T(8,128)(2,1)S(1)}, u32[]{:S(2)}) copy-start(bf16[3,304,128]{2,1,0:T(8,128)(2,1)S(1)} %added.9) | copy-start | bytes 700420
  139.8 6.8 %collective-permute-start.31 = (bf16[3,304,128]{2,1,0:T(8,128)(2,1)S(1)}, bf16[3,304,128]{2,1,0:T(8,128)(2,1)S(1)}, u32[]{:S(2)}, u32[]{:S(2)}) collective-permute-start(bf16[3,304,128]{2,1,0:T(8,128)(2,1)S(1)} %added.9), channel_id=1, source_target_pairs={{2,0},{4,2},{6,4},{7,6},{5,7},{3,5},{1,3},{0,1},{10,8},{12,10},{14... | collective-permute-start | bytes 700424 | tf_op jit(solution)/shard_map/ppermute | solution.py:258
  140.4 8.6 %collective-permute-start.30 = (bf16[3,304,128]{2,1,0:T(8,128)(2,1)S(1)}, bf16[3,304,128]{2,1,0:T(8,128)(2,1)S(1)}, u32[]{:S(2)}, u32[]{:S(2)}) collective-permute-start(bf16[3,304,128]{2,1,0:T(8,128)(2,1)S(1)} %added.9), channel_id=1, source_target_pairs={{0,2},{2,4},{4,6},{6,7},{7,5},{5,3},{3,1},{1,0},{8,10},{10,12},{12... | collective-permute-start | bytes 700424 | tf_op jit(solution)/shard_map/ppermute | solution.py:258
  141.9 12.2 %collective-permute-start.32 = (bf16[3,304,128]{2,1,0:T(8,128)(2,1)S(1)}, bf16[3,304,128]{2,1,0:T(8,128)(2,1)S(1)}, u32[]{:S(2)}, u32[]{:S(2)}) collective-permute-start(bf16[3,304,128]{2,1,0:T(8,128)(2,1)S(1)} %collective-permute-done.28.refs_2_), channel_id=1, source_target_pairs={{0,2},{2,4},{4,6},{6,7},{7,5},{5,3},{3,1},{1,0},{8,10},{10,12},{12... | collective-permute-start | bytes 700424 | tf_op jit(solution)/shard_map/ppermute | solution.py:257
  146.6 14.5 %copy-start.15 = (bf16[3,304,128]{2,1,0:T(8,128)(2,1)}, bf16[3,304,128]{2,1,0:T(8,128)(2,1)S(1)}, u32[]{:S(2)}) copy-start(bf16[3,304,128]{2,1,0:T(8,128)(2,1)S(1)} %collective-permute-done.31) | copy-start | bytes 700420
  146.6 8.9 %collective-permute-start.35 = (bf16[3,304,128]{2,1,0:T(8,128)(2,1)S(1)}, bf16[3,304,128]{2,1,0:T(8,128)(2,1)S(1)}, u32[]{:S(2)}, u32[]{:S(2)}) collective-permute-start(bf16[3,304,128]{2,1,0:T(8,128)(2,1)S(1)} %collective-permute-done.31), channel_id=1, source_target_pairs={{2,0},{4,2},{6,4},{7,6},{5,7},{3,5},{1,3},{0,1},{10,8},{12,10},{14... | collective-permute-start | bytes 700424 | tf_op jit(solution)/shard_map/ppermute | solution.py:258
  147.4 12.8 %collective-permute-start.34 = (bf16[3,304,128]{2,1,0:T(8,128)(2,1)S(1)}, bf16[3,304,128]{2,1,0:T(8,128)(2,1)S(1)}, u32[]{:S(2)}, u32[]{:S(2)}) collective-permute-start(bf16[3,304,128]{2,1,0:T(8,128)(2,1)S(1)} %collective-permute-done.29.refs_3_), channel_id=1, source_target_pairs={{2,0},{4,2},{6,4},{7,6},{5,7},{3,5},{1,3},{0,1},{10,8},{12,10},{14... | collective-permute-start | bytes 700424 | tf_op jit(solution)/shard_map/ppermute | solution.py:257
  149.1 13.4 %copy-start.16 = (bf16[3,304,128]{2,1,0:T(8,128)(2,1)}, bf16[3,304,128]{2,1,0:T(8,128)(2,1)S(1)}, u32[]{:S(2)}) copy-start(bf16[3,304,128]{2,1,0:T(8,128)(2,1)S(1)} %collective-permute-done.30) | copy-start | bytes 700420
  149.1 12.0 %collective-permute-start.33 = (bf16[3,304,128]{2,1,0:T(8,128)(2,1)S(1)}, bf16[3,304,128]{2,1,0:T(8,128)(2,1)S(1)}, u32[]{:S(2)}, u32[]{:S(2)}) collective-permute-start(bf16[3,304,128]{2,1,0:T(8,128)(2,1)S(1)} %collective-permute-done.30), channel_id=1, source_target_pairs={{0,2},{2,4},{4,6},{6,7},{7,5},{5,3},{3,1},{1,0},{8,10},{10,12},{12... | collective-permute-start | bytes 700424 | tf_op jit(solution)/shard_map/ppermute | solution.py:258
  154.1 10.0 %copy-start.17 = (bf16[3,304,128]{2,1,0:T(8,128)(2,1)}, bf16[3,304,128]{2,1,0:T(8,128)(2,1)S(1)}, u32[]{:S(2)}) copy-start(bf16[3,304,128]{2,1,0:T(8,128)(2,1)S(1)} %collective-permute-done.32) | copy-start | bytes 700420
  154.1 10.0 %collective-permute-start.36 = (bf16[3,304,128]{2,1,0:T(8,128)(2,1)S(1)}, bf16[3,304,128]{2,1,0:T(8,128)(2,1)S(1)}, u32[]{:S(2)}, u32[]{:S(2)}) collective-permute-start(bf16[3,304,128]{2,1,0:T(8,128)(2,1)S(1)} %collective-permute-done.32), channel_id=1, source_target_pairs={{0,2},{2,4},{4,6},{6,7},{7,5},{5,3},{3,1},{1,0},{8,10},{10,12},{12... | collective-permute-start | bytes 700424 | tf_op jit(solution)/shard_map/ppermute | solution.py:257
  155.5 10.0 %copy-start.18 = (bf16[3,304,128]{2,1,0:T(8,128)(2,1)}, bf16[3,304,128]{2,1,0:T(8,128)(2,1)S(1)}, u32[]{:S(2)}) copy-start(bf16[3,304,128]{2,1,0:T(8,128)(2,1)S(1)} %collective-permute-done.35) | copy-start | bytes 700420
  155.5 10.0 %collective-permute-start.39 = (bf16[3,304,128]{2,1,0:T(8,128)(2,1)S(1)}, bf16[3,304,128]{2,1,0:T(8,128)(2,1)S(1)}, u32[]{:S(2)}, u32[]{:S(2)}) collective-permute-start(bf16[3,304,128]{2,1,0:T(8,128)(2,1)S(1)} %collective-permute-done.35), channel_id=1, source_target_pairs={{2,0},{4,2},{6,4},{7,6},{5,7},{3,5},{1,3},{0,1},{10,8},{12,10},{14... | collective-permute-start | bytes 700424 | tf_op jit(solution)/shard_map/ppermute | solution.py:258
  160.2 8.2 %collective-permute-start.38 = (bf16[3,304,128]{2,1,0:T(8,128)(2,1)S(1)}, bf16[3,304,128]{2,1,0:T(8,128)(2,1)S(1)}, u32[]{:S(2)}, u32[]{:S(2)}) collective-permute-start(bf16[3,304,128]{2,1,0:T(8,128)(2,1)S(1)} %collective-permute-done.34), channel_id=1, source_target_pairs={{2,0},{4,2},{6,4},{7,6},{5,7},{3,5},{1,3},{0,1},{10,8},{12,10},{14... | collective-permute-start | bytes 700424 | tf_op jit(solution)/shard_map/ppermute | solution.py:257
  161.1 7.4 %collective-permute-start.37 = (bf16[3,304,128]{2,1,0:T(8,128)(2,1)S(1)}, bf16[3,304,128]{2,1,0:T(8,128)(2,1)S(1)}, u32[]{:S(2)}, u32[]{:S(2)}) collective-permute-start(bf16[3,304,128]{2,1,0:T(8,128)(2,1)S(1)} %collective-permute-done.33), channel_id=1, source_target_pairs={{0,2},{2,4},{4,6},{6,7},{7,5},{5,3},{3,1},{1,0},{8,10},{10,12},{12... | collective-permute-start | bytes 700424 | tf_op jit(solution)/shard_map/ppermute | solution.py:258
  164.1 6.3 %collective-permute-start.40 = (bf16[3,304,128]{2,1,0:T(8,128)(2,1)S(1)}, bf16[3,304,128]{2,1,0:T(8,128)(2,1)S(1)}, u32[]{:S(2)}, u32[]{:S(2)}) collective-permute-start(bf16[3,304,128]{2,1,0:T(8,128)(2,1)S(1)} %collective-permute-done.36), channel_id=1, source_target_pairs={{0,2},{2,4},{4,6},{6,7},{7,5},{5,3},{3,1},{1,0},{8,10},{10,12},{12... | collective-permute-start | bytes 700424 | tf_op jit(solution)/shard_map/ppermute | solution.py:260
  165.6 6.1 %collective-permute-start.41 = (bf16[3,304,128]{2,1,0:T(8,128)(2,1)S(1)}, bf16[3,304,128]{2,1,0:T(8,128)(2,1)S(1)}, u32[]{:S(2)}, u32[]{:S(2)}) collective-permute-start(bf16[3,304,128]{2,1,0:T(8,128)(2,1)S(1)} %collective-permute-done.39), channel_id=1, source_target_pairs={{2,0},{4,2},{6,4},{7,6},{5,7},{3,5},{1,3},{0,1},{10,8},{12,10},{14... | collective-permute-start | bytes 700424 | tf_op jit(solution)/shard_map/ppermute | solution.py:260
  (32 other events, 64.9 us)

commit v9 on v7

--- a/solution.py
+++ b/solution.py
@@ -339,6 +339,7 @@
     dims = (((1,), (1,)), ((), ()))
     total = acc[...]
     total_q = quad[...]
+    left, power = [], []
     for u in range(inner):
         re = part[0, pl.ds(step * inner + u, K, stride=pitch), :]
         im = part[1, pl.ds(step * inner + u, K, stride=pitch), :]
@@ -351,10 +352,18 @@
                     [(c * re - s * im).astype(BF16), (s * re + c * im).astype(BF16)], axis=1
                 )
             )
-        left = jnp.concatenate(shifted, axis=0)
-        power = (re * re + im * im).astype(BF16)
-        total = total + lax.dot_general(left, wt_ref[u], dims, preferred_element_type=F32)
-        total_q = total_q + lax.dot_general(power, sq_ref[u], dims, preferred_element_type=F32)
+        left.append(jnp.concatenate(shifted, axis=0))
+        power.append((re * re + im * im).astype(BF16))
+        if u % 4 == 3:
+            right = jnp.concatenate([wt_ref[i] for i in range(u - 3, u + 1)], axis=1)
+            right_q = jnp.concatenate([sq_ref[i] for i in range(u - 3, u + 1)], axis=1)
+            total = total + lax.dot_general(
+                jnp.concatenate(left, axis=1), right, dims, preferred_element_type=F32
+            )
+            total_q = total_q + lax.dot_general(
+                jnp.concatenate(power, axis=1), right_q, dims, preferred_element_type=F32
+            )
+            left, power = [], []
     acc[...] = total
     quad[...] = total_q
 
@@ -583,8 +592,8 @@
         )
 
         def group_step(g, carry, block=block):
-            at = block * lead + g * 4
-            for u in range(4):
+            at = block * lead + g * 8
+            for u in range(8):
                 code = code_s[at + u]
                 s = code & 1023
                 to = code >> 10
@@ -596,7 +605,7 @@
                     into[c, pl.ds(to, 2), :] = into[c, pl.ds(to, 2), :] + both * row
             return carry
 
-        lax.fori_loop(0, (jnp.minimum(len_s[block, 0], cap) + 3) // 4, group_step, 0)
+        lax.fori_loop(0, (jnp.minimum(len_s[block, 0], cap) + 7) // 8, group_step, 0)
 
     prior.wait()
     chunks = sem_out.shape[0]

time: 184 us -> 182 us (0.989)
  Pallas kernels: 62.6 us -> 59.5 us
    pallas_call x1, Pallas kernels: 11.2 us -> 9 us  [insert(): pl.pallas_call(partial(insert_kernel, count), out_shape=jax.ShapeDtypeStr...]
  transfers between devices with their start and end apart: 35 -> 35, of which waited for: 20 -> 19; matrix products, arithmetic and copies ran while one was open for 5% -> 5% of each run, Pallas kernels for 9% -> 9%
where the time goes in v9:
time: 182 us; the launch traced here: 180 us
  Pallas kernels  59.5 us (33%)
  waiting for transfers between devices  46.1 us (25%)
  starting transfers between devices  42.6 us (23%)
  between operations  14.4 us (8%)
  local copies, waits for them, and re-layouts  9.34 us (5%)
  other arithmetic  8.38 us (5%)
    pallas_call x1, Pallas kernels, extract(): pl.pallas_call(partial(extract_kernel, rows, planes_here), out_shape=[sha...  12.8 us
    pallas_call x1, Pallas kernels, project(): pl.pallas_call(project_kernel, grid=(rows // inner,), out_shape=[jax.Shap...  11.3 us
    ppermute x4, starting transfers between devices, ring_gather(): lax.ppermute(one[0], 'vol', ahead)  10.9 us
    ppermute x4, waiting for transfers between devices, ring_gather(): lax.ppermute(one[0], 'vol', ahead)  9.96 us
    ppermute x3, waiting for transfers between devices, to_pixel_rows(): lax.ppermute(sums_a[d], 'vol', along_z(n_vol, d))  9.46 us
    pallas_call x1, Pallas kernels, insert(): pl.pallas_call(partial(insert_kernel, count), out_shape=jax.ShapeDtypeStr...  9 us
    pallas_call x1, Pallas kernels, weigh(): pl.pallas_call(weigh_kernel, grid=(count // step,), out_shape=[jax.ShapeD...  8.42 us
    pallas_call x1, Pallas kernels, candidate_logits(): pl.pallas_call(logits_kernel, grid=(rows // inner,), out_shape=jax.ShapeD...  7.84 us
  transfers between devices with their start and end apart: 35, of which 19 were waited for; matrix products, arithmetic and copies ran while one was open for 5% of the time, Pallas kernels for 9%

profile of v9, /device:TPU:12, one launch (start us, length us, event | category | flops | bytes accessed | tf_op | source)
XLA Modules:
  0.0 180.3 jit_solution(3604291118547227713)
XLA Ops:
  6.5 12.8 %extract.1 = (bf16[4,2,352,128]{3,2,1,0:T(8,128)(2,1)}, bf16[4,2,352,128]{3,2,1,0:T(8,128)(2,1)}, bf16[2,2,160,128]{3,2,1,0:T(8,128)(2,1)}, bf16[2,2,160,128]{3,...) custom-call(s32[64,256]{1,0:T(8,128)} %refs_0_.1, s32[64,256]{1,0:T(8,128)} %refs_1_.1, ...), custom_call_target="tpu_custom_call" | custom-call | bytes 40590000 | tf_op jit(solution)/shard_map/extract/pallas_call | solution.py:181
  19.5 1.9 %collective-permute-start.3 = (bf16[2,2,160,128]{3,2,1,0:T(8,128)(2,1)}, bf16[2,2,160,128]{3,2,1,0:T(8,128)(2,1)S(1)}, u32[]{:S(2)}, u32[]{:S(2)}) collective-permute-start(bf16[2,2,160,128]{3,2,1,0:T(8,128)(2,1)} %get-tuple-element.164), channel_id=1, source_target_pairs={{0,6},{1,7},{2,0},{3,1},{4,2},{5,3},{6,4},{7,5},{8,14},{9,15},{10,... | collective-permute-start | bytes 491528 | tf_op jit(solution)/shard_map/ppermute | solution.py:219
  21.4 1.9 %collective-permute-start = (bf16[4,2,352,128]{3,2,1,0:T(8,128)(2,1)}, bf16[4,2,352,128]{3,2,1,0:T(8,128)(2,1)S(1)}, u32[]{:S(2)}, u32[]{:S(2)}) collective-permute-start(bf16[4,2,352,128]{3,2,1,0:T(8,128)(2,1)} %get-tuple-element.160), channel_id=1, source_target_pairs={{0,1},{1,0},{2,3},{3,2},{4,5},{5,4},{6,7},{7,6},{8,9},{9,8},{10,11... | collective-permute-start | bytes 2162696 | tf_op jit(solution)/shard_map/ppermute | solution.py:220
  23.4 1.5 multiply_cosine_fusion
  25.0 1.5 fusion.21
  26.5 8.4 %weigh.1 = (bf16[32,384,256]{2,1,0:T(8,128)(2,1)S(1)}, bf16[32,384,128]{2,1,0:T(8,128)(2,1)}) custom-call(bf16[2,384,32,128]{3,2,1,0:T(8,128)(2,1)} %img_ref.1, f32[384,32]{1,0:T(8,128)} %get-tuple-element.286.sa_ref, f32[384,32]{1,0:T(8,128)} %get-tuple-element.285.ca_ref, f32[384,128]{1,0:T(8,128)} %get-tuple-element.284.sx_ref, ...), custom_call_target="tpu_custom_call" | custom-call | bytes 44280000 | tf_op jit(solution)/shard_map/weigh/pallas_call | solution.py:283
  35.0 3.4 %collective-permute-done.got_a = bf16[4,2,352,128]{3,2,1,0:T(8,128)(2,1)S(1)} collective-permute-done((bf16[4,2,352,128]{3,2,1,0:T(8,128)(2,1)}, bf16[4,2,352,128]{3,2,1,0:T(8,128)(2,1)S(1)}, u32[]{:S(2)}, u32[]{:S(2)}) %collective-permute-start) | collective-permute-done | bytes 720928 | tf_op jit(solution)/shard_map/ppermute | solution.py:220
  38.4 0.9 copy-done.5
  39.3 2.7 %combine_first.1 = (bf16[2,352,128]{2,1,0:T(8,128)(2,1)}, bf16[2,352,128]{2,1,0:T(8,128)(2,1)}, bf16[2,352,128]{2,1,0:T(8,128)(2,1)}, bf16[2,352,128]{2,1,0:T(8,...) custom-call(bf16[4,2,352,128]{3,2,1,0:T(8,128)(2,1)} %get-tuple-element.159.keep_a, ...), custom_call_target="tpu_custom_call" | custom-call | bytes 11070000 | tf_op jit(solution)/shard_map/combine_first/pallas_call | solution.py:223
  42.0 1.7 collective-permute-start.7
  44.2 4.4 %collective-permute-start.5 = (bf16[2,352,128]{2,1,0:T(8,128)(2,1)}, bf16[2,352,128]{2,1,0:T(8,128)(2,1)S(1)}, u32[]{:S(2)}, u32[]{:S(2)}) collective-permute-start(bf16[2,352,128]{2,1,0:T(8,128)(2,1)} %get-tuple-element.167), channel_id=1, source_target_pairs={{0,4},{1,5},{2,6},{3,7},{4,0},{5,1},{6,2},{7,3},{8,12},{9,13},{10,... | collective-permute-start | bytes 540680 | tf_op jit(solution)/shard_map/ppermute | solution.py:234
  48.7 0.9 add.177.rest_2_
  49.7 1.9 %collective-permute-start.11 = (bf16[2,160,128]{2,1,0:T(8,128)(2,1)S(1)}, bf16[2,160,128]{2,1,0:T(8,128)(2,1)}, u32[]{:S(2)}, u32[]{:S(2)}) collective-permute-start(bf16[2,160,128]{2,1,0:T(8,128)(2,1)S(1)} %add.177.rest_2_), channel_id=1, source_target_pairs={{0,16},{8,24},{16,0},{24,8},{1,17},{9,25},{17,1},{25,9},{2,18},{10... | collective-permute-start | bytes 245768 | tf_op jit(solution)/shard_map/ppermute | solution.py:241
  51.7 5.3 %collective-permute-done.4 = bf16[2,352,128]{2,1,0:T(8,128)(2,1)S(1)} collective-permute-done((bf16[2,352,128]{2,1,0:T(8,128)(2,1)}, bf16[2,352,128]{2,1,0:T(8,128)(2,1)S(1)}, u32[]{:S(2)}, u32[]{:S(2)}) %collective-permute-start.4) | collective-permute-done | bytes 180256 | tf_op jit(solution)/shard_map/ppermute | solution.py:234
  57.0 1.9 %collective-permute-done.5 = bf16[2,352,128]{2,1,0:T(8,128)(2,1)S(1)} collective-permute-done((bf16[2,352,128]{2,1,0:T(8,128)(2,1)}, bf16[2,352,128]{2,1,0:T(8,128)(2,1)S(1)}, u32[]{:S(2)}, u32[]{:S(2)}) %collective-permute-start.5) | collective-permute-done | bytes 180256 | tf_op jit(solution)/shard_map/ppermute | solution.py:234
  59.0 2.2 %collective-permute-done.6 = bf16[2,352,128]{2,1,0:T(8,128)(2,1)S(1)} collective-permute-done((bf16[2,352,128]{2,1,0:T(8,128)(2,1)}, bf16[2,352,128]{2,1,0:T(8,128)(2,1)S(1)}, u32[]{:S(2)}, u32[]{:S(2)}) %collective-permute-start.6) | collective-permute-done | bytes 180256 | tf_op jit(solution)/shard_map/ppermute | solution.py:234
  61.1 1.0 add_add_fusion.rest_1_
  62.2 1.5 collective-permute-start.12
  63.6 1.4 collective-permute-start.10
  65.6 0.7 reshape.231.wgt_ref
  66.4 0.7 reshape.230.line_ref
  67.2 0.7 reshape.229.plane_ref
  67.9 5.3 %lists.1 = (s32[32,128]{1,0:T(8,128)}, s32[64,128]{1,0:T(8,128)S(1)}, f32[64,128]{1,0:T(8,128)}, s32[8,128]{1,0:T(8,128)}, s32[8,128]{1,0:T(8,128)}, /*index=5*/s32[8,128]{1,0:T(8,128)}) custom-call(s32[8,2048]{1,0:T(8,128)} %reshape.229.plane_ref, s32[8,2048]{1,0:T(8,128)} %reshape.230.line_ref, f32[8,2048]{1,0:T(8,128)} %reshape.231.wgt_ref), custom_call_target="tpu_custom_call" | custom-call | bytes 22140000 | tf_op jit(solution)/shard_map/lists/pallas_call | solution.py:766
  73.3 0.6 copy-done.33
  74.1 7.8 %logits.1 = f32[32,384]{1,0:T(8,128)} custom-call(bf16[32,384,256]{2,1,0:T(8,128)(2,1)} %copy-done, bf16[32,384,128]{2,1,0:T(8,128)(2,1)} %get-tuple-element.157.sq_ref, f32[4,32,128]{2,1,0:T(8,128)S(1)} %get-tuple-element.282.cos_ref, f32[4,32,128]{2,1,0:T(8,128)S(1)} %get-tuple-element.281.sin_ref, s32[8,384]{1,0:T(8,128)S(1)} %bitcast.97, ...), custom_call_target="tpu_custom_call" | custom-call | bytes 29520000 | tf_op jit(solution)/shard_map/logits/pallas_call | solution.py:384
  81.9 0.6 collective-permute-start.14
  82.5 3.7 %collective-permute-done.14 = f32[32,384]{1,0:T(8,128)S(1)} collective-permute-done((f32[32,384]{1,0:T(8,128)}, f32[32,384]{1,0:T(8,128)S(1)}, u32[]{:S(2)}, u32[]{:S(2)}) %collective-permute-start.14) | collective-permute-done | bytes 49184 | tf_op jit(solution)/shard_map/ppermute | solution.py:866
  86.2 0.8 add.178.rest_0_
  87.1 1.1 collective-permute-start.16
  88.2 2.5 %collective-permute-start.15 = (f32[32,384]{1,0:T(8,128)S(1)}, f32[32,384]{1,0:T(8,128)S(1)}, u32[]{:S(2)}, u32[]{:S(2)}) collective-permute-start(f32[32,384]{1,0:T(8,128)S(1)} %add.178.rest_0_), channel_id=1, source_target_pairs={{0,2},{1,3},{2,4},{3,5},{4,6},{5,7},{6,0},{7,1},{8,10},{9,11},{10,... | collective-permute-start | bytes 147464 | tf_op jit(solution)/shard_map/ppermute | solution.py:868
  90.7 0.8 collective-permute-done.17.rest_3_
  91.5 0.6 collective-permute-done.16.rest_2_
  92.1 1.0 collective-permute-done.15.rest_1_
  93.2 11.3 %project.1 = (bf16[2,3,608,128]{3,2,1,0:T(8,128)(2,1)}, bf16[2,3,608,128]{3,2,1,0:T(8,128)(2,1)}) custom-call(s32[4096]{0:T(1024)} %bitcast.104, s32[8,128]{1,0:T(8,128)} %get-tuple-element.174.len_s, s32[8,384]{1,0:T(8,128)S(1)} %bitcast.98, s32[1,384]{1,0:T(1,128)S(1)} %broadcast_in_dim.13.cnt_ref, bf16[32,384,256]{2,1,0:T(8,128)(2,1)S(1)} %bitcast.84, ...), custom_call_target="tpu_custom_call" | custom-call | bytes 44280000 | tf_op jit(solution)/shard_map/project/pallas_call | solution.py:489
  104.5 2.7 %collective-permute-done.18 = bf16[2,3,608,128]{3,2,1,0:T(8,128)(2,1)S(1)} collective-permute-done((bf16[2,3,608,128]{3,2,1,0:T(8,128)(2,1)}, bf16[2,3,608,128]{3,2,1,0:T(8,128)(2,1)S(1)}, u32[]{:S(2)}, u32[]{:S(2)}) %collective-permute-start.18) | collective-permute-done | bytes 933920 | tf_op jit(solution)/shard_map/ppermute | solution.py:518
  107.2 2.2 %fusion.17 = (bf16[3,304,128]{2,1,0:T(8,128)(2,1)S(1)}, bf16[3,304,128]{2,1,0:T(8,128)(2,1)}, bf16[3,304,128]{2,1,0:T(8,128)(2,1)S(1)}, bf16[3,304,128]{2,1,0:T(8,128)(2,1)}) fusion(bf16[2,3,608,128]{3,2,1,0:T(8,128)(2,1)S(1)} %collective-permute-done.18, bf16[2,3,608,128]{3,2,1,0:T(8,128)(2,1)} %get-tuple-element.175), kind=kLoop, calls=%fused_computation.49 | loop fusion | flops 466944 | bytes 2801664 | tf_op jit(solution)/shard_map/add | solution.py:523
  109.4 1.7 collective-permute-start.20
  111.4 6.5 %collective-permute-done.20.refs_1_ = bf16[3,304,128]{2,1,0:T(8,128)(2,1)S(1)} collective-permute-done((bf16[3,304,128]{2,1,0:T(8,128)(2,1)S(1)}, bf16[3,304,128]{2,1,0:T(8,128)(2,1)S(1)}, u32[]{:S(2)}, u32[]{:S(2)}) %collective-permute-start.20) | collective-permute-done | bytes 233504 | tf_op jit(solution)/shard_map/ppermute | solution.py:524
  117.9 0.7 copy-done.29
  118.6 1.1 added.3
  119.7 1.8 collective-permute-start.24
  121.5 0.6 collective-permute-done.19.refs_1_
  122.1 0.7 copy-done.28
  122.8 1.1 added.2
  123.9 3.4 %collective-permute-start.21 = (bf16[3,304,128]{2,1,0:T(8,128)(2,1)S(1)}, bf16[3,304,128]{2,1,0:T(8,128)(2,1)S(1)}, u32[]{:S(2)}, u32[]{:S(2)}) collective-permute-start(bf16[3,304,128]{2,1,0:T(8,128)(2,1)S(1)} %added.2), channel_id=1, source_target_pairs={{0,2},{2,4},{4,6},{6,7},{7,5},{5,3},{3,1},{1,0},{8,10},{10,12},{12... | collective-permute-start | bytes 700424 | tf_op jit(solution)/shard_map/ppermute | solution.py:251
  127.9 1.5 collective-permute-start.23
  129.4 4.1 %collective-permute-done.21 = bf16[3,304,128]{2,1,0:T(8,128)(2,1)S(1)} collective-permute-done((bf16[3,304,128]{2,1,0:T(8,128)(2,1)S(1)}, bf16[3,304,128]{2,1,0:T(8,128)(2,1)S(1)}, u32[]{:S(2)}, u32[]{:S(2)}) %collective-permute-start.21) | collective-permute-done | bytes 233504 | tf_op jit(solution)/shard_map/ppermute | solution.py:251
  133.5 2.5 %collective-permute-start.25 = (bf16[3,304,128]{2,1,0:T(8,128)(2,1)S(1)}, bf16[3,304,128]{2,1,0:T(8,128)(2,1)S(1)}, u32[]{:S(2)}, u32[]{:S(2)}) collective-permute-start(bf16[3,304,128]{2,1,0:T(8,128)(2,1)S(1)} %collective-permute-done.21), channel_id=1, source_target_pairs={{0,2},{2,4},{4,6},{6,7},{7,5},{5,3},{3,1},{1,0},{8,10},{10,12},{12... | collective-permute-start | bytes 700424 | tf_op jit(solution)/shard_map/ppermute | solution.py:251
  136.0 2.5 %collective-permute-done.22 = bf16[3,304,128]{2,1,0:T(8,128)(2,1)S(1)} collective-permute-done((bf16[3,304,128]{2,1,0:T(8,128)(2,1)S(1)}, bf16[3,304,128]{2,1,0:T(8,128)(2,1)S(1)}, u32[]{:S(2)}, u32[]{:S(2)}) %collective-permute-start.22) | collective-permute-done | bytes 233504 | tf_op jit(solution)/shard_map/ppermute | solution.py:252
  138.5 2.5 %collective-permute-start.26 = (bf16[3,304,128]{2,1,0:T(8,128)(2,1)S(1)}, bf16[3,304,128]{2,1,0:T(8,128)(2,1)S(1)}, u32[]{:S(2)}, u32[]{:S(2)}) collective-permute-start(bf16[3,304,128]{2,1,0:T(8,128)(2,1)S(1)} %collective-permute-done.22), channel_id=1, source_target_pairs={{0,2},{2,4},{4,6},{6,7},{7,5},{5,3},{3,1},{1,0},{8,10},{10,12},{12... | collective-permute-start | bytes 700424 | tf_op jit(solution)/shard_map/ppermute | solution.py:252
  141.5 2.0 %collective-permute-done.25 = bf16[3,304,128]{2,1,0:T(8,128)(2,1)S(1)} collective-permute-done((bf16[3,304,128]{2,1,0:T(8,128)(2,1)S(1)}, bf16[3,304,128]{2,1,0:T(8,128)(2,1)S(1)}, u32[]{:S(2)}, u32[]{:S(2)}) %collective-permute-start.25) | collective-permute-done | bytes 233504 | tf_op jit(solution)/shard_map/ppermute | solution.py:251
  143.5 2.5 %collective-permute-start.29 = (bf16[3,304,128]{2,1,0:T(8,128)(2,1)S(1)}, bf16[3,304,128]{2,1,0:T(8,128)(2,1)S(1)}, u32[]{:S(2)}, u32[]{:S(2)}) collective-permute-start(bf16[3,304,128]{2,1,0:T(8,128)(2,1)S(1)} %collective-permute-done.25), channel_id=1, source_target_pairs={{0,2},{2,4},{4,6},{6,7},{7,5},{5,3},{3,1},{1,0},{8,10},{10,12},{12... | collective-permute-start | bytes 700424 | tf_op jit(solution)/shard_map/ppermute | solution.py:251
  146.0 2.5 %collective-permute-done.26 = bf16[3,304,128]{2,1,0:T(8,128)(2,1)S(1)} collective-permute-done((bf16[3,304,128]{2,1,0:T(8,128)(2,1)S(1)}, bf16[3,304,128]{2,1,0:T(8,128)(2,1)S(1)}, u32[]{:S(2)}, u32[]{:S(2)}) %collective-permute-start.26) | collective-permute-done | bytes 233504 | tf_op jit(solution)/shard_map/ppermute | solution.py:252
  148.5 2.5 %collective-permute-start.30 = (bf16[3,304,128]{2,1,0:T(8,128)(2,1)S(1)}, bf16[3,304,128]{2,1,0:T(8,128)(2,1)S(1)}, u32[]{:S(2)}, u32[]{:S(2)}) collective-permute-start(bf16[3,304,128]{2,1,0:T(8,128)(2,1)S(1)} %collective-permute-done.26), channel_id=1, source_target_pairs={{0,2},{2,4},{4,6},{6,7},{7,5},{5,3},{3,1},{1,0},{8,10},{10,12},{12... | collective-permute-start | bytes 700424 | tf_op jit(solution)/shard_map/ppermute | solution.py:252
  151.4 2.1 %collective-permute-done.29 = bf16[3,304,128]{2,1,0:T(8,128)(2,1)S(1)} collective-permute-done((bf16[3,304,128]{2,1,0:T(8,128)(2,1)S(1)}, bf16[3,304,128]{2,1,0:T(8,128)(2,1)S(1)}, u32[]{:S(2)}, u32[]{:S(2)}) %collective-permute-start.29) | collective-permute-done | bytes 233504 | tf_op jit(solution)/shard_map/ppermute | solution.py:251
  153.5 2.5 %collective-permute-start.33 = (bf16[3,304,128]{2,1,0:T(8,128)(2,1)S(1)}, bf16[3,304,128]{2,1,0:T(8,128)(2,1)S(1)}, u32[]{:S(2)}, u32[]{:S(2)}) collective-permute-start(bf16[3,304,128]{2,1,0:T(8,128)(2,1)S(1)} %collective-permute-done.29), channel_id=1, source_target_pairs={{0,2},{2,4},{4,6},{6,7},{7,5},{5,3},{3,1},{1,0},{8,10},{10,12},{12... | collective-permute-start | bytes 700424 | tf_op jit(solution)/shard_map/ppermute | solution.py:255
  156.0 1.2 slice.45
  157.8 0.7 collective-permute-done.30
  158.5 1.5 collective-permute-done.34
  160.0 1.8 collective-permute-done.33
  161.8 10.3 %conditional.1 = (f32[2,32,64,128]{3,2,1,0:T(8,128)S(1)}) conditional(s32[]{:T(128)} %bitcast.20, (s32[]{:T(128)}, s32[64,256]{1,0:T(8,128)}, s32[]{:T(128)}, s32[64,256]{1,0:T(8,128)}, f32[64,256]{1,0:T(8,128)}, /*index=5*/f32[4,32,128]{2,1,0:T(8,128)S(1)}, s32[8,384]{1,0:T(8,128)S(1)}, s32[1,384]{1,0:T(1,128)}, f32[32,384]{1,0:T(8,128)}, ...), branch_computations={%region_0.10_spmd, %region_10.11_spmd} | conditional | flops 1831321088 | bytes 333904320 | solution.py:886
  161.8 0.6 copy-done.20
  163.1 9.0 %insert.1 = f32[2,32,64,128]{3,2,1,0:T(8,128)S(1)} custom-call(s32[8,128]{1,0:T(8,128)} %get-tuple-element.113.len_s, s32[8192]{0:T(1024)S(1)} %bitcast.96, f32[8192]{0:T(1024)} %bitcast.103, f32[32,64,128]{2,1,0:T(8,128)S(1)} %get-tuple-element.116.reg_hbm, bf16[3,304,128]{2,1,0:T(8,128)(2,1)} %get-tuple-element.117.rest_0_, ...), custom_call_target="tpu_custom_call" | custom-call | bytes 33210000 | tf_op jit(solution)/shard_map/cond/branch_1_fun/insert/pallas_call | solution.py:642
  172.1 1.3 copy-done.3
  (125 shorter events, 4.4 us)
Async XLA Ops:
  6.5 16.9 %copy-start.42 = (f32[384]{0:T(512)S(1)}, f32[384]{0:T(512)}, u32[]{:S(2)}) copy-start(f32[384]{0:T(512)} %param.13) | copy-start | bytes 4612
  19.3 15.6 %collective-permute-start.1 = (bf16[2,2,160,128]{3,2,1,0:T(8,128)(2,1)}, bf16[2,2,160,128]{3,2,1,0:T(8,128)(2,1)S(1)}, u32[]{:S(2)}, u32[]{:S(2)}) collective-permute-start(bf16[2,2,160,128]{3,2,1,0:T(8,128)(2,1)} %get-tuple-element.162), channel_id=1, source_target_pairs={{0,2},{1,3},{2,4},{3,5},{4,6},{5,7},{6,0},{7,1},{8,10},{9,11},{10,... | collective-permute-start | bytes 491528 | tf_op jit(solution)/shard_map/ppermute | solution.py:219
  19.4 15.6 %collective-permute-start.2 = (bf16[2,2,160,128]{3,2,1,0:T(8,128)(2,1)}, bf16[2,2,160,128]{3,2,1,0:T(8,128)(2,1)S(1)}, u32[]{:S(2)}, u32[]{:S(2)}) collective-permute-start(bf16[2,2,160,128]{3,2,1,0:T(8,128)(2,1)} %get-tuple-element.163), channel_id=1, source_target_pairs={{0,4},{1,5},{2,6},{3,7},{4,0},{5,1},{6,2},{7,3},{8,12},{9,13},{10,... | collective-permute-start | bytes 491528 | tf_op jit(solution)/shard_map/ppermute | solution.py:219
  19.5 15.5 %collective-permute-start.3 = (bf16[2,2,160,128]{3,2,1,0:T(8,128)(2,1)}, bf16[2,2,160,128]{3,2,1,0:T(8,128)(2,1)S(1)}, u32[]{:S(2)}, u32[]{:S(2)}) collective-permute-start(bf16[2,2,160,128]{3,2,1,0:T(8,128)(2,1)} %get-tuple-element.164), channel_id=1, source_target_pairs={{0,6},{1,7},{2,0},{3,1},{4,2},{5,3},{6,4},{7,5},{8,14},{9,15},{10,... | collective-permute-start | bytes 491528 | tf_op jit(solution)/shard_map/ppermute | solution.py:219
  21.4 17.0 %collective-permute-start = (bf16[4,2,352,128]{3,2,1,0:T(8,128)(2,1)}, bf16[4,2,352,128]{3,2,1,0:T(8,128)(2,1)S(1)}, u32[]{:S(2)}, u32[]{:S(2)}) collective-permute-start(bf16[4,2,352,128]{3,2,1,0:T(8,128)(2,1)} %get-tuple-element.160), channel_id=1, source_target_pairs={{0,1},{1,0},{2,3},{3,2},{4,5},{5,4},{6,7},{7,6},{8,9},{9,8},{10,11... | collective-permute-start | bytes 2162696 | tf_op jit(solution)/shard_map/ppermute | solution.py:220
  34.9 3.5 %copy-start = (bf16[32,384,256]{2,1,0:T(8,128)(2,1)}, bf16[32,384,256]{2,1,0:T(8,128)(2,1)S(1)}, u32[]{:S(2)}) copy-start(bf16[32,384,256]{2,1,0:T(8,128)(2,1)S(1)} %get-tuple-element.156.rest_3_.wt_ref) | copy-start | bytes 18874372
  34.9 30.6 %copy-start.12 = (f32[64,256]{1,0:T(8,128)S(1)}, f32[64,256]{1,0:T(8,128)}, u32[]{:S(2)}) copy-start(f32[64,256]{1,0:T(8,128)} %refs_2_.1) | copy-start | bytes 196612
  34.9 31.4 %copy-start.10 = (s32[64,256]{1,0:T(8,128)S(1)}, s32[64,256]{1,0:T(8,128)}, u32[]{:S(2)}) copy-start(s32[64,256]{1,0:T(8,128)} %refs_1_.1) | copy-start | bytes 196612
  34.9 32.2 %copy-start.8 = (s32[64,256]{1,0:T(8,128)S(1)}, s32[64,256]{1,0:T(8,128)}, u32[]{:S(2)}) copy-start(s32[64,256]{1,0:T(8,128)} %refs_0_.1) | copy-start | bytes 196612
  34.9 39.1 %copy-start.39 = (s32[384,8]{0,1:T(8,128)S(1)}, s32[384,8]{0,1:T(8,128)}, u32[]{:S(2)}) copy-start(s32[384,8]{0,1:T(8,128)} %param.14) | copy-start | bytes 36868
  35.0 3.5 %copy-start.36 = (bf16[2,2,160,128]{3,2,1,0:T(8,128)(2,1)}, bf16[2,2,160,128]{3,2,1,0:T(8,128)(2,1)S(1)}, u32[]{:S(2)}) copy-start(bf16[2,2,160,128]{3,2,1,0:T(8,128)(2,1)S(1)} %collective-permute-done.1.rest_0_) | copy-start | bytes 491524
  35.0 3.4 %copy-start.37 = (bf16[2,2,160,128]{3,2,1,0:T(8,128)(2,1)}, bf16[2,2,160,128]{3,2,1,0:T(8,128)(2,1)S(1)}, u32[]{:S(2)}) copy-start(bf16[2,2,160,128]{3,2,1,0:T(8,128)(2,1)S(1)} %collective-permute-done.2.rest_1_) | copy-start | bytes 491524
  35.0 3.4 %copy-start.38 = (bf16[2,2,160,128]{3,2,1,0:T(8,128)(2,1)}, bf16[2,2,160,128]{3,2,1,0:T(8,128)(2,1)S(1)}, u32[]{:S(2)}) copy-start(bf16[2,2,160,128]{3,2,1,0:T(8,128)(2,1)S(1)} %collective-permute-done.3.rest_2_) | copy-start | bytes 491524
  42.0 6.7 %collective-permute-start.7 = (bf16[2,160,128]{2,1,0:T(8,128)(2,1)}, bf16[2,160,128]{2,1,0:T(8,128)(2,1)S(1)}, u32[]{:S(2)}, u32[]{:S(2)}) collective-permute-start(bf16[2,160,128]{2,1,0:T(8,128)(2,1)} %get-tuple-element.170), channel_id=1, source_target_pairs={{0,1},{1,0},{2,3},{3,2},{4,5},{5,4},{6,7},{7,6},{8,9},{9,8},{10,11... | collective-permute-start | bytes 245768 | tf_op jit(solution)/shard_map/ppermute | solution.py:233
  43.7 13.3 %collective-permute-start.4 = (bf16[2,352,128]{2,1,0:T(8,128)(2,1)}, bf16[2,352,128]{2,1,0:T(8,128)(2,1)S(1)}, u32[]{:S(2)}, u32[]{:S(2)}) collective-permute-start(bf16[2,352,128]{2,1,0:T(8,128)(2,1)} %get-tuple-element.166), channel_id=1, source_target_pairs={{0,2},{1,3},{2,4},{3,5},{4,6},{5,7},{6,0},{7,1},{8,10},{9,11},{10,... | collective-permute-start | bytes 540680 | tf_op jit(solution)/shard_map/ppermute | solution.py:234
  44.2 14.8 %collective-permute-start.5 = (bf16[2,352,128]{2,1,0:T(8,128)(2,1)}, bf16[2,352,128]{2,1,0:T(8,128)(2,1)S(1)}, u32[]{:S(2)}, u32[]{:S(2)}) collective-permute-start(bf16[2,352,128]{2,1,0:T(8,128)(2,1)} %get-tuple-element.167), channel_id=1, source_target_pairs={{0,4},{1,5},{2,6},{3,7},{4,0},{5,1},{6,2},{7,3},{8,12},{9,13},{10,... | collective-permute-start | bytes 540680 | tf_op jit(solution)/shard_map/ppermute | solution.py:234
  48.7 12.5 %collective-permute-start.6 = (bf16[2,352,128]{2,1,0:T(8,128)(2,1)}, bf16[2,352,128]{2,1,0:T(8,128)(2,1)S(1)}, u32[]{:S(2)}, u32[]{:S(2)}) collective-permute-start(bf16[2,352,128]{2,1,0:T(8,128)(2,1)} %get-tuple-element.168), channel_id=1, source_target_pairs={{0,6},{1,7},{2,0},{3,1},{4,2},{5,3},{6,4},{7,5},{8,14},{9,15},{10,... | collective-permute-start | bytes 540680 | tf_op jit(solution)/shard_map/ppermute | solution.py:234
  49.7 23.6 %copy-start.13 = (bf16[2,160,128]{2,1,0:T(8,128)(2,1)}, bf16[2,160,128]{2,1,0:T(8,128)(2,1)S(1)}, u32[]{:S(2)}) copy-start(bf16[2,160,128]{2,1,0:T(8,128)(2,1)S(1)} %add.177.rest_2_) | copy-start | bytes 245764
  49.7 15.4 %collective-permute-start.13 = (bf16[2,160,128]{2,1,0:T(8,128)(2,1)S(1)}, bf16[2,160,128]{2,1,0:T(8,128)(2,1)S(1)}, u32[]{:S(2)}, u32[]{:S(2)}) collective-permute-start(bf16[2,160,128]{2,1,0:T(8,128)(2,1)S(1)} %add.177.rest_2_), channel_id=1, source_target_pairs={{0,24},{8,16},{16,8},{24,0},{1,25},{9,17},{17,9},{25,1},{2,26},{10... | collective-permute-start | bytes 245768 | tf_op jit(solution)/shard_map/ppermute | solution.py:241
  49.7 23.5 %collective-permute-start.11 = (bf16[2,160,128]{2,1,0:T(8,128)(2,1)S(1)}, bf16[2,160,128]{2,1,0:T(8,128)(2,1)}, u32[]{:S(2)}, u32[]{:S(2)}) collective-permute-start(bf16[2,160,128]{2,1,0:T(8,128)(2,1)S(1)} %add.177.rest_2_), channel_id=1, source_target_pairs={{0,16},{8,24},{16,0},{24,8},{1,17},{9,25},{17,1},{25,9},{2,18},{10... | collective-permute-start | bytes 245768 | tf_op jit(solution)/shard_map/ppermute | solution.py:241
  57.0 16.2 %collective-permute-start.9 = (bf16[2,160,128]{2,1,0:T(8,128)(2,1)S(1)}, bf16[2,160,128]{2,1,0:T(8,128)(2,1)}, u32[]{:S(2)}, u32[]{:S(2)}) collective-permute-start(bf16[2,160,128]{2,1,0:T(8,128)(2,1)S(1)} %add.177.rest_2_), channel_id=1, source_target_pairs={{0,8},{8,0},{16,24},{24,16},{1,9},{9,1},{17,25},{25,17},{2,10},{10... | collective-permute-start | bytes 245768 | tf_op jit(solution)/shard_map/ppermute | solution.py:241
  62.1 11.2 %copy-start.6 = (bf16[2,352,128]{2,1,0:T(8,128)(2,1)}, bf16[2,352,128]{2,1,0:T(8,128)(2,1)S(1)}, u32[]{:S(2)}) copy-start(bf16[2,352,128]{2,1,0:T(8,128)(2,1)S(1)} %add_add_fusion.rest_1_) | copy-start | bytes 540676
  62.1 28.6 %copy-start.43 = (s32[384]{0:T(512)S(1)}, s32[384]{0:T(512)}, u32[]{:S(2)}) copy-start(s32[384]{0:T(512)} %param.15) | copy-start | bytes 4612
  62.1 31.0 %slice-start = ((s8[6291456]{0:T(1024)(128)(4,1)}), s8[2097152]{0:T(1024)(128)(4,1)S(1)}, s32[]{:S(2)}) async-start(s8[6291456]{0:T(1024)(128)(4,1)} %bitcast.83), calls=%async_computation.5 | async-start | bytes 4194304
  62.2 11.1 %collective-permute-start.12 = (bf16[2,352,128]{2,1,0:T(8,128)(2,1)S(1)}, bf16[2,352,128]{2,1,0:T(8,128)(2,1)S(1)}, u32[]{:S(2)}, u32[]{:S(2)}) collective-permute-start(bf16[2,352,128]{2,1,0:T(8,128)(2,1)S(1)} %add_add_fusion.rest_1_), channel_id=1, source_target_pairs={{0,24},{8,16},{16,8},{24,0},{1,25},{9,17},{17,9},{25,1},{2,26},{10... | collective-permute-start | bytes 540680 | tf_op jit(solution)/shard_map/ppermute | solution.py:241
  63.6 9.6 %collective-permute-start.10 = (bf16[2,352,128]{2,1,0:T(8,128)(2,1)S(1)}, bf16[2,352,128]{2,1,0:T(8,128)(2,1)S(1)}, u32[]{:S(2)}, u32[]{:S(2)}) collective-permute-start(bf16[2,352,128]{2,1,0:T(8,128)(2,1)S(1)} %add_add_fusion.rest_1_), channel_id=1, source_target_pairs={{0,16},{8,24},{16,0},{24,8},{1,17},{9,25},{17,1},{25,9},{2,18},{10... | collective-permute-start | bytes 540680 | tf_op jit(solution)/shard_map/ppermute | solution.py:241
  65.1 8.2 %copy-start.40 = (bf16[2,160,128]{2,1,0:T(8,128)(2,1)}, bf16[2,160,128]{2,1,0:T(8,128)(2,1)S(1)}, u32[]{:S(2)}) copy-start(bf16[2,160,128]{2,1,0:T(8,128)(2,1)S(1)} %collective-permute-done.13.rest_8_) | copy-start | bytes 245764
  65.1 8.2 %collective-permute-start.8 = (bf16[2,352,128]{2,1,0:T(8,128)(2,1)S(1)}, bf16[2,352,128]{2,1,0:T(8,128)(2,1)S(1)}, u32[]{:S(2)}, u32[]{:S(2)}) collective-permute-start(bf16[2,352,128]{2,1,0:T(8,128)(2,1)S(1)} %add_add_fusion.rest_1_), channel_id=1, source_target_pairs={{0,8},{8,0},{16,24},{24,16},{1,9},{9,1},{17,25},{25,17},{2,10},{10... | collective-permute-start | bytes 540680 | tf_op jit(solution)/shard_map/ppermute | solution.py:241
  74.0 19.1 %slice-start.1 = ((s8[6291456]{0:T(1024)(128)(4,1)}), s8[4194304]{0:T(1024)(128)(4,1)S(1)}, s32[]{:S(2)}) async-start(s8[6291456]{0:T(1024)(128)(4,1)} %bitcast.83), calls=%async_computation.6 | async-start | bytes 8388608
  81.9 4.3 %collective-permute-start.14 = (f32[32,384]{1,0:T(8,128)}, f32[32,384]{1,0:T(8,128)S(1)}, u32[]{:S(2)}, u32[]{:S(2)}) collective-permute-start(f32[32,384]{1,0:T(8,128)} %logits.1), channel_id=1, source_target_pairs={{0,1},{1,0},{2,3},{3,2},{4,5},{5,4},{6,7},{7,6},{8,9},{9,8},{10,11... | collective-permute-start | bytes 147464 | tf_op jit(solution)/shard_map/ppermute | solution.py:866
  87.0 22.3 %copy-start.7 = (f32[32,384]{1,0:T(8,128)}, f32[32,384]{1,0:T(8,128)S(1)}, u32[]{:S(2)}) copy-start(f32[32,384]{1,0:T(8,128)S(1)} %add.178.rest_0_) | copy-start | bytes 147460
  87.0 4.5 %collective-permute-start.17 = (f32[32,384]{1,0:T(8,128)S(1)}, f32[32,384]{1,0:T(8,128)S(1)}, u32[]{:S(2)}, u32[]{:S(2)}) collective-permute-start(f32[32,384]{1,0:T(8,128)S(1)} %add.178.rest_0_), channel_id=1, source_target_pairs={{0,6},{1,7},{2,0},{3,1},{4,2},{5,3},{6,4},{7,5},{8,14},{9,15},{10,... | collective-permute-start | bytes 147464 | tf_op jit(solution)/shard_map/ppermute | solution.py:868
  87.1 5.1 %collective-permute-start.16 = (f32[32,384]{1,0:T(8,128)S(1)}, f32[32,384]{1,0:T(8,128)S(1)}, u32[]{:S(2)}, u32[]{:S(2)}) collective-permute-start(f32[32,384]{1,0:T(8,128)S(1)} %add.178.rest_0_), channel_id=1, source_target_pairs={{0,4},{1,5},{2,6},{3,7},{4,0},{5,1},{6,2},{7,3},{8,12},{9,13},{10,... | collective-permute-start | bytes 147464 | tf_op jit(solution)/shard_map/ppermute | solution.py:868
  88.2 5.0 %collective-permute-start.15 = (f32[32,384]{1,0:T(8,128)S(1)}, f32[32,384]{1,0:T(8,128)S(1)}, u32[]{:S(2)}, u32[]{:S(2)}) collective-permute-start(f32[32,384]{1,0:T(8,128)S(1)} %add.178.rest_0_), channel_id=1, source_target_pairs={{0,2},{1,3},{2,4},{3,5},{4,6},{5,7},{6,0},{7,1},{8,10},{9,11},{10,... | collective-permute-start | bytes 147464 | tf_op jit(solution)/shard_map/ppermute | solution.py:868
  90.7 18.6 %copy-start.41 = (s32[1,384]{1,0:T(1,128)}, s32[1,384]{1,0:T(1,128)S(1)}, u32[]{:S(2)}) copy-start(s32[1,384]{1,0:T(1,128)S(1)} %broadcast_in_dim.13.cnt_ref) | copy-start | bytes 4612
  91.5 15.7 %copy-start.30 = (f32[32,384]{1,0:T(8,128)}, f32[32,384]{1,0:T(8,128)S(1)}, u32[]{:S(2)}) copy-start(f32[32,384]{1,0:T(8,128)S(1)} %collective-permute-done.17.rest_3_) | copy-start | bytes 147460
  92.1 15.0 %copy-start.31 = (f32[32,384]{1,0:T(8,128)}, f32[32,384]{1,0:T(8,128)S(1)}, u32[]{:S(2)}) copy-start(f32[32,384]{1,0:T(8,128)S(1)} %collective-permute-done.16.rest_2_) | copy-start | bytes 147460
  93.1 14.0 %copy-start.32 = (f32[32,384]{1,0:T(8,128)}, f32[32,384]{1,0:T(8,128)S(1)}, u32[]{:S(2)}) copy-start(f32[32,384]{1,0:T(8,128)S(1)} %collective-permute-done.15.rest_1_) | copy-start | bytes 147460
  93.2 68.6 %copy-start.2 = (f32[32,64,128]{2,1,0:T(8,128)S(1)}, f32[32,64,128]{2,1,0:T(8,128)}, u32[]{:S(2)}) copy-start(f32[32,64,128]{2,1,0:T(8,128)} %param.21) | copy-start | bytes 3145732
  104.5 2.7 %collective-permute-start.18 = (bf16[2,3,608,128]{3,2,1,0:T(8,128)(2,1)}, bf16[2,3,608,128]{3,2,1,0:T(8,128)(2,1)S(1)}, u32[]{:S(2)}, u32[]{:S(2)}) collective-permute-start(bf16[2,3,608,128]{3,2,1,0:T(8,128)(2,1)} %get-tuple-element.176), channel_id=1, source_target_pairs={{0,8},{8,0},{16,24},{24,16},{1,9},{9,1},{17,25},{25,17},{2,10},{10... | collective-permute-start | bytes 2801672 | tf_op jit(solution)/shard_map/ppermute | solution.py:518
  109.4 8.6 %collective-permute-start.20 = (bf16[3,304,128]{2,1,0:T(8,128)(2,1)S(1)}, bf16[3,304,128]{2,1,0:T(8,128)(2,1)S(1)}, u32[]{:S(2)}, u32[]{:S(2)}) collective-permute-start(bf16[3,304,128]{2,1,0:T(8,128)(2,1)S(1)} %get-tuple-element.277), channel_id=1, source_target_pairs={{0,16},{8,24},{16,0},{24,8},{1,17},{9,25},{17,1},{25,9},{2,18},{10... | collective-permute-start | bytes 700424 | tf_op jit(solution)/shard_map/ppermute | solution.py:524
  111.1 11.1 %collective-permute-start.19 = (bf16[3,304,128]{2,1,0:T(8,128)(2,1)S(1)}, bf16[3,304,128]{2,1,0:T(8,128)(2,1)S(1)}, u32[]{:S(2)}, u32[]{:S(2)}) collective-permute-start(bf16[3,304,128]{2,1,0:T(8,128)(2,1)S(1)} %get-tuple-element.279), channel_id=1, source_target_pairs={{0,16},{8,24},{16,0},{24,8},{1,17},{9,25},{17,1},{25,9},{2,18},{10... | collective-permute-start | bytes 700424 | tf_op jit(solution)/shard_map/ppermute | solution.py:524
  119.7 9.6 %collective-permute-start.24 = (bf16[3,304,128]{2,1,0:T(8,128)(2,1)S(1)}, bf16[3,304,128]{2,1,0:T(8,128)(2,1)S(1)}, u32[]{:S(2)}, u32[]{:S(2)}) collective-permute-start(bf16[3,304,128]{2,1,0:T(8,128)(2,1)S(1)} %added.3), channel_id=1, source_target_pairs={{2,0},{4,2},{6,4},{7,6},{5,7},{3,5},{1,3},{0,1},{10,8},{12,10},{14... | collective-permute-start | bytes 700424 | tf_op jit(solution)/shard_map/ppermute | solution.py:252
  123.9 14.6 %copy-start.4 = (bf16[3,304,128]{2,1,0:T(8,128)(2,1)}, bf16[3,304,128]{2,1,0:T(8,128)(2,1)S(1)}, u32[]{:S(2)}) copy-start(bf16[3,304,128]{2,1,0:T(8,128)(2,1)S(1)} %added.2) | copy-start | bytes 700420
  123.9 9.6 %collective-permute-start.21 = (bf16[3,304,128]{2,1,0:T(8,128)(2,1)S(1)}, bf16[3,304,128]{2,1,0:T(8,128)(2,1)S(1)}, u32[]{:S(2)}, u32[]{:S(2)}) collective-permute-start(bf16[3,304,128]{2,1,0:T(8,128)(2,1)S(1)} %added.2), channel_id=1, source_target_pairs={{0,2},{2,4},{4,6},{6,7},{7,5},{5,3},{3,1},{1,0},{8,10},{10,12},{12... | collective-permute-start | bytes 700424 | tf_op jit(solution)/shard_map/ppermute | solution.py:251
  127.3 11.1 %collective-permute-start.22 = (bf16[3,304,128]{2,1,0:T(8,128)(2,1)S(1)}, bf16[3,304,128]{2,1,0:T(8,128)(2,1)S(1)}, u32[]{:S(2)}, u32[]{:S(2)}) collective-permute-start(bf16[3,304,128]{2,1,0:T(8,128)(2,1)S(1)} %added.3), channel_id=1, source_target_pairs={{0,2},{2,4},{4,6},{6,7},{7,5},{5,3},{3,1},{1,0},{8,10},{10,12},{12... | collective-permute-start | bytes 700424 | tf_op jit(solution)/shard_map/ppermute | solution.py:252
  127.9 13.1 %collective-permute-start.23 = (bf16[3,304,128]{2,1,0:T(8,128)(2,1)S(1)}, bf16[3,304,128]{2,1,0:T(8,128)(2,1)S(1)}, u32[]{:S(2)}, u32[]{:S(2)}) collective-permute-start(bf16[3,304,128]{2,1,0:T(8,128)(2,1)S(1)} %added.2), channel_id=1, source_target_pairs={{2,0},{4,2},{6,4},{7,6},{5,7},{3,5},{1,3},{0,1},{10,8},{12,10},{14... | collective-permute-start | bytes 700424 | tf_op jit(solution)/shard_map/ppermute | solution.py:251
  129.4 11.6 %copy-start.14 = (bf16[3,304,128]{2,1,0:T(8,128)(2,1)}, bf16[3,304,128]{2,1,0:T(8,128)(2,1)S(1)}, u32[]{:S(2)}) copy-start(bf16[3,304,128]{2,1,0:T(8,128)(2,1)S(1)} %collective-permute-done.24) | copy-start | bytes 700420
  129.4 11.7 %collective-permute-start.28 = (bf16[3,304,128]{2,1,0:T(8,128)(2,1)S(1)}, bf16[3,304,128]{2,1,0:T(8,128)(2,1)S(1)}, u32[]{:S(2)}, u32[]{:S(2)}) collective-permute-start(bf16[3,304,128]{2,1,0:T(8,128)(2,1)S(1)} %collective-permute-done.24), channel_id=1, source_target_pairs={{2,0},{4,2},{6,4},{7,6},{5,7},{3,5},{1,3},{0,1},{10,8},{12,10},{14... | collective-permute-start | bytes 700424 | tf_op jit(solution)/shard_map/ppermute | solution.py:252
  133.5 7.6 %copy-start.15 = (bf16[3,304,128]{2,1,0:T(8,128)(2,1)}, bf16[3,304,128]{2,1,0:T(8,128)(2,1)S(1)}, u32[]{:S(2)}) copy-start(bf16[3,304,128]{2,1,0:T(8,128)(2,1)S(1)} %collective-permute-done.21) | copy-start | bytes 700420
  133.5 10.0 %collective-permute-start.25 = (bf16[3,304,128]{2,1,0:T(8,128)(2,1)S(1)}, bf16[3,304,128]{2,1,0:T(8,128)(2,1)S(1)}, u32[]{:S(2)}, u32[]{:S(2)}) collective-permute-start(bf16[3,304,128]{2,1,0:T(8,128)(2,1)S(1)} %collective-permute-done.21), channel_id=1, source_target_pairs={{0,2},{2,4},{4,6},{6,7},{7,5},{5,3},{3,1},{1,0},{8,10},{10,12},{12... | collective-permute-start | bytes 700424 | tf_op jit(solution)/shard_map/ppermute | solution.py:251
  138.5 5.0 %copy-start.16 = (bf16[3,304,128]{2,1,0:T(8,128)(2,1)}, bf16[3,304,128]{2,1,0:T(8,128)(2,1)S(1)}, u32[]{:S(2)}) copy-start(bf16[3,304,128]{2,1,0:T(8,128)(2,1)S(1)} %collective-permute-done.22) | copy-start | bytes 700420
  138.5 10.0 %collective-permute-start.26 = (bf16[3,304,128]{2,1,0:T(8,128)(2,1)S(1)}, bf16[3,304,128]{2,1,0:T(8,128)(2,1)S(1)}, u32[]{:S(2)}, u32[]{:S(2)}) collective-permute-start(bf16[3,304,128]{2,1,0:T(8,128)(2,1)S(1)} %collective-permute-done.22), channel_id=1, source_target_pairs={{0,2},{2,4},{4,6},{6,7},{7,5},{5,3},{3,1},{1,0},{8,10},{10,12},{12... | collective-permute-start | bytes 700424 | tf_op jit(solution)/shard_map/ppermute | solution.py:252
  141.0 7.5 %copy-start.17 = (bf16[3,304,128]{2,1,0:T(8,128)(2,1)}, bf16[3,304,128]{2,1,0:T(8,128)(2,1)S(1)}, u32[]{:S(2)}) copy-start(bf16[3,304,128]{2,1,0:T(8,128)(2,1)S(1)} %collective-permute-done.23) | copy-start | bytes 700420
  141.0 10.0 %collective-permute-start.27 = (bf16[3,304,128]{2,1,0:T(8,128)(2,1)S(1)}, bf16[3,304,128]{2,1,0:T(8,128)(2,1)S(1)}, u32[]{:S(2)}, u32[]{:S(2)}) collective-permute-start(bf16[3,304,128]{2,1,0:T(8,128)(2,1)S(1)} %collective-permute-done.23), channel_id=1, source_target_pairs={{2,0},{4,2},{6,4},{7,6},{5,7},{3,5},{1,3},{0,1},{10,8},{12,10},{14... | collective-permute-start | bytes 700424 | tf_op jit(solution)/shard_map/ppermute | solution.py:251
  141.1 9.9 %copy-start.18 = (bf16[3,304,128]{2,1,0:T(8,128)(2,1)}, bf16[3,304,128]{2,1,0:T(8,128)(2,1)S(1)}, u32[]{:S(2)}) copy-start(bf16[3,304,128]{2,1,0:T(8,128)(2,1)S(1)} %collective-permute-done.28) | copy-start | bytes 700420
  141.1 9.9 %collective-permute-start.32 = (bf16[3,304,128]{2,1,0:T(8,128)(2,1)S(1)}, bf16[3,304,128]{2,1,0:T(8,128)(2,1)S(1)}, u32[]{:S(2)}, u32[]{:S(2)}) collective-permute-start(bf16[3,304,128]{2,1,0:T(8,128)(2,1)S(1)} %collective-permute-done.28), channel_id=1, source_target_pairs={{2,0},{4,2},{6,4},{7,6},{5,7},{3,5},{1,3},{0,1},{10,8},{12,10},{14... | collective-permute-start | bytes 700424 | tf_op jit(solution)/shard_map/ppermute | solution.py:252
  143.5 7.5 %copy-start.19 = (bf16[3,304,128]{2,1,0:T(8,128)(2,1)}, bf16[3,304,128]{2,1,0:T(8,128)(2,1)S(1)}, u32[]{:S(2)}) copy-start(bf16[3,304,128]{2,1,0:T(8,128)(2,1)S(1)} %collective-permute-done.25) | copy-start | bytes 700420
  143.5 10.0 %collective-permute-start.29 = (bf16[3,304,128]{2,1,0:T(8,128)(2,1)S(1)}, bf16[3,304,128]{2,1,0:T(8,128)(2,1)S(1)}, u32[]{:S(2)}, u32[]{:S(2)}) collective-permute-start(bf16[3,304,128]{2,1,0:T(8,128)(2,1)S(1)} %collective-permute-done.25), channel_id=1, source_target_pairs={{0,2},{2,4},{4,6},{6,7},{7,5},{5,3},{3,1},{1,0},{8,10},{10,12},{12... | collective-permute-start | bytes 700424 | tf_op jit(solution)/shard_map/ppermute | solution.py:251
  148.5 10.0 %collective-permute-start.30 = (bf16[3,304,128]{2,1,0:T(8,128)(2,1)S(1)}, bf16[3,304,128]{2,1,0:T(8,128)(2,1)S(1)}, u32[]{:S(2)}, u32[]{:S(2)}) collective-permute-start(bf16[3,304,128]{2,1,0:T(8,128)(2,1)S(1)} %collective-permute-done.26), channel_id=1, source_target_pairs={{0,2},{2,4},{4,6},{6,7},{7,5},{5,3},{3,1},{1,0},{8,10},{10,12},{12... | collective-permute-start | bytes 700424 | tf_op jit(solution)/shard_map/ppermute | solution.py:252
  151.0 7.5 %collective-permute-start.31 = (bf16[3,304,128]{2,1,0:T(8,128)(2,1)S(1)}, bf16[3,304,128]{2,1,0:T(8,128)(2,1)S(1)}, u32[]{:S(2)}, u32[]{:S(2)}) collective-permute-start(bf16[3,304,128]{2,1,0:T(8,128)(2,1)S(1)} %collective-permute-done.27), channel_id=1, source_target_pairs={{2,0},{4,2},{6,4},{7,6},{5,7},{3,5},{1,3},{0,1},{10,8},{12,10},{14... | collective-permute-start | bytes 700424 | tf_op jit(solution)/shard_map/ppermute | solution.py:251
  151.0 9.0 %collective-permute-start.34 = (bf16[3,304,128]{2,1,0:T(8,128)(2,1)S(1)}, bf16[3,304,128]{2,1,0:T(8,128)(2,1)S(1)}, u32[]{:S(2)}, u32[]{:S(2)}) collective-permute-start(bf16[3,304,128]{2,1,0:T(8,128)(2,1)S(1)} %collective-permute-done.32), channel_id=1, source_target_pairs={{2,0},{4,2},{6,4},{7,6},{5,7},{3,5},{1,3},{0,1},{10,8},{12,10},{14... | collective-permute-start | bytes 700424 | tf_op jit(solution)/shard_map/ppermute | solution.py:255
  153.5 8.3 %collective-permute-start.33 = (bf16[3,304,128]{2,1,0:T(8,128)(2,1)S(1)}, bf16[3,304,128]{2,1,0:T(8,128)(2,1)S(1)}, u32[]{:S(2)}, u32[]{:S(2)}) collective-permute-start(bf16[3,304,128]{2,1,0:T(8,128)(2,1)S(1)} %collective-permute-done.29), channel_id=1, source_target_pairs={{0,2},{2,4},{4,6},{6,7},{7,5},{5,3},{3,1},{1,0},{8,10},{10,12},{12... | collective-permute-start | bytes 700424 | tf_op jit(solution)/shard_map/ppermute | solution.py:255
  172.1 1.3 copy-start.3
  (14 other events, 12.5 us)
